TPU v7x, 32 devices: a whole 2x2x4 slice. The times are simulated.
32 devices in a mesh: shard: 8 (over y, x, core), seq: 4 (over z).
Axes of the slice: x: 2, y: 2, z: 4, core: 2. Of those that a mesh axis runs over, the one named last changes fastest.
Arguments:
- tokens: bfloat16 [8, 28, 112, 512], P('shard', 'seq'), may hold values from -6 to 6
- regions: int32 [8, 28, 112], P('shard'), may hold values from 0 to 8, as said below
- cotangent: bfloat16 [8, 28, 112, 512], P('shard', 'seq'), may hold values from -6 to 6
- gain_one: bfloat16 [512], P('shard'), may hold values from 0.5 to 1.5
- bias_one: bfloat16 [512], P('shard'), may hold values from -1 to 1
- w_qkv: bfloat16 [512, 1536], P('shard'), may hold values from -0.25 to 0.25
- bias_qv: bfloat16 [2, 512], P(None, 'shard'), may hold values from -1 to 1
- table: bfloat16 [169, 16], P(None, 'shard'), may hold values from -4 to 4
- w_proj: bfloat16 [512, 512], P('shard'), may hold values from -1 to 1
- bias_proj: bfloat16 [512], P('shard'), may hold values from -1 to 1
- gain_two: bfloat16 [512], P('shard'), may hold values from 0.5 to 1.5
- bias_two: bfloat16 [512], P('shard'), may hold values from -1 to 1
- w_in: bfloat16 [512, 2048], P('shard'), may hold values from -0.25 to 0.25
- bias_in: bfloat16 [2048], P('shard'), may hold values from -1 to 1
- w_out: bfloat16 [2048, 512], P('shard'), may hold values from -0.125 to 0.125
- bias_out: bfloat16 [512], P('shard'), may hold values from -1 to 1
Outputs:
- output: float32 [8, 28, 112, 512], P('shard', 'seq')
- grad_tokens: float32 [8, 28, 112, 512], P('shard', 'seq')
- grad_gain_one: float32 [512], P('shard')
- grad_bias_one: float32 [512], P('shard')
- grad_w_qkv: float32 [512, 1536], P('shard')
- grad_bias_qv: float32 [2, 512], P(None, 'shard')
- grad_table: float32 [169, 16], P(None, 'shard')
- grad_w_proj: float32 [512, 512], P('shard')
- grad_bias_proj: float32 [512], P('shard')
- grad_gain_two: float32 [512], P('shard')
- grad_bias_two: float32 [512], P('shard')
- grad_w_in: float32 [512, 2048], P('shard')
- grad_bias_in: float32 [2048], P('shard')
- grad_w_out: float32 [2048, 512], P('shard')
- grad_bias_out: float32 [512], P('shard')
Inputs may be any that keep to these rules, and one draw needn't show every extreme that they name: `regions`: tokens of one window attend to each other only where their labels are equal.
All inputs are finite; a program needn't handle non-finite values.
Results may differ from a plain program's by a relative error of at most 0.019.
Values may be sent and summed in bfloat16 or wider, within the bound.
No kernel may reach another device: no remote copies, remote signals or barrier semaphores. Data moves between devices by JAX's collectives and lax.ppermute only.
A program may use at most 128 MiB of HBM per device.

v0:
```python
import jax
import jax.numpy as jnp
from jax import lax
from jax.experimental import pallas as pl
from jax.experimental.pallas import tpu as pltpu
from jax.sharding import PartitionSpec as P

D = 512
HEADS = 16
HEAD = 32
WIN = 7
SHIFT = 3
FF = 2048
WIDTH = 112
WINDOWS = WIDTH // WIN
SLOT = 8
PLACES = WIN * SLOT
GROUP = 8
GROUPS = HEADS // GROUP
QUAD = 4
QUADS = HEADS // QUAD
FEAT = QUAD * HEAD
LANES = QUAD * PLACES
TOKENS = WIN * WIDTH
PADDED = WINDOWS * PLACES
TAB = 1536
TAB_USED = 768
SMALL = 32
EPS = 1e-05
SCALE = HEAD**-0.5
BF = jnp.bfloat16
F32 = jnp.float32
VMEM_LIMIT = 60 * 1024 * 1024


def shifted_2(value, axis, by):
    peers = lax.axis_size(axis)
    return lax.ppermute(value, axis, [(i, (i + by) % peers) for i in range(peers)])


def dot(left, right, dims=((1,), (0,))):
    return lax.dot_general(left, right, (dims, ((), ())), preferred_element_type=F32)


def dot_nt(left, right):
    return dot(left, right, ((1,), (1,)))


def dot_tn(left, right):
    return dot(left, right, ((0,), (0,)))


def iota(shape, axis):
    return lax.broadcasted_iota(jnp.int32, shape, axis)


def one_hot(condition):
    return jnp.where(condition, 1.0, 0.0).astype(BF)


def column_places():
    slot = iota((WINDOWS * SLOT, WIDTH), 0)
    column = iota((WINDOWS * SLOT, WIDTH), 1)
    place = slot & (SLOT - 1)
    wanted = (slot >> 3) * WIN + place + SHIFT
    wanted = jnp.where(wanted >= WIDTH, wanted - WIDTH, wanted)
    return one_hot((wanted == column) & (place < WIN))


def places_column():
    slot = iota((WIDTH, WINDOWS * SLOT), 1)
    column = iota((WIDTH, WINDOWS * SLOT), 0)
    place = slot & (SLOT - 1)
    wanted = (slot >> 3) * WIN + place + SHIFT
    wanted = jnp.where(wanted >= WIDTH, wanted - WIDTH, wanted)
    return one_hot((wanted == column) & (place < WIN))


def head_masks():
    feature = iota((1, FEAT), 1) >> 5
    return [jnp.where(feature == h, 1.0, 0.0).astype(F32) for h in range(QUAD)]


def spread(values, masks):
    return jnp.concatenate([values * mask for mask in masks], 0).astype(BF)


def own_heads(values):
    feature = iota((PLACES, FEAT), 1) >> 5
    out = values[:PLACES]
    for h in range(1, QUAD):
        out = jnp.where(feature == h, values[h * PLACES : (h + 1) * PLACES], out)
    return out


def table_pick(row_axis, quad, backwards):
    shape = (TAB_USED, LANES) if row_axis == 0 else (LANES, TAB_USED)
    lane = iota(shape, row_axis)
    pair = iota(shape, 1 - row_axis)
    head = jnp.zeros(shape, jnp.int32)
    for h in range(1, QUAD):
        head += jnp.where(pair >= h * PLACES, 1, 0)
    place = pair - head * PLACES
    row, column = place >> 3, place & (SLOT - 1)
    entry = row * (2 * WIN - 1) + column
    if backwards:
        entry = (WIN - 1) * 2 * WIN - entry
    held = head + quad % (GROUP // QUAD) * QUAD
    match = ((lane >> 3) == entry) & ((lane & 7) == held)
    return one_hot(match & (column < WIN))


def norm_stats(values):
    average = jnp.mean(values, -1, keepdims=True)
    centered = values - average
    variance = jnp.mean(centered * centered, -1, keepdims=True)
    scale = lax.rsqrt(variance + EPS)
    return centered * scale, scale


def norm_back(grad, normed, scale, gain):
    scaled = grad * gain
    first = jnp.mean(scaled, -1, keepdims=True)
    second = jnp.mean(scaled * normed, -1, keepdims=True)
    return scale * (scaled - first - normed * second)


def whole(memory=pltpu.VMEM):
    return pl.BlockSpec(memory_space=memory)


def kernel_call(
    body, outs, ins, scratch=(), smem=0, apart=0, grid=None, in_blocks=None, out_blocks=None
):
    in_specs = [whole(pltpu.SMEM)] * smem
    in_specs += in_blocks or [whole()] * (len(ins) - smem - apart) + [whole(pl.ANY)] * apart
    options = {"grid": grid} if grid else {}
    return pl.pallas_call(
        body,
        out_shape=tuple(outs),
        in_specs=in_specs,
        out_specs=tuple(out_blocks or [whole()] * len(outs)),
        scratch_shapes=list(scratch),
        cost_estimate=pl.CostEstimate(flops=1024, bytes_accessed=1024, transcendentals=0),
        compiler_params=pltpu.CompilerParams(vmem_limit_bytes=VMEM_LIMIT),
        **options,
    )(*ins)


def like(shape, dtype):
    return jax.ShapeDtypeStruct(shape, dtype)


def place(vector, lanes, me):
    w = vector.shape[1]
    pick = one_hot(iota((w, lanes), 1) == iota((w, lanes), 0) + me * w)
    wide = jnp.broadcast_to(vector, (8, w))
    return dot(wide.astype(BF), pick)[0:1]


def mine(row, w, me):
    lanes = row.shape[1]
    pick = one_hot(iota((lanes, w), 0) == iota((lanes, w), 1) + me * w)
    wide = jnp.broadcast_to(row, (8, lanes))
    return dot(wide.astype(BF), pick)[0:1]


def padded(rows, height):
    total = sum(r.shape[0] for r in rows)
    return jnp.concatenate(rows + [jnp.zeros((height - total, D), F32)], 0).astype(BF)


def pack_body(
    me_ref, g1, b1, wqkv, bqv, table, wproj, bproj, g2, b2, win, bin_, wout, bout, attn, mlp
):
    depth = wqkv.shape[0]
    me = me_ref[0]
    for c in range(3):
        attn[c * depth : (c + 1) * depth, :] = wqkv[:, c * D : (c + 1) * D]
    rows = [place(v, D, me) for v in (g1[...], b1[...], bqv[0:1, :], bqv[1:2, :])]
    held, entries = table.shape
    lane = iota((entries, TAB), 1)
    spot = iota((entries, TAB), 0) * GROUP + TAB - (WIN - 1) * 2 * WIN * GROUP
    spot = jnp.where(spot >= TAB, spot - TAB, spot)
    values = table[...].astype(F32).T
    groups = [jnp.zeros((1, TAB), F32) for _ in range(GROUPS)]
    for h in range(held):
        head = me * held + h
        inside = lane == spot + (head & (GROUP - 1))
        row = jnp.sum(jnp.where(inside, values[:, h : h + 1], 0.0), 0, keepdims=True)
        for g in range(GROUPS):
            groups[g] = groups[g] + jnp.where((head >> 3) == g, row, 0.0)
    for g in range(GROUPS):
        rows += [groups[g][:, c * D : (c + 1) * D] for c in range(TAB // D)]
    attn[3 * depth :, :] = padded(rows, SMALL)
    for c in range(FF // D):
        mlp[c * depth : (c + 1) * depth, :] = win[:, c * D : (c + 1) * D]
    mlp[4 * depth : 8 * depth, :] = wout[...]
    mlp[8 * depth : 9 * depth, :] = wproj[...]
    hidden_bias = place(bin_[...], FF, me)
    rows = [place(v, D, me) for v in (g2[...], b2[...], bout[...], bproj[...])]
    rows += [hidden_bias[:, c * D : (c + 1) * D] for c in range(FF // D)]
    mlp[9 * depth :, :] = padded(rows, SMALL)


def join_halves(late, half, back, both):
    rows = half.shape[0]
    both[pl.ds(pl.multiple_of(late * rows, 16), rows), :] = half[...]
    both[pl.ds(pl.multiple_of((1 - late) * rows, 16), rows), :] = back[...]


def unpack_attn_body(me_ref, half, back, g1, b1, wqkv, bqv, table, attn):
    depth = wqkv.shape[0]
    me = me_ref[0]
    join_halves(me_ref[1], half, back, attn)
    for c in range(3):
        wqkv[:, c * D : (c + 1) * D] = attn[c * depth : (c + 1) * depth, :].astype(F32)
    small = attn[3 * depth :, :].astype(F32)
    g1[...] = mine(small[0:1], depth, me)
    b1[...] = mine(small[1:2], depth, me)
    bqv[0:1, :] = mine(small[2:3], depth, me)
    bqv[1:2, :] = mine(small[3:4], depth, me)
    held, entries = table.shape
    lane = iota((entries, TAB), 1)
    spot = (entries - 1 - iota((entries, TAB), 0)) * GROUP
    parts = TAB // D
    rows = [
        jnp.concatenate([small[4 + g * parts + c : 5 + g * parts + c] for c in range(parts)], 1)
        for g in range(GROUPS)
    ]
    which = iota((entries, held), 1)
    total = jnp.zeros((entries, held), F32)
    for h in range(held):
        head = me * held + h
        row = rows[0]
        for g in range(1, GROUPS):
            row = jnp.where((head >> 3) == g, rows[g], row)
        inside = lane == spot + (head & (GROUP - 1))
        column = jnp.sum(jnp.where(inside, row, 0.0), 1, keepdims=True)
        total = jnp.where(which == h, column, total)
    table[...] = total.T


def unpack_mlp_body(
    me_ref, half_a, back_a, half_b, back_b, wproj, bproj, g2, b2, win, bin_, wout, bout, a, b
):
    depth = win.shape[0]
    me = me_ref[0]
    join_halves(me_ref[1], half_a, back_a, a)
    join_halves(me_ref[1], half_b, back_b, b)
    for c in range(FF // D):
        win[:, c * D : (c + 1) * D] = a[c * depth : (c + 1) * depth, :].astype(F32)
    wout[...] = b[: 4 * depth, :].astype(F32)
    wproj[...] = b[4 * depth :, :].astype(F32)
    small = a[4 * depth :, :].astype(F32)
    g2[...] = mine(small[0:1], depth, me)
    b2[...] = mine(small[1:2], depth, me)
    bout[...] = mine(small[2:3], depth, me)
    bproj[...] = mine(small[3:4], depth, me)
    hidden = jnp.concatenate([small[4 + c : 5 + c] for c in range(FF // D)], 1)
    bin_[...] = mine(hidden, depth * FF // D, me)


def put_shares(me, same, other, start, values, first=0):
    core, chip = me & 1, me >> 1
    rows = values.shape[1]
    for c in range(values.shape[0] // 2):
        one, two = values[2 * c], values[2 * c + 1]
        q = (first // 2 + c) ^ chip
        same[q, start : start + rows, :] = jnp.where(core == 0, one, two).astype(BF)
        other[q, start : start + rows, :] = jnp.where(core == 0, two, one).astype(BF)


def put_smalls(same, other, start, rows):
    block = padded(rows, SMALL)
    for q in range(same.shape[0]):
        same[q, start:, :] = block
        other[q, start:, :] = block


def exchange(value, axis, mask):
    peers = lax.axis_size(axis)
    return lax.ppermute(value, axis, [(i, i ^ mask) for i in range(peers)])


def gather_pieces(slab):
    chips = lax.axis_size("shard") // 2
    pieces = [None] * (2 * chips)
    for q in range(chips):
        pieces[2 * q] = exchange(slab, "shard", 2 * q) if q else slab
    for q in range(chips):
        pieces[2 * q + 1] = exchange(pieces[2 * q], "shard", 1)
    return pieces


def add_pair(here, came):
    return (here.astype(F32) + came.astype(F32)).astype(BF)


def add_cores(same, other):
    came = exchange(other, "shard", 1)
    return [add_pair(same[q], came[q]) for q in range(same.shape[0])]


def to_chips(sums):
    return [sums[0]] + [exchange(sums[q], "shard", 2 * q) for q in range(1, len(sums))]


def add_chips(late, parts):
    half = parts[0].shape[0] // 2
    out = []
    for start in (late * half, (1 - late) * half):
        total = 0.0
        for part in parts:
            total += lax.dynamic_slice_in_dim(part, start, half, 0).astype(F32)
        out.append(total.astype(BF))
    return out


def seq_rest(half):
    reach = 4
    while reach < lax.axis_size("seq"):
        half = add_pair(half, exchange(half, "seq", reach))
        reach *= 2
    return half


def tie(first, second):
    first, second = list(first), list(second)
    out = lax.optimization_barrier((*first, *second))
    return list(out[: len(first)]), list(out[len(first) :])


def block_of(slab, c, depth):
    return slab[:, c * depth : (c + 1) * depth, :].reshape(D, D)


def smalls_of(slab, start):
    return jnp.sum(slab[:, start:, :].astype(F32), 0)


def project_body(me_ref, tokens, halo, *refs):
    shards = len(refs) - 7
    pieces = refs[:shards]
    normed_win, query, key, value, slab, wide, sems = refs[shards:]
    copies = [
        pltpu.make_async_copy(piece, slab.at[me_ref[0] ^ p], sems.at[p])
        for p, piece in enumerate(pieces)
    ]
    for copy in copies:
        copy.start()
    columns = column_places()
    own = WIN - SHIFT
    for copy in copies:
        copy.wait()
    depth = (slab.shape[1] - SMALL) // 3
    small = smalls_of(slab, 3 * depth)
    gain, offset, bias_q, bias_v = (small[r : r + 1] for r in range(4))
    for r in range(WIN):
        x = (tokens[SHIFT + r] if r < own else halo[r - own]).astype(F32)
        normed, _ = norm_stats(x)
        low = (normed * gain + offset).astype(BF)
        wide[:, r] = dot(columns, low).reshape(WINDOWS, SLOT, D)
    normed_win[...] = wide[...].reshape(PADDED, D).astype(BF)
    query[...] = (dot(normed_win[...], block_of(slab, 0, depth)) + bias_q).astype(BF)
    key[...] = dot(normed_win[...], block_of(slab, 1, depth)).astype(BF)
    value[...] = (dot(normed_win[...], block_of(slab, 2, depth)) + bias_v).astype(BF)


def attn_forward_body(slab, reg_rows, reg_lanes, query, key, value, probs, restored, wide, bias):
    n = pl.program_id(0)

    @pl.when(n == 0)
    def _():
        depth = (slab.shape[1] - SMALL) // 3
        small = smalls_of(slab, 3 * depth)
        parts = TAB // D
        empty = (iota((PLACES, LANES), 0) & (SLOT - 1)) == WIN
        turned = []
        for g in range(GROUPS):
            first = 4 + g * parts
            row = jnp.concatenate([small[first + c : first + c + 1] for c in range(parts)], 1)
            row = jnp.broadcast_to(row, (SLOT, TAB))
            row = pltpu.roll(row, 0, 1, stride=GROUP, stride_axis=0)
            rows = [pltpu.roll(row, (2 * WIN - 1) * GROUP * r, 1)[:, :TAB_USED] for r in range(WIN)]
            turned.append(jnp.concatenate(rows, 0).astype(BF))
        for half in range(GROUP // QUAD):
            pick = table_pick(0, half, False)
            for g in range(GROUPS):
                picked = dot(turned[g], pick)
                bias[g * (GROUP // QUAD) + half] = jnp.where(empty, -1e30, picked)

    masks = head_masks()
    penalty = [
        jnp.where(reg_rows[s][:, 0:1] != reg_lanes[s], -100.0, 0.0) for s in range(2)
    ]
    for u in range(QUADS):
        feats = slice(u * FEAT, (u + 1) * FEAT)
        q2 = query[:, feats].astype(F32)
        k2 = key[:, feats].astype(F32)
        v2 = value[:, feats].astype(F32)
        held = []
        for s in range(2):
            part = slice(s * PLACES, (s + 1) * PLACES)
            k, v = k2[part].astype(BF), v2[part].astype(BF)
            logits = dot_nt(k, spread(q2[part], masks)) * SCALE + bias[u] + penalty[s]
            top = jnp.max(logits, 0, keepdims=True)
            powers = jnp.exp(logits - top)
            p = powers * (1.0 / jnp.sum(powers, 0, keepdims=True))
            held.append(p)
            o = own_heads(dot_tn(p.astype(BF), v))
            wide[2 * n + s, :, :, feats] = o.reshape(WIN, SLOT, FEAT)
        probs[0, u] = jnp.concatenate(held, 0).astype(BF)

    @pl.when(n == pl.num_programs(0) - 1)
    def _():
        back = places_column()
        for r in range(WIN):
            here = wide[:, r].reshape(WINDOWS * SLOT, D).astype(BF)
            restored[r * WIDTH : (r + 1) * WIDTH, :] = dot(back, here).astype(BF)


def gelu_parts(h):
    size = jnp.abs(h) * (0.5**0.5)
    t = 1.0 / (1.0 + 0.3275911 * size)
    bell = jnp.exp(-0.5 * h * h)
    poly = t * (
        0.254829592
        + t * (-0.284496736 + t * (1.421413741 + t * (-1.453152027 + t * 1.061405429)))
    )
    tail = 0.5 * poly * bell
    upto = jnp.where(h >= 0, 1.0 - tail, tail)
    return upto, bell * 0.3989422804014327


def mlp_body(
    me_ref,
    tokens,
    token_halo,
    cotangent,
    cot_halo,
    slab,
    restored,
    kept,
    sent,
    grad_mixed,
    grad_win,
    same_a,
    other_a,
    same_b,
    other_b,
    normed_low,
    cot,
    mixed,
    out_sum,
    back_sum,
    wide,
):
    me = me_ref[0]
    shards, height = slab.shape[:2]
    depth = (height - SMALL) // 9
    span = shards * D // FF
    small = smalls_of(slab, 9 * depth)
    gain, offset, bias_o, bias_proj = (small[r : r + 1] for r in range(4))
    own = WIN - SHIFT
    branch = dot(restored[...], block_of(slab, 8, depth)) + bias_proj
    for r in range(WIN):
        part = slice(r * WIDTH, (r + 1) * WIDTH)
        cot[part, :] = cotangent[SHIFT + r] if r < own else cot_halo[r - own]
        x = (tokens[SHIFT + r] if r < own else token_halo[r - own]).astype(F32)
        mixed[part, :] = x + branch[part]
    normed, _ = norm_stats(mixed[...])
    normed_low[...] = (normed * gain + offset).astype(BF)
    vectors = []
    for c in range(FF // D):
        w_in = block_of(slab, c, depth)
        w_out = slab[c * span : (c + 1) * span, 4 * depth : 8 * depth, :].reshape(D, D)
        hidden = dot(normed_low[...], w_in) + small[4 + c : 5 + c]
        upto, density = gelu_parts(hidden)
        active = (hidden * upto).astype(BF)
        slope = upto + hidden * density
        grad = (dot_nt(cot[...], w_out) * slope).astype(BF)
        forward = dot(active, w_out)
        backward = dot_nt(grad, w_in)
        if c == 0:
            out_sum[...] = forward
            back_sum[...] = backward
        else:
            out_sum[...] += forward
            back_sum[...] += backward
        vectors.append(jnp.sum(grad.astype(F32), 0, keepdims=True))
        put_shares(
            me, same_a, other_a, c * depth, dot_tn(normed_low[...], grad).reshape(shards, depth, D)
        )
        put_shares(
            me,
            same_b,
            other_b,
            0,
            dot_tn(active, cot[...]).reshape(span, 4 * depth, D),
            c * span,
        )
    result = mixed[...] + out_sum[...] + bias_o
    kept[...] = result[: own * WIDTH]
    sent[...] = result[own * WIDTH :].astype(BF)
    normed, scale = norm_stats(mixed[...])
    g = back_sum[...]
    gain_sum = jnp.sum(g * normed, 0, keepdims=True)
    offset_sum = jnp.sum(g, 0, keepdims=True)
    cot_sum = jnp.sum(cot[...].astype(F32), 0, keepdims=True)
    grad_mixed[...] = cot[...].astype(F32) + norm_back(g, normed, scale, gain)

    branch = grad_mixed[...].astype(BF)
    branch_sum = jnp.sum(branch.astype(F32), 0, keepdims=True)
    proj = dot_tn(restored[...], branch).reshape(shards, depth, D)
    put_shares(me, same_b, other_b, 4 * depth, proj)
    put_smalls(same_a, other_a, 4 * depth, [gain_sum, offset_sum, cot_sum, branch_sum] + vectors)
    grad_att = dot_nt(branch, block_of(slab, 8, depth)).astype(BF)
    columns = column_places()
    for r in range(WIN):
        wide[:, r] = dot(columns, grad_att[r * WIDTH : (r + 1) * WIDTH]).reshape(WINDOWS, SLOT, D)
    grad_win[...] = wide[...].reshape(PADDED, D).astype(BF)


def attn_backward_body(query, key, value, probs, grad_win, came, out, pairs):
    @pl.when(pl.program_id(0) == 0)
    def _():
        pairs[...] = came[...]

    masks = head_masks()
    for u in range(QUADS):
        feats = slice(u * FEAT, (u + 1) * FEAT)
        q2 = query[:, feats].astype(F32)
        k2 = key[:, feats].astype(F32)
        v2 = value[:, feats].astype(F32)
        go2 = grad_win[:, feats].astype(F32)
        p2 = probs[0, u].astype(F32)
        held = []
        total = pairs[u]
        for s in range(2):
            part = slice(s * PLACES, (s + 1) * PLACES)
            k, v, p_low = (a[part].astype(BF) for a in (k2, v2, p2))
            p = p2[part]
            go_big = spread(go2[part], masks)
            dp = dot_nt(v, go_big)
            dv = dot(p_low, go_big)
            inner = jnp.sum(p * dp, 0, keepdims=True)
            ds = (p * (dp - inner)).astype(BF)
            total += ds.astype(F32)
            dk = dot(ds, spread(q2[part], masks)) * SCALE
            dq = own_heads(dot_tn(ds, k)) * SCALE
            held.append((dq, dk, dv))
        pairs[u] = total
        for c in range(3):
            both = jnp.concatenate([held[0][c], held[1][c]], 0).astype(BF)
            out[:, c * D + u * FEAT : c * D + (u + 1) * FEAT] = both


def attn_last_body(
    me_ref,
    grad_mixed,
    tokens,
    halo,
    slab,
    normed_win,
    pairs,
    *refs,
):
    grads = refs[:-5]
    kept, sent, same, other, wide = refs[-5:]
    me = me_ref[0]
    shards = slab.shape[0]
    depth = (slab.shape[1] - SMALL) // 3
    small = smalls_of(slab, 3 * depth)
    gain = small[0:1]
    own = WIN - SHIFT
    vectors = []
    for c in range(3):
        cols = slice(c * D, (c + 1) * D)
        g = jnp.concatenate([part[:, cols] for part in grads], 0)
        if c != 1:
            vectors.append(jnp.sum(g.astype(F32), 0, keepdims=True))
        put_shares(
            me, same, other, c * depth, dot_tn(normed_win[...], g).reshape(shards, depth, D)
        )
        part = dot_nt(g, block_of(slab, c, depth))
        total = part if c == 0 else total + part
    wide[...] = total.reshape(WINDOWS, WIN, SLOT, D)
    back = places_column()
    gain_sum = jnp.zeros((1, D), F32)
    bias_sum = jnp.zeros((1, D), F32)
    for r in range(WIN):
        here = wide[:, r].reshape(WINDOWS * SLOT, D).astype(BF)
        g = dot(back, here)
        x = (tokens[SHIFT + r] if r < own else halo[r - own]).astype(F32)
        normed, scale = norm_stats(x)
        gain_sum += jnp.sum(g * normed, 0, keepdims=True)
        bias_sum += jnp.sum(g, 0, keepdims=True)
        grad = grad_mixed[r * WIDTH : (r + 1) * WIDTH, :] + norm_back(g, normed, scale, gain)
        if r < own:
            kept[r * WIDTH : (r + 1) * WIDTH, :] = grad
        else:
            sent[(r - own) * WIDTH : (r - own + 1) * WIDTH, :] = grad.astype(BF)

    rows = [gain_sum, bias_sum, vectors[0], vectors[1]]
    halves = GROUP // QUAD
    picks = [table_pick(1, half, True) for half in range(halves)]
    for g in range(GROUPS):
        laid = jnp.zeros((PLACES, TAB_USED), F32)
        for half in range(halves):
            total = pairs[g * halves + half]
            high = total.astype(BF)
            low = (total - high.astype(F32)).astype(BF)
            laid += dot(high, picks[half]) + dot(low, picks[half])
        laid = jnp.concatenate([laid, jnp.zeros((PLACES, TAB - TAB_USED), F32)], 1)
        total = jnp.zeros((SLOT, TAB), F32)
        for r in range(WIN):
            total += pltpu.roll(
                laid[r * SLOT : (r + 1) * SLOT], (2 * WIN - 1) * GROUP * r, 1
            )
        total = pltpu.roll(total, 0, 1, stride=GROUP, stride_axis=0)
        row = jnp.sum(total, 0, keepdims=True)
        rows += [row[:, c * D : (c + 1) * D] for c in range(TAB // D)]
    put_smalls(same, other, 3 * depth, rows)


def region_views(regions, rows, place):
    here = lax.dynamic_slice_in_dim(regions[0], place * rows, rows, 0)
    windows = here.reshape(WIN, WINDOWS, WIN).transpose(1, 0, 2)
    windows = jnp.pad(windows, ((0, 0), (0, 0), (0, SLOT - WIN))).astype(F32)
    windows = windows.reshape(WINDOWS, PLACES)
    by_row = jnp.broadcast_to(windows[:, :, None], (WINDOWS, PLACES, 128))
    by_lane = jnp.tile(windows, (1, QUAD))
    return by_row, by_lane[:, None, :]


def per_device(
    tokens,
    regions,
    cotangent,
    gain_one,
    bias_one,
    w_qkv,
    bias_qv,
    table,
    w_proj,
    bias_proj,
    gain_two,
    bias_two,
    w_in,
    bias_in,
    w_out,
    bias_out,
):
    images, local_rows, columns, _ = tokens.shape
    assert images == 1 and local_rows == WIN and columns == WIDTH
    shards = lax.axis_size("shard")
    me = lax.axis_index("shard").astype(jnp.int32)
    seq = lax.axis_index("seq").astype(jnp.int32)
    where = jnp.stack([me, seq & 1])
    chips = shards // 2
    depth = D // shards
    own = WIN - SHIFT
    attn_params = (gain_one[None], bias_one[None], w_qkv, bias_qv, table.T)
    mlp_params = (
        w_proj,
        bias_proj[None],
        gain_two[None],
        bias_two[None],
        w_in,
        bias_in[None],
        w_out,
        bias_out[None],
    )
    late = seq & 1
    attn_slab, mlp_slab = kernel_call(
        pack_body,
        [like((3 * depth + SMALL, D), BF), like((9 * depth + SMALL, D), BF)],
        (where, *attn_params, *mlp_params),
        smem=1,
    )
    pieces = gather_pieces(attn_slab)
    mlp_all = lax.all_gather(mlp_slab, "shard")
    tokens_here = tokens[0]
    token_halo = shifted_2(tokens_here[:SHIFT], "seq", -1)
    cot_here = cotangent[0]
    cot_halo = shifted_2(cot_here[:SHIFT], "seq", -1)
    by_row, by_lane = region_views(regions, local_rows, seq)

    normed_win, query, key, value, attn_all = kernel_call(
        project_body,
        [like((PADDED, D), BF)] * 4 + [like((shards, *attn_slab.shape), BF)],
        (where, tokens_here, token_halo, *pieces),
        scratch=[
            pltpu.VMEM((WINDOWS, WIN, SLOT, D), F32),
            pltpu.SemaphoreType.DMA((shards,)),
        ],
        smem=1,
        apart=shards,
    )
    pair_rows = 2 * PLACES
    steps = WINDOWS // 2

    def rows_from(first, width=D):
        return pl.BlockSpec((pair_rows, width), lambda i: (first + i, 0))

    def probs_from(first):
        return pl.BlockSpec((1, QUADS, pair_rows, LANES), lambda i: (first + i, 0, 0, 0))

    def fixed(shape):
        return pl.BlockSpec(shape, lambda i: (0,) * len(shape))

    probs, restored = kernel_call(
        attn_forward_body,
        [like((steps, QUADS, pair_rows, LANES), BF), like((TOKENS, D), BF)],
        (attn_all, by_row, by_lane, query, key, value),
        grid=(steps,),
        in_blocks=[
            fixed(attn_all.shape),
            pl.BlockSpec((2, *by_row.shape[1:]), lambda i: (i, 0, 0)),
            pl.BlockSpec((2, *by_lane.shape[1:]), lambda i: (i, 0, 0)),
            rows_from(0),
            rows_from(0),
            rows_from(0),
        ],
        out_blocks=[probs_from(0), fixed((TOKENS, D))],
        scratch=[
            pltpu.VMEM((WINDOWS, WIN, SLOT, D), F32),
            pltpu.VMEM((QUADS, PLACES, LANES), F32),
        ],
    )
    share_a = like((chips, 4 * depth + SMALL, D), BF)
    share_b = like((chips, 5 * depth, D), BF)
    out_kept, out_sent, grad_mixed, grad_win, same_a, other_a, same_b, other_b = kernel_call(
        mlp_body,
        [
            like((own * WIDTH, D), F32),
            like((SHIFT * WIDTH, D), BF),
            like((TOKENS, D), F32),
            like((PADDED, D), BF),
            share_a,
            share_a,
            share_b,
            share_b,
        ],
        (where, tokens_here, token_halo, cot_here, cot_halo, mlp_all, restored),
        scratch=[
            pltpu.VMEM((TOKENS, D), BF),
            pltpu.VMEM((TOKENS, D), BF),
            pltpu.VMEM((TOKENS, D), F32),
            pltpu.VMEM((TOKENS, D), F32),
            pltpu.VMEM((TOKENS, D), F32),
            pltpu.VMEM((WINDOWS, WIN, SLOT, D), F32),
        ],
        smem=1,
    )

    def backward(first, count, grad_win, came):
        sums = like((QUADS, PLACES, LANES), F32)
        return kernel_call(
            attn_backward_body,
            [like((count * pair_rows, 3 * D), BF), sums],
            (query, key, value, probs, grad_win, came),
            grid=(count,),
            in_blocks=[rows_from(first)] * 3
            + [probs_from(first), rows_from(first), fixed(sums.shape)],
            out_blocks=[rows_from(0, 3 * D), fixed(sums.shape)],
            )

    none = jnp.zeros((QUADS, PLACES, LANES), F32)
    count = steps // 2
    early, pairs = backward(0, count, grad_win, none)
    sums, (pairs,) = tie(add_cores(same_a, other_a) + add_cores(same_b, other_b), [pairs])
    parts_a, parts_b = to_chips(sums[:chips]), to_chips(sums[chips:])
    late_part, pairs = backward(count, count, grad_win, pairs)
    (out_halo, *parts_a), (pairs,) = tie([shifted_2(out_sent, "seq", 1), *parts_a], [pairs])
    tok_kept, tok_sent, attn_same, attn_other = kernel_call(
        attn_last_body,
        [
            like((own * WIDTH, D), F32),
            like((SHIFT * WIDTH, D), BF),
            like((chips, 3 * depth + SMALL, D), BF),
            like((chips, 3 * depth + SMALL, D), BF),
        ],
        (where, grad_mixed, tokens_here, token_halo, attn_all, normed_win, pairs, early, late_part),
        scratch=[pltpu.VMEM((WINDOWS, WIN, SLOT, D), F32)],
        smem=1,
    )
    tok_halo = shifted_2(tok_sent, "seq", 1)
    cores = exchange(attn_other, "shard", 1)
    keep, send = add_chips(late, parts_a)
    (send,), (cores,) = tie([send], [cores])
    near_a = exchange(send, "seq", 1)
    sums = [add_pair(attn_same[q], cores[q]) for q in range(chips)]
    sums, (near_a,) = tie(sums, [near_a])
    parts = to_chips(sums)
    half_a = add_pair(keep, near_a)
    (half_a,), parts_b = tie([half_a], parts_b)
    far_a = exchange(half_a, "seq", 2)
    keep_b, send_b = add_chips(late, parts_b)
    (keep_b, send_b), (far_a,) = tie([keep_b, send_b], [far_a])
    near_b = exchange(send_b, "seq", 1)
    half_a = seq_rest(add_pair(half_a, far_a))
    (half_a,), parts = tie([half_a], parts)
    back_a = exchange(half_a, "seq", 1)
    keep, send = add_chips(late, parts)
    (keep, send), (near_b,) = tie([keep, send], [near_b])
    near = exchange(send, "seq", 1)
    half_b = add_pair(keep_b, near_b)
    (half_b,), (near,) = tie([half_b], [near])
    far_b = exchange(half_b, "seq", 2)
    half = add_pair(keep, near)
    (half,), (far_b,) = tie([half], [far_b])
    far = exchange(half, "seq", 2)
    half_b = seq_rest(add_pair(half_b, far_b))
    (half_b,), (far,) = tie([half_b], [far])
    back_b = exchange(half_b, "seq", 1)
    half = seq_rest(add_pair(half, far))
    back = exchange(half, "seq", 1)
    mlp_grads = kernel_call(
        unpack_mlp_body,
        [like(p.shape, F32) for p in mlp_params],
        (where, half_a, back_a, half_b, back_b),
        scratch=[
            pltpu.VMEM((4 * depth + SMALL, D), BF),
            pltpu.VMEM((5 * depth, D), BF),
        ],
        smem=1,
    )
    attn_grads = kernel_call(
        unpack_attn_body,
        [like(p.shape, F32) for p in attn_params],
        (where, half, back),
        scratch=[pltpu.VMEM((3 * depth + SMALL, D), BF)],
        smem=1,
    )
    summed = [*attn_grads[:4], attn_grads[4].T, *mlp_grads]

    def joined(halo, kept):
        return jnp.concatenate([halo.astype(F32), kept], 0).reshape(tokens.shape)

    targets = (
        gain_one,
        bias_one,
        w_qkv,
        bias_qv,
        table,
        w_proj,
        bias_proj,
        gain_two,
        bias_two,
        w_in,
        bias_in,
        w_out,
        bias_out,
    )
    grads = [g.reshape(p.shape) for g, p in zip(summed, targets)]
    return (joined(out_halo, out_kept), joined(tok_halo, tok_kept), *grads)


def solution(mesh):
    return jax.shard_map(
        per_device,
        mesh=mesh,
        in_specs=(
            P("shard", "seq", None, None),
            P("shard", None, None),
            P("shard", "seq", None, None),
            P("shard"),
            P("shard"),
            P("shard", None),
            P(None, "shard"),
            P(None, "shard"),
            P("shard", None),
            P("shard"),
            P("shard"),
            P("shard"),
            P("shard", None),
            P("shard"),
            P("shard", None),
            P("shard"),
        ),
        out_specs=(
            P("shard", "seq", None, None),
            P("shard", "seq", None, None),
            P("shard"),
            P("shard"),
            P("shard", None),
            P(None, "shard"),
            P(None, "shard"),
            P("shard", None),
            P("shard"),
            P("shard"),
            P("shard"),
            P("shard", None),
            P("shard"),
            P("shard", None),
            P("shard"),
        ),
        check_vma=False,
    )
```

profile of v0, /device:TPU:0, one launch (start us, length us, event | category | flops | bytes accessed | tf_op | source)
XLA Modules:
  0.0 205.1 jit_solution(5376315831623482683)
XLA Ops:
  9.1 2.8 %shard_map.271 = (bf16[224,512]{1,0:T(8,128)(2,1)}, bf16[608,512]{1,0:T(8,128)(2,1)}) custom-call(s32[2]{0:T(128)} %pad_add_fusion.me_ref, bf16[1,64]{1,0:T(2,128)(2,1)} %bitcast.62, bf16[1,64]{1,0:T(2,128)(2,1)} %bitcast.63, bf16[64,1536]{1,0:T(8,128)(2,1)} %wqkv.1, bf16[2,64]{1,0:T(2,128)(2,1)} %bqv.1, bf16[2,169]{1,0:T(2,128)(2,1)} %bitcast.61, ...), custom_call_target="tpu_custom_call" | custom-call | flops 1024 | bytes 1024 | tf_op jit(solution)/shard_map/pallas_call | solution.py:138
  11.9 3.0 %collective-permute-start.3 = (bf16[224,512]{1,0:T(8,128)(2,1)}, bf16[224,512]{1,0:T(8,128)(2,1)S(1)}, u32[]{:S(2)}, u32[]{:S(2)}) collective-permute-start(bf16[224,512]{1,0:T(8,128)(2,1)} %get-tuple-element.98.refs_0_), channel_id=1, source_target_pairs={{0,8},{4,12},{8,0},{12,4},{16,24},{20,28},{24,16},{28,20},{1,9},{5... | collective-permute-start | bytes 688136 | tf_op jit(solution)/shard_map/ppermute | solution.py:283
  14.9 1.5 collective-permute-start.5
  17.5 4.1 %collective-permute-start = (bf16[3,112,512]{2,1,0:T(8,128)(2,1)S(1)}, bf16[3,112,512]{2,1,0:T(8,128)(2,1)S(1)}, u32[]{:S(2)}, u32[]{:S(2)}) collective-permute-start(bf16[3,112,512]{2,1,0:T(8,128)(2,1)S(1)} %slice_bitcast_fusion.1), channel_id=1, source_target_pairs={{0,3},{1,0},{2,1},{3,2},{4,7},{5,4},{6,5},{7,6},{8,11},{9,8},{10,9... | collective-permute-start | bytes 1032200 | tf_op jit(solution)/shard_map/ppermute | solution.py:38
  22.7 3.1 %collective-permute-start.1 = (bf16[3,112,512]{2,1,0:T(8,128)(2,1)S(1)}, bf16[3,112,512]{2,1,0:T(8,128)(2,1)S(1)}, u32[]{:S(2)}, u32[]{:S(2)}) collective-permute-start(bf16[3,112,512]{2,1,0:T(8,128)(2,1)S(1)} %slice_bitcast_fusion), channel_id=1, source_target_pairs={{0,3},{1,0},{2,1},{3,2},{4,7},{5,4},{6,5},{7,6},{8,11},{9,8},{10,9... | collective-permute-start | bytes 1032200 | tf_op jit(solution)/shard_map/ppermute | solution.py:38
  25.8 3.2 %collective-permute-done.5.refs_4_ = bf16[224,512]{1,0:T(8,128)(2,1)S(1)} collective-permute-done((bf16[224,512]{1,0:T(8,128)(2,1)}, bf16[224,512]{1,0:T(8,128)(2,1)S(1)}, u32[]{:S(2)}, u32[]{:S(2)}) %collective-permute-start.5) | collective-permute-done | bytes 229408 | tf_op jit(solution)/shard_map/ppermute | solution.py:283
  31.8 6.8 %shard_map.272 = (bf16[896,512]{1,0:T(8,128)(2,1)}, bf16[896,512]{1,0:T(8,128)(2,1)}, bf16[896,512]{1,0:T(8,128)(2,1)}, bf16[896,512]{1,0:T(8,128)(2,1)}, bf16[8,224,512]{2,1,0:T(8,128)(2,1)}) custom-call(s32[2]{0:T(128)} %pad_add_fusion.me_ref, bf16[7,112,512]{2,1,0:T(8,128)(2,1)} %bitcast.53, bf16[3,112,512]{2,1,0:T(8,128)(2,1)} %copy-done.1, ...), custom_call_target="tpu_custom_call" | custom-call | flops 1024 | bytes 1024 | tf_op jit(solution)/shard_map/pallas_call | solution.py:138
  39.6 21.9 %shard_map.273 = (bf16[8,4,112,224]{3,2,1,0:T(8,128)(2,1)}, bf16[784,512]{1,0:T(8,128)(2,1)}) custom-call(bf16[8,224,512]{2,1,0:T(8,128)(2,1)} %get-tuple-element.99.slab, f32[16,56,128]{2,1,0:T(8,128)} %broadcast_in_dim.39.reg_rows, f32[16,1,224]{2,1,0:T(1,128)} %tile.8.reg_lanes, bf16[896,512]{1,0:T(8,128)(2,1)} %get-tuple-element.100.query, ...), custom_call_target="tpu_custom_call" | custom-call | flops 1024 | bytes 1024 | tf_op jit(solution)/shard_map/pallas_call | solution.py:138
  62.2 24.1 %shard_map.274 = (f32[448,512]{1,0:T(8,128)}, bf16[336,512]{1,0:T(8,128)(2,1)}, f32[784,512]{1,0:T(8,128)}, bf16[896,512]{1,0:T(8,128)(2,1)}, bf16[4,288,512]{2,...) custom-call(s32[2]{0:T(128)} %pad_add_fusion.me_ref, ...), custom_call_target="tpu_custom_call" | custom-call | flops 1024 | bytes 1024 | tf_op jit(solution)/shard_map/pallas_call | solution.py:138
  86.8 1.8 collective-permute-start.9
  89.3 9.9 %shard_map.275 = (bf16[448,1536]{1,0:T(8,128)(2,1)}, f32[4,56,224]{2,1,0:T(8,128)}) custom-call(bf16[896,512]{1,0:T(8,128)(2,1)} %get-tuple-element.100.query, bf16[896,512]{1,0:T(8,128)(2,1)} %get-tuple-element.101.key, bf16[896,512]{1,0:T(8,128)(2,1)} %get-tuple-element.102.value, bf16[8,4,112,224]{3,2,1,0:T(8,128)(2,1)} %get-tuple-element.109.probs, ...), custom_call_target="tpu_custom_call" | custom-call | flops 1024 | bytes 1024 | tf_op jit(solution)/shard_map/pallas_call | solution.py:138
  99.2 2.5 %fusion.7 = (bf16[288,512]{1,0:T(8,128)(2,1)S(1)}, bf16[288,512]{1,0:T(8,128)(2,1)}, bf16[288,512]{1,0:T(8,128)(2,1)}, bf16[288,512]{1,0:T(8,128)(2,1)S(1)}) fusion(bf16[4,288,512]{2,1,0:T(8,128)(2,1)} %collective-permute-done.10, bf16[4,288,512]{2,1,0:T(8,128)(2,1)S(1)} %copy-done.3), kind=kLoop, calls=%fused_computation.27 | loop fusion | flops 2359296 | bytes 3538944 | tf_op jit(solution)/shard_map/convert_element_type | solution.py:297
  102.9 1.6 collective-permute-start.12
  106.4 9.8 %shard_map.276 = (bf16[448,1536]{1,0:T(8,128)(2,1)}, f32[4,56,224]{2,1,0:T(8,128)}) custom-call(bf16[896,512]{1,0:T(8,128)(2,1)} %get-tuple-element.100.query, bf16[896,512]{1,0:T(8,128)(2,1)} %get-tuple-element.101.key, bf16[896,512]{1,0:T(8,128)(2,1)} %get-tuple-element.102.value, bf16[8,4,112,224]{3,2,1,0:T(8,128)(2,1)} %get-tuple-element.109.probs, ...), custom_call_target="tpu_custom_call" | custom-call | flops 1024 | bytes 1024 | tf_op jit(solution)/shard_map/pallas_call | solution.py:138
  116.2 3.4 %collective-permute-done.13 = bf16[288,512]{1,0:T(8,128)(2,1)S(1)} collective-permute-done((bf16[288,512]{1,0:T(8,128)(2,1)}, bf16[288,512]{1,0:T(8,128)(2,1)S(1)}, u32[]{:S(2)}, u32[]{:S(2)}) %collective-permute-start.13) | collective-permute-done | bytes 294944 | tf_op jit(solution)/shard_map/ppermute | solution.py:283
  120.4 9.5 %shard_map.277 = (f32[448,512]{1,0:T(8,128)}, bf16[336,512]{1,0:T(8,128)(2,1)}, bf16[4,224,512]{2,1,0:T(8,128)(2,1)}, bf16[4,224,512]{2,1,0:T(8,128)(2,1)}) custom-call(s32[2]{0:T(128)} %pad_add_fusion.me_ref, f32[784,512]{1,0:T(8,128)} %get-tuple-element.120.grad_mixed, bf16[7,112,512]{2,1,0:T(8,128)(2,1)} %bitcast.55, bf16[3,112,512]{2,1,0:T(8,128)(2,1)} %copy-done.1, ...), custom_call_target="tpu_custom_call" | custom-call | flops 1024 | bytes 1024 | tf_op jit(solution)/shard_map/pallas_call | solution.py:138
  132.0 1.5 collective-permute-start.20
  133.5 1.7 collective-permute-start.15
  136.3 1.8 collective-permute-start.17
  138.3 9.9 %collective-permute-done.17 = bf16[144,512]{1,0:T(8,128)(2,1)S(1)} collective-permute-done((bf16[144,512]{1,0:T(8,128)(2,1)S(1)}, bf16[144,512]{1,0:T(8,128)(2,1)S(1)}, u32[]{:S(2)}, u32[]{:S(2)}) %collective-permute-start.17) | collective-permute-done | bytes 147488 | tf_op jit(solution)/shard_map/ppermute | solution.py:283
  148.3 2.1 %collective-permute-start.21 = (bf16[144,512]{1,0:T(8,128)(2,1)S(1)}, bf16[144,512]{1,0:T(8,128)(2,1)S(1)}, u32[]{:S(2)}, u32[]{:S(2)}) collective-permute-start(bf16[144,512]{1,0:T(8,128)(2,1)S(1)} %add_convert_fusion.17), channel_id=1, source_target_pairs={{0,2},{1,3},{2,0},{3,1},{4,6},{5,7},{6,4},{7,5},{8,10},{9,11},{10,... | collective-permute-start | bytes 442376 | tf_op jit(solution)/shard_map/ppermute | solution.py:283
  155.5 2.7 %collective-permute-done.21 = bf16[144,512]{1,0:T(8,128)(2,1)S(1)} collective-permute-done((bf16[144,512]{1,0:T(8,128)(2,1)S(1)}, bf16[144,512]{1,0:T(8,128)(2,1)S(1)}, u32[]{:S(2)}, u32[]{:S(2)}) %collective-permute-start.21) | collective-permute-done | bytes 147488 | tf_op jit(solution)/shard_map/ppermute | solution.py:283
  158.3 2.1 %collective-permute-done.22 = bf16[224,512]{1,0:T(8,128)(2,1)S(1)} collective-permute-done((bf16[224,512]{1,0:T(8,128)(2,1)S(1)}, bf16[224,512]{1,0:T(8,128)(2,1)S(1)}, u32[]{:S(2)}, u32[]{:S(2)}) %collective-permute-start.22) | collective-permute-done | bytes 229408 | tf_op jit(solution)/shard_map/ppermute | solution.py:283
  161.0 3.3 %collective-permute-done.24 = bf16[224,512]{1,0:T(8,128)(2,1)S(1)} collective-permute-done((bf16[224,512]{1,0:T(8,128)(2,1)S(1)}, bf16[224,512]{1,0:T(8,128)(2,1)S(1)}, u32[]{:S(2)}, u32[]{:S(2)}) %collective-permute-start.24) | collective-permute-done | bytes 229408 | tf_op jit(solution)/shard_map/ppermute | solution.py:283
  166.5 4.4 %collective-permute-done.26 = bf16[112,512]{1,0:T(8,128)(2,1)S(1)} collective-permute-done((bf16[112,512]{1,0:T(8,128)(2,1)S(1)}, bf16[112,512]{1,0:T(8,128)(2,1)S(1)}, u32[]{:S(2)}, u32[]{:S(2)}) %collective-permute-start.26) | collective-permute-done | bytes 114720 | tf_op jit(solution)/shard_map/ppermute | solution.py:283
  170.8 2.7 %collective-permute-start.27 = (bf16[160,512]{1,0:T(8,128)(2,1)S(1)}, bf16[160,512]{1,0:T(8,128)(2,1)S(1)}, u32[]{:S(2)}, u32[]{:S(2)}) collective-permute-start(bf16[160,512]{1,0:T(8,128)(2,1)S(1)} %add_convert_fusion.13), channel_id=1, source_target_pairs={{0,2},{1,3},{2,0},{3,1},{4,6},{5,7},{6,4},{7,5},{8,10},{9,11},{10,... | collective-permute-start | bytes 491528 | tf_op jit(solution)/shard_map/ppermute | solution.py:283
  173.5 5.3 %collective-permute-done.27 = bf16[160,512]{1,0:T(8,128)(2,1)S(1)} collective-permute-done((bf16[160,512]{1,0:T(8,128)(2,1)S(1)}, bf16[160,512]{1,0:T(8,128)(2,1)S(1)}, u32[]{:S(2)}, u32[]{:S(2)}) %collective-permute-start.27) | collective-permute-done | bytes 163872 | tf_op jit(solution)/shard_map/ppermute | solution.py:283
  180.3 4.9 %collective-permute-done.28 = bf16[112,512]{1,0:T(8,128)(2,1)S(1)} collective-permute-done((bf16[112,512]{1,0:T(8,128)(2,1)S(1)}, bf16[112,512]{1,0:T(8,128)(2,1)S(1)}, u32[]{:S(2)}, u32[]{:S(2)}) %collective-permute-start.28) | collective-permute-done | bytes 114720 | tf_op jit(solution)/shard_map/ppermute | solution.py:283
  185.1 1.7 collective-permute-start.31
  188.6 3.2 %collective-permute-done.29.back = bf16[112,512]{1,0:T(8,128)(2,1)S(1)} collective-permute-done((bf16[112,512]{1,0:T(8,128)(2,1)S(1)}, bf16[112,512]{1,0:T(8,128)(2,1)S(1)}, u32[]{:S(2)}, u32[]{:S(2)}) %collective-permute-start.29) | collective-permute-done | bytes 114720 | tf_op jit(solution)/shard_map/ppermute | solution.py:283
  192.4 2.1 %shard_map.278 = (f32[1,64]{1,0:T(1,128)}, f32[1,64]{1,0:T(1,128)}, f32[64,1536]{1,0:T(8,128)}, f32[2,64]{1,0:T(2,128)}, f32[2,169]{1,0:T(2,128)}) custom-call(s32[2]{0:T(128)} %pad_add_fusion.me_ref, bf16[112,512]{1,0:T(8,128)(2,1)} %copy-done.9, bf16[112,512]{1,0:T(8,128)(2,1)} %copy-done.22), custom_call_target="tpu_custom_call" | custom-call | flops 1024 | bytes 1024 | tf_op jit(solution)/shard_map/pallas_call | solution.py:138
  195.8 2.4 %shard_map.279 = (f32[64,512]{1,0:T(8,128)}, f32[1,64]{1,0:T(1,128)}, f32[1,64]{1,0:T(1,128)}, f32[1,64]{1,0:T(1,128)}, f32[64,2048]{1,0:T(8,128)}, /*index=5*/f...) custom-call(s32[2]{0:T(128)} %pad_add_fusion.me_ref, bf16[144,512]{1,0:T(8,128)(2,1)} %copy-done.8, ...), custom_call_target="tpu_custom_call" | custom-call | flops 1024 | bytes 1024 | tf_op jit(solution)/shard_map/pallas_call | solution.py:138
  (119 shorter events, 30.1 us)
Async XLA Ops:
  7.2 54.3 %all-gather.3.cloned.1.call-start = ((), (), s32[]{:S(2)}) async-start(), calls=%async_computation | async-start | bytes 5603328 | tf_op jit(solution)/shard_map/all_gather | solution.py:683
  11.9 10.7 %collective-permute-start.3 = (bf16[224,512]{1,0:T(8,128)(2,1)}, bf16[224,512]{1,0:T(8,128)(2,1)S(1)}, u32[]{:S(2)}, u32[]{:S(2)}) collective-permute-start(bf16[224,512]{1,0:T(8,128)(2,1)} %get-tuple-element.98.refs_0_), channel_id=1, source_target_pairs={{0,8},{4,12},{8,0},{12,4},{16,24},{20,28},{24,16},{28,20},{1,9},{5... | collective-permute-start | bytes 688136 | tf_op jit(solution)/shard_map/ppermute | solution.py:283
  14.9 14.0 %collective-permute-start.5 = (bf16[224,512]{1,0:T(8,128)(2,1)}, bf16[224,512]{1,0:T(8,128)(2,1)S(1)}, u32[]{:S(2)}, u32[]{:S(2)}) collective-permute-start(bf16[224,512]{1,0:T(8,128)(2,1)} %get-tuple-element.98.refs_0_), channel_id=1, source_target_pairs={{0,16},{4,20},{8,24},{12,28},{16,0},{20,4},{24,8},{28,12},{1,17},{... | collective-permute-start | bytes 688136 | tf_op jit(solution)/shard_map/ppermute | solution.py:283
  16.5 12.5 %collective-permute-start.7 = (bf16[224,512]{1,0:T(8,128)(2,1)}, bf16[224,512]{1,0:T(8,128)(2,1)S(1)}, u32[]{:S(2)}, u32[]{:S(2)}) collective-permute-start(bf16[224,512]{1,0:T(8,128)(2,1)} %get-tuple-element.98.refs_0_), channel_id=1, source_target_pairs={{0,24},{4,28},{8,16},{12,20},{16,8},{20,12},{24,0},{28,4},{1,25},{... | collective-permute-start | bytes 688136 | tf_op jit(solution)/shard_map/ppermute | solution.py:283
  16.5 13.0 %collective-permute-start.2 = (bf16[224,512]{1,0:T(8,128)(2,1)}, bf16[224,512]{1,0:T(8,128)(2,1)S(1)}, u32[]{:S(2)}, u32[]{:S(2)}) collective-permute-start(bf16[224,512]{1,0:T(8,128)(2,1)} %get-tuple-element.98.refs_0_), channel_id=1, source_target_pairs={{0,4},{4,0},{8,12},{12,8},{16,20},{20,16},{24,28},{28,24},{1,5},{5... | collective-permute-start | bytes 688136 | tf_op jit(solution)/shard_map/ppermute | solution.py:283
  17.5 13.1 %collective-permute-start = (bf16[3,112,512]{2,1,0:T(8,128)(2,1)S(1)}, bf16[3,112,512]{2,1,0:T(8,128)(2,1)S(1)}, u32[]{:S(2)}, u32[]{:S(2)}) collective-permute-start(bf16[3,112,512]{2,1,0:T(8,128)(2,1)S(1)} %slice_bitcast_fusion.1), channel_id=1, source_target_pairs={{0,3},{1,0},{2,1},{3,2},{4,7},{5,4},{6,5},{7,6},{8,11},{9,8},{10,9... | collective-permute-start | bytes 1032200 | tf_op jit(solution)/shard_map/ppermute | solution.py:38
  22.7 38.8 %collective-permute-start.1 = (bf16[3,112,512]{2,1,0:T(8,128)(2,1)S(1)}, bf16[3,112,512]{2,1,0:T(8,128)(2,1)S(1)}, u32[]{:S(2)}, u32[]{:S(2)}) collective-permute-start(bf16[3,112,512]{2,1,0:T(8,128)(2,1)S(1)} %slice_bitcast_fusion), channel_id=1, source_target_pairs={{0,3},{1,0},{2,1},{3,2},{4,7},{5,4},{6,5},{7,6},{8,11},{9,8},{10,9... | collective-permute-start | bytes 1032200 | tf_op jit(solution)/shard_map/ppermute | solution.py:38
  29.0 1.6 collective-permute-start.4
  29.0 1.8 collective-permute-start.6
  86.3 12.9 %collective-permute-start.10 = (bf16[4,288,512]{2,1,0:T(8,128)(2,1)}, bf16[4,288,512]{2,1,0:T(8,128)(2,1)}, u32[]{:S(2)}, u32[]{:S(2)}) collective-permute-start(bf16[4,288,512]{2,1,0:T(8,128)(2,1)} %get-tuple-element.106), channel_id=1, source_target_pairs={{0,4},{4,0},{8,12},{12,8},{16,20},{20,16},{24,28},{28,24},{1,5},{5... | collective-permute-start | bytes 3538952 | tf_op jit(solution)/shard_map/ppermute | solution.py:283
  86.6 15.2 %collective-permute-start.11 = (bf16[4,320,512]{2,1,0:T(8,128)(2,1)}, bf16[4,320,512]{2,1,0:T(8,128)(2,1)S(1)}, u32[]{:S(2)}, u32[]{:S(2)}) collective-permute-start(bf16[4,320,512]{2,1,0:T(8,128)(2,1)} %get-tuple-element.108), channel_id=1, source_target_pairs={{0,4},{4,0},{8,12},{12,8},{16,20},{20,16},{24,28},{28,24},{1,5},{5... | collective-permute-start | bytes 3932168 | tf_op jit(solution)/shard_map/ppermute | solution.py:283
  86.8 29.4 %collective-permute-start.9 = (bf16[336,512]{1,0:T(8,128)(2,1)}, bf16[336,512]{1,0:T(8,128)(2,1)S(1)}, u32[]{:S(2)}, u32[]{:S(2)}) collective-permute-start(bf16[336,512]{1,0:T(8,128)(2,1)} %get-tuple-element.104), channel_id=1, source_target_pairs={{0,1},{1,2},{2,3},{3,0},{4,5},{5,6},{6,7},{7,4},{8,9},{9,10},{10,1... | collective-permute-start | bytes 1032200 | tf_op jit(solution)/shard_map/ppermute | solution.py:38
  102.9 13.3 %collective-permute-start.12 = (bf16[288,512]{1,0:T(8,128)(2,1)}, bf16[288,512]{1,0:T(8,128)(2,1)S(1)}, u32[]{:S(2)}, u32[]{:S(2)}) collective-permute-start(bf16[288,512]{1,0:T(8,128)(2,1)} %get-tuple-element.113), channel_id=1, source_target_pairs={{0,8},{4,12},{8,0},{12,4},{16,24},{20,28},{24,16},{28,20},{1,9},{5... | collective-permute-start | bytes 884744 | tf_op jit(solution)/shard_map/ppermute | solution.py:283
  104.6 15.1 %collective-permute-start.13 = (bf16[288,512]{1,0:T(8,128)(2,1)}, bf16[288,512]{1,0:T(8,128)(2,1)S(1)}, u32[]{:S(2)}, u32[]{:S(2)}) collective-permute-start(bf16[288,512]{1,0:T(8,128)(2,1)} %get-tuple-element.114), channel_id=1, source_target_pairs={{0,16},{4,20},{8,24},{12,28},{16,0},{20,4},{24,8},{28,12},{1,17},{... | collective-permute-start | bytes 884744 | tf_op jit(solution)/shard_map/ppermute | solution.py:283
  105.9 13.8 %collective-permute-start.14 = (bf16[288,512]{1,0:T(8,128)(2,1)S(1)}, bf16[288,512]{1,0:T(8,128)(2,1)S(1)}, u32[]{:S(2)}, u32[]{:S(2)}) collective-permute-start(bf16[288,512]{1,0:T(8,128)(2,1)S(1)} %get-tuple-element.115), channel_id=1, source_target_pairs={{0,24},{4,28},{8,16},{12,20},{16,8},{20,12},{24,0},{28,4},{1,25},{... | collective-permute-start | bytes 884744 | tf_op jit(solution)/shard_map/ppermute | solution.py:283
  129.9 6.4 %collective-permute-start.16 = (bf16[4,224,512]{2,1,0:T(8,128)(2,1)}, bf16[4,224,512]{2,1,0:T(8,128)(2,1)S(1)}, u32[]{:S(2)}, u32[]{:S(2)}) collective-permute-start(bf16[4,224,512]{2,1,0:T(8,128)(2,1)} %get-tuple-element.132), channel_id=1, source_target_pairs={{0,4},{4,0},{8,12},{12,8},{16,20},{20,16},{24,28},{28,24},{1,5},{5... | collective-permute-start | bytes 2752520 | tf_op jit(solution)/shard_map/ppermute | solution.py:283
  129.9 18.4 %collective-permute-start.18 = (bf16[320,512]{1,0:T(8,128)(2,1)}, bf16[320,512]{1,0:T(8,128)(2,1)S(1)}, u32[]{:S(2)}, u32[]{:S(2)}) collective-permute-start(bf16[320,512]{1,0:T(8,128)(2,1)} %get-tuple-element.137), channel_id=1, source_target_pairs={{0,8},{4,12},{8,0},{12,4},{16,24},{20,28},{24,16},{28,20},{1,9},{5... | collective-permute-start | bytes 983048 | tf_op jit(solution)/shard_map/ppermute | solution.py:283
  131.0 17.3 %collective-permute-start.19 = (bf16[320,512]{1,0:T(8,128)(2,1)}, bf16[320,512]{1,0:T(8,128)(2,1)S(1)}, u32[]{:S(2)}, u32[]{:S(2)}) collective-permute-start(bf16[320,512]{1,0:T(8,128)(2,1)} %get-tuple-element.138), channel_id=1, source_target_pairs={{0,16},{4,20},{8,24},{12,28},{16,0},{20,4},{24,8},{28,12},{1,17},{... | collective-permute-start | bytes 983048 | tf_op jit(solution)/shard_map/ppermute | solution.py:283
  132.0 16.3 %collective-permute-start.20 = (bf16[320,512]{1,0:T(8,128)(2,1)}, bf16[320,512]{1,0:T(8,128)(2,1)S(1)}, u32[]{:S(2)}, u32[]{:S(2)}) collective-permute-start(bf16[320,512]{1,0:T(8,128)(2,1)} %get-tuple-element.139), channel_id=1, source_target_pairs={{0,24},{4,28},{8,16},{12,20},{16,8},{20,12},{24,0},{28,4},{1,25},{... | collective-permute-start | bytes 983048 | tf_op jit(solution)/shard_map/ppermute | solution.py:283
  133.5 18.2 %collective-permute-start.15 = (bf16[336,512]{1,0:T(8,128)(2,1)}, bf16[336,512]{1,0:T(8,128)(2,1)S(1)}, u32[]{:S(2)}, u32[]{:S(2)}) collective-permute-start(bf16[336,512]{1,0:T(8,128)(2,1)} %get-tuple-element.125), channel_id=1, source_target_pairs={{0,1},{1,2},{2,3},{3,0},{4,5},{5,6},{6,7},{7,4},{8,9},{9,10},{10,1... | collective-permute-start | bytes 1032200 | tf_op jit(solution)/shard_map/ppermute | solution.py:38
  136.3 11.9 %collective-permute-start.17 = (bf16[144,512]{1,0:T(8,128)(2,1)S(1)}, bf16[144,512]{1,0:T(8,128)(2,1)S(1)}, u32[]{:S(2)}, u32[]{:S(2)}) collective-permute-start(bf16[144,512]{1,0:T(8,128)(2,1)S(1)} %add_convert_fusion.18), channel_id=1, source_target_pairs={{0,1},{1,0},{2,3},{3,2},{4,5},{5,4},{6,7},{7,6},{8,9},{9,8},{10,11... | collective-permute-start | bytes 442376 | tf_op jit(solution)/shard_map/ppermute | solution.py:283
  148.3 9.9 %collective-permute-start.21 = (bf16[144,512]{1,0:T(8,128)(2,1)S(1)}, bf16[144,512]{1,0:T(8,128)(2,1)S(1)}, u32[]{:S(2)}, u32[]{:S(2)}) collective-permute-start(bf16[144,512]{1,0:T(8,128)(2,1)S(1)} %add_convert_fusion.17), channel_id=1, source_target_pairs={{0,2},{1,3},{2,0},{3,1},{4,6},{5,7},{6,4},{7,5},{8,10},{9,11},{10,... | collective-permute-start | bytes 442376 | tf_op jit(solution)/shard_map/ppermute | solution.py:283
  151.8 8.6 %collective-permute-start.22 = (bf16[224,512]{1,0:T(8,128)(2,1)S(1)}, bf16[224,512]{1,0:T(8,128)(2,1)S(1)}, u32[]{:S(2)}, u32[]{:S(2)}) collective-permute-start(bf16[224,512]{1,0:T(8,128)(2,1)S(1)} %get-tuple-element.147), channel_id=1, source_target_pairs={{0,8},{4,12},{8,0},{12,4},{16,24},{20,28},{24,16},{28,20},{1,9},{5... | collective-permute-start | bytes 688136 | tf_op jit(solution)/shard_map/ppermute | solution.py:283
  153.2 7.7 %collective-permute-start.23 = (bf16[224,512]{1,0:T(8,128)(2,1)S(1)}, bf16[224,512]{1,0:T(8,128)(2,1)S(1)}, u32[]{:S(2)}, u32[]{:S(2)}) collective-permute-start(bf16[224,512]{1,0:T(8,128)(2,1)S(1)} %get-tuple-element.148), channel_id=1, source_target_pairs={{0,16},{4,20},{8,24},{12,28},{16,0},{20,4},{24,8},{28,12},{1,17},{... | collective-permute-start | bytes 688136 | tf_op jit(solution)/shard_map/ppermute | solution.py:283
  154.2 10.0 %collective-permute-start.24 = (bf16[224,512]{1,0:T(8,128)(2,1)S(1)}, bf16[224,512]{1,0:T(8,128)(2,1)S(1)}, u32[]{:S(2)}, u32[]{:S(2)}) collective-permute-start(bf16[224,512]{1,0:T(8,128)(2,1)S(1)} %get-tuple-element.149), channel_id=1, source_target_pairs={{0,24},{4,28},{8,16},{12,20},{16,8},{20,12},{24,0},{28,4},{1,25},{... | collective-permute-start | bytes 688136 | tf_op jit(solution)/shard_map/ppermute | solution.py:283
  158.2 6.8 %collective-permute-start.25 = (bf16[160,512]{1,0:T(8,128)(2,1)S(1)}, bf16[160,512]{1,0:T(8,128)(2,1)S(1)}, u32[]{:S(2)}, u32[]{:S(2)}) collective-permute-start(bf16[160,512]{1,0:T(8,128)(2,1)S(1)} %get-tuple-element.154), channel_id=1, source_target_pairs={{0,1},{1,0},{2,3},{3,2},{4,5},{5,4},{6,7},{7,6},{8,9},{9,8},{10,11... | collective-permute-start | bytes 491528 | tf_op jit(solution)/shard_map/ppermute | solution.py:283
  164.2 30.3 %collective-permute-start.30 = (bf16[144,512]{1,0:T(8,128)(2,1)S(1)}, bf16[144,512]{1,0:T(8,128)(2,1)S(1)}, u32[]{:S(2)}, u32[]{:S(2)}) collective-permute-start(bf16[144,512]{1,0:T(8,128)(2,1)S(1)} %add_convert_fusion.16.half_a), channel_id=1, source_target_pairs={{0,1},{1,0},{2,3},{3,2},{4,5},{5,4},{6,7},{7,6},{8,9},{9,8},{10,11... | collective-permute-start | bytes 442376 | tf_op jit(solution)/shard_map/ppermute | solution.py:283
  165.0 5.8 %collective-permute-start.26 = (bf16[112,512]{1,0:T(8,128)(2,1)S(1)}, bf16[112,512]{1,0:T(8,128)(2,1)S(1)}, u32[]{:S(2)}, u32[]{:S(2)}) collective-permute-start(bf16[112,512]{1,0:T(8,128)(2,1)S(1)} %get-tuple-element.158), channel_id=1, source_target_pairs={{0,1},{1,0},{2,3},{3,2},{4,5},{5,4},{6,7},{7,6},{8,9},{9,8},{10,11... | collective-permute-start | bytes 344072 | tf_op jit(solution)/shard_map/ppermute | solution.py:283
  170.8 7.9 %collective-permute-start.27 = (bf16[160,512]{1,0:T(8,128)(2,1)S(1)}, bf16[160,512]{1,0:T(8,128)(2,1)S(1)}, u32[]{:S(2)}, u32[]{:S(2)}) collective-permute-start(bf16[160,512]{1,0:T(8,128)(2,1)S(1)} %add_convert_fusion.13), channel_id=1, source_target_pairs={{0,2},{1,3},{2,0},{3,1},{4,6},{5,7},{6,4},{7,5},{8,10},{9,11},{10,... | collective-permute-start | bytes 491528 | tf_op jit(solution)/shard_map/ppermute | solution.py:283
  178.8 6.3 %collective-permute-start.28 = (bf16[112,512]{1,0:T(8,128)(2,1)S(1)}, bf16[112,512]{1,0:T(8,128)(2,1)S(1)}, u32[]{:S(2)}, u32[]{:S(2)}) collective-permute-start(bf16[112,512]{1,0:T(8,128)(2,1)S(1)} %add_convert_fusion.21), channel_id=1, source_target_pairs={{0,2},{1,3},{2,0},{3,1},{4,6},{5,7},{6,4},{7,5},{8,10},{9,11},{10,... | collective-permute-start | bytes 344072 | tf_op jit(solution)/shard_map/ppermute | solution.py:283
  185.1 9.4 %collective-permute-start.31 = (bf16[160,512]{1,0:T(8,128)(2,1)S(1)}, bf16[160,512]{1,0:T(8,128)(2,1)S(1)}, u32[]{:S(2)}, u32[]{:S(2)}) collective-permute-start(bf16[160,512]{1,0:T(8,128)(2,1)S(1)} %add_convert_fusion.12.half_b), channel_id=1, source_target_pairs={{0,1},{1,0},{2,3},{3,2},{4,5},{5,4},{6,7},{7,6},{8,9},{9,8},{10,11... | collective-permute-start | bytes 491528 | tf_op jit(solution)/shard_map/ppermute | solution.py:283
  186.9 4.9 %collective-permute-start.29 = (bf16[112,512]{1,0:T(8,128)(2,1)S(1)}, bf16[112,512]{1,0:T(8,128)(2,1)S(1)}, u32[]{:S(2)}, u32[]{:S(2)}) collective-permute-start(bf16[112,512]{1,0:T(8,128)(2,1)S(1)} %add_convert_fusion.20.half), channel_id=1, source_target_pairs={{0,1},{1,0},{2,3},{3,2},{4,5},{5,4},{6,7},{7,6},{8,9},{9,8},{10,11... | collective-permute-start | bytes 344072 | tf_op jit(solution)/shard_map/ppermute | solution.py:283
  (24 other events, 160.0 us)
Sparse Core Ops, SparseCore 0:
  12.1 44.8 all-gather.2
where the time goes:
time: 206 us; the launch traced here: 205 us
  Pallas kernels  89.4 us (43%)
  waiting for transfers between devices  43.5 us (21%)
  starting transfers between devices  39 us (19%)
  between operations  14.4 us (7%)
  local copies, waits for them, and re-layouts  10 us (5%)
  other arithmetic  8.88 us (4%)
    pallas_call x9, Pallas kernels, kernel_call(): pl.pallas_call(body, out_shape=tuple(outs), in_specs=in_specs, out_specs=...  89.4 us
    ppermute x28, waiting for transfers between devices, exchange(): return lax.ppermute(value, axis, [(i, i ^ mask) for i in range(peers)])  43.4 us
    ppermute x28, starting transfers between devices, exchange(): return lax.ppermute(value, axis, [(i, i ^ mask) for i in range(peers)])  28.3 us
    ppermute x4, starting transfers between devices, shifted_2(): lax.ppermute(value, axis, [(i, (i + by) % peers) for i in range(peers)])  10.6 us
    convert_element_type x9, other arithmetic, add_pair(): return (here.astype(F32) + came.astype(F32)).astype(BF)  4.24 us
  transfers between devices with their start and end apart: 33, of which 13 were waited for; matrix products, arithmetic and copies ran while one was open for 6% of the time, Pallas kernels for 25%

commit v1 on v0

--- a/solution.py
+++ b/solution.py
@@ -20,7 +20,8 @@
 QUAD = 4
 QUADS = HEADS // QUAD
 FEAT = QUAD * HEAD
-LANES = QUAD * PLACES
+HOLD = 64
+LANES = QUAD * HOLD
 TOKENS = WIN * WIDTH
 PADDED = WINDOWS * PLACES
 TAB = 1536
@@ -82,14 +83,18 @@
 
 
 def spread(values, masks):
-    return jnp.concatenate([values * mask for mask in masks], 0).astype(BF)
+    empty = jnp.zeros((HOLD - PLACES, FEAT), F32)
+    rows = []
+    for mask in masks:
+        rows += [values * mask, empty]
+    return jnp.concatenate(rows, 0).astype(BF)
 
 
 def own_heads(values):
     feature = iota((PLACES, FEAT), 1) >> 5
     out = values[:PLACES]
     for h in range(1, QUAD):
-        out = jnp.where(feature == h, values[h * PLACES : (h + 1) * PLACES], out)
+        out = jnp.where(feature == h, values[h * HOLD : h * HOLD + PLACES], out)
     return out
 
 
@@ -97,17 +102,14 @@
     shape = (TAB_USED, LANES) if row_axis == 0 else (LANES, TAB_USED)
     lane = iota(shape, row_axis)
     pair = iota(shape, 1 - row_axis)
-    head = jnp.zeros(shape, jnp.int32)
-    for h in range(1, QUAD):
-        head += jnp.where(pair >= h * PLACES, 1, 0)
-    place = pair - head * PLACES
+    head, place = pair >> 6, pair & (HOLD - 1)
     row, column = place >> 3, place & (SLOT - 1)
     entry = row * (2 * WIN - 1) + column
     if backwards:
         entry = (WIN - 1) * 2 * WIN - entry
     held = head + quad % (GROUP // QUAD) * QUAD
     match = ((lane >> 3) == entry) & ((lane & 7) == held)
-    return one_hot(match & (column < WIN))
+    return one_hot(match & (column < WIN) & (row < WIN))
 
 
 def norm_stats(values):
@@ -130,7 +132,8 @@
 
 
 def kernel_call(
-    body, outs, ins, scratch=(), smem=0, apart=0, grid=None, in_blocks=None, out_blocks=None
+    body, outs, ins, scratch=(), smem=0, apart=0, grid=None, in_blocks=None, out_blocks=None,
+    vmem=VMEM_LIMIT,
 ):
     in_specs = [whole(pltpu.SMEM)] * smem
     in_specs += in_blocks or [whole()] * (len(ins) - smem - apart) + [whole(pl.ANY)] * apart
@@ -142,7 +145,7 @@
         out_specs=tuple(out_blocks or [whole()] * len(outs)),
         scratch_shapes=list(scratch),
         cost_estimate=pl.CostEstimate(flops=1024, bytes_accessed=1024, transcendentals=0),
-        compiler_params=pltpu.CompilerParams(vmem_limit_bytes=VMEM_LIMIT),
+        compiler_params=pltpu.CompilerParams(vmem_limit_bytes=vmem),
         **options,
     )(*ins)
 
@@ -177,7 +180,9 @@
     me = me_ref[0]
     for c in range(3):
         attn[c * depth : (c + 1) * depth, :] = wqkv[:, c * D : (c + 1) * D]
-    rows = [place(v, D, me) for v in (g1[...], b1[...], bqv[0:1, :], bqv[1:2, :])]
+    attn[3 * depth : 4 * depth, :] = wproj[...]
+    vectors = (g1[...], b1[...], bqv[0:1, :], bqv[1:2, :], bproj[...])
+    rows = [place(v, D, me) for v in vectors]
     held, entries = table.shape
     lane = iota((entries, TAB), 1)
     spot = iota((entries, TAB), 0) * GROUP + TAB - (WIN - 1) * 2 * WIN * GROUP
@@ -192,27 +197,32 @@
             groups[g] = groups[g] + jnp.where((head >> 3) == g, row, 0.0)
     for g in range(GROUPS):
         rows += [groups[g][:, c * D : (c + 1) * D] for c in range(TAB // D)]
-    attn[3 * depth :, :] = padded(rows, SMALL)
+    attn[4 * depth :, :] = padded(rows, SMALL)
     for c in range(FF // D):
         mlp[c * depth : (c + 1) * depth, :] = win[:, c * D : (c + 1) * D]
     mlp[4 * depth : 8 * depth, :] = wout[...]
-    mlp[8 * depth : 9 * depth, :] = wproj[...]
     hidden_bias = place(bin_[...], FF, me)
-    rows = [place(v, D, me) for v in (g2[...], b2[...], bout[...], bproj[...])]
+    rows = [place(v, D, me) for v in (g2[...], b2[...], bout[...])]
     rows += [hidden_bias[:, c * D : (c + 1) * D] for c in range(FF // D)]
-    mlp[9 * depth :, :] = padded(rows, SMALL)
-
-
-def join_halves(late, half, back, both):
+    mlp[8 * depth :, :] = padded(rows, SMALL)
+
+
+def join_halves(late, half, back, both, sems):
     rows = half.shape[0]
-    both[pl.ds(pl.multiple_of(late * rows, 16), rows), :] = half[...]
-    both[pl.ds(pl.multiple_of((1 - late) * rows, 16), rows), :] = back[...]
-
-
-def unpack_attn_body(me_ref, half, back, g1, b1, wqkv, bqv, table, attn):
+    copies = []
+    for n, (part, at) in enumerate(((half, late), (back, 1 - late))):
+        to = both.at[pl.ds(pl.multiple_of(at * rows, 16), rows), :]
+        copies.append(pltpu.make_async_copy(part, to, sems.at[n]))
+    for copy in copies:
+        copy.start()
+    for copy in copies:
+        copy.wait()
+
+
+def unpack_attn_body(me_ref, half, back, g1, b1, wqkv, bqv, table, attn, sems):
     depth = wqkv.shape[0]
     me = me_ref[0]
-    join_halves(me_ref[1], half, back, attn)
+    join_halves(me_ref[1], half, back, attn, sems)
     for c in range(3):
         wqkv[:, c * D : (c + 1) * D] = attn[c * depth : (c + 1) * depth, :].astype(F32)
     small = attn[3 * depth :, :].astype(F32)
@@ -242,17 +252,16 @@
 
 
 def unpack_mlp_body(
-    me_ref, half_a, back_a, half_b, back_b, wproj, bproj, g2, b2, win, bin_, wout, bout, a, b
+    me_ref, half, back, wproj, bproj, g2, b2, win, bin_, wout, bout, mlp, sems
 ):
     depth = win.shape[0]
     me = me_ref[0]
-    join_halves(me_ref[1], half_a, back_a, a)
-    join_halves(me_ref[1], half_b, back_b, b)
+    join_halves(me_ref[1], half, back, mlp, sems)
     for c in range(FF // D):
-        win[:, c * D : (c + 1) * D] = a[c * depth : (c + 1) * depth, :].astype(F32)
-    wout[...] = b[: 4 * depth, :].astype(F32)
-    wproj[...] = b[4 * depth :, :].astype(F32)
-    small = a[4 * depth :, :].astype(F32)
+        win[:, c * D : (c + 1) * D] = mlp[c * depth : (c + 1) * depth, :].astype(F32)
+    wout[...] = mlp[4 * depth : 8 * depth, :].astype(F32)
+    wproj[...] = mlp[8 * depth : 9 * depth, :].astype(F32)
+    small = mlp[9 * depth :, :].astype(F32)
     g2[...] = mine(small[0:1], depth, me)
     b2[...] = mine(small[1:2], depth, me)
     bout[...] = mine(small[2:3], depth, me)
@@ -297,21 +306,20 @@
     return (here.astype(F32) + came.astype(F32)).astype(BF)
 
 
-def add_cores(same, other):
-    came = exchange(other, "shard", 1)
-    return [add_pair(same[q], came[q]) for q in range(same.shape[0])]
+def add_cores(same, came):
+    return [add_pair(same[q], came[q]) for q in range(1, same.shape[0])]
 
 
 def to_chips(sums):
-    return [sums[0]] + [exchange(sums[q], "shard", 2 * q) for q in range(1, len(sums))]
-
-
-def add_chips(late, parts):
-    half = parts[0].shape[0] // 2
+    return [exchange(s, "shard", 2 * q + 2) for q, s in enumerate(sums)]
+
+
+def add_chips(late, same, came, parts):
+    half = same.shape[1] // 2
     out = []
     for start in (late * half, (1 - late) * half):
         total = 0.0
-        for part in parts:
+        for part in (same[0], came[0], *parts):
             total += lax.dynamic_slice_in_dim(part, start, half, 0).astype(F32)
         out.append(total.astype(BF))
     return out
@@ -353,8 +361,8 @@
     own = WIN - SHIFT
     for copy in copies:
         copy.wait()
-    depth = (slab.shape[1] - SMALL) // 3
-    small = smalls_of(slab, 3 * depth)
+    depth = (slab.shape[1] - SMALL) // 4
+    small = smalls_of(slab, 4 * depth)
     gain, offset, bias_q, bias_v = (small[r : r + 1] for r in range(4))
     for r in range(WIN):
         x = (tokens[SHIFT + r] if r < own else halo[r - own]).astype(F32)
@@ -367,18 +375,20 @@
     value[...] = (dot(normed_win[...], block_of(slab, 2, depth)) + bias_v).astype(BF)
 
 
-def attn_forward_body(slab, reg_rows, reg_lanes, query, key, value, probs, restored, wide, bias):
+def attn_forward_body(
+    slab, reg_rows, reg_lanes, tokens, halo, query, key, value, probs, restored, mixed, wide, bias
+):
     n = pl.program_id(0)
+    depth = (slab.shape[1] - SMALL) // 4
 
     @pl.when(n == 0)
     def _():
-        depth = (slab.shape[1] - SMALL) // 3
-        small = smalls_of(slab, 3 * depth)
+        small = smalls_of(slab, 4 * depth)
         parts = TAB // D
         empty = (iota((PLACES, LANES), 0) & (SLOT - 1)) == WIN
         turned = []
         for g in range(GROUPS):
-            first = 4 + g * parts
+            first = 5 + g * parts
             row = jnp.concatenate([small[first + c : first + c + 1] for c in range(parts)], 1)
             row = jnp.broadcast_to(row, (SLOT, TAB))
             row = pltpu.roll(row, 0, 1, stride=GROUP, stride_axis=0)
@@ -394,30 +404,40 @@
     penalty = [
         jnp.where(reg_rows[s][:, 0:1] != reg_lanes[s], -100.0, 0.0) for s in range(2)
     ]
+    parts = [slice(s * PLACES, (s + 1) * PLACES) for s in range(2)]
+    units = [(u, s) for u in range(QUADS) for s in range(2)]
+    feats = [slice(u * FEAT, (u + 1) * FEAT) for u in range(QUADS)]
+    values, scores = [], []
     for u in range(QUADS):
-        feats = slice(u * FEAT, (u + 1) * FEAT)
-        q2 = query[:, feats].astype(F32)
-        k2 = key[:, feats].astype(F32)
-        v2 = value[:, feats].astype(F32)
-        held = []
+        q2 = query[:, feats[u]].astype(F32)
+        k2 = key[:, feats[u]].astype(F32)
+        v2 = value[:, feats[u]].astype(F32)
         for s in range(2):
-            part = slice(s * PLACES, (s + 1) * PLACES)
-            k, v = k2[part].astype(BF), v2[part].astype(BF)
-            logits = dot_nt(k, spread(q2[part], masks)) * SCALE + bias[u] + penalty[s]
-            top = jnp.max(logits, 0, keepdims=True)
-            powers = jnp.exp(logits - top)
-            p = powers * (1.0 / jnp.sum(powers, 0, keepdims=True))
-            held.append(p)
-            o = own_heads(dot_tn(p.astype(BF), v))
-            wide[2 * n + s, :, :, feats] = o.reshape(WIN, SLOT, FEAT)
-        probs[0, u] = jnp.concatenate(held, 0).astype(BF)
+            values.append(v2[parts[s]].astype(BF))
+            scores.append(dot_nt(k2[parts[s]].astype(BF), spread(q2[parts[s]], masks)))
+    shares = []
+    for (u, s), score in zip(units, scores):
+        logits = score * SCALE + bias[u] + penalty[s]
+        powers = jnp.exp(logits - jnp.max(logits, 0, keepdims=True))
+        shares.append(powers * (1.0 / jnp.sum(powers, 0, keepdims=True)))
+    wholes = [dot_tn(p.astype(BF), v) for p, v in zip(shares, values)]
+    for (u, s), o in zip(units, wholes):
+        wide[2 * n + s, :, :, feats[u]] = own_heads(o).reshape(WIN, SLOT, FEAT)
+    for u in range(QUADS):
+        probs[0, u] = jnp.concatenate(shares[2 * u : 2 * u + 2], 0).astype(BF)
 
     @pl.when(n == pl.num_programs(0) - 1)
     def _():
+        bias_proj = smalls_of(slab, 4 * depth)[4:5]
         back = places_column()
+        own = WIN - SHIFT
         for r in range(WIN):
             here = wide[:, r].reshape(WINDOWS * SLOT, D).astype(BF)
             restored[r * WIDTH : (r + 1) * WIDTH, :] = dot(back, here).astype(BF)
+        branch = dot(restored[...], block_of(slab, 3, depth)) + bias_proj
+        for r in range(WIN):
+            x = (tokens[SHIFT + r] if r < own else halo[r - own]).astype(F32)
+            mixed[r * WIDTH : (r + 1) * WIDTH, :] = x + branch[r * WIDTH : (r + 1) * WIDTH]
 
 
 def gelu_parts(h):
@@ -435,53 +455,58 @@
 
 def mlp_body(
     me_ref,
-    tokens,
-    token_halo,
+    mixed,
     cotangent,
     cot_halo,
     slab,
+    attn_slab,
     restored,
     kept,
     sent,
     grad_mixed,
     grad_win,
-    same_a,
-    other_a,
-    same_b,
-    other_b,
+    same,
+    other,
     normed_low,
     cot,
-    mixed,
     out_sum,
     back_sum,
     wide,
 ):
     me = me_ref[0]
     shards, height = slab.shape[:2]
-    depth = (height - SMALL) // 9
+    depth = (height - SMALL) // 8
     span = shards * D // FF
-    small = smalls_of(slab, 9 * depth)
-    gain, offset, bias_o, bias_proj = (small[r : r + 1] for r in range(4))
+    small = smalls_of(slab, 8 * depth)
+    gain, offset, bias_o = (small[r : r + 1] for r in range(3))
     own = WIN - SHIFT
-    branch = dot(restored[...], block_of(slab, 8, depth)) + bias_proj
     for r in range(WIN):
         part = slice(r * WIDTH, (r + 1) * WIDTH)
         cot[part, :] = cotangent[SHIFT + r] if r < own else cot_halo[r - own]
-        x = (tokens[SHIFT + r] if r < own else token_halo[r - own]).astype(F32)
-        mixed[part, :] = x + branch[part]
     normed, _ = norm_stats(mixed[...])
     normed_low[...] = (normed * gain + offset).astype(BF)
+
+    def w_in(c):
+        return block_of(slab, c, depth)
+
+    def w_out(c):
+        return slab[c * span : (c + 1) * span, 4 * depth : 8 * depth, :].reshape(D, D)
+
+    def ahead(c):
+        return dot(normed_low[...], w_in(c)), dot_nt(cot[...], w_out(c))
+
     vectors = []
+    now = ahead(0)
     for c in range(FF // D):
-        w_in = block_of(slab, c, depth)
-        w_out = slab[c * span : (c + 1) * span, 4 * depth : 8 * depth, :].reshape(D, D)
-        hidden = dot(normed_low[...], w_in) + small[4 + c : 5 + c]
+        hidden, grad = now
+        if c + 1 < FF // D:
+            now = ahead(c + 1)
+        hidden = hidden + small[3 + c : 4 + c]
         upto, density = gelu_parts(hidden)
         active = (hidden * upto).astype(BF)
-        slope = upto + hidden * density
-        grad = (dot_nt(cot[...], w_out) * slope).astype(BF)
-        forward = dot(active, w_out)
-        backward = dot_nt(grad, w_in)
+        grad = (grad * (upto + hidden * density)).astype(BF)
+        forward = dot(active, w_out(c))
+        backward = dot_nt(grad, w_in(c))
         if c == 0:
             out_sum[...] = forward
             back_sum[...] = backward
@@ -490,13 +515,13 @@
             back_sum[...] += backward
         vectors.append(jnp.sum(grad.astype(F32), 0, keepdims=True))
         put_shares(
-            me, same_a, other_a, c * depth, dot_tn(normed_low[...], grad).reshape(shards, depth, D)
+            me, same, other, c * depth, dot_tn(normed_low[...], grad).reshape(shards, depth, D)
         )
         put_shares(
             me,
-            same_b,
-            other_b,
-            0,
+            same,
+            other,
+            4 * depth,
             dot_tn(active, cot[...]).reshape(span, 4 * depth, D),
             c * span,
         )
@@ -513,9 +538,9 @@
     branch = grad_mixed[...].astype(BF)
     branch_sum = jnp.sum(branch.astype(F32), 0, keepdims=True)
     proj = dot_tn(restored[...], branch).reshape(shards, depth, D)
-    put_shares(me, same_b, other_b, 4 * depth, proj)
-    put_smalls(same_a, other_a, 4 * depth, [gain_sum, offset_sum, cot_sum, branch_sum] + vectors)
-    grad_att = dot_nt(branch, block_of(slab, 8, depth)).astype(BF)
+    put_shares(me, same, other, 8 * depth, proj)
+    put_smalls(same, other, 9 * depth, [gain_sum, offset_sum, cot_sum, branch_sum] + vectors)
+    grad_att = dot_nt(branch, block_of(attn_slab, 3, depth)).astype(BF)
     columns = column_places()
     for r in range(WIN):
         wide[:, r] = dot(columns, grad_att[r * WIDTH : (r + 1) * WIDTH]).reshape(WINDOWS, SLOT, D)
@@ -528,31 +553,39 @@
         pairs[...] = came[...]
 
     masks = head_masks()
+    parts = [slice(s * PLACES, (s + 1) * PLACES) for s in range(2)]
+    feats = [slice(u * FEAT, (u + 1) * FEAT) for u in range(QUADS)]
+    keys, shares, grads, queries, slopes = [], [], [], [], []
     for u in range(QUADS):
-        feats = slice(u * FEAT, (u + 1) * FEAT)
-        q2 = query[:, feats].astype(F32)
-        k2 = key[:, feats].astype(F32)
-        v2 = value[:, feats].astype(F32)
-        go2 = grad_win[:, feats].astype(F32)
+        q2 = query[:, feats[u]].astype(F32)
+        k2 = key[:, feats[u]].astype(F32)
+        v2 = value[:, feats[u]].astype(F32)
+        go2 = grad_win[:, feats[u]].astype(F32)
         p2 = probs[0, u].astype(F32)
-        held = []
-        total = pairs[u]
-        for s in range(2):
-            part = slice(s * PLACES, (s + 1) * PLACES)
-            k, v, p_low = (a[part].astype(BF) for a in (k2, v2, p2))
-            p = p2[part]
-            go_big = spread(go2[part], masks)
-            dp = dot_nt(v, go_big)
-            dv = dot(p_low, go_big)
-            inner = jnp.sum(p * dp, 0, keepdims=True)
-            ds = (p * (dp - inner)).astype(BF)
-            total += ds.astype(F32)
-            dk = dot(ds, spread(q2[part], masks)) * SCALE
-            dq = own_heads(dot_tn(ds, k)) * SCALE
-            held.append((dq, dk, dv))
-        pairs[u] = total
-        for c in range(3):
-            both = jnp.concatenate([held[0][c], held[1][c]], 0).astype(BF)
+        for part in parts:
+            keys.append(k2[part].astype(BF))
+            shares.append(p2[part])
+            grads.append(spread(go2[part], masks))
+            queries.append(spread(q2[part], masks))
+            slopes.append(dot_nt(v2[part].astype(BF), grads[-1]))
+    lows = []
+    for p, dp in zip(shares, slopes):
+        inner = jnp.sum(p * dp, 0, keepdims=True)
+        lows.append((p * (dp - inner)).astype(BF))
+    dvs = [dot(p.astype(BF), go) for p, go in zip(shares, grads)]
+    dks = [dot(ds, q) for ds, q in zip(lows, queries)]
+    dqs = [dot_tn(ds, k) for ds, k in zip(lows, keys)]
+    for u in range(QUADS):
+        two = slice(2 * u, 2 * u + 2)
+        pairs[u] += lows[2 * u].astype(F32) + lows[2 * u + 1].astype(F32)
+        for c, held in enumerate(
+            (
+                [own_heads(dq) * SCALE for dq in dqs[two]],
+                [dk * SCALE for dk in dks[two]],
+                dvs[two],
+            )
+        ):
+            both = jnp.concatenate(held, 0).astype(BF)
             out[:, c * D + u * FEAT : c * D + (u + 1) * FEAT] = both
 
 
@@ -566,12 +599,12 @@
     pairs,
     *refs,
 ):
-    grads = refs[:-5]
-    kept, sent, same, other, wide = refs[-5:]
+    grads = refs[:-7]
+    kept, sent, same, other_low, other_high, wide, other = refs[-7:]
     me = me_ref[0]
     shards = slab.shape[0]
-    depth = (slab.shape[1] - SMALL) // 3
-    small = smalls_of(slab, 3 * depth)
+    depth = (slab.shape[1] - SMALL) // 4
+    small = smalls_of(slab, 4 * depth)
     gain = small[0:1]
     own = WIN - SHIFT
     vectors = []
@@ -622,6 +655,9 @@
         row = jnp.sum(total, 0, keepdims=True)
         rows += [row[:, c * D : (c + 1) * D] for c in range(TAB // D)]
     put_smalls(same, other, 3 * depth, rows)
+    half = other_low.shape[0]
+    other_low[...] = other[:half]
+    other_high[...] = other[half:]
 
 
 def region_views(regions, rows, place):
@@ -630,7 +666,7 @@
     windows = jnp.pad(windows, ((0, 0), (0, 0), (0, SLOT - WIN))).astype(F32)
     windows = windows.reshape(WINDOWS, PLACES)
     by_row = jnp.broadcast_to(windows[:, :, None], (WINDOWS, PLACES, 128))
-    by_lane = jnp.tile(windows, (1, QUAD))
+    by_lane = jnp.tile(jnp.pad(windows, ((0, 0), (0, HOLD - PLACES))), (1, QUAD))
     return by_row, by_lane[:, None, :]
 
 
@@ -675,7 +711,7 @@
     late = seq & 1
     attn_slab, mlp_slab = kernel_call(
         pack_body,
-        [like((3 * depth + SMALL, D), BF), like((9 * depth + SMALL, D), BF)],
+        [like((4 * depth + SMALL, D), BF), like((8 * depth + SMALL, D), BF)],
         (where, *attn_params, *mlp_params),
         smem=1,
     )
@@ -710,44 +746,46 @@
     def fixed(shape):
         return pl.BlockSpec(shape, lambda i: (0,) * len(shape))
 
-    probs, restored = kernel_call(
+    probs, restored, mixed = kernel_call(
         attn_forward_body,
-        [like((steps, QUADS, pair_rows, LANES), BF), like((TOKENS, D), BF)],
-        (attn_all, by_row, by_lane, query, key, value),
+        [
+            like((steps, QUADS, pair_rows, LANES), BF),
+            like((TOKENS, D), BF),
+            like((TOKENS, D), F32),
+        ],
+        (attn_all, by_row, by_lane, tokens_here, token_halo, query, key, value),
         grid=(steps,),
         in_blocks=[
             fixed(attn_all.shape),
             pl.BlockSpec((2, *by_row.shape[1:]), lambda i: (i, 0, 0)),
             pl.BlockSpec((2, *by_lane.shape[1:]), lambda i: (i, 0, 0)),
+            fixed(tokens_here.shape),
+            fixed(token_halo.shape),
             rows_from(0),
             rows_from(0),
             rows_from(0),
         ],
-        out_blocks=[probs_from(0), fixed((TOKENS, D))],
+        out_blocks=[probs_from(0), fixed((TOKENS, D)), fixed((TOKENS, D))],
         scratch=[
             pltpu.VMEM((WINDOWS, WIN, SLOT, D), F32),
             pltpu.VMEM((QUADS, PLACES, LANES), F32),
         ],
     )
-    share_a = like((chips, 4 * depth + SMALL, D), BF)
-    share_b = like((chips, 5 * depth, D), BF)
-    out_kept, out_sent, grad_mixed, grad_win, same_a, other_a, same_b, other_b = kernel_call(
+    share = like((chips, 9 * depth + SMALL, D), BF)
+    out_kept, out_sent, grad_mixed, grad_win, mlp_same, mlp_other = kernel_call(
         mlp_body,
         [
             like((own * WIDTH, D), F32),
             like((SHIFT * WIDTH, D), BF),
             like((TOKENS, D), F32),
             like((PADDED, D), BF),
-            share_a,
-            share_a,
-            share_b,
-            share_b,
+            share,
+            share,
         ],
-        (where, tokens_here, token_halo, cot_here, cot_halo, mlp_all, restored),
+        (where, mixed, cot_here, cot_halo, mlp_all, attn_all, restored),
         scratch=[
             pltpu.VMEM((TOKENS, D), BF),
             pltpu.VMEM((TOKENS, D), BF),
-            pltpu.VMEM((TOKENS, D), F32),
             pltpu.VMEM((TOKENS, D), F32),
             pltpu.VMEM((TOKENS, D), F32),
             pltpu.VMEM((WINDOWS, WIN, SLOT, D), F32),
@@ -769,71 +807,68 @@
 
     none = jnp.zeros((QUADS, PLACES, LANES), F32)
     count = steps // 2
+    mlp_came = exchange(mlp_other, "shard", 1)
     early, pairs = backward(0, count, grad_win, none)
-    sums, (pairs,) = tie(add_cores(same_a, other_a) + add_cores(same_b, other_b), [pairs])
-    parts_a, parts_b = to_chips(sums[:chips]), to_chips(sums[chips:])
+    sums, (pairs,) = tie(add_cores(mlp_same, mlp_came), [pairs])
+    mlp_parts = to_chips(sums)
     late_part, pairs = backward(count, count, grad_win, pairs)
-    (out_halo, *parts_a), (pairs,) = tie([shifted_2(out_sent, "seq", 1), *parts_a], [pairs])
-    tok_kept, tok_sent, attn_same, attn_other = kernel_call(
+    (out_halo,), (pairs,) = tie([shifted_2(out_sent, "seq", 1)], [pairs])
+    tok_kept, tok_sent, attn_same, *attn_others = kernel_call(
         attn_last_body,
         [
             like((own * WIDTH, D), F32),
             like((SHIFT * WIDTH, D), BF),
             like((chips, 3 * depth + SMALL, D), BF),
-            like((chips, 3 * depth + SMALL, D), BF),
+            like((chips // 2, 3 * depth + SMALL, D), BF),
+            like((chips // 2, 3 * depth + SMALL, D), BF),
         ],
         (where, grad_mixed, tokens_here, token_halo, attn_all, normed_win, pairs, early, late_part),
-        scratch=[pltpu.VMEM((WINDOWS, WIN, SLOT, D), F32)],
-        smem=1,
-    )
-    tok_halo = shifted_2(tok_sent, "seq", 1)
-    cores = exchange(attn_other, "shard", 1)
-    keep, send = add_chips(late, parts_a)
-    (send,), (cores,) = tie([send], [cores])
-    near_a = exchange(send, "seq", 1)
-    sums = [add_pair(attn_same[q], cores[q]) for q in range(chips)]
-    sums, (near_a,) = tie(sums, [near_a])
-    parts = to_chips(sums)
-    half_a = add_pair(keep, near_a)
-    (half_a,), parts_b = tie([half_a], parts_b)
-    far_a = exchange(half_a, "seq", 2)
-    keep_b, send_b = add_chips(late, parts_b)
-    (keep_b, send_b), (far_a,) = tie([keep_b, send_b], [far_a])
-    near_b = exchange(send_b, "seq", 1)
-    half_a = seq_rest(add_pair(half_a, far_a))
-    (half_a,), parts = tie([half_a], parts)
-    back_a = exchange(half_a, "seq", 1)
-    keep, send = add_chips(late, parts)
-    (keep, send), (near_b,) = tie([keep, send], [near_b])
-    near = exchange(send, "seq", 1)
-    half_b = add_pair(keep_b, near_b)
-    (half_b,), (near,) = tie([half_b], [near])
-    far_b = exchange(half_b, "seq", 2)
-    half = add_pair(keep, near)
-    (half,), (far_b,) = tie([half], [far_b])
-    far = exchange(half, "seq", 2)
-    half_b = seq_rest(add_pair(half_b, far_b))
-    (half_b,), (far,) = tie([half_b], [far])
-    back_b = exchange(half_b, "seq", 1)
-    half = seq_rest(add_pair(half, far))
-    back = exchange(half, "seq", 1)
-    mlp_grads = kernel_call(
-        unpack_mlp_body,
-        [like(p.shape, F32) for p in mlp_params],
-        (where, half_a, back_a, half_b, back_b),
         scratch=[
-            pltpu.VMEM((4 * depth + SMALL, D), BF),
-            pltpu.VMEM((5 * depth, D), BF),
+            pltpu.VMEM((WINDOWS, WIN, SLOT, D), F32),
+            pltpu.VMEM((chips, 3 * depth + SMALL, D), BF),
         ],
         smem=1,
     )
-    attn_grads = kernel_call(
-        unpack_attn_body,
-        [like(p.shape, F32) for p in attn_params],
-        (where, half, back),
-        scratch=[pltpu.VMEM((3 * depth + SMALL, D), BF)],
-        smem=1,
-    )
+    attn_came = [exchange(other, "shard", 1) for other in attn_others]
+    mlp_parts, attn_came = tie(mlp_parts, attn_came)
+    keep_m, send = add_chips(late, mlp_same, mlp_came, mlp_parts)
+    (send,), attn_came = tie([send], attn_came)
+    attn_came = [came[q] for came in attn_came for q in range(chips // 2)]
+    near_m = exchange(send, "seq", 1)
+    attn_parts = to_chips(add_cores(attn_same, attn_came))
+    half_m = add_pair(keep_m, near_m)
+    (half_m,), attn_parts = tie([half_m], attn_parts)
+    far_m = exchange(half_m, "seq", 2)
+    keep, send = add_chips(late, attn_same, attn_came, attn_parts)
+    near = exchange(send, "seq", 1)
+    tok_halo = shifted_2(tok_sent, "seq", 1)
+    (near, tok_halo), (far_m,) = tie([near, tok_halo], [far_m])
+    half = add_pair(keep, near)
+    (half,), (far_m,) = tie([half], [far_m])
+    far = exchange(half, "seq", 2)
+    half_m = seq_rest(add_pair(half_m, far_m))
+    (half_m,), (far,) = tie([half_m], [far])
+    back_m = exchange(half_m, "seq", 1)
+    half = seq_rest(add_pair(half, far))
+    (half,), (back_m,) = tie([half], [back_m])
+    back = exchange(half, "seq", 1)
+    def unpack(body, params, half, back):
+        return kernel_call(
+            body,
+            [like(p.shape, F32) for p in params],
+            (where, half, back),
+            scratch=[
+                pltpu.VMEM((2 * half.shape[0], D), BF),
+                pltpu.SemaphoreType.DMA((2,)),
+            ],
+            smem=1,
+            apart=2,
+            vmem=16 * 1024 * 1024,
+        )
+
+    mlp_grads = unpack(unpack_mlp_body, mlp_params, half_m, back_m)
+    mlp_grads, (back,) = tie(mlp_grads, [back])
+    attn_grads = unpack(unpack_attn_body, attn_params, half, back)
     summed = [*attn_grads[:4], attn_grads[4].T, *mlp_grads]
 
     def joined(halo, kept):

time: 206 us -> 190 us (0.922)
  Pallas kernels: 89.4 us -> 72.2 us
  starting transfers between devices: 39 us -> 29.3 us
  waiting for transfers between devices: 43.5 us -> 48.9 us
  other arithmetic: 8.88 us -> 13.4 us
    pallas_call x9, Pallas kernels: 89.4 us -> 72.2 us  [kernel_call(): pl.pallas_call(body, out_shape=tuple(outs), in_specs=in_specs, out_specs=...]
    ppermute x28 -> x22, starting transfers between devices: 28.3 us -> 18.9 us  [exchange(): return lax.ppermute(value, axis, [(i, i ^ mask) for i in range(peers)])]
    ppermute x28 -> x22, waiting for transfers between devices: 43.4 us -> 48.9 us  [exchange(): return lax.ppermute(value, axis, [(i, i ^ mask) for i in range(peers)])]
    convert_element_type x9 -> x6, other arithmetic: 4.24 us -> 6.98 us  [add_pair(): return (here.astype(F32) + came.astype(F32)).astype(BF)]
    slice x0 -> x4, local copies, waits for them, and re-layouts: none -> 2.25 us  [the longest x1 1.2 us: add_chips(): came[0]]
  transfers between devices with their start and end apart: 33 -> 27, of which waited for: 13 -> 14; matrix products, arithmetic and copies ran while one was open for 6% -> 9% of each run, Pallas kernels for 25% -> 23%
where the time goes in v1:
time: 190 us; the launch traced here: 189 us
  Pallas kernels  72.2 us (38%)
  waiting for transfers between devices  48.9 us (26%)
  starting transfers between devices  29.3 us (15%)
  between operations  14.3 us (8%)
  other arithmetic  13.4 us (7%)
  local copies, waits for them, and re-layouts  11 us (6%)
    pallas_call x9, Pallas kernels, kernel_call(): pl.pallas_call(body, out_shape=tuple(outs), in_specs=in_specs, out_specs=...  72.2 us
    ppermute x22, waiting for transfers between devices, exchange(): return lax.ppermute(value, axis, [(i, i ^ mask) for i in range(peers)])  48.9 us
    ppermute x22, starting transfers between devices, exchange(): return lax.ppermute(value, axis, [(i, i ^ mask) for i in range(peers)])  18.9 us
    ppermute x4, starting transfers between devices, shifted_2(): lax.ppermute(value, axis, [(i, (i + by) % peers) for i in range(peers)])  10.4 us
    convert_element_type x6, other arithmetic, add_pair(): return (here.astype(F32) + came.astype(F32)).astype(BF)  6.98 us
  transfers between devices with their start and end apart: 27, of which 14 were waited for; matrix products, arithmetic and copies ran while one was open for 9% of the time, Pallas kernels for 23%

profile of v1, /device:TPU:0, one launch (start us, length us, event | category | flops | bytes accessed | tf_op | source)
XLA Modules:
  0.0 189.1 jit_solution(96226764692064268)
XLA Ops:
  9.1 2.9 %shard_map.271 = (bf16[288,512]{1,0:T(8,128)(2,1)}, bf16[544,512]{1,0:T(8,128)(2,1)}) custom-call(s32[2]{0:T(128)} %pad_add_fusion.me_ref, bf16[1,64]{1,0:T(2,128)(2,1)} %bitcast.86, bf16[1,64]{1,0:T(2,128)(2,1)} %bitcast.87, bf16[64,1536]{1,0:T(8,128)(2,1)} %wqkv.1, bf16[2,64]{1,0:T(2,128)(2,1)} %bqv.1, bf16[2,169]{1,0:T(2,128)(2,1)} %bitcast.85, ...), custom_call_target="tpu_custom_call" | custom-call | flops 1024 | bytes 1024 | tf_op jit(solution)/shard_map/pallas_call | solution.py:141
  11.9 3.0 %collective-permute-start.2 = (bf16[288,512]{1,0:T(8,128)(2,1)}, bf16[288,512]{1,0:T(8,128)(2,1)S(1)}, u32[]{:S(2)}, u32[]{:S(2)}) collective-permute-start(bf16[288,512]{1,0:T(8,128)(2,1)} %get-tuple-element.89.refs_0_), channel_id=1, source_target_pairs={{0,8},{4,12},{8,0},{12,4},{16,24},{20,28},{24,16},{28,20},{1,9},{5... | collective-permute-start | bytes 884744 | tf_op jit(solution)/shard_map/ppermute | solution.py:292
  14.9 1.5 collective-permute-start.4
  17.5 4.1 %collective-permute-start = (bf16[3,112,512]{2,1,0:T(8,128)(2,1)S(1)}, bf16[3,112,512]{2,1,0:T(8,128)(2,1)S(1)}, u32[]{:S(2)}, u32[]{:S(2)}) collective-permute-start(bf16[3,112,512]{2,1,0:T(8,128)(2,1)S(1)} %slice_bitcast_fusion.1), channel_id=1, source_target_pairs={{0,3},{1,0},{2,1},{3,2},{4,7},{5,4},{6,5},{7,6},{8,11},{9,8},{10,9... | collective-permute-start | bytes 1032200 | tf_op jit(solution)/shard_map/ppermute | solution.py:39
  23.0 4.2 %collective-permute-start.8 = (bf16[3,112,512]{2,1,0:T(8,128)(2,1)S(1)}, bf16[3,112,512]{2,1,0:T(8,128)(2,1)S(1)}, u32[]{:S(2)}, u32[]{:S(2)}) collective-permute-start(bf16[3,112,512]{2,1,0:T(8,128)(2,1)S(1)} %slice_bitcast_fusion), channel_id=1, source_target_pairs={{0,3},{1,0},{2,1},{3,2},{4,7},{5,4},{6,5},{7,6},{8,11},{9,8},{10,9... | collective-permute-start | bytes 1032200 | tf_op jit(solution)/shard_map/ppermute | solution.py:39
  27.1 4.0 %collective-permute-done.4.refs_4_ = bf16[288,512]{1,0:T(8,128)(2,1)S(1)} collective-permute-done((bf16[288,512]{1,0:T(8,128)(2,1)}, bf16[288,512]{1,0:T(8,128)(2,1)S(1)}, u32[]{:S(2)}, u32[]{:S(2)}) %collective-permute-start.4) | collective-permute-done | bytes 294944 | tf_op jit(solution)/shard_map/ppermute | solution.py:292
  31.2 3.4 %collective-permute-done.6.refs_6_ = bf16[288,512]{1,0:T(8,128)(2,1)S(1)} collective-permute-done((bf16[288,512]{1,0:T(8,128)(2,1)}, bf16[288,512]{1,0:T(8,128)(2,1)S(1)}, u32[]{:S(2)}, u32[]{:S(2)}) %collective-permute-start.6) | collective-permute-done | bytes 294944 | tf_op jit(solution)/shard_map/ppermute | solution.py:292
  37.3 7.0 %shard_map.272 = (bf16[896,512]{1,0:T(8,128)(2,1)}, bf16[896,512]{1,0:T(8,128)(2,1)}, bf16[896,512]{1,0:T(8,128)(2,1)}, bf16[896,512]{1,0:T(8,128)(2,1)}, bf16[8,288,512]{2,1,0:T(8,128)(2,1)}) custom-call(s32[2]{0:T(128)} %pad_add_fusion.me_ref, bf16[7,112,512]{2,1,0:T(8,128)(2,1)} %bitcast.77, bf16[3,112,512]{2,1,0:T(8,128)(2,1)} %copy-done.2, ...), custom_call_target="tpu_custom_call" | custom-call | flops 1024 | bytes 1024 | tf_op jit(solution)/shard_map/pallas_call | solution.py:141
  45.2 12.3 %shard_map.273 = (bf16[8,4,112,256]{3,2,1,0:T(8,128)(2,1)}, bf16[784,512]{1,0:T(8,128)(2,1)}, f32[784,512]{1,0:T(8,128)}) custom-call(bf16[8,288,512]{2,1,0:T(8,128)(2,1)} %get-tuple-element.90.slab.attn_slab, f32[16,56,128]{2,1,0:T(8,128)} %broadcast_in_dim.39.reg_rows, f32[16,1,256]{2,1,0:T(1,128)} %tile.9.reg_lanes, bf16[7,112,512]{2,1,0:T(8,128)(2,1)} %bitcast.78, ...), custom_call_target="tpu_custom_call" | custom-call | flops 1024 | bytes 1024 | tf_op jit(solution)/shard_map/pallas_call | solution.py:141
  58.3 24.7 %shard_map.274 = (f32[448,512]{1,0:T(8,128)}, bf16[336,512]{1,0:T(8,128)(2,1)}, f32[784,512]{1,0:T(8,128)}, bf16[896,512]{1,0:T(8,128)(2,1)}, bf16[4,608,512]{2,...) custom-call(s32[2]{0:T(128)} %pad_add_fusion.me_ref, f32[784,512]{1,0:T(8,128)} %get-tuple-element.94.mixed, ...), custom_call_target="tpu_custom_call" | custom-call | flops 1024 | bytes 1024 | tf_op jit(solution)/shard_map/pallas_call | solution.py:141
  83.1 1.7 collective-permute-start.9
  85.5 5.7 %shard_map.275 = (bf16[448,1536]{1,0:T(8,128)(2,1)}, f32[4,56,256]{2,1,0:T(8,128)}) custom-call(bf16[896,512]{1,0:T(8,128)(2,1)} %get-tuple-element.91.query, bf16[896,512]{1,0:T(8,128)(2,1)} %get-tuple-element.92.key, bf16[896,512]{1,0:T(8,128)(2,1)} %get-tuple-element.93.value, bf16[8,4,112,256]{3,2,1,0:T(8,128)(2,1)} %get-tuple-element.98.probs, ...), custom_call_target="tpu_custom_call" | custom-call | flops 1024 | bytes 1024 | tf_op jit(solution)/shard_map/pallas_call | solution.py:141
  91.3 3.0 %fusion.2 = (bf16[608,512]{1,0:T(8,128)(2,1)}, bf16[608,512]{1,0:T(8,128)(2,1)}, bf16[608,512]{1,0:T(8,128)(2,1)}) fusion(bf16[4,608,512]{2,1,0:T(8,128)(2,1)} %collective-permute-done.10, bf16[4,608,512]{2,1,0:T(8,128)(2,1)S(1)} %copy-done.3), kind=kLoop, calls=%fused_computation.7 | loop fusion | flops 3735552 | bytes 5603328 | tf_op jit(solution)/shard_map/convert_element_type | solution.py:306
  94.3 2.3 %collective-permute-start.11 = (bf16[608,512]{1,0:T(8,128)(2,1)}, bf16[608,512]{1,0:T(8,128)(2,1)}, u32[]{:S(2)}, u32[]{:S(2)}) collective-permute-start(bf16[608,512]{1,0:T(8,128)(2,1)} %get-tuple-element.113), channel_id=1, source_target_pairs={{0,8},{4,12},{8,0},{12,4},{16,24},{20,28},{24,16},{28,20},{1,9},{5... | collective-permute-start | bytes 1867784 | tf_op jit(solution)/shard_map/ppermute | solution.py:292
  98.1 5.6 %shard_map.276 = (bf16[448,1536]{1,0:T(8,128)(2,1)}, f32[4,56,256]{2,1,0:T(8,128)}) custom-call(bf16[896,512]{1,0:T(8,128)(2,1)} %get-tuple-element.91.query, bf16[896,512]{1,0:T(8,128)(2,1)} %get-tuple-element.92.key, bf16[896,512]{1,0:T(8,128)(2,1)} %get-tuple-element.93.value, bf16[8,4,112,256]{3,2,1,0:T(8,128)(2,1)} %get-tuple-element.98.probs, ...), custom_call_target="tpu_custom_call" | custom-call | flops 1024 | bytes 1024 | tf_op jit(solution)/shard_map/pallas_call | solution.py:141
  103.7 10.0 %shard_map.277 = (f32[448,512]{1,0:T(8,128)}, bf16[336,512]{1,0:T(8,128)(2,1)}, bf16[4,224,512]{2,1,0:T(8,128)(2,1)}, bf16[2,224,512]{2,1,0:T(8,128)(2,1)}, bf16[2,224,512]{2,1,0:T(8,128)(2,1)}) custom-call(s32[2]{0:T(128)} %pad_add_fusion.me_ref, f32[784,512]{1,0:T(8,128)} %get-tuple-element.107.grad_mixed, bf16[7,112,512]{2,1,0:T(8,128)(2,1)} %bitcast.79, ...), custom_call_target="tpu_custom_call" | custom-call | flops 1024 | bytes 1024 | tf_op jit(solution)/shard_map/pallas_call | solution.py:141
  116.5 9.5 %collective-permute-done.12 = bf16[608,512]{1,0:T(8,128)(2,1)} collective-permute-done((bf16[608,512]{1,0:T(8,128)(2,1)}, bf16[608,512]{1,0:T(8,128)(2,1)}, u32[]{:S(2)}, u32[]{:S(2)}) %collective-permute-start.12) | collective-permute-done | bytes 622624 | tf_op jit(solution)/shard_map/ppermute | solution.py:292
  126.0 1.4 fusion.8
  127.4 1.7 collective-permute-start.16
  129.5 1.3 fusion.11
  131.2 1.5 collective-permute-start.18
  132.6 1.8 collective-permute-start.19
  134.4 2.6 %collective-permute-done.16 = bf16[304,512]{1,0:T(8,128)(2,1)} collective-permute-done((bf16[304,512]{1,0:T(8,128)(2,1)S(1)}, bf16[304,512]{1,0:T(8,128)(2,1)}, u32[]{:S(2)}, u32[]{:S(2)}) %collective-permute-start.16) | collective-permute-done | bytes 311328 | tf_op jit(solution)/shard_map/ppermute | solution.py:292
  137.0 1.5 add_convert_fusion.4
  139.4 2.8 %collective-permute-done.18 = bf16[224,512]{1,0:T(8,128)(2,1)S(1)} collective-permute-done((bf16[224,512]{1,0:T(8,128)(2,1)S(1)}, bf16[224,512]{1,0:T(8,128)(2,1)S(1)}, u32[]{:S(2)}, u32[]{:S(2)}) %collective-permute-start.18) | collective-permute-done | bytes 229408 | tf_op jit(solution)/shard_map/ppermute | solution.py:292
  143.6 2.7 %collective-permute-start.22 = (bf16[304,512]{1,0:T(8,128)(2,1)S(1)}, bf16[304,512]{1,0:T(8,128)(2,1)S(1)}, u32[]{:S(2)}, u32[]{:S(2)}) collective-permute-start(bf16[304,512]{1,0:T(8,128)(2,1)S(1)} %add_convert_fusion.4), channel_id=1, source_target_pairs={{0,2},{1,3},{2,0},{3,1},{4,6},{5,7},{6,4},{7,5},{8,10},{9,11},{10,... | collective-permute-start | bytes 933896 | tf_op jit(solution)/shard_map/ppermute | solution.py:292
  147.3 1.8 fusion.17
  150.2 9.3 %collective-permute-done.20 = bf16[112,512]{1,0:T(8,128)(2,1)} collective-permute-done((bf16[112,512]{1,0:T(8,128)(2,1)}, bf16[112,512]{1,0:T(8,128)(2,1)}, u32[]{:S(2)}, u32[]{:S(2)}) %collective-permute-start.20) | collective-permute-done | bytes 114720 | tf_op jit(solution)/shard_map/ppermute | solution.py:292
  160.7 6.3 %collective-permute-done.23 = bf16[112,512]{1,0:T(8,128)(2,1)S(1)} collective-permute-done((bf16[112,512]{1,0:T(8,128)(2,1)S(1)}, bf16[112,512]{1,0:T(8,128)(2,1)S(1)}, u32[]{:S(2)}, u32[]{:S(2)}) %collective-permute-start.23) | collective-permute-done | bytes 114720 | tf_op jit(solution)/shard_map/ppermute | solution.py:292
  168.4 7.0 %collective-permute-done.24.back = bf16[304,512]{1,0:T(8,128)(2,1)S(1)} collective-permute-done((bf16[304,512]{1,0:T(8,128)(2,1)S(1)}, bf16[304,512]{1,0:T(8,128)(2,1)S(1)}, u32[]{:S(2)}, u32[]{:S(2)}) %collective-permute-start.24) | collective-permute-done | bytes 311328 | tf_op jit(solution)/shard_map/ppermute | solution.py:292
  177.0 2.0 %shard_map.278 = (f32[64,512]{1,0:T(8,128)}, f32[1,64]{1,0:T(1,128)}, f32[1,64]{1,0:T(1,128)}, f32[1,64]{1,0:T(1,128)}, f32[64,2048]{1,0:T(8,128)}, /*index=5*/f...) custom-call(s32[2]{0:T(128)S(1)} %copy-done.1, bf16[304,512]{1,0:T(8,128)(2,1)S(1)} %add_convert_fusion.3.half, ...), custom_call_target="tpu_custom_call" | custom-call | flops 1024 | bytes 1024 | tf_op jit(solution)/shard_map/pallas_call | solution.py:141
  180.3 2.0 %shard_map.279 = (f32[1,64]{1,0:T(1,128)}, f32[1,64]{1,0:T(1,128)}, f32[64,1536]{1,0:T(8,128)}, f32[2,64]{1,0:T(2,128)}, f32[2,169]{1,0:T(2,128)}) custom-call(s32[2]{0:T(128)S(1)} %copy-done.1, bf16[112,512]{1,0:T(8,128)(2,1)S(1)} %add_convert_fusion.8.half, bf16[112,512]{1,0:T(8,128)(2,1)S(1)} %collective-permute-done.25.back), custom_call_target="tpu_custom_call" | custom-call | flops 1024 | bytes 1024 | tf_op jit(solution)/shard_map/pallas_call | solution.py:141
  (100 shorter events, 24.3 us)
Async XLA Ops:
  7.2 27.9 %copy-start = (s32[1,28,112]{2,0,1:T(1,128)S(1)}, s32[1,28,112]{2,0,1:T(1,128)}, u32[]{:S(2)}) copy-start(s32[1,28,112]{2,0,1:T(1,128)} %param.17) | copy-start | bytes 37636
  7.2 50.4 %all-gather.3.cloned.1.call-start = ((), (), s32[]{:S(2)}) async-start(), calls=%async_computation | async-start | bytes 5013504 | tf_op jit(solution)/shard_map/all_gather | solution.py:719
  11.9 11.1 %collective-permute-start.2 = (bf16[288,512]{1,0:T(8,128)(2,1)}, bf16[288,512]{1,0:T(8,128)(2,1)S(1)}, u32[]{:S(2)}, u32[]{:S(2)}) collective-permute-start(bf16[288,512]{1,0:T(8,128)(2,1)} %get-tuple-element.89.refs_0_), channel_id=1, source_target_pairs={{0,8},{4,12},{8,0},{12,4},{16,24},{20,28},{24,16},{28,20},{1,9},{5... | collective-permute-start | bytes 884744 | tf_op jit(solution)/shard_map/ppermute | solution.py:292
  14.9 16.2 %collective-permute-start.4 = (bf16[288,512]{1,0:T(8,128)(2,1)}, bf16[288,512]{1,0:T(8,128)(2,1)S(1)}, u32[]{:S(2)}, u32[]{:S(2)}) collective-permute-start(bf16[288,512]{1,0:T(8,128)(2,1)} %get-tuple-element.89.refs_0_), channel_id=1, source_target_pairs={{0,16},{4,20},{8,24},{12,28},{16,0},{20,4},{24,8},{28,12},{1,17},{... | collective-permute-start | bytes 884744 | tf_op jit(solution)/shard_map/ppermute | solution.py:292
  16.5 18.1 %collective-permute-start.6 = (bf16[288,512]{1,0:T(8,128)(2,1)}, bf16[288,512]{1,0:T(8,128)(2,1)S(1)}, u32[]{:S(2)}, u32[]{:S(2)}) collective-permute-start(bf16[288,512]{1,0:T(8,128)(2,1)} %get-tuple-element.89.refs_0_), channel_id=1, source_target_pairs={{0,24},{4,28},{8,16},{12,20},{16,8},{20,12},{24,0},{28,4},{1,25},{... | collective-permute-start | bytes 884744 | tf_op jit(solution)/shard_map/ppermute | solution.py:292
  16.5 18.1 %collective-permute-start.1 = (bf16[288,512]{1,0:T(8,128)(2,1)}, bf16[288,512]{1,0:T(8,128)(2,1)S(1)}, u32[]{:S(2)}, u32[]{:S(2)}) collective-permute-start(bf16[288,512]{1,0:T(8,128)(2,1)} %get-tuple-element.89.refs_0_), channel_id=1, source_target_pairs={{0,4},{4,0},{8,12},{12,8},{16,20},{20,16},{24,28},{28,24},{1,5},{5... | collective-permute-start | bytes 884744 | tf_op jit(solution)/shard_map/ppermute | solution.py:292
  17.5 18.6 %collective-permute-start = (bf16[3,112,512]{2,1,0:T(8,128)(2,1)S(1)}, bf16[3,112,512]{2,1,0:T(8,128)(2,1)S(1)}, u32[]{:S(2)}, u32[]{:S(2)}) collective-permute-start(bf16[3,112,512]{2,1,0:T(8,128)(2,1)S(1)} %slice_bitcast_fusion.1), channel_id=1, source_target_pairs={{0,3},{1,0},{2,1},{3,2},{4,7},{5,4},{6,5},{7,6},{8,11},{9,8},{10,9... | collective-permute-start | bytes 1032200 | tf_op jit(solution)/shard_map/ppermute | solution.py:39
  23.0 13.6 %copy-start.8 = (bf16[288,512]{1,0:T(8,128)(2,1)}, bf16[288,512]{1,0:T(8,128)(2,1)S(1)}, u32[]{:S(2)}) copy-start(bf16[288,512]{1,0:T(8,128)(2,1)S(1)} %collective-permute-done.2.refs_2_) | copy-start | bytes 884740
  23.0 34.6 %collective-permute-start.8 = (bf16[3,112,512]{2,1,0:T(8,128)(2,1)S(1)}, bf16[3,112,512]{2,1,0:T(8,128)(2,1)S(1)}, u32[]{:S(2)}, u32[]{:S(2)}) collective-permute-start(bf16[3,112,512]{2,1,0:T(8,128)(2,1)S(1)} %slice_bitcast_fusion), channel_id=1, source_target_pairs={{0,3},{1,0},{2,1},{3,2},{4,7},{5,4},{6,5},{7,6},{8,11},{9,8},{10,9... | collective-permute-start | bytes 1032200 | tf_op jit(solution)/shard_map/ppermute | solution.py:39
  31.2 4.9 %collective-permute-start.3 = (bf16[288,512]{1,0:T(8,128)(2,1)S(1)}, bf16[288,512]{1,0:T(8,128)(2,1)S(1)}, u32[]{:S(2)}, u32[]{:S(2)}) collective-permute-start(bf16[288,512]{1,0:T(8,128)(2,1)S(1)} %collective-permute-done.2.refs_2_), channel_id=1, source_target_pairs={{0,4},{4,0},{8,12},{12,8},{16,20},{20,16},{24,28},{28,24},{1,5},{5... | collective-permute-start | bytes 884744 | tf_op jit(solution)/shard_map/ppermute | solution.py:292
  34.6 1.6 collective-permute-start.5
  34.6 2.0 %collective-permute-start.7 = (bf16[288,512]{1,0:T(8,128)(2,1)S(1)}, bf16[288,512]{1,0:T(8,128)(2,1)S(1)}, u32[]{:S(2)}, u32[]{:S(2)}) collective-permute-start(bf16[288,512]{1,0:T(8,128)(2,1)S(1)} %collective-permute-done.6.refs_6_), channel_id=1, source_target_pairs={{0,4},{4,0},{8,12},{12,8},{16,20},{20,16},{24,28},{28,24},{1,5},{5... | collective-permute-start | bytes 884744 | tf_op jit(solution)/shard_map/ppermute | solution.py:292
  83.0 8.3 %collective-permute-start.10 = (bf16[4,608,512]{2,1,0:T(8,128)(2,1)}, bf16[4,608,512]{2,1,0:T(8,128)(2,1)}, u32[]{:S(2)}, u32[]{:S(2)}) collective-permute-start(bf16[4,608,512]{2,1,0:T(8,128)(2,1)} %get-tuple-element.101), channel_id=1, source_target_pairs={{0,4},{4,0},{8,12},{12,8},{16,20},{20,16},{24,28},{28,24},{1,5},{5... | collective-permute-start | bytes 7471112 | tf_op jit(solution)/shard_map/ppermute | solution.py:292
  83.1 20.6 %collective-permute-start.9 = (bf16[336,512]{1,0:T(8,128)(2,1)}, bf16[336,512]{1,0:T(8,128)(2,1)S(1)}, u32[]{:S(2)}, u32[]{:S(2)}) collective-permute-start(bf16[336,512]{1,0:T(8,128)(2,1)} %get-tuple-element.97), channel_id=1, source_target_pairs={{0,1},{1,2},{2,3},{3,0},{4,5},{5,6},{6,7},{7,4},{8,9},{9,10},{10,1... | collective-permute-start | bytes 1032200 | tf_op jit(solution)/shard_map/ppermute | solution.py:39
  94.3 22.2 %collective-permute-start.11 = (bf16[608,512]{1,0:T(8,128)(2,1)}, bf16[608,512]{1,0:T(8,128)(2,1)}, u32[]{:S(2)}, u32[]{:S(2)}) collective-permute-start(bf16[608,512]{1,0:T(8,128)(2,1)} %get-tuple-element.113), channel_id=1, source_target_pairs={{0,8},{4,12},{8,0},{12,4},{16,24},{20,28},{24,16},{28,20},{1,9},{5... | collective-permute-start | bytes 1867784 | tf_op jit(solution)/shard_map/ppermute | solution.py:292
  96.6 29.4 %collective-permute-start.12 = (bf16[608,512]{1,0:T(8,128)(2,1)}, bf16[608,512]{1,0:T(8,128)(2,1)}, u32[]{:S(2)}, u32[]{:S(2)}) collective-permute-start(bf16[608,512]{1,0:T(8,128)(2,1)} %get-tuple-element.114), channel_id=1, source_target_pairs={{0,16},{4,20},{8,24},{12,28},{16,0},{20,4},{24,8},{28,12},{1,17},{... | collective-permute-start | bytes 1867784 | tf_op jit(solution)/shard_map/ppermute | solution.py:292
  97.1 28.9 %collective-permute-start.13 = (bf16[608,512]{1,0:T(8,128)(2,1)}, bf16[608,512]{1,0:T(8,128)(2,1)}, u32[]{:S(2)}, u32[]{:S(2)}) collective-permute-start(bf16[608,512]{1,0:T(8,128)(2,1)} %get-tuple-element.115), channel_id=1, source_target_pairs={{0,24},{4,28},{8,16},{12,20},{16,8},{20,12},{24,0},{28,4},{1,25},{... | collective-permute-start | bytes 1867784 | tf_op jit(solution)/shard_map/ppermute | solution.py:292
  113.7 2.2 %collective-permute-start.14 = (bf16[2,224,512]{2,1,0:T(8,128)(2,1)}, bf16[2,224,512]{2,1,0:T(8,128)(2,1)}, u32[]{:S(2)}, u32[]{:S(2)}) collective-permute-start(bf16[2,224,512]{2,1,0:T(8,128)(2,1)} %get-tuple-element.116), channel_id=1, source_target_pairs={{0,4},{4,0},{8,12},{12,8},{16,20},{20,16},{24,28},{28,24},{1,5},{5... | collective-permute-start | bytes 1376264 | tf_op jit(solution)/shard_map/ppermute | solution.py:292
  113.7 2.8 %collective-permute-start.15 = (bf16[2,224,512]{2,1,0:T(8,128)(2,1)}, bf16[2,224,512]{2,1,0:T(8,128)(2,1)}, u32[]{:S(2)}, u32[]{:S(2)}) collective-permute-start(bf16[2,224,512]{2,1,0:T(8,128)(2,1)} %get-tuple-element.117), channel_id=1, source_target_pairs={{0,4},{4,0},{8,12},{12,8},{16,20},{20,16},{24,28},{28,24},{1,5},{5... | collective-permute-start | bytes 1376264 | tf_op jit(solution)/shard_map/ppermute | solution.py:292
  114.3 15.2 %copy-start.4 = (bf16[4,224,512]{2,1,0:T(8,128)(2,1)S(1)}, bf16[4,224,512]{2,1,0:T(8,128)(2,1)}, u32[]{:S(2)}) copy-start(bf16[4,224,512]{2,1,0:T(8,128)(2,1)} %get-tuple-element.112) | copy-start | bytes 2752516
  127.4 9.6 %collective-permute-start.16 = (bf16[304,512]{1,0:T(8,128)(2,1)S(1)}, bf16[304,512]{1,0:T(8,128)(2,1)}, u32[]{:S(2)}, u32[]{:S(2)}) collective-permute-start(bf16[304,512]{1,0:T(8,128)(2,1)S(1)} %fusion.8), channel_id=1, source_target_pairs={{0,1},{1,0},{2,3},{3,2},{4,5},{5,4},{6,7},{7,6},{8,9},{9,8},{10,11... | collective-permute-start | bytes 933896 | tf_op jit(solution)/shard_map/ppermute | solution.py:292
  129.1 21.1 %collective-permute-start.21 = (bf16[336,512]{1,0:T(8,128)(2,1)}, bf16[336,512]{1,0:T(8,128)(2,1)S(1)}, u32[]{:S(2)}, u32[]{:S(2)}) collective-permute-start(bf16[336,512]{1,0:T(8,128)(2,1)} %get-tuple-element.129), channel_id=1, source_target_pairs={{0,1},{1,2},{2,3},{3,0},{4,5},{5,6},{6,7},{7,4},{8,9},{9,10},{10,1... | collective-permute-start | bytes 1032200 | tf_op jit(solution)/shard_map/ppermute | solution.py:39
  130.8 8.6 %collective-permute-start.17 = (bf16[224,512]{1,0:T(8,128)(2,1)S(1)}, bf16[224,512]{1,0:T(8,128)(2,1)S(1)}, u32[]{:S(2)}, u32[]{:S(2)}) collective-permute-start(bf16[224,512]{1,0:T(8,128)(2,1)S(1)} %get-tuple-element.168), channel_id=1, source_target_pairs={{0,8},{4,12},{8,0},{12,4},{16,24},{20,28},{24,16},{28,20},{1,9},{5... | collective-permute-start | bytes 688136 | tf_op jit(solution)/shard_map/ppermute | solution.py:292
  131.2 11.0 %collective-permute-start.18 = (bf16[224,512]{1,0:T(8,128)(2,1)S(1)}, bf16[224,512]{1,0:T(8,128)(2,1)S(1)}, u32[]{:S(2)}, u32[]{:S(2)}) collective-permute-start(bf16[224,512]{1,0:T(8,128)(2,1)S(1)} %get-tuple-element.167), channel_id=1, source_target_pairs={{0,16},{4,20},{8,24},{12,28},{16,0},{20,4},{24,8},{28,12},{1,17},{... | collective-permute-start | bytes 688136 | tf_op jit(solution)/shard_map/ppermute | solution.py:292
  132.6 10.2 %collective-permute-start.19 = (bf16[224,512]{1,0:T(8,128)(2,1)S(1)}, bf16[224,512]{1,0:T(8,128)(2,1)S(1)}, u32[]{:S(2)}, u32[]{:S(2)}) collective-permute-start(bf16[224,512]{1,0:T(8,128)(2,1)S(1)} %get-tuple-element.166), channel_id=1, source_target_pairs={{0,24},{4,28},{8,16},{12,20},{16,8},{20,12},{24,0},{28,4},{1,25},{... | collective-permute-start | bytes 688136 | tf_op jit(solution)/shard_map/ppermute | solution.py:292
  143.6 15.9 %copy-start.16 = (bf16[224,512]{1,0:T(8,128)(2,1)S(1)}, bf16[224,512]{1,0:T(8,128)(2,1)}, u32[]{:S(2)}) copy-start(bf16[224,512]{1,0:T(8,128)(2,1)} %copy-done.15) | copy-start | bytes 688132
  143.6 15.9 %collective-permute-start.22 = (bf16[304,512]{1,0:T(8,128)(2,1)S(1)}, bf16[304,512]{1,0:T(8,128)(2,1)S(1)}, u32[]{:S(2)}, u32[]{:S(2)}) collective-permute-start(bf16[304,512]{1,0:T(8,128)(2,1)S(1)} %add_convert_fusion.4), channel_id=1, source_target_pairs={{0,2},{1,3},{2,0},{3,1},{4,6},{5,7},{6,4},{7,5},{8,10},{9,11},{10,... | collective-permute-start | bytes 933896 | tf_op jit(solution)/shard_map/ppermute | solution.py:292
  147.3 19.7 %copy-start.5 = (f32[448,512]{1,0:T(8,128)S(1)}, f32[448,512]{1,0:T(8,128)}, u32[]{:S(2)}) copy-start(f32[448,512]{1,0:T(8,128)} %get-tuple-element.106) | copy-start | bytes 2752516
  149.1 10.4 %collective-permute-start.20 = (bf16[112,512]{1,0:T(8,128)(2,1)}, bf16[112,512]{1,0:T(8,128)(2,1)}, u32[]{:S(2)}, u32[]{:S(2)}) collective-permute-start(bf16[112,512]{1,0:T(8,128)(2,1)} %fusion.17), channel_id=1, source_target_pairs={{0,1},{1,0},{2,3},{3,2},{4,5},{5,4},{6,7},{7,6},{8,9},{9,8},{10,11... | collective-permute-start | bytes 344072 | tf_op jit(solution)/shard_map/ppermute | solution.py:292
  160.5 6.5 %collective-permute-start.23 = (bf16[112,512]{1,0:T(8,128)(2,1)S(1)}, bf16[112,512]{1,0:T(8,128)(2,1)S(1)}, u32[]{:S(2)}, u32[]{:S(2)}) collective-permute-start(bf16[112,512]{1,0:T(8,128)(2,1)S(1)} %add_convert_fusion.9), channel_id=1, source_target_pairs={{0,2},{1,3},{2,0},{3,1},{4,6},{5,7},{6,4},{7,5},{8,10},{9,11},{10,... | collective-permute-start | bytes 344072 | tf_op jit(solution)/shard_map/ppermute | solution.py:292
  167.0 8.5 %collective-permute-start.24 = (bf16[304,512]{1,0:T(8,128)(2,1)S(1)}, bf16[304,512]{1,0:T(8,128)(2,1)S(1)}, u32[]{:S(2)}, u32[]{:S(2)}) collective-permute-start(bf16[304,512]{1,0:T(8,128)(2,1)S(1)} %add_convert_fusion.3.half), channel_id=1, source_target_pairs={{0,1},{1,0},{2,3},{3,2},{4,5},{5,4},{6,7},{7,6},{8,9},{9,8},{10,11... | collective-permute-start | bytes 933896 | tf_op jit(solution)/shard_map/ppermute | solution.py:292
  175.5 4.8 %collective-permute-start.25 = (bf16[112,512]{1,0:T(8,128)(2,1)S(1)}, bf16[112,512]{1,0:T(8,128)(2,1)S(1)}, u32[]{:S(2)}, u32[]{:S(2)}) collective-permute-start(bf16[112,512]{1,0:T(8,128)(2,1)S(1)} %add_convert_fusion.8.half), channel_id=1, source_target_pairs={{0,1},{1,0},{2,3},{3,2},{4,5},{5,4},{6,7},{7,6},{8,9},{9,8},{10,11... | collective-permute-start | bytes 344072 | tf_op jit(solution)/shard_map/ppermute | solution.py:292
  (14 other events, 43.7 us)
Sparse Core Ops, SparseCore 0:
  12.1 45.4 all-gather.2

commit v2 on v1

--- a/solution.py
+++ b/solution.py
@@ -1,3 +1,5 @@
+import math
+
 import jax
 import jax.numpy as jnp
 from jax import lax
@@ -31,7 +33,7 @@
 SCALE = HEAD**-0.5
 BF = jnp.bfloat16
 F32 = jnp.float32
-VMEM_LIMIT = 60 * 1024 * 1024
+VMEM_LIMIT = 36 * 1024 * 1024
 
 
 def shifted_2(value, axis, by):
@@ -53,6 +55,14 @@
 
 def iota(shape, axis):
     return lax.broadcasted_iota(jnp.int32, shape, axis)
+
+
+def shard_place():
+    return lax.axis_index("shard").astype(jnp.int32)
+
+
+def late_place():
+    return lax.axis_index("seq").astype(jnp.int32) & 1
 
 
 def one_hot(condition):
@@ -132,11 +142,10 @@
 
 
 def kernel_call(
-    body, outs, ins, scratch=(), smem=0, apart=0, grid=None, in_blocks=None, out_blocks=None,
+    body, outs, ins, scratch=(), apart=0, grid=None, in_blocks=None, out_blocks=None,
     vmem=VMEM_LIMIT,
 ):
-    in_specs = [whole(pltpu.SMEM)] * smem
-    in_specs += in_blocks or [whole()] * (len(ins) - smem - apart) + [whole(pl.ANY)] * apart
+    in_specs = in_blocks or [whole()] * (len(ins) - apart) + [whole(pl.ANY)] * apart
     options = {"grid": grid} if grid else {}
     return pl.pallas_call(
         body,
@@ -174,10 +183,10 @@
 
 
 def pack_body(
-    me_ref, g1, b1, wqkv, bqv, table, wproj, bproj, g2, b2, win, bin_, wout, bout, attn, mlp
+    g1, b1, wqkv, bqv, table, wproj, bproj, g2, b2, win, bin_, wout, bout, attn, mlp
 ):
     depth = wqkv.shape[0]
-    me = me_ref[0]
+    me = shard_place()
     for c in range(3):
         attn[c * depth : (c + 1) * depth, :] = wqkv[:, c * D : (c + 1) * D]
     attn[3 * depth : 4 * depth, :] = wproj[...]
@@ -201,7 +210,8 @@
     for c in range(FF // D):
         mlp[c * depth : (c + 1) * depth, :] = win[:, c * D : (c + 1) * D]
     mlp[4 * depth : 8 * depth, :] = wout[...]
-    hidden_bias = place(bin_[...], FF, me)
+    held = jnp.concatenate([bin_[r : r + 1] for r in range(bin_.shape[0])], 1)
+    hidden_bias = place(held, FF, me)
     rows = [place(v, D, me) for v in (g2[...], b2[...], bout[...])]
     rows += [hidden_bias[:, c * D : (c + 1) * D] for c in range(FF // D)]
     mlp[8 * depth :, :] = padded(rows, SMALL)
@@ -219,10 +229,10 @@
         copy.wait()
 
 
-def unpack_attn_body(me_ref, half, back, g1, b1, wqkv, bqv, table, attn, sems):
+def unpack_attn_body(half, back, g1, b1, wqkv, bqv, table, attn, sems):
     depth = wqkv.shape[0]
-    me = me_ref[0]
-    join_halves(me_ref[1], half, back, attn, sems)
+    me = shard_place()
+    join_halves(late_place(), half, back, attn, sems)
     for c in range(3):
         wqkv[:, c * D : (c + 1) * D] = attn[c * depth : (c + 1) * depth, :].astype(F32)
     small = attn[3 * depth :, :].astype(F32)
@@ -252,11 +262,11 @@
 
 
 def unpack_mlp_body(
-    me_ref, half, back, wproj, bproj, g2, b2, win, bin_, wout, bout, mlp, sems
+    half, back, wproj, bproj, g2, b2, win, bin_, wout, bout, mlp, sems
 ):
     depth = win.shape[0]
-    me = me_ref[0]
-    join_halves(me_ref[1], half, back, mlp, sems)
+    me = shard_place()
+    join_halves(late_place(), half, back, mlp, sems)
     for c in range(FF // D):
         win[:, c * D : (c + 1) * D] = mlp[c * depth : (c + 1) * depth, :].astype(F32)
     wout[...] = mlp[4 * depth : 8 * depth, :].astype(F32)
@@ -267,7 +277,9 @@
     bout[...] = mine(small[2:3], depth, me)
     bproj[...] = mine(small[3:4], depth, me)
     hidden = jnp.concatenate([small[4 + c : 5 + c] for c in range(FF // D)], 1)
-    bin_[...] = mine(hidden, depth * FF // D, me)
+    hidden = mine(hidden, depth * FF // D, me)
+    for r in range(bin_.shape[0]):
+        bin_[r : r + 1] = hidden[:, r * 128 : (r + 1) * 128]
 
 
 def put_shares(me, same, other, start, values, first=0):
@@ -319,7 +331,10 @@
     out = []
     for start in (late * half, (1 - late) * half):
         total = 0.0
-        for part in (same[0], came[0], *parts):
+        for whole_part in (same, came):
+            part = lax.dynamic_slice(whole_part, (0, start, 0), (1, half, D))
+            total += part.reshape(half, D).astype(F32)
+        for part in parts:
             total += lax.dynamic_slice_in_dim(part, start, half, 0).astype(F32)
         out.append(total.astype(BF))
     return out
@@ -347,12 +362,12 @@
     return jnp.sum(slab[:, start:, :].astype(F32), 0)
 
 
-def project_body(me_ref, tokens, halo, *refs):
+def project_body(tokens, halo, *refs):
     shards = len(refs) - 7
     pieces = refs[:shards]
     normed_win, query, key, value, slab, wide, sems = refs[shards:]
     copies = [
-        pltpu.make_async_copy(piece, slab.at[me_ref[0] ^ p], sems.at[p])
+        pltpu.make_async_copy(piece, slab.at[shard_place() ^ p], sems.at[p])
         for p, piece in enumerate(pieces)
     ]
     for copy in copies:
@@ -441,20 +456,20 @@
 
 
 def gelu_parts(h):
-    size = jnp.abs(h) * (0.5**0.5)
-    t = 1.0 / (1.0 + 0.3275911 * size)
-    bell = jnp.exp(-0.5 * h * h)
+    under = 1.0 + (0.3275911 * 0.5**0.5) * jnp.abs(h)
+    t = pl.reciprocal(under, approx=True)
+    t = t * (2.0 - under * t)
+    bell = jnp.exp2(h * h * (-0.5 / math.log(2.0)))
     poly = t * (
-        0.254829592
-        + t * (-0.284496736 + t * (1.421413741 + t * (-1.453152027 + t * 1.061405429)))
+        0.127414796
+        + t * (-0.142248368 + t * (0.7107068705 + t * (-0.7265760135 + t * 0.5307027145)))
     )
-    tail = 0.5 * poly * bell
+    tail = poly * bell
     upto = jnp.where(h >= 0, 1.0 - tail, tail)
     return upto, bell * 0.3989422804014327
 
 
 def mlp_body(
-    me_ref,
     mixed,
     cotangent,
     cot_halo,
@@ -473,7 +488,7 @@
     back_sum,
     wide,
 ):
-    me = me_ref[0]
+    me = shard_place()
     shards, height = slab.shape[:2]
     depth = (height - SMALL) // 8
     span = shards * D // FF
@@ -590,7 +605,6 @@
 
 
 def attn_last_body(
-    me_ref,
     grad_mixed,
     tokens,
     halo,
@@ -601,7 +615,7 @@
 ):
     grads = refs[:-7]
     kept, sent, same, other_low, other_high, wide, other = refs[-7:]
-    me = me_ref[0]
+    me = shard_place()
     shards = slab.shape[0]
     depth = (slab.shape[1] - SMALL) // 4
     small = smalls_of(slab, 4 * depth)
@@ -691,9 +705,7 @@
     images, local_rows, columns, _ = tokens.shape
     assert images == 1 and local_rows == WIN and columns == WIDTH
     shards = lax.axis_size("shard")
-    me = lax.axis_index("shard").astype(jnp.int32)
     seq = lax.axis_index("seq").astype(jnp.int32)
-    where = jnp.stack([me, seq & 1])
     chips = shards // 2
     depth = D // shards
     own = WIN - SHIFT
@@ -704,7 +716,7 @@
         gain_two[None],
         bias_two[None],
         w_in,
-        bias_in[None],
+        bias_in.reshape(-1, 128),
         w_out,
         bias_out[None],
     )
@@ -712,8 +724,8 @@
     attn_slab, mlp_slab = kernel_call(
         pack_body,
         [like((4 * depth + SMALL, D), BF), like((8 * depth + SMALL, D), BF)],
-        (where, *attn_params, *mlp_params),
-        smem=1,
+        (*attn_params, *mlp_params),
+        vmem=60 * 1024 * 1024,
     )
     pieces = gather_pieces(attn_slab)
     mlp_all = lax.all_gather(mlp_slab, "shard")
@@ -726,12 +738,11 @@
     normed_win, query, key, value, attn_all = kernel_call(
         project_body,
         [like((PADDED, D), BF)] * 4 + [like((shards, *attn_slab.shape), BF)],
-        (where, tokens_here, token_halo, *pieces),
+        (tokens_here, token_halo, *pieces),
         scratch=[
             pltpu.VMEM((WINDOWS, WIN, SLOT, D), F32),
             pltpu.SemaphoreType.DMA((shards,)),
         ],
-        smem=1,
         apart=shards,
     )
     pair_rows = 2 * PLACES
@@ -782,7 +793,7 @@
             share,
             share,
         ],
-        (where, mixed, cot_here, cot_halo, mlp_all, attn_all, restored),
+        (mixed, cot_here, cot_halo, mlp_all, attn_all, restored),
         scratch=[
             pltpu.VMEM((TOKENS, D), BF),
             pltpu.VMEM((TOKENS, D), BF),
@@ -790,7 +801,6 @@
             pltpu.VMEM((TOKENS, D), F32),
             pltpu.VMEM((WINDOWS, WIN, SLOT, D), F32),
         ],
-        smem=1,
     )
 
     def backward(first, count, grad_win, came):
@@ -822,24 +832,22 @@
             like((chips // 2, 3 * depth + SMALL, D), BF),
             like((chips // 2, 3 * depth + SMALL, D), BF),
         ],
-        (where, grad_mixed, tokens_here, token_halo, attn_all, normed_win, pairs, early, late_part),
+        (grad_mixed, tokens_here, token_halo, attn_all, normed_win, pairs, early, late_part),
         scratch=[
             pltpu.VMEM((WINDOWS, WIN, SLOT, D), F32),
             pltpu.VMEM((chips, 3 * depth + SMALL, D), BF),
         ],
-        smem=1,
     )
     attn_came = [exchange(other, "shard", 1) for other in attn_others]
     mlp_parts, attn_came = tie(mlp_parts, attn_came)
     keep_m, send = add_chips(late, mlp_same, mlp_came, mlp_parts)
-    (send,), attn_came = tie([send], attn_came)
-    attn_came = [came[q] for came in attn_came for q in range(chips // 2)]
     near_m = exchange(send, "seq", 1)
-    attn_parts = to_chips(add_cores(attn_same, attn_came))
+    came = [c[q] for c in attn_came for q in range(chips // 2)]
+    attn_parts = to_chips([add_pair(attn_same[q], came[q]) for q in range(1, chips)])
     half_m = add_pair(keep_m, near_m)
     (half_m,), attn_parts = tie([half_m], attn_parts)
     far_m = exchange(half_m, "seq", 2)
-    keep, send = add_chips(late, attn_same, attn_came, attn_parts)
+    keep, send = add_chips(late, attn_same, attn_came[0], attn_parts)
     near = exchange(send, "seq", 1)
     tok_halo = shifted_2(tok_sent, "seq", 1)
     (near, tok_halo), (far_m,) = tie([near, tok_halo], [far_m])
@@ -856,13 +864,12 @@
         return kernel_call(
             body,
             [like(p.shape, F32) for p in params],
-            (where, half, back),
+            (half, back),
             scratch=[
                 pltpu.VMEM((2 * half.shape[0], D), BF),
                 pltpu.SemaphoreType.DMA((2,)),
             ],
-            smem=1,
-            apart=2,
+                apart=2,
             vmem=16 * 1024 * 1024,
         )
 

time: 190 us -> 187 us (0.984)
  Pallas kernels: 72.2 us -> 48.9 us
  local copies, waits for them, and re-layouts: 11 us -> 26.4 us
  waiting for transfers between devices: 48.9 us -> 54.1 us
    pallas_call x9, Pallas kernels: 72.2 us -> 48.9 us  [kernel_call(): pl.pallas_call(body, out_shape=tuple(outs), in_specs=in_specs, out_specs=...]
    unnamed x38 -> x92, local copies, waits for them, and re-layouts: 2.82 us -> 24.1 us
    ppermute x22, waiting for transfers between devices: 48.9 us -> 54 us  [exchange(): return lax.ppermute(value, axis, [(i, i ^ mask) for i in range(peers)])]
    slice x4 -> x0, local copies, waits for them, and re-layouts: 2.25 us -> none  [the longest x1 1.2 us: add_chips(): came[0]]
  transfers between devices with their start and end apart: 27 -> 27, of which waited for: 14 -> 13; matrix products, arithmetic and copies ran while one was open for 9% -> 7% of each run, Pallas kernels for 23% -> 12%
where the time goes in v2:
time: 187 us; the launch traced here: 186 us
  waiting for transfers between devices  54.1 us (29%)
  Pallas kernels  48.9 us (26%)
  starting transfers between devices  29.4 us (16%)
  local copies, waits for them, and re-layouts  26.4 us (14%)
  between operations  14.5 us (8%)
  other arithmetic  13 us (7%)
    ppermute x22, waiting for transfers between devices, exchange(): return lax.ppermute(value, axis, [(i, i ^ mask) for i in range(peers)])  54 us
    pallas_call x9, Pallas kernels, kernel_call(): pl.pallas_call(body, out_shape=tuple(outs), in_specs=in_specs, out_specs=...  48.9 us
    unnamed x92, local copies, waits for them, and re-layouts  24.1 us
    ppermute x22, starting transfers between devices, exchange(): return lax.ppermute(value, axis, [(i, i ^ mask) for i in range(peers)])  19 us
    ppermute x4, starting transfers between devices, shifted_2(): lax.ppermute(value, axis, [(i, (i + by) % peers) for i in range(peers)])  10.4 us
    convert_element_type x6, other arithmetic, add_pair(): return (here.astype(F32) + came.astype(F32)).astype(BF)  5.94 us
  transfers between devices with their start and end apart: 27, of which 13 were waited for; matrix products, arithmetic and copies ran while one was open for 7% of the time, Pallas kernels for 12%

profile of v2, /device:TPU:0, one launch (start us, length us, event | category | flops | bytes accessed | tf_op | source)
XLA Modules:
  0.0 186.2 jit_solution(11036295270973975010)
XLA Ops:
  7.3 2.9 %shard_map.271 = (bf16[288,512]{1,0:T(8,128)(2,1)}, bf16[544,512]{1,0:T(8,128)(2,1)}) custom-call(bf16[1,64]{1,0:T(2,128)(2,1)} %bitcast.85, bf16[1,64]{1,0:T(2,128)(2,1)} %bitcast.86, bf16[64,1536]{1,0:T(8,128)(2,1)} %wqkv.1, bf16[2,64]{1,0:T(2,128)(2,1)} %bqv.1, bf16[2,169]{1,0:T(2,128)(2,1)} %bitcast.84, bf16[64,512]{1,0:T(8,128)(2,1)} %wproj.1, ...), custom_call_target="tpu_custom_call" | custom-call | flops 1024 | bytes 1024 | tf_op jit(solution)/shard_map/pallas_call | solution.py:150
  10.2 3.0 %collective-permute-start.2 = (bf16[288,512]{1,0:T(8,128)(2,1)}, bf16[288,512]{1,0:T(8,128)(2,1)S(1)}, u32[]{:S(2)}, u32[]{:S(2)}) collective-permute-start(bf16[288,512]{1,0:T(8,128)(2,1)} %get-tuple-element.86.refs_0_), channel_id=1, source_target_pairs={{0,8},{4,12},{8,0},{12,4},{16,24},{20,28},{24,16},{28,20},{1,9},{5... | collective-permute-start | bytes 884744 | tf_op jit(solution)/shard_map/ppermute | solution.py:304
  13.2 1.5 collective-permute-start.4
  14.8 4.1 %collective-permute-start = (bf16[3,112,512]{2,1,0:T(8,128)(2,1)S(1)}, bf16[3,112,512]{2,1,0:T(8,128)(2,1)S(1)}, u32[]{:S(2)}, u32[]{:S(2)}) collective-permute-start(bf16[3,112,512]{2,1,0:T(8,128)(2,1)S(1)} %slice_bitcast_fusion.1), channel_id=1, source_target_pairs={{0,3},{1,0},{2,1},{3,2},{4,7},{5,4},{6,5},{7,6},{8,11},{9,8},{10,9... | collective-permute-start | bytes 1032200 | tf_op jit(solution)/shard_map/ppermute | solution.py:41
  18.9 1.8 slice_bitcast_fusion
  21.2 4.2 %collective-permute-start.8 = (bf16[3,112,512]{2,1,0:T(8,128)(2,1)}, bf16[3,112,512]{2,1,0:T(8,128)(2,1)}, u32[]{:S(2)}, u32[]{:S(2)}) collective-permute-start(bf16[3,112,512]{2,1,0:T(8,128)(2,1)} %slice_bitcast_fusion), channel_id=1, source_target_pairs={{0,3},{1,0},{2,1},{3,2},{4,7},{5,4},{6,5},{7,6},{8,11},{9,8},{10,9... | collective-permute-start | bytes 1032200 | tf_op jit(solution)/shard_map/ppermute | solution.py:41
  25.4 4.0 %collective-permute-done.4.refs_4_ = bf16[288,512]{1,0:T(8,128)(2,1)S(1)} collective-permute-done((bf16[288,512]{1,0:T(8,128)(2,1)}, bf16[288,512]{1,0:T(8,128)(2,1)S(1)}, u32[]{:S(2)}, u32[]{:S(2)}) %collective-permute-start.4) | collective-permute-done | bytes 294944 | tf_op jit(solution)/shard_map/ppermute | solution.py:304
  29.4 3.4 %collective-permute-done.6.refs_6_ = bf16[288,512]{1,0:T(8,128)(2,1)S(1)} collective-permute-done((bf16[288,512]{1,0:T(8,128)(2,1)}, bf16[288,512]{1,0:T(8,128)(2,1)S(1)}, u32[]{:S(2)}, u32[]{:S(2)}) %collective-permute-start.6) | collective-permute-done | bytes 294944 | tf_op jit(solution)/shard_map/ppermute | solution.py:304
  45.8 3.0 %shard_map.272 = (bf16[896,512]{1,0:T(8,128)(2,1)S(1)}, bf16[896,512]{1,0:T(8,128)(2,1)S(1)}, bf16[896,512]{1,0:T(8,128)(2,1)S(1)}, bf16[896,512]{1,0:T(8,128)(2,1)S(1)}, bf16[8,288,512]{2,1,0:T(8,128)(2,1)S(1)}) custom-call(bf16[7,112,512]{2,1,0:T(8,128)(2,1)S(1)} %bitcast.76, bf16[3,112,512]{2,1,0:T(8,128)(2,1)S(1)} %collective-permute-done.halo, ...), custom_call_target="tpu_custom_call" | custom-call | flops 1024 | bytes 1024 | tf_op jit(solution)/shard_map/pallas_call | solution.py:150
  49.9 7.1 %shard_map.273 = (bf16[8,4,112,256]{3,2,1,0:T(8,128)(2,1)S(1)}, bf16[784,512]{1,0:T(8,128)(2,1)S(1)}, f32[784,512]{1,0:T(8,128)S(1)}) custom-call(bf16[8,288,512]{2,1,0:T(8,128)(2,1)S(1)} %get-tuple-element.87.slab.attn_slab, f32[16,56,128]{2,1,0:T(8,128)S(1)} %broadcast_in_dim.35.reg_rows, f32[16,1,256]{2,1,0:T(1,128)S(1)} %tile.9.reg_lanes, ...), custom_call_target="tpu_custom_call" | custom-call | flops 1024 | bytes 1024 | tf_op jit(solution)/shard_map/pallas_call | solution.py:150
  64.1 21.4 %shard_map.274 = (f32[448,512]{1,0:T(8,128)S(1)}, bf16[336,512]{1,0:T(8,128)(2,1)S(1)}, f32[784,512]{1,0:T(8,128)S(1)}, bf16[896,512]{1,0:T(8,128)(2,1)S(1)}, bf...) custom-call(f32[784,512]{1,0:T(8,128)S(1)} %copy-done.13, bf16[7,112,512]{2,1,0:T(8,128)(2,1)S(1)} %bitcast.79, ...), custom_call_target="tpu_custom_call" | custom-call | flops 1024 | bytes 1024 | tf_op jit(solution)/shard_map/pallas_call | solution.py:150
  85.6 1.7 collective-permute-start.9
  87.4 2.9 %shard_map.275 = (bf16[448,1536]{1,0:T(8,128)(2,1)S(1)}, f32[4,56,256]{2,1,0:T(8,128)S(1)}) custom-call(bf16[896,512]{1,0:T(8,128)(2,1)S(1)} %copy-done.3, bf16[896,512]{1,0:T(8,128)(2,1)S(1)} %copy-done.5, bf16[896,512]{1,0:T(8,128)(2,1)S(1)} %copy-done.7, bf16[8,4,112,256]{3,2,1,0:T(8,128)(2,1)S(1)} %copy-done.9, ...), custom_call_target="tpu_custom_call" | custom-call | flops 1024 | bytes 1024 | tf_op jit(solution)/shard_map/pallas_call | solution.py:150
  90.4 2.0 %fusion.2 = (bf16[608,512]{1,0:T(8,128)(2,1)}, bf16[608,512]{1,0:T(8,128)(2,1)}, bf16[608,512]{1,0:T(8,128)(2,1)}) fusion(bf16[4,608,512]{2,1,0:T(8,128)(2,1)S(1)} %collective-permute-done.10, bf16[4,608,512]{2,1,0:T(8,128)(2,1)S(1)} %get-tuple-element.97), kind=kLoop, calls=%fused_computation.7 | loop fusion | flops 3735552 | bytes 5603328 | tf_op jit(solution)/shard_map/convert_element_type | solution.py:318
  92.5 2.4 %collective-permute-start.11 = (bf16[608,512]{1,0:T(8,128)(2,1)}, bf16[608,512]{1,0:T(8,128)(2,1)}, u32[]{:S(2)}, u32[]{:S(2)}) collective-permute-start(bf16[608,512]{1,0:T(8,128)(2,1)} %get-tuple-element.110), channel_id=1, source_target_pairs={{0,8},{4,12},{8,0},{12,4},{16,24},{20,28},{24,16},{28,20},{1,9},{5... | collective-permute-start | bytes 1867784 | tf_op jit(solution)/shard_map/ppermute | solution.py:304
  96.3 2.9 %shard_map.276 = (bf16[448,1536]{1,0:T(8,128)(2,1)S(1)}, f32[4,56,256]{2,1,0:T(8,128)S(1)}) custom-call(bf16[896,512]{1,0:T(8,128)(2,1)S(1)} %copy-done.3, bf16[896,512]{1,0:T(8,128)(2,1)S(1)} %copy-done.5, bf16[896,512]{1,0:T(8,128)(2,1)S(1)} %copy-done.7, bf16[8,4,112,256]{3,2,1,0:T(8,128)(2,1)S(1)} %copy-done.9, ...), custom_call_target="tpu_custom_call" | custom-call | flops 1024 | bytes 1024 | tf_op jit(solution)/shard_map/pallas_call | solution.py:150
  99.2 5.9 %shard_map.277 = (f32[448,512]{1,0:T(8,128)S(1)}, bf16[336,512]{1,0:T(8,128)(2,1)S(1)}, bf16[4,224,512]{2,1,0:T(8,128)(2,1)S(1)}, bf16[2,224,512]{2,1,0:T(8,128)(2,1)}, bf16[2,224,512]{2,1,0:T(8,128)(2,1)}) custom-call(f32[784,512]{1,0:T(8,128)S(1)} %get-tuple-element.104.grad_mixed, bf16[7,112,512]{2,1,0:T(8,128)(2,1)S(1)} %bitcast.78, ...), custom_call_target="tpu_custom_call" | custom-call | flops 1024 | bytes 1024 | tf_op jit(solution)/shard_map/pallas_call | solution.py:150
  108.2 1.5 collective-permute-done.14
  110.4 13.9 %collective-permute-done.12 = bf16[608,512]{1,0:T(8,128)(2,1)} collective-permute-done((bf16[608,512]{1,0:T(8,128)(2,1)}, bf16[608,512]{1,0:T(8,128)(2,1)}, u32[]{:S(2)}, u32[]{:S(2)}) %collective-permute-start.12) | collective-permute-done | bytes 622624 | tf_op jit(solution)/shard_map/ppermute | solution.py:304
  124.3 1.5 fusion.5
  125.9 1.7 collective-permute-start.16
  130.0 1.8 collective-permute-start.19
  131.7 3.7 %collective-permute-done.16 = bf16[304,512]{1,0:T(8,128)(2,1)S(1)} collective-permute-done((bf16[304,512]{1,0:T(8,128)(2,1)S(1)}, bf16[304,512]{1,0:T(8,128)(2,1)S(1)}, u32[]{:S(2)}, u32[]{:S(2)}) %collective-permute-start.16) | collective-permute-done | bytes 311328 | tf_op jit(solution)/shard_map/ppermute | solution.py:304
  135.4 1.6 add_convert_fusion.4
  137.0 2.6 %collective-permute-done.18 = bf16[224,512]{1,0:T(8,128)(2,1)S(1)} collective-permute-done((bf16[224,512]{1,0:T(8,128)(2,1)S(1)}, bf16[224,512]{1,0:T(8,128)(2,1)S(1)}, u32[]{:S(2)}, u32[]{:S(2)}) %collective-permute-start.18) | collective-permute-done | bytes 229408 | tf_op jit(solution)/shard_map/ppermute | solution.py:304
  141.0 2.6 %collective-permute-start.22 = (bf16[304,512]{1,0:T(8,128)(2,1)S(1)}, bf16[304,512]{1,0:T(8,128)(2,1)}, u32[]{:S(2)}, u32[]{:S(2)}) collective-permute-start(bf16[304,512]{1,0:T(8,128)(2,1)S(1)} %add_convert_fusion.4), channel_id=1, source_target_pairs={{0,2},{1,3},{2,0},{3,1},{4,6},{5,7},{6,4},{7,5},{8,10},{9,11},{10,... | collective-permute-start | bytes 933896 | tf_op jit(solution)/shard_map/ppermute | solution.py:304
  143.6 1.8 fusion.17
  146.7 3.8 %collective-permute-done.20 = bf16[112,512]{1,0:T(8,128)(2,1)} collective-permute-done((bf16[112,512]{1,0:T(8,128)(2,1)}, bf16[112,512]{1,0:T(8,128)(2,1)}, u32[]{:S(2)}, u32[]{:S(2)}) %collective-permute-start.20) | collective-permute-done | bytes 114720 | tf_op jit(solution)/shard_map/ppermute | solution.py:304
  150.5 6.7 %collective-permute-done.22 = bf16[304,512]{1,0:T(8,128)(2,1)} collective-permute-done((bf16[304,512]{1,0:T(8,128)(2,1)S(1)}, bf16[304,512]{1,0:T(8,128)(2,1)}, u32[]{:S(2)}, u32[]{:S(2)}) %collective-permute-start.22) | collective-permute-done | bytes 311328 | tf_op jit(solution)/shard_map/ppermute | solution.py:304
  159.4 5.1 %collective-permute-done.23 = bf16[112,512]{1,0:T(8,128)(2,1)S(1)} collective-permute-done((bf16[112,512]{1,0:T(8,128)(2,1)S(1)}, bf16[112,512]{1,0:T(8,128)(2,1)S(1)}, u32[]{:S(2)}, u32[]{:S(2)}) %collective-permute-start.23) | collective-permute-done | bytes 114720 | tf_op jit(solution)/shard_map/ppermute | solution.py:304
  166.9 6.2 %collective-permute-done.24.back = bf16[304,512]{1,0:T(8,128)(2,1)S(1)} collective-permute-done((bf16[304,512]{1,0:T(8,128)(2,1)S(1)}, bf16[304,512]{1,0:T(8,128)(2,1)S(1)}, u32[]{:S(2)}, u32[]{:S(2)}) %collective-permute-start.24) | collective-permute-done | bytes 311328 | tf_op jit(solution)/shard_map/ppermute | solution.py:304
  176.1 1.8 collective-permute-done.25.back
  (148 shorter events, 41.3 us)
Async XLA Ops:
  7.2 28.3 %copy-start = (s32[1,28,112]{2,0,1:T(1,128)S(1)}, s32[1,28,112]{2,0,1:T(1,128)}, u32[]{:S(2)}) copy-start(s32[1,28,112]{2,0,1:T(1,128)} %param.17) | copy-start | bytes 37636
  7.2 53.2 %all-gather.3.cloned.1.call-start = ((), (), s32[]{:S(2)}) async-start(), calls=%async_computation | async-start | bytes 5013504 | tf_op jit(solution)/shard_map/all_gather | solution.py:731
  10.2 11.1 %collective-permute-start.2 = (bf16[288,512]{1,0:T(8,128)(2,1)}, bf16[288,512]{1,0:T(8,128)(2,1)S(1)}, u32[]{:S(2)}, u32[]{:S(2)}) collective-permute-start(bf16[288,512]{1,0:T(8,128)(2,1)} %get-tuple-element.86.refs_0_), channel_id=1, source_target_pairs={{0,8},{4,12},{8,0},{12,4},{16,24},{20,28},{24,16},{28,20},{1,9},{5... | collective-permute-start | bytes 884744 | tf_op jit(solution)/shard_map/ppermute | solution.py:304
  13.2 16.2 %collective-permute-start.4 = (bf16[288,512]{1,0:T(8,128)(2,1)}, bf16[288,512]{1,0:T(8,128)(2,1)S(1)}, u32[]{:S(2)}, u32[]{:S(2)}) collective-permute-start(bf16[288,512]{1,0:T(8,128)(2,1)} %get-tuple-element.86.refs_0_), channel_id=1, source_target_pairs={{0,16},{4,20},{8,24},{12,28},{16,0},{20,4},{24,8},{28,12},{1,17},{... | collective-permute-start | bytes 884744 | tf_op jit(solution)/shard_map/ppermute | solution.py:304
  14.7 18.1 %collective-permute-start.6 = (bf16[288,512]{1,0:T(8,128)(2,1)}, bf16[288,512]{1,0:T(8,128)(2,1)S(1)}, u32[]{:S(2)}, u32[]{:S(2)}) collective-permute-start(bf16[288,512]{1,0:T(8,128)(2,1)} %get-tuple-element.86.refs_0_), channel_id=1, source_target_pairs={{0,24},{4,28},{8,16},{12,20},{16,8},{20,12},{24,0},{28,4},{1,25},{... | collective-permute-start | bytes 884744 | tf_op jit(solution)/shard_map/ppermute | solution.py:304
  14.7 18.8 %collective-permute-start.1 = (bf16[288,512]{1,0:T(8,128)(2,1)}, bf16[288,512]{1,0:T(8,128)(2,1)S(1)}, u32[]{:S(2)}, u32[]{:S(2)}) collective-permute-start(bf16[288,512]{1,0:T(8,128)(2,1)} %get-tuple-element.86.refs_0_), channel_id=1, source_target_pairs={{0,4},{4,0},{8,12},{12,8},{16,20},{20,16},{24,28},{28,24},{1,5},{5... | collective-permute-start | bytes 884744 | tf_op jit(solution)/shard_map/ppermute | solution.py:304
  14.8 21.1 %collective-permute-start = (bf16[3,112,512]{2,1,0:T(8,128)(2,1)S(1)}, bf16[3,112,512]{2,1,0:T(8,128)(2,1)S(1)}, u32[]{:S(2)}, u32[]{:S(2)}) collective-permute-start(bf16[3,112,512]{2,1,0:T(8,128)(2,1)S(1)} %slice_bitcast_fusion.1), channel_id=1, source_target_pairs={{0,3},{1,0},{2,1},{3,2},{4,7},{5,4},{6,5},{7,6},{8,11},{9,8},{10,9... | collective-permute-start | bytes 1032200 | tf_op jit(solution)/shard_map/ppermute | solution.py:41
  21.2 39.2 %collective-permute-start.8 = (bf16[3,112,512]{2,1,0:T(8,128)(2,1)}, bf16[3,112,512]{2,1,0:T(8,128)(2,1)}, u32[]{:S(2)}, u32[]{:S(2)}) collective-permute-start(bf16[3,112,512]{2,1,0:T(8,128)(2,1)} %slice_bitcast_fusion), channel_id=1, source_target_pairs={{0,3},{1,0},{2,1},{3,2},{4,7},{5,4},{6,5},{7,6},{8,11},{9,8},{10,9... | collective-permute-start | bytes 1032200 | tf_op jit(solution)/shard_map/ppermute | solution.py:41
  29.4 6.5 %collective-permute-start.3 = (bf16[288,512]{1,0:T(8,128)(2,1)S(1)}, bf16[288,512]{1,0:T(8,128)(2,1)S(1)}, u32[]{:S(2)}, u32[]{:S(2)}) collective-permute-start(bf16[288,512]{1,0:T(8,128)(2,1)S(1)} %collective-permute-done.2.refs_2_), channel_id=1, source_target_pairs={{0,4},{4,0},{8,12},{12,8},{16,20},{20,16},{24,28},{28,24},{1,5},{5... | collective-permute-start | bytes 884744 | tf_op jit(solution)/shard_map/ppermute | solution.py:304
  32.8 3.8 %collective-permute-start.5 = (bf16[288,512]{1,0:T(8,128)(2,1)S(1)}, bf16[288,512]{1,0:T(8,128)(2,1)S(1)}, u32[]{:S(2)}, u32[]{:S(2)}) collective-permute-start(bf16[288,512]{1,0:T(8,128)(2,1)S(1)} %collective-permute-done.4.refs_4_), channel_id=1, source_target_pairs={{0,4},{4,0},{8,12},{12,8},{16,20},{20,16},{24,28},{28,24},{1,5},{5... | collective-permute-start | bytes 884744 | tf_op jit(solution)/shard_map/ppermute | solution.py:304
  34.2 3.1 %collective-permute-start.7 = (bf16[288,512]{1,0:T(8,128)(2,1)S(1)}, bf16[288,512]{1,0:T(8,128)(2,1)S(1)}, u32[]{:S(2)}, u32[]{:S(2)}) collective-permute-start(bf16[288,512]{1,0:T(8,128)(2,1)S(1)} %collective-permute-done.6.refs_6_), channel_id=1, source_target_pairs={{0,4},{4,0},{8,12},{12,8},{16,20},{20,16},{24,28},{28,24},{1,5},{5... | collective-permute-start | bytes 884744 | tf_op jit(solution)/shard_map/ppermute | solution.py:304
  64.1 23.3 %copy-start.3 = (bf16[896,512]{1,0:T(8,128)(2,1)S(1)}, bf16[896,512]{1,0:T(8,128)(2,1)}, u32[]{:S(2)}) copy-start(bf16[896,512]{1,0:T(8,128)(2,1)} %copy-done.2) | copy-start | bytes 2752516
  64.1 23.3 %copy-start.5 = (bf16[896,512]{1,0:T(8,128)(2,1)S(1)}, bf16[896,512]{1,0:T(8,128)(2,1)}, u32[]{:S(2)}) copy-start(bf16[896,512]{1,0:T(8,128)(2,1)} %copy-done.4) | copy-start | bytes 2752516
  64.1 23.3 %copy-start.7 = (bf16[896,512]{1,0:T(8,128)(2,1)S(1)}, bf16[896,512]{1,0:T(8,128)(2,1)}, u32[]{:S(2)}) copy-start(bf16[896,512]{1,0:T(8,128)(2,1)} %copy-done.6) | copy-start | bytes 2752516
  64.1 23.3 %copy-start.9 = (bf16[8,4,112,256]{3,2,1,0:T(8,128)(2,1)S(1)}, bf16[8,4,112,256]{3,2,1,0:T(8,128)(2,1)}, u32[]{:S(2)}) copy-start(bf16[8,4,112,256]{3,2,1,0:T(8,128)(2,1)} %copy-done.8) | copy-start | bytes 5505028
  85.5 4.8 %collective-permute-start.10 = (bf16[4,608,512]{2,1,0:T(8,128)(2,1)S(1)}, bf16[4,608,512]{2,1,0:T(8,128)(2,1)S(1)}, u32[]{:S(2)}, u32[]{:S(2)}) collective-permute-start(bf16[4,608,512]{2,1,0:T(8,128)(2,1)S(1)} %get-tuple-element.98), channel_id=1, source_target_pairs={{0,4},{4,0},{8,12},{12,8},{16,20},{20,16},{24,28},{28,24},{1,5},{5... | collective-permute-start | bytes 7471112 | tf_op jit(solution)/shard_map/ppermute | solution.py:304
  85.6 13.6 %collective-permute-start.9 = (bf16[336,512]{1,0:T(8,128)(2,1)S(1)}, bf16[336,512]{1,0:T(8,128)(2,1)S(1)}, u32[]{:S(2)}, u32[]{:S(2)}) collective-permute-start(bf16[336,512]{1,0:T(8,128)(2,1)S(1)} %get-tuple-element.94), channel_id=1, source_target_pairs={{0,1},{1,2},{2,3},{3,0},{4,5},{5,6},{6,7},{7,4},{8,9},{9,10},{10,1... | collective-permute-start | bytes 1032200 | tf_op jit(solution)/shard_map/ppermute | solution.py:41
  92.5 17.9 %collective-permute-start.11 = (bf16[608,512]{1,0:T(8,128)(2,1)}, bf16[608,512]{1,0:T(8,128)(2,1)}, u32[]{:S(2)}, u32[]{:S(2)}) collective-permute-start(bf16[608,512]{1,0:T(8,128)(2,1)} %get-tuple-element.110), channel_id=1, source_target_pairs={{0,8},{4,12},{8,0},{12,4},{16,24},{20,28},{24,16},{28,20},{1,9},{5... | collective-permute-start | bytes 1867784 | tf_op jit(solution)/shard_map/ppermute | solution.py:304
  94.9 29.4 %collective-permute-start.12 = (bf16[608,512]{1,0:T(8,128)(2,1)}, bf16[608,512]{1,0:T(8,128)(2,1)}, u32[]{:S(2)}, u32[]{:S(2)}) collective-permute-start(bf16[608,512]{1,0:T(8,128)(2,1)} %get-tuple-element.111), channel_id=1, source_target_pairs={{0,16},{4,20},{8,24},{12,28},{16,0},{20,4},{24,8},{28,12},{1,17},{... | collective-permute-start | bytes 1867784 | tf_op jit(solution)/shard_map/ppermute | solution.py:304
  95.5 28.8 %collective-permute-start.13 = (bf16[608,512]{1,0:T(8,128)(2,1)}, bf16[608,512]{1,0:T(8,128)(2,1)}, u32[]{:S(2)}, u32[]{:S(2)}) collective-permute-start(bf16[608,512]{1,0:T(8,128)(2,1)} %get-tuple-element.112), channel_id=1, source_target_pairs={{0,24},{4,28},{8,16},{12,20},{16,8},{20,12},{24,0},{28,4},{1,25},{... | collective-permute-start | bytes 1867784 | tf_op jit(solution)/shard_map/ppermute | solution.py:304
  107.7 2.0 %collective-permute-start.14 = (bf16[2,224,512]{2,1,0:T(8,128)(2,1)}, bf16[2,224,512]{2,1,0:T(8,128)(2,1)S(1)}, u32[]{:S(2)}, u32[]{:S(2)}) collective-permute-start(bf16[2,224,512]{2,1,0:T(8,128)(2,1)} %get-tuple-element.113), channel_id=1, source_target_pairs={{0,4},{4,0},{8,12},{12,8},{16,20},{20,16},{24,28},{28,24},{1,5},{5... | collective-permute-start | bytes 1376264 | tf_op jit(solution)/shard_map/ppermute | solution.py:304
  107.7 2.7 %collective-permute-start.15 = (bf16[2,224,512]{2,1,0:T(8,128)(2,1)}, bf16[2,224,512]{2,1,0:T(8,128)(2,1)S(1)}, u32[]{:S(2)}, u32[]{:S(2)}) collective-permute-start(bf16[2,224,512]{2,1,0:T(8,128)(2,1)} %get-tuple-element.114), channel_id=1, source_target_pairs={{0,4},{4,0},{8,12},{12,8},{16,20},{20,16},{24,28},{28,24},{1,5},{5... | collective-permute-start | bytes 1376264 | tf_op jit(solution)/shard_map/ppermute | solution.py:304
  125.9 9.6 %collective-permute-start.16 = (bf16[304,512]{1,0:T(8,128)(2,1)S(1)}, bf16[304,512]{1,0:T(8,128)(2,1)S(1)}, u32[]{:S(2)}, u32[]{:S(2)}) collective-permute-start(bf16[304,512]{1,0:T(8,128)(2,1)S(1)} %fusion.5), channel_id=1, source_target_pairs={{0,1},{1,0},{2,3},{3,2},{4,5},{5,4},{6,7},{7,6},{8,9},{9,8},{10,11... | collective-permute-start | bytes 933896 | tf_op jit(solution)/shard_map/ppermute | solution.py:304
  127.6 19.0 %collective-permute-start.21 = (bf16[336,512]{1,0:T(8,128)(2,1)S(1)}, bf16[336,512]{1,0:T(8,128)(2,1)}, u32[]{:S(2)}, u32[]{:S(2)}) collective-permute-start(bf16[336,512]{1,0:T(8,128)(2,1)S(1)} %copy-done.40), channel_id=1, source_target_pairs={{0,1},{1,2},{2,3},{3,0},{4,5},{5,6},{6,7},{7,4},{8,9},{9,10},{10,1... | collective-permute-start | bytes 1032200 | tf_op jit(solution)/shard_map/ppermute | solution.py:41
  128.2 8.8 %collective-permute-start.17 = (bf16[224,512]{1,0:T(8,128)(2,1)S(1)}, bf16[224,512]{1,0:T(8,128)(2,1)S(1)}, u32[]{:S(2)}, u32[]{:S(2)}) collective-permute-start(bf16[224,512]{1,0:T(8,128)(2,1)S(1)} %get-tuple-element.162), channel_id=1, source_target_pairs={{0,8},{4,12},{8,0},{12,4},{16,24},{20,28},{24,16},{28,20},{1,9},{5... | collective-permute-start | bytes 688136 | tf_op jit(solution)/shard_map/ppermute | solution.py:304
  128.6 11.0 %collective-permute-start.18 = (bf16[224,512]{1,0:T(8,128)(2,1)S(1)}, bf16[224,512]{1,0:T(8,128)(2,1)S(1)}, u32[]{:S(2)}, u32[]{:S(2)}) collective-permute-start(bf16[224,512]{1,0:T(8,128)(2,1)S(1)} %get-tuple-element.161), channel_id=1, source_target_pairs={{0,16},{4,20},{8,24},{12,28},{16,0},{20,4},{24,8},{28,12},{1,17},{... | collective-permute-start | bytes 688136 | tf_op jit(solution)/shard_map/ppermute | solution.py:304
  130.0 10.4 %collective-permute-start.19 = (bf16[224,512]{1,0:T(8,128)(2,1)S(1)}, bf16[224,512]{1,0:T(8,128)(2,1)S(1)}, u32[]{:S(2)}, u32[]{:S(2)}) collective-permute-start(bf16[224,512]{1,0:T(8,128)(2,1)S(1)} %get-tuple-element.160), channel_id=1, source_target_pairs={{0,24},{4,28},{8,16},{12,20},{16,8},{20,12},{24,0},{28,4},{1,25},{... | collective-permute-start | bytes 688136 | tf_op jit(solution)/shard_map/ppermute | solution.py:304
  141.0 16.2 %collective-permute-start.22 = (bf16[304,512]{1,0:T(8,128)(2,1)S(1)}, bf16[304,512]{1,0:T(8,128)(2,1)}, u32[]{:S(2)}, u32[]{:S(2)}) collective-permute-start(bf16[304,512]{1,0:T(8,128)(2,1)S(1)} %add_convert_fusion.4), channel_id=1, source_target_pairs={{0,2},{1,3},{2,0},{3,1},{4,6},{5,7},{6,4},{7,5},{8,10},{9,11},{10,... | collective-permute-start | bytes 933896 | tf_op jit(solution)/shard_map/ppermute | solution.py:304
  145.4 5.1 %collective-permute-start.20 = (bf16[112,512]{1,0:T(8,128)(2,1)}, bf16[112,512]{1,0:T(8,128)(2,1)}, u32[]{:S(2)}, u32[]{:S(2)}) collective-permute-start(bf16[112,512]{1,0:T(8,128)(2,1)} %fusion.17), channel_id=1, source_target_pairs={{0,1},{1,0},{2,3},{3,2},{4,5},{5,4},{6,7},{7,6},{8,9},{9,8},{10,11... | collective-permute-start | bytes 344072 | tf_op jit(solution)/shard_map/ppermute | solution.py:304
  158.3 6.2 %collective-permute-start.23 = (bf16[112,512]{1,0:T(8,128)(2,1)S(1)}, bf16[112,512]{1,0:T(8,128)(2,1)S(1)}, u32[]{:S(2)}, u32[]{:S(2)}) collective-permute-start(bf16[112,512]{1,0:T(8,128)(2,1)S(1)} %add_convert_fusion.9), channel_id=1, source_target_pairs={{0,2},{1,3},{2,0},{3,1},{4,6},{5,7},{6,4},{7,5},{8,10},{9,11},{10,... | collective-permute-start | bytes 344072 | tf_op jit(solution)/shard_map/ppermute | solution.py:304
  164.5 8.6 %collective-permute-start.24 = (bf16[304,512]{1,0:T(8,128)(2,1)S(1)}, bf16[304,512]{1,0:T(8,128)(2,1)S(1)}, u32[]{:S(2)}, u32[]{:S(2)}) collective-permute-start(bf16[304,512]{1,0:T(8,128)(2,1)S(1)} %add_convert_fusion.3.half), channel_id=1, source_target_pairs={{0,1},{1,0},{2,3},{3,2},{4,5},{5,4},{6,7},{7,6},{8,9},{9,8},{10,11... | collective-permute-start | bytes 933896 | tf_op jit(solution)/shard_map/ppermute | solution.py:304
  173.1 4.8 %collective-permute-start.25 = (bf16[112,512]{1,0:T(8,128)(2,1)S(1)}, bf16[112,512]{1,0:T(8,128)(2,1)S(1)}, u32[]{:S(2)}, u32[]{:S(2)}) collective-permute-start(bf16[112,512]{1,0:T(8,128)(2,1)S(1)} %add_convert_fusion.8.half), channel_id=1, source_target_pairs={{0,1},{1,0},{2,3},{3,2},{4,5},{5,4},{6,7},{7,6},{8,9},{9,8},{10,11... | collective-permute-start | bytes 344072 | tf_op jit(solution)/shard_map/ppermute | solution.py:304
  (41 other events, 182.4 us)
Sparse Core Ops, SparseCore 0:
  10.3 45.4 all-gather.2

commit v3 on v2

--- a/solution.py
+++ b/solution.py
@@ -33,7 +33,6 @@
 SCALE = HEAD**-0.5
 BF = jnp.bfloat16
 F32 = jnp.float32
-VMEM_LIMIT = 36 * 1024 * 1024
 
 
 def shifted_2(value, axis, by):
@@ -143,7 +142,8 @@
 
 def kernel_call(
     body, outs, ins, scratch=(), apart=0, grid=None, in_blocks=None, out_blocks=None,
-    vmem=VMEM_LIMIT,
+    vmem=16,
+    flops=1024,
 ):
     in_specs = in_blocks or [whole()] * (len(ins) - apart) + [whole(pl.ANY)] * apart
     options = {"grid": grid} if grid else {}
@@ -153,8 +153,8 @@
         in_specs=in_specs,
         out_specs=tuple(out_blocks or [whole()] * len(outs)),
         scratch_shapes=list(scratch),
-        cost_estimate=pl.CostEstimate(flops=1024, bytes_accessed=1024, transcendentals=0),
-        compiler_params=pltpu.CompilerParams(vmem_limit_bytes=vmem),
+        cost_estimate=pl.CostEstimate(flops=flops, bytes_accessed=1024, transcendentals=0),
+        compiler_params=pltpu.CompilerParams(vmem_limit_bytes=vmem * 1024 * 1024),
         **options,
     )(*ins)
 
@@ -261,25 +261,29 @@
     table[...] = total.T
 
 
-def unpack_mlp_body(
-    half, back, wproj, bproj, g2, b2, win, bin_, wout, bout, mlp, sems
-):
+def unpack_in_body(half, back, win, bin_, both, sems):
     depth = win.shape[0]
+    join_halves(late_place(), half, back, both, sems)
+    for c in range(FF // D):
+        win[:, c * D : (c + 1) * D] = both[c * depth : (c + 1) * depth, :].astype(F32)
+    small = both[4 * depth :, :].astype(F32)
+    hidden = jnp.concatenate([small[c : c + 1] for c in range(FF // D)], 1)
+    hidden = mine(hidden, depth * FF // D, shard_place())
+    for r in range(bin_.shape[0]):
+        bin_[r : r + 1] = hidden[:, r * 128 : (r + 1) * 128]
+
+
+def unpack_out_body(half, back, wout, wproj, g2, b2, bout, bproj, both, sems):
+    depth = wproj.shape[0]
     me = shard_place()
-    join_halves(late_place(), half, back, mlp, sems)
-    for c in range(FF // D):
-        win[:, c * D : (c + 1) * D] = mlp[c * depth : (c + 1) * depth, :].astype(F32)
-    wout[...] = mlp[4 * depth : 8 * depth, :].astype(F32)
-    wproj[...] = mlp[8 * depth : 9 * depth, :].astype(F32)
-    small = mlp[9 * depth :, :].astype(F32)
+    join_halves(late_place(), half, back, both, sems)
+    wout[...] = both[: 4 * depth, :].astype(F32)
+    wproj[...] = both[4 * depth : 5 * depth, :].astype(F32)
+    small = both[5 * depth :, :].astype(F32)
     g2[...] = mine(small[0:1], depth, me)
     b2[...] = mine(small[1:2], depth, me)
     bout[...] = mine(small[2:3], depth, me)
     bproj[...] = mine(small[3:4], depth, me)
-    hidden = jnp.concatenate([small[4 + c : 5 + c] for c in range(FF // D)], 1)
-    hidden = mine(hidden, depth * FF // D, me)
-    for r in range(bin_.shape[0]):
-        bin_[r : r + 1] = hidden[:, r * 128 : (r + 1) * 128]
 
 
 def put_shares(me, same, other, start, values, first=0):
@@ -326,18 +330,20 @@
     return [exchange(s, "shard", 2 * q + 2) for q, s in enumerate(sums)]
 
 
-def add_chips(late, same, came, parts):
-    half = same.shape[1] // 2
-    out = []
-    for start in (late * half, (1 - late) * half):
-        total = 0.0
-        for whole_part in (same, came):
-            part = lax.dynamic_slice(whole_part, (0, start, 0), (1, half, D))
-            total += part.reshape(half, D).astype(F32)
+def add_chips_body(same, came, *refs):
+    parts, (keep, send) = refs[:-2], refs[-2:]
+    half = keep.shape[0]
+    for at, target in ((late_place(), keep), (1 - late_place(), send)):
+        rows = pl.ds(pl.multiple_of(at * half, 16), half)
+        total = same[0, rows, :].astype(F32) + came[0, rows, :].astype(F32)
         for part in parts:
-            total += lax.dynamic_slice_in_dim(part, start, half, 0).astype(F32)
-        out.append(total.astype(BF))
-    return out
+            total += part[rows, :].astype(F32)
+        target[...] = total.astype(BF)
+
+
+def add_chips(same, came, parts, flops=1024):
+    half = like((same.shape[1] // 2, D), BF)
+    return kernel_call(add_chips_body, [half, half], (same, came, *parts), flops=flops)
 
 
 def seq_rest(half):
@@ -469,37 +475,25 @@
     return upto, bell * 0.3989422804014327
 
 
-def mlp_body(
-    mixed,
-    cotangent,
-    cot_halo,
-    slab,
-    attn_slab,
-    restored,
-    kept,
-    sent,
-    grad_mixed,
-    grad_win,
-    same,
-    other,
-    normed_low,
-    cot,
-    out_sum,
-    back_sum,
-    wide,
+def mlp_forward_body(
+    mixed, cotangent, cot_halo, slab, kept, sent, cot, actives, back_sum, vectors, same, other
 ):
     me = shard_place()
     shards, height = slab.shape[:2]
     depth = (height - SMALL) // 8
     span = shards * D // FF
+    chunks = FF // D
     small = smalls_of(slab, 8 * depth)
+    vectors[...] = small
     gain, offset, bias_o = (small[r : r + 1] for r in range(3))
     own = WIN - SHIFT
-    for r in range(WIN):
-        part = slice(r * WIDTH, (r + 1) * WIDTH)
+    parts = [slice(r * WIDTH, (r + 1) * WIDTH) for r in range(WIN)]
+    lows = []
+    for r, part in enumerate(parts):
         cot[part, :] = cotangent[SHIFT + r] if r < own else cot_halo[r - own]
-    normed, _ = norm_stats(mixed[...])
-    normed_low[...] = (normed * gain + offset).astype(BF)
+        normed, _ = norm_stats(mixed[part, :])
+        lows.append((normed * gain + offset).astype(BF))
+    normed_low = jnp.concatenate(lows, 0)
 
     def w_in(c):
         return block_of(slab, c, depth)
@@ -507,58 +501,98 @@
     def w_out(c):
         return slab[c * span : (c + 1) * span, 4 * depth : 8 * depth, :].reshape(D, D)
 
-    def ahead(c):
-        return dot(normed_low[...], w_in(c)), dot_nt(cot[...], w_out(c))
-
-    vectors = []
-    now = ahead(0)
-    for c in range(FF // D):
-        hidden, grad = now
-        if c + 1 < FF // D:
-            now = ahead(c + 1)
-        hidden = hidden + small[3 + c : 4 + c]
-        upto, density = gelu_parts(hidden)
-        active = (hidden * upto).astype(BF)
-        grad = (grad * (upto + hidden * density)).astype(BF)
-        forward = dot(active, w_out(c))
-        backward = dot_nt(grad, w_in(c))
-        if c == 0:
-            out_sum[...] = forward
-            back_sum[...] = backward
+    hiddens, slopes, grads, forward, backward, bias_sums = {}, {}, {}, None, None, []
+    for step in range(-1, chunks + 1):
+        ahead, behind = step + 1, step - 1
+        products = []
+        if ahead < chunks:
+            products.append(lambda: hiddens.update({ahead: dot(normed_low, w_in(ahead))}))
+            products.append(lambda: slopes.update({ahead: dot_nt(cot[...], w_out(ahead))}))
+        if behind >= 0:
+            active = actives[:, behind * D : (behind + 1) * D]
+            grad = grads.pop(behind)
+
+            def add_forward():
+                nonlocal forward
+                one = dot(active, w_out(behind))
+                forward = one if forward is None else forward + one
+
+            def add_backward():
+                nonlocal backward
+                one = dot_nt(grad, w_in(behind))
+                backward = one if backward is None else backward + one
+
+            def weight():
+                one = dot_tn(normed_low, grad).reshape(shards, depth, D)
+                put_shares(me, same, other, behind * depth, one)
+
+            products += [add_forward, add_backward, weight]
+        rows = []
+        if 0 <= step < chunks:
+            hidden, slope = hiddens.pop(step), slopes.pop(step)
+            bias_sum = 0.0
+            for r, part in enumerate(parts):
+                h = hidden[part] + small[3 + step : 4 + step]
+                upto, density = gelu_parts(h)
+                actives[part, step * D : (step + 1) * D] = (h * upto).astype(BF)
+                rows.append((slope[part] * (upto + h * density)).astype(BF))
+                bias_sum += jnp.sum(rows[-1].astype(F32), 0, keepdims=True)
+                if r < len(products):
+                    products[r]()
+            bias_sums.append(bias_sum)
+            grads[step] = jnp.concatenate(rows, 0)
         else:
-            out_sum[...] += forward
-            back_sum[...] += backward
-        vectors.append(jnp.sum(grad.astype(F32), 0, keepdims=True))
-        put_shares(
-            me, same, other, c * depth, dot_tn(normed_low[...], grad).reshape(shards, depth, D)
-        )
-        put_shares(
-            me,
-            same,
-            other,
-            4 * depth,
-            dot_tn(active, cot[...]).reshape(span, 4 * depth, D),
-            c * span,
-        )
-    result = mixed[...] + out_sum[...] + bias_o
+            for product in products:
+                product()
+    back_sum[...] = backward
+    result = mixed[...] + forward + bias_o
     kept[...] = result[: own * WIDTH]
     sent[...] = result[own * WIDTH :].astype(BF)
-    normed, scale = norm_stats(mixed[...])
-    g = back_sum[...]
-    gain_sum = jnp.sum(g * normed, 0, keepdims=True)
-    offset_sum = jnp.sum(g, 0, keepdims=True)
-    cot_sum = jnp.sum(cot[...].astype(F32), 0, keepdims=True)
-    grad_mixed[...] = cot[...].astype(F32) + norm_back(g, normed, scale, gain)
-
-    branch = grad_mixed[...].astype(BF)
-    branch_sum = jnp.sum(branch.astype(F32), 0, keepdims=True)
-    proj = dot_tn(restored[...], branch).reshape(shards, depth, D)
-    put_shares(me, same, other, 8 * depth, proj)
-    put_smalls(same, other, 9 * depth, [gain_sum, offset_sum, cot_sum, branch_sum] + vectors)
-    grad_att = dot_nt(branch, block_of(attn_slab, 3, depth)).astype(BF)
+    put_smalls(same, other, 4 * depth, bias_sums)
+
+
+def mlp_backward_body(
+    mixed,
+    cot,
+    actives,
+    back_sum,
+    vectors,
+    attn_slab,
+    restored,
+    grad_mixed,
+    grad_win,
+    same,
+    other,
+    wide,
+):
+    me = shard_place()
+    shards, height = attn_slab.shape[:2]
+    depth = (height - SMALL) // 4
+    span = shards * D // FF
+    gain = vectors[0:1]
+    parts = [slice(r * WIDTH, (r + 1) * WIDTH) for r in range(WIN)]
     columns = column_places()
-    for r in range(WIN):
-        wide[:, r] = dot(columns, grad_att[r * WIDTH : (r + 1) * WIDTH]).reshape(WINDOWS, SLOT, D)
+    w_proj = block_of(attn_slab, 3, depth)
+    sums = [0.0] * 4
+    branches = []
+    for r, part in enumerate(parts):
+        if r < FF // D:
+            one = dot_tn(actives[:, r * D : (r + 1) * D], cot[...])
+            put_shares(me, same, other, 0, one.reshape(span, 4 * depth, D), r * span)
+        normed, scale = norm_stats(mixed[part, :])
+        g = back_sum[part, :]
+        c = cot[part, :].astype(F32)
+        grad = c + norm_back(g, normed, scale, gain)
+        grad_mixed[part, :] = grad
+        branch = grad.astype(BF)
+        branches.append(branch)
+        for n, one in enumerate((g * normed, g, c, branch.astype(F32))):
+            sums[n] += jnp.sum(one, 0, keepdims=True)
+        grad_att = dot_nt(branch, w_proj).astype(BF)
+        wide[:, r] = dot(columns, grad_att).reshape(WINDOWS, SLOT, D)
+    proj = dot_tn(restored[...], jnp.concatenate(branches, 0)).reshape(shards, depth, D)
+    put_shares(me, same, other, 4 * depth, proj)
+    put_smalls(same, other, 5 * depth, sums)
     grad_win[...] = wide[...].reshape(PADDED, D).astype(BF)
 
 
@@ -710,22 +744,22 @@
     depth = D // shards
     own = WIN - SHIFT
     attn_params = (gain_one[None], bias_one[None], w_qkv, bias_qv, table.T)
+    bin_rows = bias_in.reshape(-1, 128)
     mlp_params = (
         w_proj,
         bias_proj[None],
         gain_two[None],
         bias_two[None],
         w_in,
-        bias_in.reshape(-1, 128),
+        bin_rows,
         w_out,
         bias_out[None],
     )
-    late = seq & 1
     attn_slab, mlp_slab = kernel_call(
         pack_body,
         [like((4 * depth + SMALL, D), BF), like((8 * depth + SMALL, D), BF)],
         (*attn_params, *mlp_params),
-        vmem=60 * 1024 * 1024,
+        vmem=60,
     )
     pieces = gather_pieces(attn_slab)
     mlp_all = lax.all_gather(mlp_slab, "shard")
@@ -782,25 +816,28 @@
             pltpu.VMEM((QUADS, PLACES, LANES), F32),
         ],
     )
-    share = like((chips, 9 * depth + SMALL, D), BF)
-    out_kept, out_sent, grad_mixed, grad_win, mlp_same, mlp_other = kernel_call(
-        mlp_body,
+    share_a = like((chips, 4 * depth + SMALL, D), BF)
+    share_b = like((chips, 5 * depth + SMALL, D), BF)
+    out_kept, out_sent, cot, actives, back_sum, vectors, same_a, other_a = kernel_call(
+        mlp_forward_body,
         [
             like((own * WIDTH, D), F32),
             like((SHIFT * WIDTH, D), BF),
+            like((TOKENS, D), BF),
+            like((TOKENS, FF), BF),
             like((TOKENS, D), F32),
-            like((PADDED, D), BF),
-            share,
-            share,
+            like((SMALL, D), F32),
+            share_a,
+            share_a,
         ],
-        (mixed, cot_here, cot_halo, mlp_all, attn_all, restored),
-        scratch=[
-            pltpu.VMEM((TOKENS, D), BF),
-            pltpu.VMEM((TOKENS, D), BF),
-            pltpu.VMEM((TOKENS, D), F32),
-            pltpu.VMEM((TOKENS, D), F32),
-            pltpu.VMEM((WINDOWS, WIN, SLOT, D), F32),
-        ],
+        (mixed, cot_here, cot_halo, mlp_all),
+        vmem=24,
+    )
+    grad_mixed, grad_win, same_b, other_b = kernel_call(
+        mlp_backward_body,
+        [like((TOKENS, D), F32), like((PADDED, D), BF), share_b, share_b],
+        (mixed, cot, actives, back_sum, vectors, attn_all, restored),
+        scratch=[pltpu.VMEM((WINDOWS, WIN, SLOT, D), F32)],
     )
 
     def backward(first, count, grad_win, came):
@@ -817,11 +854,15 @@
 
     none = jnp.zeros((QUADS, PLACES, LANES), F32)
     count = steps // 2
-    mlp_came = exchange(mlp_other, "shard", 1)
+    came_a = exchange(other_a, "shard", 1)
+    sums, (grad_win,) = tie(add_cores(same_a, came_a), [grad_win])
+    parts_a = to_chips(sums)
+    came_b = exchange(other_b, "shard", 1)
     early, pairs = backward(0, count, grad_win, none)
-    sums, (pairs,) = tie(add_cores(mlp_same, mlp_came), [pairs])
-    mlp_parts = to_chips(sums)
+    sums, (pairs,) = tie(add_cores(same_b, came_b), [pairs])
+    parts_b = to_chips(sums)
     late_part, pairs = backward(count, count, grad_win, pairs)
+    parts_a, (pairs,) = tie(parts_a, [pairs])
     (out_halo,), (pairs,) = tie([shifted_2(out_sent, "seq", 1)], [pairs])
     tok_kept, tok_sent, attn_same, *attn_others = kernel_call(
         attn_last_body,
@@ -839,26 +880,37 @@
         ],
     )
     attn_came = [exchange(other, "shard", 1) for other in attn_others]
-    mlp_parts, attn_came = tie(mlp_parts, attn_came)
-    keep_m, send = add_chips(late, mlp_same, mlp_came, mlp_parts)
-    near_m = exchange(send, "seq", 1)
+    keep_a, send = add_chips(same_a, came_a, parts_a)
+    (send,), parts_b = tie([send], parts_b)
+    near_a = exchange(send, "seq", 1)
+    keep_b, send = add_chips(same_b, came_b, parts_b, 10_000_000_000)
+    (send,), attn_came = tie([send], attn_came)
+    near_b = exchange(send, "seq", 1)
     came = [c[q] for c in attn_came for q in range(chips // 2)]
-    attn_parts = to_chips([add_pair(attn_same[q], came[q]) for q in range(1, chips)])
-    half_m = add_pair(keep_m, near_m)
-    (half_m,), attn_parts = tie([half_m], attn_parts)
-    far_m = exchange(half_m, "seq", 2)
-    keep, send = add_chips(late, attn_same, attn_came[0], attn_parts)
+    sums = [add_pair(attn_same[q], came[q]) for q in range(1, chips)]
+    sums, (near_a,) = tie(sums, [near_a])
+    attn_parts = to_chips(sums)
+    half_a = add_pair(keep_a, near_a)
+    (half_a,), (near_b,) = tie([half_a], [near_b])
+    far_a = exchange(half_a, "seq", 2)
+    half_b = add_pair(keep_b, near_b)
+    (half_b,), attn_parts = tie([half_b], attn_parts)
+    far_b = exchange(half_b, "seq", 2)
+    keep, send = add_chips(attn_same, attn_came[0], attn_parts)
+    tok_halo = shifted_2(tok_sent, "seq", 1)
+    (keep, send, tok_halo), (far_a,) = tie([keep, send, tok_halo], [far_a])
     near = exchange(send, "seq", 1)
-    tok_halo = shifted_2(tok_sent, "seq", 1)
-    (near, tok_halo), (far_m,) = tie([near, tok_halo], [far_m])
+    half_a = seq_rest(add_pair(half_a, far_a))
+    (half_a,), (near,) = tie([half_a], [near])
+    back_a = exchange(half_a, "seq", 1)
     half = add_pair(keep, near)
-    (half,), (far_m,) = tie([half], [far_m])
+    (half,), (far_b,) = tie([half], [far_b])
     far = exchange(half, "seq", 2)
-    half_m = seq_rest(add_pair(half_m, far_m))
-    (half_m,), (far,) = tie([half_m], [far])
-    back_m = exchange(half_m, "seq", 1)
+    half_b = seq_rest(add_pair(half_b, far_b))
+    (half_b,), (far,) = tie([half_b], [far])
+    back_b = exchange(half_b, "seq", 1)
     half = seq_rest(add_pair(half, far))
-    (half,), (back_m,) = tie([half], [back_m])
+    (half,), (back_a,) = tie([half], [back_a])
     back = exchange(half, "seq", 1)
     def unpack(body, params, half, back):
         return kernel_call(
@@ -870,13 +922,17 @@
                 pltpu.SemaphoreType.DMA((2,)),
             ],
                 apart=2,
-            vmem=16 * 1024 * 1024,
         )
 
-    mlp_grads = unpack(unpack_mlp_body, mlp_params, half_m, back_m)
-    mlp_grads, (back,) = tie(mlp_grads, [back])
+    in_grads = unpack(unpack_in_body, (w_in, bin_rows), half_a, back_a)
+    in_grads, (back_b,) = tie(in_grads, [back_b])
+    column = gain_two[None]
+    out_grads = unpack(unpack_out_body, (w_out, w_proj, *[column] * 4), half_b, back_b)
+    out_grads, (back,) = tie(out_grads, [back])
     attn_grads = unpack(unpack_attn_body, attn_params, half, back)
-    summed = [*attn_grads[:4], attn_grads[4].T, *mlp_grads]
+    g_wout, g_wproj, g_gain, g_offset, g_bout, g_bproj = out_grads
+    summed = [*attn_grads[:4], attn_grads[4].T, g_wproj, g_bproj, g_gain, g_offset]
+    summed += [*in_grads, g_wout, g_bout]
 
     def joined(halo, kept):
         return jnp.concatenate([halo.astype(F32), kept], 0).reshape(tokens.shape)

time: 187 us -> 173 us (0.925)
  other arithmetic: 13 us -> 3.77 us
  waiting for transfers between devices: 54.1 us -> 45.5 us
  starting transfers between devices: 29.4 us -> 37.9 us
  local copies, waits for them, and re-layouts: 26.4 us -> 22.5 us
    ppermute x22 -> x29, waiting for transfers between devices: 54 us -> 45.5 us  [exchange(): return lax.ppermute(value, axis, [(i, i ^ mask) for i in range(peers)])]
    ppermute x22 -> x29, starting transfers between devices: 19 us -> 26.5 us  [exchange(): return lax.ppermute(value, axis, [(i, i ^ mask) for i in range(peers)])]
    convert_element_type x6 -> x9, other arithmetic: 5.94 us -> 0.95 us  [add_pair(): return (here.astype(F32) + came.astype(F32)).astype(BF)]
    unnamed x92 -> x68, local copies, waits for them, and re-layouts: 24.1 us -> 20.2 us
    convert_element_type x2 -> x0, other arithmetic: 3.3 us -> none  [add_chips(): out.append(total.astype(BF))]
    pallas_call x9 -> x14, Pallas kernels: 48.9 us -> 48.4 us  [kernel_call(): pl.pallas_call(body, out_shape=tuple(outs), in_specs=in_specs, out_specs=...]
  transfers between devices with their start and end apart: 27 -> 34, of which waited for: 13 -> 12; matrix products, arithmetic and copies ran while one was open for 7% -> 4% of each run, Pallas kernels for 12% -> 17%
where the time goes in v3:
time: 173 us
  Pallas kernels  48.4 us (28%)
  waiting for transfers between devices  45.5 us (26%)
  starting transfers between devices  37.9 us (22%)
  local copies, waits for them, and re-layouts  22.5 us (13%)
  between operations  14.6 us (8%)
  other arithmetic  3.77 us (2%)
    pallas_call x14, Pallas kernels, kernel_call(): pl.pallas_call(body, out_shape=tuple(outs), in_specs=in_specs, out_specs=...  48.4 us
    ppermute x29, waiting for transfers between devices, exchange(): return lax.ppermute(value, axis, [(i, i ^ mask) for i in range(peers)])  45.5 us
    ppermute x29, starting transfers between devices, exchange(): return lax.ppermute(value, axis, [(i, i ^ mask) for i in range(peers)])  26.5 us
    unnamed x68, local copies, waits for them, and re-layouts  20.2 us
    ppermute x4, starting transfers between devices, shifted_2(): lax.ppermute(value, axis, [(i, (i + by) % peers) for i in range(peers)])  11.3 us
  transfers between devices with their start and end apart: 34, of which 12 were waited for; matrix products, arithmetic and copies ran while one was open for 4% of the time, Pallas kernels for 17%

profile of v3, /device:TPU:0, one launch (start us, length us, event | category | flops | bytes accessed | tf_op | source)
XLA Modules:
  0.0 172.7 jit_solution(11834234348131842875)
XLA Ops:
  7.3 2.9 %shard_map.271 = (bf16[288,512]{1,0:T(8,128)(2,1)}, bf16[544,512]{1,0:T(8,128)(2,1)}) custom-call(bf16[1,64]{1,0:T(2,128)(2,1)} %bitcast.55, bf16[1,64]{1,0:T(2,128)(2,1)} %bitcast.56, bf16[64,1536]{1,0:T(8,128)(2,1)} %wqkv.1, bf16[2,64]{1,0:T(2,128)(2,1)} %bqv.1, bf16[2,169]{1,0:T(2,128)(2,1)} %bitcast.54, bf16[64,512]{1,0:T(8,128)(2,1)} %wproj.1, ...), custom_call_target="tpu_custom_call" | custom-call | flops 1024 | bytes 1024 | tf_op jit(solution)/shard_map/pallas_call | solution.py:150
  10.2 3.0 %collective-permute-start.2 = (bf16[288,512]{1,0:T(8,128)(2,1)}, bf16[288,512]{1,0:T(8,128)(2,1)S(1)}, u32[]{:S(2)}, u32[]{:S(2)}) collective-permute-start(bf16[288,512]{1,0:T(8,128)(2,1)} %get-tuple-element.118.refs_0_), channel_id=1, source_target_pairs={{0,8},{4,12},{8,0},{12,4},{16,24},{20,28},{24,16},{28,20},{1,9},{5... | collective-permute-start | bytes 884744 | tf_op jit(solution)/shard_map/ppermute | solution.py:308
  13.2 1.5 collective-permute-start.4
  14.8 4.1 %collective-permute-start = (bf16[3,112,512]{2,1,0:T(8,128)(2,1)S(1)}, bf16[3,112,512]{2,1,0:T(8,128)(2,1)S(1)}, u32[]{:S(2)}, u32[]{:S(2)}) collective-permute-start(bf16[3,112,512]{2,1,0:T(8,128)(2,1)S(1)} %slice_bitcast_fusion.1), channel_id=1, source_target_pairs={{0,3},{1,0},{2,1},{3,2},{4,7},{5,4},{6,5},{7,6},{8,11},{9,8},{10,9... | collective-permute-start | bytes 1032200 | tf_op jit(solution)/shard_map/ppermute | solution.py:40
  18.9 1.8 %slice_bitcast_fusion = bf16[3,112,512]{2,1,0:T(8,128)(2,1)} fusion(bf16[1,7,112,512]{3,2,1,0:T(8,128)(2,1)} %param.18), kind=kLoop, calls=%fused_computation.16 | loop fusion | bytes 688128 | tf_op jit(solution)/shard_map/slice | solution.py:769
  21.3 4.2 %collective-permute-start.8 = (bf16[3,112,512]{2,1,0:T(8,128)(2,1)}, bf16[3,112,512]{2,1,0:T(8,128)(2,1)}, u32[]{:S(2)}, u32[]{:S(2)}) collective-permute-start(bf16[3,112,512]{2,1,0:T(8,128)(2,1)} %slice_bitcast_fusion), channel_id=1, source_target_pairs={{0,3},{1,0},{2,1},{3,2},{4,7},{5,4},{6,5},{7,6},{8,11},{9,8},{10,9... | collective-permute-start | bytes 1032200 | tf_op jit(solution)/shard_map/ppermute | solution.py:40
  25.4 4.0 %collective-permute-done.4.refs_4_ = bf16[288,512]{1,0:T(8,128)(2,1)S(1)} collective-permute-done((bf16[288,512]{1,0:T(8,128)(2,1)}, bf16[288,512]{1,0:T(8,128)(2,1)S(1)}, u32[]{:S(2)}, u32[]{:S(2)}) %collective-permute-start.4) | collective-permute-done | bytes 294944 | tf_op jit(solution)/shard_map/ppermute | solution.py:308
  29.4 3.4 %collective-permute-done.6.refs_6_ = bf16[288,512]{1,0:T(8,128)(2,1)S(1)} collective-permute-done((bf16[288,512]{1,0:T(8,128)(2,1)}, bf16[288,512]{1,0:T(8,128)(2,1)S(1)}, u32[]{:S(2)}, u32[]{:S(2)}) %collective-permute-start.6) | collective-permute-done | bytes 294944 | tf_op jit(solution)/shard_map/ppermute | solution.py:308
  45.8 3.0 %shard_map.272 = (bf16[896,512]{1,0:T(8,128)(2,1)S(1)}, bf16[896,512]{1,0:T(8,128)(2,1)S(1)}, bf16[896,512]{1,0:T(8,128)(2,1)S(1)}, bf16[896,512]{1,0:T(8,128)(2,1)S(1)}, bf16[8,288,512]{2,1,0:T(8,128)(2,1)S(1)}) custom-call(bf16[7,112,512]{2,1,0:T(8,128)(2,1)S(1)} %bitcast.46, bf16[3,112,512]{2,1,0:T(8,128)(2,1)S(1)} %collective-permute-done.halo, ...), custom_call_target="tpu_custom_call" | custom-call | flops 1024 | bytes 1024 | tf_op jit(solution)/shard_map/pallas_call | solution.py:150
  49.1 7.1 %shard_map.273 = (bf16[8,4,112,256]{3,2,1,0:T(8,128)(2,1)S(1)}, bf16[784,512]{1,0:T(8,128)(2,1)S(1)}, f32[784,512]{1,0:T(8,128)S(1)}) custom-call(bf16[8,288,512]{2,1,0:T(8,128)(2,1)S(1)} %get-tuple-element.119.slab.attn_slab, f32[16,56,128]{2,1,0:T(8,128)S(1)} %broadcast_in_dim.35.reg_rows, f32[16,1,256]{2,1,0:T(1,128)S(1)} %tile.9.reg_lanes, ...), custom_call_target="tpu_custom_call" | custom-call | flops 1024 | bytes 1024 | tf_op jit(solution)/shard_map/pallas_call | solution.py:150
  61.0 2.3 %copy-done.13 = bf16[4352,512]{1,0:T(8,128)(2,1)S(1)} copy-done((bf16[4352,512]{1,0:T(8,128)(2,1)S(1)}, bf16[4352,512]{1,0:T(8,128)(2,1)}, u32[]{:S(2)}) %copy-start.13) | copy-done | bytes 4456472
  64.4 14.4 %shard_map.274 = (f32[448,512]{1,0:T(8,128)S(1)}, bf16[336,512]{1,0:T(8,128)(2,1)S(1)}, bf16[784,512]{1,0:T(8,128)(2,1)S(1)}, bf16[784,2048]{1,0:T(8,128)(2,1)S(...) custom-call(f32[784,512]{1,0:T(8,128)S(1)} %copy-done.11, ...), custom_call_target="tpu_custom_call" | custom-call | flops 1024 | bytes 1024 | tf_op jit(solution)/shard_map/pallas_call | solution.py:150
  78.9 5.4 %shard_map.275 = (f32[784,512]{1,0:T(8,128)S(1)}, bf16[896,512]{1,0:T(8,128)(2,1)S(1)}, bf16[4,352,512]{2,1,0:T(8,128)(2,1)S(1)}, bf16[4,352,512]{2,1,0:T(8,128)(2,1)S(1)}) custom-call(f32[784,512]{1,0:T(8,128)S(1)} %copy-done.12, bf16[784,512]{1,0:T(8,128)(2,1)S(1)} %get-tuple-element.128.cot, bf16[784,2048]{1,0:T(8,128)(2,1)S(1)} %get-tuple-element.129.actives, ...), custom_call_target="tpu_custom_call" | custom-call | flops 1024 | bytes 1024 | tf_op jit(solution)/shard_map/pallas_call | solution.py:150
  85.2 2.5 %collective-permute-start.11 = (bf16[288,512]{1,0:T(8,128)(2,1)S(1)}, bf16[288,512]{1,0:T(8,128)(2,1)S(1)}, u32[]{:S(2)}, u32[]{:S(2)}) collective-permute-start(bf16[288,512]{1,0:T(8,128)(2,1)S(1)} %get-tuple-element.134), channel_id=1, source_target_pairs={{0,8},{4,12},{8,0},{12,4},{16,24},{20,28},{24,16},{28,20},{1,9},{5... | collective-permute-start | bytes 884744 | tf_op jit(solution)/shard_map/ppermute | solution.py:308
  90.9 2.9 %shard_map.276 = (bf16[448,1536]{1,0:T(8,128)(2,1)S(1)}, f32[4,56,256]{2,1,0:T(8,128)S(1)}) custom-call(bf16[896,512]{1,0:T(8,128)(2,1)S(1)} %copy-done.3, bf16[896,512]{1,0:T(8,128)(2,1)S(1)} %copy-done.5, bf16[896,512]{1,0:T(8,128)(2,1)S(1)} %copy-done.7, bf16[8,4,112,256]{3,2,1,0:T(8,128)(2,1)S(1)} %copy-done.9, ...), custom_call_target="tpu_custom_call" | custom-call | flops 1024 | bytes 1024 | tf_op jit(solution)/shard_map/pallas_call | solution.py:150
  94.1 2.0 %collective-permute-start.15 = (bf16[352,512]{1,0:T(8,128)(2,1)S(1)}, bf16[352,512]{1,0:T(8,128)(2,1)S(1)}, u32[]{:S(2)}, u32[]{:S(2)}) collective-permute-start(bf16[352,512]{1,0:T(8,128)(2,1)S(1)} %get-tuple-element.157), channel_id=1, source_target_pairs={{0,8},{4,12},{8,0},{12,4},{16,24},{20,28},{24,16},{28,20},{1,9},{5... | collective-permute-start | bytes 1081352 | tf_op jit(solution)/shard_map/ppermute | solution.py:308
  96.6 7.3 %collective-permute-done.12.refs_1_ = bf16[288,512]{1,0:T(8,128)(2,1)S(1)} collective-permute-done((bf16[288,512]{1,0:T(8,128)(2,1)S(1)}, bf16[288,512]{1,0:T(8,128)(2,1)S(1)}, u32[]{:S(2)}, u32[]{:S(2)}) %collective-permute-start.12) | collective-permute-done | bytes 294944 | tf_op jit(solution)/shard_map/ppermute | solution.py:308
  103.9 2.9 %shard_map.277 = (bf16[448,1536]{1,0:T(8,128)(2,1)S(1)}, f32[4,56,256]{2,1,0:T(8,128)S(1)}) custom-call(bf16[896,512]{1,0:T(8,128)(2,1)S(1)} %copy-done.3, bf16[896,512]{1,0:T(8,128)(2,1)S(1)} %copy-done.5, bf16[896,512]{1,0:T(8,128)(2,1)S(1)} %copy-done.7, bf16[8,4,112,256]{3,2,1,0:T(8,128)(2,1)S(1)} %copy-done.9, ...), custom_call_target="tpu_custom_call" | custom-call | flops 1024 | bytes 1024 | tf_op jit(solution)/shard_map/pallas_call | solution.py:150
  106.8 4.9 %shard_map.278 = (f32[448,512]{1,0:T(8,128)S(1)}, bf16[336,512]{1,0:T(8,128)(2,1)S(1)}, bf16[4,224,512]{2,1,0:T(8,128)(2,1)S(1)}, bf16[2,224,512]{2,1,0:T(8,128)(2,1)S(1)}, bf16[2,224,512]{2,1,0:T(8,128)(2,1)S(1)}) custom-call(f32[784,512]{1,0:T(8,128)S(1)} %get-tuple-element.147.grad_mixed, bf16[7,112,512]{2,1,0:T(8,128)(2,1)S(1)} %bitcast.48, ...), custom_call_target="tpu_custom_call" | custom-call | flops 1024 | bytes 1024 | tf_op jit(solution)/shard_map/pallas_call | solution.py:150
  114.0 1.6 collective-permute-start.25
  115.6 2.5 %collective-permute-done.16.refs_1_ = bf16[352,512]{1,0:T(8,128)(2,1)S(1)} collective-permute-done((bf16[352,512]{1,0:T(8,128)(2,1)S(1)}, bf16[352,512]{1,0:T(8,128)(2,1)S(1)}, u32[]{:S(2)}, u32[]{:S(2)}) %collective-permute-start.16) | collective-permute-done | bytes 360480 | tf_op jit(solution)/shard_map/ppermute | solution.py:308
  118.1 1.6 collective-permute-start.20
  120.6 8.6 %collective-permute-done.20 = bf16[144,512]{1,0:T(8,128)(2,1)S(1)} collective-permute-done((bf16[144,512]{1,0:T(8,128)(2,1)S(1)}, bf16[144,512]{1,0:T(8,128)(2,1)S(1)}, u32[]{:S(2)}, u32[]{:S(2)}) %collective-permute-start.20) | collective-permute-done | bytes 147488 | tf_op jit(solution)/shard_map/ppermute | solution.py:308
  130.4 2.4 %collective-permute-start.23 = (bf16[224,512]{1,0:T(8,128)(2,1)S(1)}, bf16[224,512]{1,0:T(8,128)(2,1)S(1)}, u32[]{:S(2)}, u32[]{:S(2)}) collective-permute-start(bf16[224,512]{1,0:T(8,128)(2,1)S(1)} %get-tuple-element.175), channel_id=1, source_target_pairs={{0,16},{4,20},{8,24},{12,28},{16,0},{20,4},{24,8},{28,12},{1,17},{... | collective-permute-start | bytes 688136 | tf_op jit(solution)/shard_map/ppermute | solution.py:308
  134.0 3.7 %collective-permute-done.22.refs_0_ = bf16[224,512]{1,0:T(8,128)(2,1)S(1)} collective-permute-done((bf16[224,512]{1,0:T(8,128)(2,1)S(1)}, bf16[224,512]{1,0:T(8,128)(2,1)S(1)}, u32[]{:S(2)}, u32[]{:S(2)}) %collective-permute-start.22) | collective-permute-done | bytes 229408 | tf_op jit(solution)/shard_map/ppermute | solution.py:308
  137.7 4.8 %collective-permute-done.23.refs_1_ = bf16[224,512]{1,0:T(8,128)(2,1)S(1)} collective-permute-done((bf16[224,512]{1,0:T(8,128)(2,1)S(1)}, bf16[224,512]{1,0:T(8,128)(2,1)S(1)}, u32[]{:S(2)}, u32[]{:S(2)}) %collective-permute-start.23) | collective-permute-done | bytes 229408 | tf_op jit(solution)/shard_map/ppermute | solution.py:308
  143.2 1.6 collective-permute-start.27
  145.0 5.7 %collective-permute-done.27 = bf16[112,512]{1,0:T(8,128)(2,1)S(1)} collective-permute-done((bf16[112,512]{1,0:T(8,128)(2,1)S(1)}, bf16[112,512]{1,0:T(8,128)(2,1)S(1)}, u32[]{:S(2)}, u32[]{:S(2)}) %collective-permute-start.27) | collective-permute-done | bytes 114720 | tf_op jit(solution)/shard_map/ppermute | solution.py:308
  150.9 2.6 %collective-permute-start.30 = (bf16[144,512]{1,0:T(8,128)(2,1)S(1)}, bf16[144,512]{1,0:T(8,128)(2,1)S(1)}, u32[]{:S(2)}, u32[]{:S(2)}) collective-permute-start(bf16[144,512]{1,0:T(8,128)(2,1)S(1)} %add_convert_fusion.11.half), channel_id=1, source_target_pairs={{0,1},{1,0},{2,3},{3,2},{4,5},{5,4},{6,7},{7,6},{8,9},{9,8},{10,11... | collective-permute-start | bytes 442376 | tf_op jit(solution)/shard_map/ppermute | solution.py:308
  153.5 3.9 %collective-permute-done.29 = bf16[112,512]{1,0:T(8,128)(2,1)S(1)} collective-permute-done((bf16[112,512]{1,0:T(8,128)(2,1)S(1)}, bf16[112,512]{1,0:T(8,128)(2,1)S(1)}, u32[]{:S(2)}, u32[]{:S(2)}) %collective-permute-start.29) | collective-permute-done | bytes 114720 | tf_op jit(solution)/shard_map/ppermute | solution.py:308
  158.2 2.1 %collective-permute-start.32 = (bf16[112,512]{1,0:T(8,128)(2,1)S(1)}, bf16[112,512]{1,0:T(8,128)(2,1)S(1)}, u32[]{:S(2)}, u32[]{:S(2)}) collective-permute-start(bf16[112,512]{1,0:T(8,128)(2,1)S(1)} %add_convert_fusion.13.half), channel_id=1, source_target_pairs={{0,1},{1,0},{2,3},{3,2},{4,5},{5,4},{6,7},{7,6},{8,9},{9,8},{10,11... | collective-permute-start | bytes 344072 | tf_op jit(solution)/shard_map/ppermute | solution.py:308
  164.4 1.5 shard_map.284
  (144 shorter events, 35.9 us)
Async XLA Ops:
  7.2 52.3 %all-gather.3.cloned.1.call-start = ((), (), s32[]{:S(2)}) async-start(), calls=%async_computation | async-start | bytes 5013504 | tf_op jit(solution)/shard_map/all_gather | solution.py:765
  10.2 11.1 %collective-permute-start.2 = (bf16[288,512]{1,0:T(8,128)(2,1)}, bf16[288,512]{1,0:T(8,128)(2,1)S(1)}, u32[]{:S(2)}, u32[]{:S(2)}) collective-permute-start(bf16[288,512]{1,0:T(8,128)(2,1)} %get-tuple-element.118.refs_0_), channel_id=1, source_target_pairs={{0,8},{4,12},{8,0},{12,4},{16,24},{20,28},{24,16},{28,20},{1,9},{5... | collective-permute-start | bytes 884744 | tf_op jit(solution)/shard_map/ppermute | solution.py:308
  13.2 16.2 %collective-permute-start.4 = (bf16[288,512]{1,0:T(8,128)(2,1)}, bf16[288,512]{1,0:T(8,128)(2,1)S(1)}, u32[]{:S(2)}, u32[]{:S(2)}) collective-permute-start(bf16[288,512]{1,0:T(8,128)(2,1)} %get-tuple-element.118.refs_0_), channel_id=1, source_target_pairs={{0,16},{4,20},{8,24},{12,28},{16,0},{20,4},{24,8},{28,12},{1,17},{... | collective-permute-start | bytes 884744 | tf_op jit(solution)/shard_map/ppermute | solution.py:308
  14.7 18.1 %collective-permute-start.6 = (bf16[288,512]{1,0:T(8,128)(2,1)}, bf16[288,512]{1,0:T(8,128)(2,1)S(1)}, u32[]{:S(2)}, u32[]{:S(2)}) collective-permute-start(bf16[288,512]{1,0:T(8,128)(2,1)} %get-tuple-element.118.refs_0_), channel_id=1, source_target_pairs={{0,24},{4,28},{8,16},{12,20},{16,8},{20,12},{24,0},{28,4},{1,25},{... | collective-permute-start | bytes 884744 | tf_op jit(solution)/shard_map/ppermute | solution.py:308
  14.7 18.8 %collective-permute-start.1 = (bf16[288,512]{1,0:T(8,128)(2,1)}, bf16[288,512]{1,0:T(8,128)(2,1)S(1)}, u32[]{:S(2)}, u32[]{:S(2)}) collective-permute-start(bf16[288,512]{1,0:T(8,128)(2,1)} %get-tuple-element.118.refs_0_), channel_id=1, source_target_pairs={{0,4},{4,0},{8,12},{12,8},{16,20},{20,16},{24,28},{28,24},{1,5},{5... | collective-permute-start | bytes 884744 | tf_op jit(solution)/shard_map/ppermute | solution.py:308
  14.8 21.1 %collective-permute-start = (bf16[3,112,512]{2,1,0:T(8,128)(2,1)S(1)}, bf16[3,112,512]{2,1,0:T(8,128)(2,1)S(1)}, u32[]{:S(2)}, u32[]{:S(2)}) collective-permute-start(bf16[3,112,512]{2,1,0:T(8,128)(2,1)S(1)} %slice_bitcast_fusion.1), channel_id=1, source_target_pairs={{0,3},{1,0},{2,1},{3,2},{4,7},{5,4},{6,5},{7,6},{8,11},{9,8},{10,9... | collective-permute-start | bytes 1032200 | tf_op jit(solution)/shard_map/ppermute | solution.py:40
  21.3 38.3 %collective-permute-start.8 = (bf16[3,112,512]{2,1,0:T(8,128)(2,1)}, bf16[3,112,512]{2,1,0:T(8,128)(2,1)}, u32[]{:S(2)}, u32[]{:S(2)}) collective-permute-start(bf16[3,112,512]{2,1,0:T(8,128)(2,1)} %slice_bitcast_fusion), channel_id=1, source_target_pairs={{0,3},{1,0},{2,1},{3,2},{4,7},{5,4},{6,5},{7,6},{8,11},{9,8},{10,9... | collective-permute-start | bytes 1032200 | tf_op jit(solution)/shard_map/ppermute | solution.py:40
  29.4 6.5 %collective-permute-start.3 = (bf16[288,512]{1,0:T(8,128)(2,1)S(1)}, bf16[288,512]{1,0:T(8,128)(2,1)S(1)}, u32[]{:S(2)}, u32[]{:S(2)}) collective-permute-start(bf16[288,512]{1,0:T(8,128)(2,1)S(1)} %collective-permute-done.2.refs_2_), channel_id=1, source_target_pairs={{0,4},{4,0},{8,12},{12,8},{16,20},{20,16},{24,28},{28,24},{1,5},{5... | collective-permute-start | bytes 884744 | tf_op jit(solution)/shard_map/ppermute | solution.py:308
  78.8 6.1 %collective-permute-start.10 = (bf16[4,288,512]{2,1,0:T(8,128)(2,1)S(1)}, bf16[4,288,512]{2,1,0:T(8,128)(2,1)S(1)}, u32[]{:S(2)}, u32[]{:S(2)}) collective-permute-start(bf16[4,288,512]{2,1,0:T(8,128)(2,1)S(1)} %get-tuple-element.127), channel_id=1, source_target_pairs={{0,4},{4,0},{8,12},{12,8},{16,20},{20,16},{24,28},{28,24},{1,5},{5... | collective-permute-start | bytes 3538952 | tf_op jit(solution)/shard_map/ppermute | solution.py:308
  84.4 9.4 %collective-permute-start.14 = (bf16[4,352,512]{2,1,0:T(8,128)(2,1)S(1)}, bf16[4,352,512]{2,1,0:T(8,128)(2,1)S(1)}, u32[]{:S(2)}, u32[]{:S(2)}) collective-permute-start(bf16[4,352,512]{2,1,0:T(8,128)(2,1)S(1)} %get-tuple-element.140), channel_id=1, source_target_pairs={{0,4},{4,0},{8,12},{12,8},{16,20},{20,16},{24,28},{28,24},{1,5},{5... | collective-permute-start | bytes 4325384 | tf_op jit(solution)/shard_map/ppermute | solution.py:308
  85.2 11.0 %collective-permute-start.11 = (bf16[288,512]{1,0:T(8,128)(2,1)S(1)}, bf16[288,512]{1,0:T(8,128)(2,1)S(1)}, u32[]{:S(2)}, u32[]{:S(2)}) collective-permute-start(bf16[288,512]{1,0:T(8,128)(2,1)S(1)} %get-tuple-element.134), channel_id=1, source_target_pairs={{0,8},{4,12},{8,0},{12,4},{16,24},{20,28},{24,16},{28,20},{1,9},{5... | collective-permute-start | bytes 884744 | tf_op jit(solution)/shard_map/ppermute | solution.py:308
  87.7 16.2 %collective-permute-start.12 = (bf16[288,512]{1,0:T(8,128)(2,1)S(1)}, bf16[288,512]{1,0:T(8,128)(2,1)S(1)}, u32[]{:S(2)}, u32[]{:S(2)}) collective-permute-start(bf16[288,512]{1,0:T(8,128)(2,1)S(1)} %get-tuple-element.135), channel_id=1, source_target_pairs={{0,16},{4,20},{8,24},{12,28},{16,0},{20,4},{24,8},{28,12},{1,17},{... | collective-permute-start | bytes 884744 | tf_op jit(solution)/shard_map/ppermute | solution.py:308
  88.3 18.5 %collective-permute-start.9 = (bf16[336,512]{1,0:T(8,128)(2,1)S(1)}, bf16[336,512]{1,0:T(8,128)(2,1)S(1)}, u32[]{:S(2)}, u32[]{:S(2)}) collective-permute-start(bf16[336,512]{1,0:T(8,128)(2,1)S(1)} %get-tuple-element.125), channel_id=1, source_target_pairs={{0,1},{1,2},{2,3},{3,0},{4,5},{5,6},{6,7},{7,4},{8,9},{9,10},{10,1... | collective-permute-start | bytes 1032200 | tf_op jit(solution)/shard_map/ppermute | solution.py:40
  89.8 17.0 %collective-permute-start.13 = (bf16[288,512]{1,0:T(8,128)(2,1)S(1)}, bf16[288,512]{1,0:T(8,128)(2,1)S(1)}, u32[]{:S(2)}, u32[]{:S(2)}) collective-permute-start(bf16[288,512]{1,0:T(8,128)(2,1)S(1)} %get-tuple-element.136), channel_id=1, source_target_pairs={{0,24},{4,28},{8,16},{12,20},{16,8},{20,12},{24,0},{28,4},{1,25},{... | collective-permute-start | bytes 884744 | tf_op jit(solution)/shard_map/ppermute | solution.py:308
  94.1 19.8 %collective-permute-start.15 = (bf16[352,512]{1,0:T(8,128)(2,1)S(1)}, bf16[352,512]{1,0:T(8,128)(2,1)S(1)}, u32[]{:S(2)}, u32[]{:S(2)}) collective-permute-start(bf16[352,512]{1,0:T(8,128)(2,1)S(1)} %get-tuple-element.157), channel_id=1, source_target_pairs={{0,8},{4,12},{8,0},{12,4},{16,24},{20,28},{24,16},{28,20},{1,9},{5... | collective-permute-start | bytes 1081352 | tf_op jit(solution)/shard_map/ppermute | solution.py:308
  96.2 22.0 %collective-permute-start.16 = (bf16[352,512]{1,0:T(8,128)(2,1)S(1)}, bf16[352,512]{1,0:T(8,128)(2,1)S(1)}, u32[]{:S(2)}, u32[]{:S(2)}) collective-permute-start(bf16[352,512]{1,0:T(8,128)(2,1)S(1)} %get-tuple-element.158), channel_id=1, source_target_pairs={{0,16},{4,20},{8,24},{12,28},{16,0},{20,4},{24,8},{28,12},{1,17},{... | collective-permute-start | bytes 1081352 | tf_op jit(solution)/shard_map/ppermute | solution.py:308
  103.9 14.2 %collective-permute-start.17 = (bf16[352,512]{1,0:T(8,128)(2,1)S(1)}, bf16[352,512]{1,0:T(8,128)(2,1)S(1)}, u32[]{:S(2)}, u32[]{:S(2)}) collective-permute-start(bf16[352,512]{1,0:T(8,128)(2,1)S(1)} %get-tuple-element.159), channel_id=1, source_target_pairs={{0,24},{4,28},{8,16},{12,20},{16,8},{20,12},{24,0},{28,4},{1,25},{... | collective-permute-start | bytes 1081352 | tf_op jit(solution)/shard_map/ppermute | solution.py:308
  111.8 8.2 %collective-permute-start.18 = (bf16[2,224,512]{2,1,0:T(8,128)(2,1)S(1)}, bf16[2,224,512]{2,1,0:T(8,128)(2,1)S(1)}, u32[]{:S(2)}, u32[]{:S(2)}) collective-permute-start(bf16[2,224,512]{2,1,0:T(8,128)(2,1)S(1)} %get-tuple-element.164), channel_id=1, source_target_pairs={{0,4},{4,0},{8,12},{12,8},{16,20},{20,16},{24,28},{28,24},{1,5},{5... | collective-permute-start | bytes 1376264 | tf_op jit(solution)/shard_map/ppermute | solution.py:308
  111.9 8.1 %collective-permute-start.19 = (bf16[2,224,512]{2,1,0:T(8,128)(2,1)S(1)}, bf16[2,224,512]{2,1,0:T(8,128)(2,1)S(1)}, u32[]{:S(2)}, u32[]{:S(2)}) collective-permute-start(bf16[2,224,512]{2,1,0:T(8,128)(2,1)S(1)} %get-tuple-element.165), channel_id=1, source_target_pairs={{0,4},{4,0},{8,12},{12,8},{16,20},{20,16},{24,28},{28,24},{1,5},{5... | collective-permute-start | bytes 1376264 | tf_op jit(solution)/shard_map/ppermute | solution.py:308
  114.0 29.3 %collective-permute-start.25 = (bf16[336,512]{1,0:T(8,128)(2,1)S(1)}, bf16[336,512]{1,0:T(8,128)(2,1)S(1)}, u32[]{:S(2)}, u32[]{:S(2)}) collective-permute-start(bf16[336,512]{1,0:T(8,128)(2,1)S(1)} %get-tuple-element.182), channel_id=1, source_target_pairs={{0,1},{1,2},{2,3},{3,0},{4,5},{5,6},{6,7},{7,4},{8,9},{9,10},{10,1... | collective-permute-start | bytes 1032200 | tf_op jit(solution)/shard_map/ppermute | solution.py:40
  118.1 11.1 %collective-permute-start.20 = (bf16[144,512]{1,0:T(8,128)(2,1)S(1)}, bf16[144,512]{1,0:T(8,128)(2,1)S(1)}, u32[]{:S(2)}, u32[]{:S(2)}) collective-permute-start(bf16[144,512]{1,0:T(8,128)(2,1)S(1)} %get-tuple-element.170), channel_id=1, source_target_pairs={{0,1},{1,0},{2,3},{3,2},{4,5},{5,4},{6,7},{7,6},{8,9},{9,8},{10,11... | collective-permute-start | bytes 442376 | tf_op jit(solution)/shard_map/ppermute | solution.py:308
  120.0 13.0 %collective-permute-start.21 = (bf16[176,512]{1,0:T(8,128)(2,1)S(1)}, bf16[176,512]{1,0:T(8,128)(2,1)S(1)}, u32[]{:S(2)}, u32[]{:S(2)}) collective-permute-start(bf16[176,512]{1,0:T(8,128)(2,1)S(1)} %get-tuple-element.172), channel_id=1, source_target_pairs={{0,1},{1,0},{2,3},{3,2},{4,5},{5,4},{6,7},{7,6},{8,9},{9,8},{10,11... | collective-permute-start | bytes 540680 | tf_op jit(solution)/shard_map/ppermute | solution.py:308
  129.3 8.5 %collective-permute-start.22 = (bf16[224,512]{1,0:T(8,128)(2,1)S(1)}, bf16[224,512]{1,0:T(8,128)(2,1)S(1)}, u32[]{:S(2)}, u32[]{:S(2)}) collective-permute-start(bf16[224,512]{1,0:T(8,128)(2,1)S(1)} %get-tuple-element.174), channel_id=1, source_target_pairs={{0,8},{4,12},{8,0},{12,4},{16,24},{20,28},{24,16},{28,20},{1,9},{5... | collective-permute-start | bytes 688136 | tf_op jit(solution)/shard_map/ppermute | solution.py:308
  130.4 12.1 %collective-permute-start.23 = (bf16[224,512]{1,0:T(8,128)(2,1)S(1)}, bf16[224,512]{1,0:T(8,128)(2,1)S(1)}, u32[]{:S(2)}, u32[]{:S(2)}) collective-permute-start(bf16[224,512]{1,0:T(8,128)(2,1)S(1)} %get-tuple-element.175), channel_id=1, source_target_pairs={{0,16},{4,20},{8,24},{12,28},{16,0},{20,4},{24,8},{28,12},{1,17},{... | collective-permute-start | bytes 688136 | tf_op jit(solution)/shard_map/ppermute | solution.py:308
  132.8 9.7 %collective-permute-start.24 = (bf16[224,512]{1,0:T(8,128)(2,1)S(1)}, bf16[224,512]{1,0:T(8,128)(2,1)S(1)}, u32[]{:S(2)}, u32[]{:S(2)}) collective-permute-start(bf16[224,512]{1,0:T(8,128)(2,1)S(1)} %get-tuple-element.176), channel_id=1, source_target_pairs={{0,24},{4,28},{8,16},{12,20},{16,8},{20,12},{24,0},{28,4},{1,25},{... | collective-permute-start | bytes 688136 | tf_op jit(solution)/shard_map/ppermute | solution.py:308
  133.0 10.2 %collective-permute-start.26 = (bf16[144,512]{1,0:T(8,128)(2,1)S(1)}, bf16[144,512]{1,0:T(8,128)(2,1)S(1)}, u32[]{:S(2)}, u32[]{:S(2)}) collective-permute-start(bf16[144,512]{1,0:T(8,128)(2,1)S(1)} %add_convert_fusion.12), channel_id=1, source_target_pairs={{0,2},{1,3},{2,0},{3,1},{4,6},{5,7},{6,4},{7,5},{8,10},{9,11},{10,... | collective-permute-start | bytes 442376 | tf_op jit(solution)/shard_map/ppermute | solution.py:308
  142.5 8.2 %collective-permute-start.28 = (bf16[176,512]{1,0:T(8,128)(2,1)S(1)}, bf16[176,512]{1,0:T(8,128)(2,1)S(1)}, u32[]{:S(2)}, u32[]{:S(2)}) collective-permute-start(bf16[176,512]{1,0:T(8,128)(2,1)S(1)} %add_convert_fusion.10), channel_id=1, source_target_pairs={{0,2},{1,3},{2,0},{3,1},{4,6},{5,7},{6,4},{7,5},{8,10},{9,11},{10,... | collective-permute-start | bytes 540680 | tf_op jit(solution)/shard_map/ppermute | solution.py:308
  143.2 7.4 %collective-permute-start.27 = (bf16[112,512]{1,0:T(8,128)(2,1)S(1)}, bf16[112,512]{1,0:T(8,128)(2,1)S(1)}, u32[]{:S(2)}, u32[]{:S(2)}) collective-permute-start(bf16[112,512]{1,0:T(8,128)(2,1)S(1)} %get-tuple-element.188), channel_id=1, source_target_pairs={{0,1},{1,0},{2,3},{3,2},{4,5},{5,4},{6,7},{7,6},{8,9},{9,8},{10,11... | collective-permute-start | bytes 344072 | tf_op jit(solution)/shard_map/ppermute | solution.py:308
  150.7 6.7 %collective-permute-start.29 = (bf16[112,512]{1,0:T(8,128)(2,1)S(1)}, bf16[112,512]{1,0:T(8,128)(2,1)S(1)}, u32[]{:S(2)}, u32[]{:S(2)}) collective-permute-start(bf16[112,512]{1,0:T(8,128)(2,1)S(1)} %add_convert_fusion.14), channel_id=1, source_target_pairs={{0,2},{1,3},{2,0},{3,1},{4,6},{5,7},{6,4},{7,5},{8,10},{9,11},{10,... | collective-permute-start | bytes 344072 | tf_op jit(solution)/shard_map/ppermute | solution.py:308
  150.9 7.3 %collective-permute-start.30 = (bf16[144,512]{1,0:T(8,128)(2,1)S(1)}, bf16[144,512]{1,0:T(8,128)(2,1)S(1)}, u32[]{:S(2)}, u32[]{:S(2)}) collective-permute-start(bf16[144,512]{1,0:T(8,128)(2,1)S(1)} %add_convert_fusion.11.half), channel_id=1, source_target_pairs={{0,1},{1,0},{2,3},{3,2},{4,5},{5,4},{6,7},{7,6},{8,9},{9,8},{10,11... | collective-permute-start | bytes 442376 | tf_op jit(solution)/shard_map/ppermute | solution.py:308
  157.4 5.5 %collective-permute-start.31 = (bf16[176,512]{1,0:T(8,128)(2,1)S(1)}, bf16[176,512]{1,0:T(8,128)(2,1)S(1)}, u32[]{:S(2)}, u32[]{:S(2)}) collective-permute-start(bf16[176,512]{1,0:T(8,128)(2,1)S(1)} %add_convert_fusion.9.half), channel_id=1, source_target_pairs={{0,1},{1,0},{2,3},{3,2},{4,5},{5,4},{6,7},{7,6},{8,9},{9,8},{10,11... | collective-permute-start | bytes 540680 | tf_op jit(solution)/shard_map/ppermute | solution.py:308
  158.2 6.2 %collective-permute-start.32 = (bf16[112,512]{1,0:T(8,128)(2,1)S(1)}, bf16[112,512]{1,0:T(8,128)(2,1)S(1)}, u32[]{:S(2)}, u32[]{:S(2)}) collective-permute-start(bf16[112,512]{1,0:T(8,128)(2,1)S(1)} %add_convert_fusion.13.half), channel_id=1, source_target_pairs={{0,1},{1,0},{2,3},{3,2},{4,5},{5,4},{6,7},{7,6},{8,9},{9,8},{10,11... | collective-permute-start | bytes 344072 | tf_op jit(solution)/shard_map/ppermute | solution.py:308
  (36 other events, 181.7 us)
Sparse Core Ops, SparseCore 0:
  10.3 45.4 all-gather.2

commit v4 on v3

--- a/solution.py
+++ b/solution.py
@@ -183,7 +183,7 @@
 
 
 def pack_body(
-    g1, b1, wqkv, bqv, table, wproj, bproj, g2, b2, win, bin_, wout, bout, attn, mlp
+    g1, b1, wqkv, bqv, table, wproj, bproj, g2, b2, win, bin_, wout, bout, attn, mlp, out
 ):
     depth = wqkv.shape[0]
     me = shard_place()
@@ -209,12 +209,12 @@
     attn[4 * depth :, :] = padded(rows, SMALL)
     for c in range(FF // D):
         mlp[c * depth : (c + 1) * depth, :] = win[:, c * D : (c + 1) * D]
-    mlp[4 * depth : 8 * depth, :] = wout[...]
+    out[...] = wout[...]
     held = jnp.concatenate([bin_[r : r + 1] for r in range(bin_.shape[0])], 1)
     hidden_bias = place(held, FF, me)
     rows = [place(v, D, me) for v in (g2[...], b2[...], bout[...])]
     rows += [hidden_bias[:, c * D : (c + 1) * D] for c in range(FF // D)]
-    mlp[8 * depth :, :] = padded(rows, SMALL)
+    mlp[4 * depth :, :] = padded(rows, SMALL)
 
 
 def join_halves(late, half, back, both, sems):
@@ -361,27 +361,18 @@
 
 
 def block_of(slab, c, depth):
-    return slab[:, c * depth : (c + 1) * depth, :].reshape(D, D)
+    me = shard_place()
+    rows = [slab[k ^ me, c * depth : (c + 1) * depth, :] for k in range(slab.shape[0])]
+    return jnp.concatenate(rows, 0)
 
 
 def smalls_of(slab, start):
     return jnp.sum(slab[:, start:, :].astype(F32), 0)
 
 
-def project_body(tokens, halo, *refs):
-    shards = len(refs) - 7
-    pieces = refs[:shards]
-    normed_win, query, key, value, slab, wide, sems = refs[shards:]
-    copies = [
-        pltpu.make_async_copy(piece, slab.at[shard_place() ^ p], sems.at[p])
-        for p, piece in enumerate(pieces)
-    ]
-    for copy in copies:
-        copy.start()
+def project_body(tokens, halo, slab, normed_win, query, key, value, wide):
     columns = column_places()
     own = WIN - SHIFT
-    for copy in copies:
-        copy.wait()
     depth = (slab.shape[1] - SMALL) // 4
     small = smalls_of(slab, 4 * depth)
     gain, offset, bias_q, bias_v = (small[r : r + 1] for r in range(4))
@@ -476,14 +467,26 @@
 
 
 def mlp_forward_body(
-    mixed, cotangent, cot_halo, slab, kept, sent, cot, actives, back_sum, vectors, same, other
+    mixed,
+    cotangent,
+    cot_halo,
+    slab,
+    out_slab,
+    kept,
+    sent,
+    cot,
+    actives,
+    back_sum,
+    vectors,
+    same,
+    other,
 ):
     me = shard_place()
     shards, height = slab.shape[:2]
-    depth = (height - SMALL) // 8
+    depth = (height - SMALL) // 4
     span = shards * D // FF
     chunks = FF // D
-    small = smalls_of(slab, 8 * depth)
+    small = smalls_of(slab, 4 * depth)
     vectors[...] = small
     gain, offset, bias_o = (small[r : r + 1] for r in range(3))
     own = WIN - SHIFT
@@ -496,10 +499,11 @@
     normed_low = jnp.concatenate(lows, 0)
 
     def w_in(c):
-        return block_of(slab, c, depth)
+        return slab[:, c * depth : (c + 1) * depth, :].reshape(D, D)
 
     def w_out(c):
-        return slab[c * span : (c + 1) * span, 4 * depth : 8 * depth, :].reshape(D, D)
+        rows = [out_slab[k ^ me] for k in range(c * span, (c + 1) * span)]
+        return jnp.concatenate(rows, 0)
 
     hiddens, slopes, grads, forward, backward, bias_sums = {}, {}, {}, None, None, []
     for step in range(-1, chunks + 1):
@@ -647,8 +651,8 @@
     pairs,
     *refs,
 ):
-    grads = refs[:-7]
-    kept, sent, same, other_low, other_high, wide, other = refs[-7:]
+    grads = refs[:-5]
+    kept, sent, same, other, wide = refs[-5:]
     me = shard_place()
     shards = slab.shape[0]
     depth = (slab.shape[1] - SMALL) // 4
@@ -703,9 +707,6 @@
         row = jnp.sum(total, 0, keepdims=True)
         rows += [row[:, c * D : (c + 1) * D] for c in range(TAB // D)]
     put_smalls(same, other, 3 * depth, rows)
-    half = other_low.shape[0]
-    other_low[...] = other[:half]
-    other_high[...] = other[half:]
 
 
 def region_views(regions, rows, place):
@@ -755,13 +756,16 @@
         w_out,
         bias_out[None],
     )
-    attn_slab, mlp_slab = kernel_call(
+    attn_slab, mlp_slab, out_slab = kernel_call(
         pack_body,
-        [like((4 * depth + SMALL, D), BF), like((8 * depth + SMALL, D), BF)],
+        [like((4 * depth + SMALL, D), BF)] * 2 + [like((4 * depth, D), BF)],
         (*attn_params, *mlp_params),
         vmem=60,
     )
     pieces = gather_pieces(attn_slab)
+    pieces, (out_slab,) = tie(pieces, [out_slab])
+    attn_all = jnp.stack(pieces)
+    out_pieces = gather_pieces(out_slab)
     mlp_all = lax.all_gather(mlp_slab, "shard")
     tokens_here = tokens[0]
     token_halo = shifted_2(tokens_here[:SHIFT], "seq", -1)
@@ -769,15 +773,11 @@
     cot_halo = shifted_2(cot_here[:SHIFT], "seq", -1)
     by_row, by_lane = region_views(regions, local_rows, seq)
 
-    normed_win, query, key, value, attn_all = kernel_call(
+    normed_win, query, key, value = kernel_call(
         project_body,
-        [like((PADDED, D), BF)] * 4 + [like((shards, *attn_slab.shape), BF)],
-        (tokens_here, token_halo, *pieces),
-        scratch=[
-            pltpu.VMEM((WINDOWS, WIN, SLOT, D), F32),
-            pltpu.SemaphoreType.DMA((shards,)),
-        ],
-        apart=shards,
+        [like((PADDED, D), BF)] * 4,
+        (tokens_here, token_halo, attn_all),
+        scratch=[pltpu.VMEM((WINDOWS, WIN, SLOT, D), F32)],
     )
     pair_rows = 2 * PLACES
     steps = WINDOWS // 2
@@ -830,8 +830,7 @@
             share_a,
             share_a,
         ],
-        (mixed, cot_here, cot_halo, mlp_all),
-        vmem=24,
+        (mixed, cot_here, cot_halo, mlp_all, jnp.stack(out_pieces)),
     )
     grad_mixed, grad_win, same_b, other_b = kernel_call(
         mlp_backward_body,
@@ -862,49 +861,41 @@
     sums, (pairs,) = tie(add_cores(same_b, came_b), [pairs])
     parts_b = to_chips(sums)
     late_part, pairs = backward(count, count, grad_win, pairs)
-    parts_a, (pairs,) = tie(parts_a, [pairs])
+    keep_a, send = add_chips(same_a, came_a, parts_a)
+    (send,), (pairs,) = tie([send], [pairs])
+    near_a = exchange(send, "seq", 1)
     (out_halo,), (pairs,) = tie([shifted_2(out_sent, "seq", 1)], [pairs])
-    tok_kept, tok_sent, attn_same, *attn_others = kernel_call(
+    tok_kept, tok_sent, attn_same, attn_other = kernel_call(
         attn_last_body,
         [
             like((own * WIDTH, D), F32),
             like((SHIFT * WIDTH, D), BF),
             like((chips, 3 * depth + SMALL, D), BF),
-            like((chips // 2, 3 * depth + SMALL, D), BF),
-            like((chips // 2, 3 * depth + SMALL, D), BF),
+            like((chips, 3 * depth + SMALL, D), BF),
         ],
         (grad_mixed, tokens_here, token_halo, attn_all, normed_win, pairs, early, late_part),
-        scratch=[
-            pltpu.VMEM((WINDOWS, WIN, SLOT, D), F32),
-            pltpu.VMEM((chips, 3 * depth + SMALL, D), BF),
-        ],
+        scratch=[pltpu.VMEM((WINDOWS, WIN, SLOT, D), F32)],
     )
-    attn_came = [exchange(other, "shard", 1) for other in attn_others]
-    keep_a, send = add_chips(same_a, came_a, parts_a)
-    (send,), parts_b = tie([send], parts_b)
-    near_a = exchange(send, "seq", 1)
+    half_a = add_pair(keep_a, near_a)
+    (half_a,), (attn_other, tok_sent) = tie([half_a], [attn_other, tok_sent])
+    far_a = exchange(half_a, "seq", 2)
+    attn_came = exchange(attn_other, "shard", 1)
     keep_b, send = add_chips(same_b, came_b, parts_b, 10_000_000_000)
-    (send,), attn_came = tie([send], attn_came)
+    (send,), (attn_came,) = tie([send], [attn_came])
     near_b = exchange(send, "seq", 1)
-    came = [c[q] for c in attn_came for q in range(chips // 2)]
-    sums = [add_pair(attn_same[q], came[q]) for q in range(1, chips)]
-    sums, (near_a,) = tie(sums, [near_a])
+    sums, (far_a,) = tie(add_cores(attn_same, attn_came), [far_a])
     attn_parts = to_chips(sums)
-    half_a = add_pair(keep_a, near_a)
-    (half_a,), (near_b,) = tie([half_a], [near_b])
-    far_a = exchange(half_a, "seq", 2)
+    half_a = seq_rest(add_pair(half_a, far_a))
+    (half_a,), (near_b, tok_sent) = tie([half_a], [near_b, tok_sent])
+    tok_halo = shifted_2(tok_sent, "seq", 1)
     half_b = add_pair(keep_b, near_b)
     (half_b,), attn_parts = tie([half_b], attn_parts)
     far_b = exchange(half_b, "seq", 2)
-    keep, send = add_chips(attn_same, attn_came[0], attn_parts)
-    tok_halo = shifted_2(tok_sent, "seq", 1)
-    (keep, send, tok_halo), (far_a,) = tie([keep, send, tok_halo], [far_a])
+    keep, send = add_chips(attn_same, attn_came, attn_parts)
     near = exchange(send, "seq", 1)
-    half_a = seq_rest(add_pair(half_a, far_a))
-    (half_a,), (near,) = tie([half_a], [near])
     back_a = exchange(half_a, "seq", 1)
     half = add_pair(keep, near)
-    (half,), (far_b,) = tie([half], [far_b])
+    (half, tok_halo), (far_b,) = tie([half, tok_halo], [far_b])
     far = exchange(half, "seq", 2)
     half_b = seq_rest(add_pair(half_b, far_b))
     (half_b,), (far,) = tie([half_b], [far])

time: 173 us -> 168 us (0.971)
  local copies, waits for them, and re-layouts: 22.5 us -> 16.5 us
  waiting for transfers between devices: 45.5 us -> 47.3 us
    unnamed x68 -> x84, local copies, waits for them, and re-layouts: 20.2 us -> 13.1 us
    ppermute x29 -> x35, starting transfers between devices: 26.5 us -> 30 us  [exchange(): return lax.ppermute(value, axis, [(i, i ^ mask) for i in range(peers)])]
    ppermute x4, starting transfers between devices: 11.3 us -> 8 us  [shifted_2(): lax.ppermute(value, axis, [(i, (i + by) % peers) for i in range(peers)])]
    ppermute x29 -> x35, waiting for transfers between devices: 45.5 us -> 47.3 us  [exchange(): return lax.ppermute(value, axis, [(i, i ^ mask) for i in range(peers)])]
  transfers between devices with their start and end apart: 34 -> 40, of which waited for: 12 -> 18; matrix products, arithmetic and copies ran while one was open for 4% -> 6% of each run, Pallas kernels for 17% -> 17%
where the time goes in v4:
time: 168 us
  Pallas kernels  47.4 us (28%)
  waiting for transfers between devices  47.3 us (28%)
  starting transfers between devices  38 us (23%)
  local copies, waits for them, and re-layouts  16.5 us (10%)
  between operations  14.8 us (9%)
  other arithmetic  3.72 us (2%)
    pallas_call x14, Pallas kernels, kernel_call(): pl.pallas_call(body, out_shape=tuple(outs), in_specs=in_specs, out_specs=...  47.4 us
    ppermute x35, waiting for transfers between devices, exchange(): return lax.ppermute(value, axis, [(i, i ^ mask) for i in range(peers)])  47.3 us
    ppermute x35, starting transfers between devices, exchange(): return lax.ppermute(value, axis, [(i, i ^ mask) for i in range(peers)])  30 us
    unnamed x84, local copies, waits for them, and re-layouts  13.1 us
    ppermute x4, starting transfers between devices, shifted_2(): lax.ppermute(value, axis, [(i, (i + by) % peers) for i in range(peers)])  8 us
  transfers between devices with their start and end apart: 40, of which 18 were waited for; matrix products, arithmetic and copies ran while one was open for 6% of the time, Pallas kernels for 17%

profile of v4, /device:TPU:0, one launch (start us, length us, event | category | flops | bytes accessed | tf_op | source)
XLA Modules:
  0.0 167.8 jit_solution(5687213269780594991)
XLA Ops:
  7.2 2.9 %shard_map.271 = (bf16[288,512]{1,0:T(8,128)(2,1)}, bf16[288,512]{1,0:T(8,128)(2,1)}, bf16[256,512]{1,0:T(8,128)(2,1)}) custom-call(bf16[1,64]{1,0:T(2,128)(2,1)} %bitcast.87, bf16[1,64]{1,0:T(2,128)(2,1)} %bitcast.88, bf16[64,1536]{1,0:T(8,128)(2,1)} %wqkv.1, bf16[2,64]{1,0:T(2,128)(2,1)} %bqv.1, bf16[2,169]{1,0:T(2,128)(2,1)} %bitcast.86, ...), custom_call_target="tpu_custom_call" | custom-call | flops 1024 | bytes 1024 | tf_op jit(solution)/shard_map/pallas_call | solution.py:150
  10.1 2.9 %collective-permute-start.1 = (bf16[288,512]{1,0:T(8,128)(2,1)}, bf16[288,512]{1,0:T(8,128)(2,1)S(1)}, u32[]{:S(2)}, u32[]{:S(2)}) collective-permute-start(bf16[288,512]{1,0:T(8,128)(2,1)} %get-tuple-element.120), channel_id=1, source_target_pairs={{0,8},{4,12},{8,0},{12,4},{16,24},{20,28},{24,16},{28,20},{1,9},{5... | collective-permute-start | bytes 884744 | tf_op jit(solution)/shard_map/ppermute | solution.py:308
  13.0 1.5 collective-permute-start.3
  14.6 1.7 %slice_bitcast_fusion.1 = bf16[3,112,512]{2,1,0:T(8,128)(2,1)} fusion(bf16[1,7,112,512]{3,2,1,0:T(8,128)(2,1)} %param.16), kind=kLoop, calls=%fused_computation.17 | loop fusion | bytes 688128 | tf_op jit(solution)/shard_map/slice | solution.py:771
  16.3 4.1 %collective-permute-start.7 = (bf16[3,112,512]{2,1,0:T(8,128)(2,1)}, bf16[3,112,512]{2,1,0:T(8,128)(2,1)S(1)}, u32[]{:S(2)}, u32[]{:S(2)}) collective-permute-start(bf16[3,112,512]{2,1,0:T(8,128)(2,1)} %slice_bitcast_fusion.1), channel_id=1, source_target_pairs={{0,3},{1,0},{2,1},{3,2},{4,7},{5,4},{6,5},{7,6},{8,11},{9,8},{10,9... | collective-permute-start | bytes 1032200 | tf_op jit(solution)/shard_map/ppermute | solution.py:40
  21.2 6.9 %collective-permute-done.3 = bf16[288,512]{1,0:T(8,128)(2,1)S(1)} collective-permute-done((bf16[288,512]{1,0:T(8,128)(2,1)}, bf16[288,512]{1,0:T(8,128)(2,1)S(1)}, u32[]{:S(2)}, u32[]{:S(2)}) %collective-permute-start.3) | collective-permute-done | bytes 294944 | tf_op jit(solution)/shard_map/ppermute | solution.py:308
  32.3 1.5 collective-permute-start.14
  37.1 3.7 %collective-permute-start.8 = (bf16[3,112,512]{2,1,0:T(8,128)(2,1)S(1)}, bf16[3,112,512]{2,1,0:T(8,128)(2,1)S(1)}, u32[]{:S(2)}, u32[]{:S(2)}) collective-permute-start(bf16[3,112,512]{2,1,0:T(8,128)(2,1)S(1)} %slice_bitcast_fusion), channel_id=1, source_target_pairs={{0,3},{1,0},{2,1},{3,2},{4,7},{5,4},{6,5},{7,6},{8,11},{9,8},{10,9... | collective-permute-start | bytes 1032200 | tf_op jit(solution)/shard_map/ppermute | solution.py:40
  40.8 2.4 %shard_map.272 = (bf16[896,512]{1,0:T(8,128)(2,1)S(1)}, bf16[896,512]{1,0:T(8,128)(2,1)S(1)}, bf16[896,512]{1,0:T(8,128)(2,1)S(1)}, bf16[896,512]{1,0:T(8,128)(2,1)S(1)}) custom-call(bf16[7,112,512]{2,1,0:T(8,128)(2,1)S(1)} %bitcast.78, bf16[3,112,512]{2,1,0:T(8,128)(2,1)S(1)} %collective-permute-done.7.halo, ...), custom_call_target="tpu_custom_call" | custom-call | flops 1024 | bytes 1024 | tf_op jit(solution)/shard_map/pallas_call | solution.py:150
  43.4 7.1 %shard_map.273 = (bf16[8,4,112,256]{3,2,1,0:T(8,128)(2,1)S(1)}, bf16[784,512]{1,0:T(8,128)(2,1)S(1)}, f32[784,512]{1,0:T(8,128)S(1)}) custom-call(bf16[8,288,512]{2,1,0:T(8,128)(2,1)S(1)} %bitcast_dynamic-update-slice_fusion.slab.attn_slab, f32[16,56,128]{2,1,0:T(8,128)S(1)} %broadcast_in_dim.35.reg_rows, f32[16,1,256]{2,1,0:T(1,128)S(1)} %tile.9.reg_lanes, ...), custom_call_target="tpu_custom_call" | custom-call | flops 1024 | bytes 1024 | tf_op jit(solution)/shard_map/pallas_call | solution.py:150
  57.6 1.6 copy-done.13
  59.2 1.7 copy-done.14
  63.0 13.8 %shard_map.274 = (f32[448,512]{1,0:T(8,128)S(1)}, bf16[336,512]{1,0:T(8,128)(2,1)S(1)}, bf16[784,512]{1,0:T(8,128)(2,1)S(1)}, bf16[784,2048]{1,0:T(8,128)(2,1)S(...) custom-call(f32[784,512]{1,0:T(8,128)S(1)} %copy-done.11, ...), custom_call_target="tpu_custom_call" | custom-call | flops 1024 | bytes 1024 | tf_op jit(solution)/shard_map/pallas_call | solution.py:150
  76.9 5.5 %shard_map.275 = (f32[784,512]{1,0:T(8,128)S(1)}, bf16[896,512]{1,0:T(8,128)(2,1)S(1)}, bf16[4,352,512]{2,1,0:T(8,128)(2,1)S(1)}, bf16[4,352,512]{2,1,0:T(8,128)(2,1)S(1)}) custom-call(f32[784,512]{1,0:T(8,128)S(1)} %copy-done.11, bf16[784,512]{1,0:T(8,128)(2,1)S(1)} %get-tuple-element.137.cot, bf16[784,2048]{1,0:T(8,128)(2,1)S(1)} %get-tuple-element.138.actives, ...), custom_call_target="tpu_custom_call" | custom-call | flops 1024 | bytes 1024 | tf_op jit(solution)/shard_map/pallas_call | solution.py:150
  86.8 3.0 %shard_map.277 = (bf16[448,1536]{1,0:T(8,128)(2,1)S(1)}, f32[4,56,256]{2,1,0:T(8,128)S(1)}) custom-call(bf16[896,512]{1,0:T(8,128)(2,1)S(1)} %copy-done.3, bf16[896,512]{1,0:T(8,128)(2,1)S(1)} %copy-done.5, bf16[896,512]{1,0:T(8,128)(2,1)S(1)} %copy-done.7, bf16[8,4,112,256]{3,2,1,0:T(8,128)(2,1)S(1)} %copy-done.9, ...), custom_call_target="tpu_custom_call" | custom-call | flops 1024 | bytes 1024 | tf_op jit(solution)/shard_map/pallas_call | solution.py:150
  90.1 3.0 %shard_map.278 = (bf16[448,1536]{1,0:T(8,128)(2,1)S(1)}, f32[4,56,256]{2,1,0:T(8,128)S(1)}) custom-call(bf16[896,512]{1,0:T(8,128)(2,1)S(1)} %copy-done.3, bf16[896,512]{1,0:T(8,128)(2,1)S(1)} %copy-done.5, bf16[896,512]{1,0:T(8,128)(2,1)S(1)} %copy-done.7, bf16[8,4,112,256]{3,2,1,0:T(8,128)(2,1)S(1)} %copy-done.9, ...), custom_call_target="tpu_custom_call" | custom-call | flops 1024 | bytes 1024 | tf_op jit(solution)/shard_map/pallas_call | solution.py:150
  93.1 4.8 %collective-permute-done.19.refs_1_ = bf16[288,512]{1,0:T(8,128)(2,1)S(1)} collective-permute-done((bf16[288,512]{1,0:T(8,128)(2,1)S(1)}, bf16[288,512]{1,0:T(8,128)(2,1)S(1)}, u32[]{:S(2)}, u32[]{:S(2)}) %collective-permute-start.19) | collective-permute-done | bytes 294944 | tf_op jit(solution)/shard_map/ppermute | solution.py:308
  97.9 1.8 %collective-permute-done.20.refs_2_ = bf16[288,512]{1,0:T(8,128)(2,1)S(1)} collective-permute-done((bf16[288,512]{1,0:T(8,128)(2,1)S(1)}, bf16[288,512]{1,0:T(8,128)(2,1)S(1)}, u32[]{:S(2)}, u32[]{:S(2)}) %collective-permute-start.20) | collective-permute-done | bytes 294944 | tf_op jit(solution)/shard_map/ppermute | solution.py:308
  100.6 1.7 %collective-permute-start.23 = (bf16[352,512]{1,0:T(8,128)(2,1)S(1)}, bf16[352,512]{1,0:T(8,128)(2,1)S(1)}, u32[]{:S(2)}, u32[]{:S(2)}) collective-permute-start(bf16[352,512]{1,0:T(8,128)(2,1)S(1)} %get-tuple-element.164), channel_id=1, source_target_pairs={{0,16},{4,20},{8,24},{12,28},{16,0},{20,4},{24,8},{28,12},{1,17},{... | collective-permute-start | bytes 1081352 | tf_op jit(solution)/shard_map/ppermute | solution.py:308
  103.5 5.1 %shard_map.279 = (f32[448,512]{1,0:T(8,128)S(1)}, bf16[336,512]{1,0:T(8,128)(2,1)S(1)}, bf16[4,224,512]{2,1,0:T(8,128)(2,1)S(1)}, bf16[4,224,512]{2,1,0:T(8,128)(2,1)S(1)}) custom-call(f32[784,512]{1,0:T(8,128)S(1)} %get-tuple-element.157.grad_mixed, bf16[7,112,512]{2,1,0:T(8,128)(2,1)S(1)} %bitcast.80, ...), custom_call_target="tpu_custom_call" | custom-call | flops 1024 | bytes 1024 | tf_op jit(solution)/shard_map/pallas_call | solution.py:150
  108.8 2.3 %collective-permute-start.27 = (bf16[144,512]{1,0:T(8,128)(2,1)S(1)}, bf16[144,512]{1,0:T(8,128)(2,1)S(1)}, u32[]{:S(2)}, u32[]{:S(2)}) collective-permute-start(bf16[144,512]{1,0:T(8,128)(2,1)S(1)} %add_convert_fusion.12), channel_id=1, source_target_pairs={{0,2},{1,3},{2,0},{3,1},{4,6},{5,7},{6,4},{7,5},{8,10},{9,11},{10,... | collective-permute-start | bytes 442376 | tf_op jit(solution)/shard_map/ppermute | solution.py:308
  111.4 6.1 %collective-permute-done.23.refs_1_ = bf16[352,512]{1,0:T(8,128)(2,1)S(1)} collective-permute-done((bf16[352,512]{1,0:T(8,128)(2,1)S(1)}, bf16[352,512]{1,0:T(8,128)(2,1)S(1)}, u32[]{:S(2)}, u32[]{:S(2)}) %collective-permute-start.23) | collective-permute-done | bytes 360480 | tf_op jit(solution)/shard_map/ppermute | solution.py:308
  119.7 1.7 collective-permute-start.29
  123.2 2.1 %collective-permute-done.28 = bf16[176,512]{1,0:T(8,128)(2,1)S(1)} collective-permute-done((bf16[176,512]{1,0:T(8,128)(2,1)S(1)}, bf16[176,512]{1,0:T(8,128)(2,1)S(1)}, u32[]{:S(2)}, u32[]{:S(2)}) %collective-permute-start.28) | collective-permute-done | bytes 180256 | tf_op jit(solution)/shard_map/ppermute | solution.py:308
  125.6 2.6 %collective-permute-done.29.refs_0_ = bf16[224,512]{1,0:T(8,128)(2,1)S(1)} collective-permute-done((bf16[224,512]{1,0:T(8,128)(2,1)S(1)}, bf16[224,512]{1,0:T(8,128)(2,1)S(1)}, u32[]{:S(2)}, u32[]{:S(2)}) %collective-permute-start.29) | collective-permute-done | bytes 229408 | tf_op jit(solution)/shard_map/ppermute | solution.py:308
  128.2 4.2 %collective-permute-done.30.refs_1_ = bf16[224,512]{1,0:T(8,128)(2,1)S(1)} collective-permute-done((bf16[224,512]{1,0:T(8,128)(2,1)S(1)}, bf16[224,512]{1,0:T(8,128)(2,1)S(1)}, u32[]{:S(2)}, u32[]{:S(2)}) %collective-permute-start.30) | collective-permute-done | bytes 229408 | tf_op jit(solution)/shard_map/ppermute | solution.py:308
  132.6 1.8 %collective-permute-start.32 = (bf16[112,512]{1,0:T(8,128)(2,1)S(1)}, bf16[112,512]{1,0:T(8,128)(2,1)S(1)}, u32[]{:S(2)}, u32[]{:S(2)}) collective-permute-start(bf16[112,512]{1,0:T(8,128)(2,1)S(1)} %get-tuple-element.186), channel_id=1, source_target_pairs={{0,1},{1,0},{2,3},{3,2},{4,5},{5,4},{6,7},{7,6},{8,9},{9,8},{10,11... | collective-permute-start | bytes 344072 | tf_op jit(solution)/shard_map/ppermute | solution.py:308
  136.0 2.3 %collective-permute-start.34 = (bf16[176,512]{1,0:T(8,128)(2,1)S(1)}, bf16[176,512]{1,0:T(8,128)(2,1)S(1)}, u32[]{:S(2)}, u32[]{:S(2)}) collective-permute-start(bf16[176,512]{1,0:T(8,128)(2,1)S(1)} %add_convert_fusion.10), channel_id=1, source_target_pairs={{0,2},{1,3},{2,0},{3,1},{4,6},{5,7},{6,4},{7,5},{8,10},{9,11},{10,... | collective-permute-start | bytes 540680 | tf_op jit(solution)/shard_map/ppermute | solution.py:308
  138.2 3.2 %collective-permute-done.32 = bf16[112,512]{1,0:T(8,128)(2,1)S(1)} collective-permute-done((bf16[112,512]{1,0:T(8,128)(2,1)S(1)}, bf16[112,512]{1,0:T(8,128)(2,1)S(1)}, u32[]{:S(2)}, u32[]{:S(2)}) %collective-permute-start.32) | collective-permute-done | bytes 114720 | tf_op jit(solution)/shard_map/ppermute | solution.py:308
  141.4 4.4 %collective-permute-done.34 = bf16[176,512]{1,0:T(8,128)(2,1)S(1)} collective-permute-done((bf16[176,512]{1,0:T(8,128)(2,1)S(1)}, bf16[176,512]{1,0:T(8,128)(2,1)S(1)}, u32[]{:S(2)}, u32[]{:S(2)}) %collective-permute-start.34) | collective-permute-done | bytes 180256 | tf_op jit(solution)/shard_map/ppermute | solution.py:308
  145.9 6.6 %collective-permute-done.35 = bf16[112,512]{1,0:T(8,128)(2,1)S(1)} collective-permute-done((bf16[112,512]{1,0:T(8,128)(2,1)S(1)}, bf16[112,512]{1,0:T(8,128)(2,1)S(1)}, u32[]{:S(2)}, u32[]{:S(2)}) %collective-permute-start.35) | collective-permute-done | bytes 114720 | tf_op jit(solution)/shard_map/ppermute | solution.py:308
  152.7 2.0 %collective-permute-start.38 = (bf16[112,512]{1,0:T(8,128)(2,1)S(1)}, bf16[112,512]{1,0:T(8,128)(2,1)S(1)}, u32[]{:S(2)}, u32[]{:S(2)}) collective-permute-start(bf16[112,512]{1,0:T(8,128)(2,1)S(1)} %add_convert_fusion.13.half), channel_id=1, source_target_pairs={{0,1},{1,0},{2,3},{3,2},{4,5},{5,4},{6,7},{7,6},{8,9},{9,8},{10,11... | collective-permute-start | bytes 344072 | tf_op jit(solution)/shard_map/ppermute | solution.py:308
  (174 shorter events, 37.3 us)
Async XLA Ops:
  7.2 49.0 %all-gather.3.cloned.1.call-start = ((), (), s32[]{:S(2)}) async-start(), calls=%async_computation | async-start | bytes 2654208 | tf_op jit(solution)/shard_map/all_gather | solution.py:769
  10.1 11.1 %collective-permute-start.1 = (bf16[288,512]{1,0:T(8,128)(2,1)}, bf16[288,512]{1,0:T(8,128)(2,1)S(1)}, u32[]{:S(2)}, u32[]{:S(2)}) collective-permute-start(bf16[288,512]{1,0:T(8,128)(2,1)} %get-tuple-element.120), channel_id=1, source_target_pairs={{0,8},{4,12},{8,0},{12,4},{16,24},{20,28},{24,16},{28,20},{1,9},{5... | collective-permute-start | bytes 884744 | tf_op jit(solution)/shard_map/ppermute | solution.py:308
  13.0 15.0 %collective-permute-start.3 = (bf16[288,512]{1,0:T(8,128)(2,1)}, bf16[288,512]{1,0:T(8,128)(2,1)S(1)}, u32[]{:S(2)}, u32[]{:S(2)}) collective-permute-start(bf16[288,512]{1,0:T(8,128)(2,1)} %get-tuple-element.120), channel_id=1, source_target_pairs={{0,16},{4,20},{8,24},{12,28},{16,0},{20,4},{24,8},{28,12},{1,17},{... | collective-permute-start | bytes 884744 | tf_op jit(solution)/shard_map/ppermute | solution.py:308
  14.6 13.5 %collective-permute-start.5 = (bf16[288,512]{1,0:T(8,128)(2,1)}, bf16[288,512]{1,0:T(8,128)(2,1)S(1)}, u32[]{:S(2)}, u32[]{:S(2)}) collective-permute-start(bf16[288,512]{1,0:T(8,128)(2,1)} %get-tuple-element.120), channel_id=1, source_target_pairs={{0,24},{4,28},{8,16},{12,20},{16,8},{20,12},{24,0},{28,4},{1,25},{... | collective-permute-start | bytes 884744 | tf_op jit(solution)/shard_map/ppermute | solution.py:308
  14.6 15.2 %collective-permute-start = (bf16[288,512]{1,0:T(8,128)(2,1)}, bf16[288,512]{1,0:T(8,128)(2,1)S(1)}, u32[]{:S(2)}, u32[]{:S(2)}) collective-permute-start(bf16[288,512]{1,0:T(8,128)(2,1)} %get-tuple-element.120), channel_id=1, source_target_pairs={{0,4},{4,0},{8,12},{12,8},{16,20},{20,16},{24,28},{28,24},{1,5},{5... | collective-permute-start | bytes 884744 | tf_op jit(solution)/shard_map/ppermute | solution.py:308
  16.3 20.8 %collective-permute-start.7 = (bf16[3,112,512]{2,1,0:T(8,128)(2,1)}, bf16[3,112,512]{2,1,0:T(8,128)(2,1)S(1)}, u32[]{:S(2)}, u32[]{:S(2)}) collective-permute-start(bf16[3,112,512]{2,1,0:T(8,128)(2,1)} %slice_bitcast_fusion.1), channel_id=1, source_target_pairs={{0,3},{1,0},{2,1},{3,2},{4,7},{5,4},{6,5},{7,6},{8,11},{9,8},{10,9... | collective-permute-start | bytes 1032200 | tf_op jit(solution)/shard_map/ppermute | solution.py:40
  21.2 8.6 %collective-permute-start.2 = (bf16[288,512]{1,0:T(8,128)(2,1)S(1)}, bf16[288,512]{1,0:T(8,128)(2,1)S(1)}, u32[]{:S(2)}, u32[]{:S(2)}) collective-permute-start(bf16[288,512]{1,0:T(8,128)(2,1)S(1)} %collective-permute-done.1), channel_id=1, source_target_pairs={{0,4},{4,0},{8,12},{12,8},{16,20},{20,16},{24,28},{28,24},{1,5},{5... | collective-permute-start | bytes 884744 | tf_op jit(solution)/shard_map/ppermute | solution.py:308
  30.0 22.2 %collective-permute-start.9 = (bf16[256,512]{1,0:T(8,128)(2,1)}, bf16[256,512]{1,0:T(8,128)(2,1)S(1)}, u32[]{:S(2)}, u32[]{:S(2)}) collective-permute-start(bf16[256,512]{1,0:T(8,128)(2,1)} %get-tuple-element.133), channel_id=1, source_target_pairs={{0,4},{4,0},{8,12},{12,8},{16,20},{20,16},{24,28},{28,24},{1,5},{5... | collective-permute-start | bytes 786440 | tf_op jit(solution)/shard_map/ppermute | solution.py:308
  30.2 21.4 %collective-permute-start.10 = (bf16[256,512]{1,0:T(8,128)(2,1)}, bf16[256,512]{1,0:T(8,128)(2,1)S(1)}, u32[]{:S(2)}, u32[]{:S(2)}) collective-permute-start(bf16[256,512]{1,0:T(8,128)(2,1)} %get-tuple-element.133), channel_id=1, source_target_pairs={{0,8},{4,12},{8,0},{12,4},{16,24},{20,28},{24,16},{28,20},{1,9},{5... | collective-permute-start | bytes 786440 | tf_op jit(solution)/shard_map/ppermute | solution.py:308
  31.1 20.5 %collective-permute-start.12 = (bf16[256,512]{1,0:T(8,128)(2,1)}, bf16[256,512]{1,0:T(8,128)(2,1)S(1)}, u32[]{:S(2)}, u32[]{:S(2)}) collective-permute-start(bf16[256,512]{1,0:T(8,128)(2,1)} %get-tuple-element.133), channel_id=1, source_target_pairs={{0,16},{4,20},{8,24},{12,28},{16,0},{20,4},{24,8},{28,12},{1,17},{... | collective-permute-start | bytes 786440 | tf_op jit(solution)/shard_map/ppermute | solution.py:308
  32.3 19.8 %collective-permute-start.14 = (bf16[256,512]{1,0:T(8,128)(2,1)}, bf16[256,512]{1,0:T(8,128)(2,1)S(1)}, u32[]{:S(2)}, u32[]{:S(2)}) collective-permute-start(bf16[256,512]{1,0:T(8,128)(2,1)} %get-tuple-element.133), channel_id=1, source_target_pairs={{0,24},{4,28},{8,16},{12,20},{16,8},{20,12},{24,0},{28,4},{1,25},{... | collective-permute-start | bytes 786440 | tf_op jit(solution)/shard_map/ppermute | solution.py:308
  37.1 18.3 %collective-permute-start.8 = (bf16[3,112,512]{2,1,0:T(8,128)(2,1)S(1)}, bf16[3,112,512]{2,1,0:T(8,128)(2,1)S(1)}, u32[]{:S(2)}, u32[]{:S(2)}) collective-permute-start(bf16[3,112,512]{2,1,0:T(8,128)(2,1)S(1)} %slice_bitcast_fusion), channel_id=1, source_target_pairs={{0,3},{1,0},{2,1},{3,2},{4,7},{5,4},{6,5},{7,6},{8,11},{9,8},{10,9... | collective-permute-start | bytes 1032200 | tf_op jit(solution)/shard_map/ppermute | solution.py:40
  82.4 7.3 %collective-permute-start.21 = (bf16[4,352,512]{2,1,0:T(8,128)(2,1)S(1)}, bf16[4,352,512]{2,1,0:T(8,128)(2,1)S(1)}, u32[]{:S(2)}, u32[]{:S(2)}) collective-permute-start(bf16[4,352,512]{2,1,0:T(8,128)(2,1)S(1)} %get-tuple-element.150), channel_id=1, source_target_pairs={{0,4},{4,0},{8,12},{12,8},{16,20},{20,16},{24,28},{28,24},{1,5},{5... | collective-permute-start | bytes 4325384 | tf_op jit(solution)/shard_map/ppermute | solution.py:308
  83.1 9.9 %collective-permute-start.18 = (bf16[288,512]{1,0:T(8,128)(2,1)S(1)}, bf16[288,512]{1,0:T(8,128)(2,1)S(1)}, u32[]{:S(2)}, u32[]{:S(2)}) collective-permute-start(bf16[288,512]{1,0:T(8,128)(2,1)S(1)} %get-tuple-element.143), channel_id=1, source_target_pairs={{0,8},{4,12},{8,0},{12,4},{16,24},{20,28},{24,16},{28,20},{1,9},{5... | collective-permute-start | bytes 884744 | tf_op jit(solution)/shard_map/ppermute | solution.py:308
  84.1 13.8 %collective-permute-start.19 = (bf16[288,512]{1,0:T(8,128)(2,1)S(1)}, bf16[288,512]{1,0:T(8,128)(2,1)S(1)}, u32[]{:S(2)}, u32[]{:S(2)}) collective-permute-start(bf16[288,512]{1,0:T(8,128)(2,1)S(1)} %get-tuple-element.144), channel_id=1, source_target_pairs={{0,16},{4,20},{8,24},{12,28},{16,0},{20,4},{24,8},{28,12},{1,17},{... | collective-permute-start | bytes 884744 | tf_op jit(solution)/shard_map/ppermute | solution.py:308
  85.3 14.4 %collective-permute-start.20 = (bf16[288,512]{1,0:T(8,128)(2,1)S(1)}, bf16[288,512]{1,0:T(8,128)(2,1)S(1)}, u32[]{:S(2)}, u32[]{:S(2)}) collective-permute-start(bf16[288,512]{1,0:T(8,128)(2,1)S(1)} %get-tuple-element.145), channel_id=1, source_target_pairs={{0,24},{4,28},{8,16},{12,20},{16,8},{20,12},{24,0},{28,4},{1,25},{... | collective-permute-start | bytes 884744 | tf_op jit(solution)/shard_map/ppermute | solution.py:308
  86.7 16.8 %collective-permute-start.16 = (bf16[336,512]{1,0:T(8,128)(2,1)S(1)}, bf16[336,512]{1,0:T(8,128)(2,1)S(1)}, u32[]{:S(2)}, u32[]{:S(2)}) collective-permute-start(bf16[336,512]{1,0:T(8,128)(2,1)S(1)} %get-tuple-element.134), channel_id=1, source_target_pairs={{0,1},{1,2},{2,3},{3,0},{4,5},{5,6},{6,7},{7,4},{8,9},{9,10},{10,1... | collective-permute-start | bytes 1032200 | tf_op jit(solution)/shard_map/ppermute | solution.py:40
  99.9 8.8 %collective-permute-start.25 = (bf16[144,512]{1,0:T(8,128)(2,1)S(1)}, bf16[144,512]{1,0:T(8,128)(2,1)S(1)}, u32[]{:S(2)}, u32[]{:S(2)}) collective-permute-start(bf16[144,512]{1,0:T(8,128)(2,1)S(1)} %get-tuple-element.168), channel_id=1, source_target_pairs={{0,1},{1,0},{2,3},{3,2},{4,5},{5,4},{6,7},{7,6},{8,9},{9,8},{10,11... | collective-permute-start | bytes 442376 | tf_op jit(solution)/shard_map/ppermute | solution.py:308
  100.0 11.4 %collective-permute-start.22 = (bf16[352,512]{1,0:T(8,128)(2,1)S(1)}, bf16[352,512]{1,0:T(8,128)(2,1)S(1)}, u32[]{:S(2)}, u32[]{:S(2)}) collective-permute-start(bf16[352,512]{1,0:T(8,128)(2,1)S(1)} %get-tuple-element.163), channel_id=1, source_target_pairs={{0,8},{4,12},{8,0},{12,4},{16,24},{20,28},{24,16},{28,20},{1,9},{5... | collective-permute-start | bytes 1081352 | tf_op jit(solution)/shard_map/ppermute | solution.py:308
  100.6 16.8 %collective-permute-start.23 = (bf16[352,512]{1,0:T(8,128)(2,1)S(1)}, bf16[352,512]{1,0:T(8,128)(2,1)S(1)}, u32[]{:S(2)}, u32[]{:S(2)}) collective-permute-start(bf16[352,512]{1,0:T(8,128)(2,1)S(1)} %get-tuple-element.164), channel_id=1, source_target_pairs={{0,16},{4,20},{8,24},{12,28},{16,0},{20,4},{24,8},{28,12},{1,17},{... | collective-permute-start | bytes 1081352 | tf_op jit(solution)/shard_map/ppermute | solution.py:308
  102.4 15.1 %collective-permute-start.24 = (bf16[352,512]{1,0:T(8,128)(2,1)S(1)}, bf16[352,512]{1,0:T(8,128)(2,1)S(1)}, u32[]{:S(2)}, u32[]{:S(2)}) collective-permute-start(bf16[352,512]{1,0:T(8,128)(2,1)S(1)} %get-tuple-element.165), channel_id=1, source_target_pairs={{0,24},{4,28},{8,16},{12,20},{16,8},{20,12},{24,0},{28,4},{1,25},{... | collective-permute-start | bytes 1081352 | tf_op jit(solution)/shard_map/ppermute | solution.py:308
  108.8 9.0 %collective-permute-start.26 = (bf16[4,224,512]{2,1,0:T(8,128)(2,1)S(1)}, bf16[4,224,512]{2,1,0:T(8,128)(2,1)S(1)}, u32[]{:S(2)}, u32[]{:S(2)}) collective-permute-start(bf16[4,224,512]{2,1,0:T(8,128)(2,1)S(1)} %get-tuple-element.171), channel_id=1, source_target_pairs={{0,4},{4,0},{8,12},{12,8},{16,20},{20,16},{24,28},{28,24},{1,5},{5... | collective-permute-start | bytes 2752520 | tf_op jit(solution)/shard_map/ppermute | solution.py:308
  108.8 10.3 %collective-permute-start.27 = (bf16[144,512]{1,0:T(8,128)(2,1)S(1)}, bf16[144,512]{1,0:T(8,128)(2,1)S(1)}, u32[]{:S(2)}, u32[]{:S(2)}) collective-permute-start(bf16[144,512]{1,0:T(8,128)(2,1)S(1)} %add_convert_fusion.12), channel_id=1, source_target_pairs={{0,2},{1,3},{2,0},{3,1},{4,6},{5,7},{6,4},{7,5},{8,10},{9,11},{10,... | collective-permute-start | bytes 442376 | tf_op jit(solution)/shard_map/ppermute | solution.py:308
  119.7 8.5 %collective-permute-start.29 = (bf16[224,512]{1,0:T(8,128)(2,1)S(1)}, bf16[224,512]{1,0:T(8,128)(2,1)S(1)}, u32[]{:S(2)}, u32[]{:S(2)}) collective-permute-start(bf16[224,512]{1,0:T(8,128)(2,1)S(1)} %get-tuple-element.179), channel_id=1, source_target_pairs={{0,8},{4,12},{8,0},{12,4},{16,24},{20,28},{24,16},{28,20},{1,9},{5... | collective-permute-start | bytes 688136 | tf_op jit(solution)/shard_map/ppermute | solution.py:308
  121.3 11.1 %collective-permute-start.30 = (bf16[224,512]{1,0:T(8,128)(2,1)S(1)}, bf16[224,512]{1,0:T(8,128)(2,1)S(1)}, u32[]{:S(2)}, u32[]{:S(2)}) collective-permute-start(bf16[224,512]{1,0:T(8,128)(2,1)S(1)} %get-tuple-element.180), channel_id=1, source_target_pairs={{0,16},{4,20},{8,24},{12,28},{16,0},{20,4},{24,8},{28,12},{1,17},{... | collective-permute-start | bytes 688136 | tf_op jit(solution)/shard_map/ppermute | solution.py:308
  121.7 10.8 %collective-permute-start.31 = (bf16[224,512]{1,0:T(8,128)(2,1)S(1)}, bf16[224,512]{1,0:T(8,128)(2,1)S(1)}, u32[]{:S(2)}, u32[]{:S(2)}) collective-permute-start(bf16[224,512]{1,0:T(8,128)(2,1)S(1)} %get-tuple-element.181), channel_id=1, source_target_pairs={{0,24},{4,28},{8,16},{12,20},{16,8},{20,12},{24,0},{28,4},{1,25},{... | collective-permute-start | bytes 688136 | tf_op jit(solution)/shard_map/ppermute | solution.py:308
  125.3 20.5 %collective-permute-start.33 = (bf16[336,512]{1,0:T(8,128)(2,1)S(1)}, bf16[336,512]{1,0:T(8,128)(2,1)S(1)}, u32[]{:S(2)}, u32[]{:S(2)}) collective-permute-start(bf16[336,512]{1,0:T(8,128)(2,1)S(1)} %get-tuple-element.187), channel_id=1, source_target_pairs={{0,1},{1,2},{2,3},{3,0},{4,5},{5,6},{6,7},{7,4},{8,9},{9,10},{10,1... | collective-permute-start | bytes 1032200 | tf_op jit(solution)/shard_map/ppermute | solution.py:40
  132.6 8.8 %collective-permute-start.32 = (bf16[112,512]{1,0:T(8,128)(2,1)S(1)}, bf16[112,512]{1,0:T(8,128)(2,1)S(1)}, u32[]{:S(2)}, u32[]{:S(2)}) collective-permute-start(bf16[112,512]{1,0:T(8,128)(2,1)S(1)} %get-tuple-element.186), channel_id=1, source_target_pairs={{0,1},{1,0},{2,3},{3,2},{4,5},{5,4},{6,7},{7,6},{8,9},{9,8},{10,11... | collective-permute-start | bytes 344072 | tf_op jit(solution)/shard_map/ppermute | solution.py:308
  135.7 17.0 %collective-permute-start.36 = (bf16[144,512]{1,0:T(8,128)(2,1)S(1)}, bf16[144,512]{1,0:T(8,128)(2,1)S(1)}, u32[]{:S(2)}, u32[]{:S(2)}) collective-permute-start(bf16[144,512]{1,0:T(8,128)(2,1)S(1)} %add_convert_fusion.11.half), channel_id=1, source_target_pairs={{0,1},{1,0},{2,3},{3,2},{4,5},{5,4},{6,7},{7,6},{8,9},{9,8},{10,11... | collective-permute-start | bytes 442376 | tf_op jit(solution)/shard_map/ppermute | solution.py:308
  136.0 9.9 %collective-permute-start.34 = (bf16[176,512]{1,0:T(8,128)(2,1)S(1)}, bf16[176,512]{1,0:T(8,128)(2,1)S(1)}, u32[]{:S(2)}, u32[]{:S(2)}) collective-permute-start(bf16[176,512]{1,0:T(8,128)(2,1)S(1)} %add_convert_fusion.10), channel_id=1, source_target_pairs={{0,2},{1,3},{2,0},{3,1},{4,6},{5,7},{6,4},{7,5},{8,10},{9,11},{10,... | collective-permute-start | bytes 540680 | tf_op jit(solution)/shard_map/ppermute | solution.py:308
  145.8 6.7 %collective-permute-start.35 = (bf16[112,512]{1,0:T(8,128)(2,1)S(1)}, bf16[112,512]{1,0:T(8,128)(2,1)S(1)}, u32[]{:S(2)}, u32[]{:S(2)}) collective-permute-start(bf16[112,512]{1,0:T(8,128)(2,1)S(1)} %add_convert_fusion.14), channel_id=1, source_target_pairs={{0,2},{1,3},{2,0},{3,1},{4,6},{5,7},{6,4},{7,5},{8,10},{9,11},{10,... | collective-permute-start | bytes 344072 | tf_op jit(solution)/shard_map/ppermute | solution.py:308
  152.7 6.7 %collective-permute-start.38 = (bf16[112,512]{1,0:T(8,128)(2,1)S(1)}, bf16[112,512]{1,0:T(8,128)(2,1)S(1)}, u32[]{:S(2)}, u32[]{:S(2)}) collective-permute-start(bf16[112,512]{1,0:T(8,128)(2,1)S(1)} %add_convert_fusion.13.half), channel_id=1, source_target_pairs={{0,1},{1,0},{2,3},{3,2},{4,5},{5,4},{6,7},{7,6},{8,9},{9,8},{10,11... | collective-permute-start | bytes 344072 | tf_op jit(solution)/shard_map/ppermute | solution.py:308
  (43 other events, 214.3 us)
Sparse Core Ops, SparseCore 0:
  20.5 32.9 all-gather.2

commit v5 on v4

--- a/solution.py
+++ b/solution.py
@@ -889,20 +889,11 @@
     (half_a,), (near_b, tok_sent) = tie([half_a], [near_b, tok_sent])
     tok_halo = shifted_2(tok_sent, "seq", 1)
     half_b = add_pair(keep_b, near_b)
+    far_b = exchange(half_b, "seq", 2)
+    attn_parts, (far_b,) = tie(attn_parts, [far_b])
+    half_b = seq_rest(add_pair(half_b, far_b))
     (half_b,), attn_parts = tie([half_b], attn_parts)
-    far_b = exchange(half_b, "seq", 2)
     keep, send = add_chips(attn_same, attn_came, attn_parts)
-    near = exchange(send, "seq", 1)
-    back_a = exchange(half_a, "seq", 1)
-    half = add_pair(keep, near)
-    (half, tok_halo), (far_b,) = tie([half, tok_halo], [far_b])
-    far = exchange(half, "seq", 2)
-    half_b = seq_rest(add_pair(half_b, far_b))
-    (half_b,), (far,) = tie([half_b], [far])
-    back_b = exchange(half_b, "seq", 1)
-    half = seq_rest(add_pair(half, far))
-    (half,), (back_a,) = tie([half], [back_a])
-    back = exchange(half, "seq", 1)
     def unpack(body, params, half, back):
         return kernel_call(
             body,
@@ -915,18 +906,27 @@
                 apart=2,
         )
 
+    def joined(halo, kept):
+        return jnp.concatenate([halo.astype(F32), kept], 0).reshape(tokens.shape)
+
+    near = exchange(send, "seq", 1)
+    back_b = exchange(half_b, "seq", 1)
+    half = add_pair(keep, near)
+    far = exchange(half, "seq", 2)
+    back_a = exchange(half_a, "seq", 1)
+    half = seq_rest(add_pair(half, far))
+    back = exchange(half, "seq", 1)
     in_grads = unpack(unpack_in_body, (w_in, bin_rows), half_a, back_a)
-    in_grads, (back_b,) = tie(in_grads, [back_b])
     column = gain_two[None]
     out_grads = unpack(unpack_out_body, (w_out, w_proj, *[column] * 4), half_b, back_b)
-    out_grads, (back,) = tie(out_grads, [back])
+    grad_tokens = joined(tok_halo, tok_kept)
+    output = joined(out_halo, out_kept)
+    early, (back,) = tie([*in_grads, *out_grads, grad_tokens, output], [back])
+    in_grads, out_grads, (grad_tokens, output) = early[:2], early[2:8], early[8:]
     attn_grads = unpack(unpack_attn_body, attn_params, half, back)
     g_wout, g_wproj, g_gain, g_offset, g_bout, g_bproj = out_grads
     summed = [*attn_grads[:4], attn_grads[4].T, g_wproj, g_bproj, g_gain, g_offset]
     summed += [*in_grads, g_wout, g_bout]
-
-    def joined(halo, kept):
-        return jnp.concatenate([halo.astype(F32), kept], 0).reshape(tokens.shape)
 
     targets = (
         gain_one,
@@ -944,7 +944,7 @@
         bias_out,
     )
     grads = [g.reshape(p.shape) for g, p in zip(summed, targets)]
-    return (joined(out_halo, out_kept), joined(tok_halo, tok_kept), *grads)
+    return (output, grad_tokens, *grads)
 
 
 def solution(mesh):

time: 168 us -> 169 us (level)
  waiting for transfers between devices: 47.3 us -> 49 us
    ppermute x35, waiting for transfers between devices: 47.3 us -> 49 us  [exchange(): return lax.ppermute(value, axis, [(i, i ^ mask) for i in range(peers)])]
  transfers between devices with their start and end apart: 40 -> 40, of which waited for: 18 -> 19; matrix products, arithmetic and copies ran while one was open for 6% -> 6% of each run, Pallas kernels for 17% -> 17%
where the time goes in v5:
time: 169 us
  waiting for transfers between devices  49 us (29%)
  Pallas kernels  47.4 us (28%)
  starting transfers between devices  37.5 us (22%)
  local copies, waits for them, and re-layouts  16.5 us (10%)
  between operations  14.8 us (9%)
  other arithmetic  3.72 us (2%)
    ppermute x35, waiting for transfers between devices, exchange(): return lax.ppermute(value, axis, [(i, i ^ mask) for i in range(peers)])  49 us
    pallas_call x14, Pallas kernels, kernel_call(): pl.pallas_call(body, out_shape=tuple(outs), in_specs=in_specs, out_specs=...  47.4 us
    ppermute x35, starting transfers between devices, exchange(): return lax.ppermute(value, axis, [(i, i ^ mask) for i in range(peers)])  29.6 us
    unnamed x84, local copies, waits for them, and re-layouts  13.1 us
    ppermute x4, starting transfers between devices, shifted_2(): lax.ppermute(value, axis, [(i, (i + by) % peers) for i in range(peers)])  7.79 us
  transfers between devices with their start and end apart: 40, of which 19 were waited for; matrix products, arithmetic and copies ran while one was open for 6% of the time, Pallas kernels for 17%

profile of v5, /device:TPU:0, one launch (start us, length us, event | category | flops | bytes accessed | tf_op | source)
XLA Modules:
  0.0 168.9 jit_solution(17348022217261518180)
XLA Ops:
  7.2 2.9 %shard_map.271 = (bf16[288,512]{1,0:T(8,128)(2,1)}, bf16[288,512]{1,0:T(8,128)(2,1)}, bf16[256,512]{1,0:T(8,128)(2,1)}) custom-call(bf16[1,64]{1,0:T(2,128)(2,1)} %bitcast.87, bf16[1,64]{1,0:T(2,128)(2,1)} %bitcast.88, bf16[64,1536]{1,0:T(8,128)(2,1)} %wqkv.1, bf16[2,64]{1,0:T(2,128)(2,1)} %bqv.1, bf16[2,169]{1,0:T(2,128)(2,1)} %bitcast.86, ...), custom_call_target="tpu_custom_call" | custom-call | flops 1024 | bytes 1024 | tf_op jit(solution)/shard_map/pallas_call | solution.py:150
  10.1 2.9 %collective-permute-start.1 = (bf16[288,512]{1,0:T(8,128)(2,1)}, bf16[288,512]{1,0:T(8,128)(2,1)S(1)}, u32[]{:S(2)}, u32[]{:S(2)}) collective-permute-start(bf16[288,512]{1,0:T(8,128)(2,1)} %get-tuple-element.118), channel_id=1, source_target_pairs={{0,8},{4,12},{8,0},{12,4},{16,24},{20,28},{24,16},{28,20},{1,9},{5... | collective-permute-start | bytes 884744 | tf_op jit(solution)/shard_map/ppermute | solution.py:308
  13.0 1.5 collective-permute-start.3
  14.6 1.7 %slice_bitcast_fusion.1 = bf16[3,112,512]{2,1,0:T(8,128)(2,1)} fusion(bf16[1,7,112,512]{3,2,1,0:T(8,128)(2,1)} %param.16), kind=kLoop, calls=%fused_computation.17 | loop fusion | bytes 688128 | tf_op jit(solution)/shard_map/slice | solution.py:771
  16.3 4.1 %collective-permute-start.7 = (bf16[3,112,512]{2,1,0:T(8,128)(2,1)}, bf16[3,112,512]{2,1,0:T(8,128)(2,1)S(1)}, u32[]{:S(2)}, u32[]{:S(2)}) collective-permute-start(bf16[3,112,512]{2,1,0:T(8,128)(2,1)} %slice_bitcast_fusion.1), channel_id=1, source_target_pairs={{0,3},{1,0},{2,1},{3,2},{4,7},{5,4},{6,5},{7,6},{8,11},{9,8},{10,9... | collective-permute-start | bytes 1032200 | tf_op jit(solution)/shard_map/ppermute | solution.py:40
  21.2 6.9 %collective-permute-done.3 = bf16[288,512]{1,0:T(8,128)(2,1)S(1)} collective-permute-done((bf16[288,512]{1,0:T(8,128)(2,1)}, bf16[288,512]{1,0:T(8,128)(2,1)S(1)}, u32[]{:S(2)}, u32[]{:S(2)}) %collective-permute-start.3) | collective-permute-done | bytes 294944 | tf_op jit(solution)/shard_map/ppermute | solution.py:308
  37.1 3.7 %collective-permute-start.8 = (bf16[3,112,512]{2,1,0:T(8,128)(2,1)S(1)}, bf16[3,112,512]{2,1,0:T(8,128)(2,1)S(1)}, u32[]{:S(2)}, u32[]{:S(2)}) collective-permute-start(bf16[3,112,512]{2,1,0:T(8,128)(2,1)S(1)} %slice_bitcast_fusion), channel_id=1, source_target_pairs={{0,3},{1,0},{2,1},{3,2},{4,7},{5,4},{6,5},{7,6},{8,11},{9,8},{10,9... | collective-permute-start | bytes 1032200 | tf_op jit(solution)/shard_map/ppermute | solution.py:40
  40.8 2.4 %shard_map.272 = (bf16[896,512]{1,0:T(8,128)(2,1)S(1)}, bf16[896,512]{1,0:T(8,128)(2,1)S(1)}, bf16[896,512]{1,0:T(8,128)(2,1)S(1)}, bf16[896,512]{1,0:T(8,128)(2,1)S(1)}) custom-call(bf16[7,112,512]{2,1,0:T(8,128)(2,1)S(1)} %bitcast.78, bf16[3,112,512]{2,1,0:T(8,128)(2,1)S(1)} %collective-permute-done.7.halo, ...), custom_call_target="tpu_custom_call" | custom-call | flops 1024 | bytes 1024 | tf_op jit(solution)/shard_map/pallas_call | solution.py:150
  43.4 7.1 %shard_map.273 = (bf16[8,4,112,256]{3,2,1,0:T(8,128)(2,1)S(1)}, bf16[784,512]{1,0:T(8,128)(2,1)S(1)}, f32[784,512]{1,0:T(8,128)S(1)}) custom-call(bf16[8,288,512]{2,1,0:T(8,128)(2,1)S(1)} %bitcast_dynamic-update-slice_fusion.slab.attn_slab, f32[16,56,128]{2,1,0:T(8,128)S(1)} %broadcast_in_dim.35.reg_rows, f32[16,1,256]{2,1,0:T(1,128)S(1)} %tile.9.reg_lanes, ...), custom_call_target="tpu_custom_call" | custom-call | flops 1024 | bytes 1024 | tf_op jit(solution)/shard_map/pallas_call | solution.py:150
  57.6 1.6 copy-done.13
  59.2 1.7 copy-done.14
  63.0 13.7 %shard_map.274 = (f32[448,512]{1,0:T(8,128)S(1)}, bf16[336,512]{1,0:T(8,128)(2,1)S(1)}, bf16[784,512]{1,0:T(8,128)(2,1)S(1)}, bf16[784,2048]{1,0:T(8,128)(2,1)S(...) custom-call(f32[784,512]{1,0:T(8,128)S(1)} %copy-done.11, ...), custom_call_target="tpu_custom_call" | custom-call | flops 1024 | bytes 1024 | tf_op jit(solution)/shard_map/pallas_call | solution.py:150
  76.9 5.5 %shard_map.275 = (f32[784,512]{1,0:T(8,128)S(1)}, bf16[896,512]{1,0:T(8,128)(2,1)S(1)}, bf16[4,352,512]{2,1,0:T(8,128)(2,1)S(1)}, bf16[4,352,512]{2,1,0:T(8,128)(2,1)S(1)}) custom-call(f32[784,512]{1,0:T(8,128)S(1)} %copy-done.11, bf16[784,512]{1,0:T(8,128)(2,1)S(1)} %get-tuple-element.134.cot, bf16[784,2048]{1,0:T(8,128)(2,1)S(1)} %get-tuple-element.135.actives, ...), custom_call_target="tpu_custom_call" | custom-call | flops 1024 | bytes 1024 | tf_op jit(solution)/shard_map/pallas_call | solution.py:150
  86.7 3.0 %shard_map.277 = (bf16[448,1536]{1,0:T(8,128)(2,1)S(1)}, f32[4,56,256]{2,1,0:T(8,128)S(1)}) custom-call(bf16[896,512]{1,0:T(8,128)(2,1)S(1)} %copy-done.3, bf16[896,512]{1,0:T(8,128)(2,1)S(1)} %copy-done.5, bf16[896,512]{1,0:T(8,128)(2,1)S(1)} %copy-done.7, bf16[8,4,112,256]{3,2,1,0:T(8,128)(2,1)S(1)} %copy-done.9, ...), custom_call_target="tpu_custom_call" | custom-call | flops 1024 | bytes 1024 | tf_op jit(solution)/shard_map/pallas_call | solution.py:150
  90.1 3.0 %shard_map.278 = (bf16[448,1536]{1,0:T(8,128)(2,1)S(1)}, f32[4,56,256]{2,1,0:T(8,128)S(1)}) custom-call(bf16[896,512]{1,0:T(8,128)(2,1)S(1)} %copy-done.3, bf16[896,512]{1,0:T(8,128)(2,1)S(1)} %copy-done.5, bf16[896,512]{1,0:T(8,128)(2,1)S(1)} %copy-done.7, bf16[8,4,112,256]{3,2,1,0:T(8,128)(2,1)S(1)} %copy-done.9, ...), custom_call_target="tpu_custom_call" | custom-call | flops 1024 | bytes 1024 | tf_op jit(solution)/shard_map/pallas_call | solution.py:150
  93.1 4.9 %collective-permute-done.18.refs_1_ = bf16[288,512]{1,0:T(8,128)(2,1)S(1)} collective-permute-done((bf16[288,512]{1,0:T(8,128)(2,1)S(1)}, bf16[288,512]{1,0:T(8,128)(2,1)S(1)}, u32[]{:S(2)}, u32[]{:S(2)}) %collective-permute-start.18) | collective-permute-done | bytes 294944 | tf_op jit(solution)/shard_map/ppermute | solution.py:308
  97.9 1.8 %collective-permute-done.19.refs_2_ = bf16[288,512]{1,0:T(8,128)(2,1)S(1)} collective-permute-done((bf16[288,512]{1,0:T(8,128)(2,1)S(1)}, bf16[288,512]{1,0:T(8,128)(2,1)S(1)}, u32[]{:S(2)}, u32[]{:S(2)}) %collective-permute-start.19) | collective-permute-done | bytes 294944 | tf_op jit(solution)/shard_map/ppermute | solution.py:308
  100.6 1.7 %collective-permute-start.24 = (bf16[352,512]{1,0:T(8,128)(2,1)S(1)}, bf16[352,512]{1,0:T(8,128)(2,1)S(1)}, u32[]{:S(2)}, u32[]{:S(2)}) collective-permute-start(bf16[352,512]{1,0:T(8,128)(2,1)S(1)} %get-tuple-element.165), channel_id=1, source_target_pairs={{0,16},{4,20},{8,24},{12,28},{16,0},{20,4},{24,8},{28,12},{1,17},{... | collective-permute-start | bytes 1081352 | tf_op jit(solution)/shard_map/ppermute | solution.py:308
  103.5 5.1 %shard_map.279 = (f32[448,512]{1,0:T(8,128)S(1)}, bf16[336,512]{1,0:T(8,128)(2,1)S(1)}, bf16[4,224,512]{2,1,0:T(8,128)(2,1)S(1)}, bf16[4,224,512]{2,1,0:T(8,128)(2,1)S(1)}) custom-call(f32[784,512]{1,0:T(8,128)S(1)} %get-tuple-element.153.grad_mixed, bf16[7,112,512]{2,1,0:T(8,128)(2,1)S(1)} %bitcast.80, ...), custom_call_target="tpu_custom_call" | custom-call | flops 1024 | bytes 1024 | tf_op jit(solution)/shard_map/pallas_call | solution.py:150
  108.8 2.3 %collective-permute-start.27 = (bf16[144,512]{1,0:T(8,128)(2,1)S(1)}, bf16[144,512]{1,0:T(8,128)(2,1)S(1)}, u32[]{:S(2)}, u32[]{:S(2)}) collective-permute-start(bf16[144,512]{1,0:T(8,128)(2,1)S(1)} %add_convert_fusion.12), channel_id=1, source_target_pairs={{0,2},{1,3},{2,0},{3,1},{4,6},{5,7},{6,4},{7,5},{8,10},{9,11},{10,... | collective-permute-start | bytes 442376 | tf_op jit(solution)/shard_map/ppermute | solution.py:308
  111.4 6.1 %collective-permute-done.24.refs_1_ = bf16[352,512]{1,0:T(8,128)(2,1)S(1)} collective-permute-done((bf16[352,512]{1,0:T(8,128)(2,1)S(1)}, bf16[352,512]{1,0:T(8,128)(2,1)S(1)}, u32[]{:S(2)}, u32[]{:S(2)}) %collective-permute-start.24) | collective-permute-done | bytes 360480 | tf_op jit(solution)/shard_map/ppermute | solution.py:308
  119.7 1.6 collective-permute-start.30
  121.6 1.5 collective-permute-start.32
  123.2 2.0 %collective-permute-done.28 = bf16[176,512]{1,0:T(8,128)(2,1)S(1)} collective-permute-done((bf16[176,512]{1,0:T(8,128)(2,1)S(1)}, bf16[176,512]{1,0:T(8,128)(2,1)S(1)}, u32[]{:S(2)}, u32[]{:S(2)}) %collective-permute-start.28) | collective-permute-done | bytes 180256 | tf_op jit(solution)/shard_map/ppermute | solution.py:308
  126.6 1.6 collective-permute-done.30.refs_0_
  128.2 4.2 %collective-permute-done.31.refs_1_ = bf16[224,512]{1,0:T(8,128)(2,1)S(1)} collective-permute-done((bf16[224,512]{1,0:T(8,128)(2,1)S(1)}, bf16[224,512]{1,0:T(8,128)(2,1)S(1)}, u32[]{:S(2)}, u32[]{:S(2)}) %collective-permute-start.31) | collective-permute-done | bytes 229408 | tf_op jit(solution)/shard_map/ppermute | solution.py:308
  132.4 2.3 %collective-permute-done.33 = bf16[176,512]{1,0:T(8,128)(2,1)S(1)} collective-permute-done((bf16[176,512]{1,0:T(8,128)(2,1)S(1)}, bf16[176,512]{1,0:T(8,128)(2,1)S(1)}, u32[]{:S(2)}, u32[]{:S(2)}) %collective-permute-start.33) | collective-permute-done | bytes 180256 | tf_op jit(solution)/shard_map/ppermute | solution.py:308
  135.0 2.1 %collective-permute-start.29 = (bf16[144,512]{1,0:T(8,128)(2,1)S(1)}, bf16[144,512]{1,0:T(8,128)(2,1)S(1)}, u32[]{:S(2)}, u32[]{:S(2)}) collective-permute-start(bf16[144,512]{1,0:T(8,128)(2,1)S(1)} %add_convert_fusion.11.half), channel_id=1, source_target_pairs={{0,1},{1,0},{2,3},{3,2},{4,5},{5,4},{6,7},{7,6},{8,9},{9,8},{10,11... | collective-permute-start | bytes 442376 | tf_op jit(solution)/shard_map/ppermute | solution.py:308
  137.2 3.7 %collective-permute-done.36 = bf16[112,512]{1,0:T(8,128)(2,1)S(1)} collective-permute-done((bf16[112,512]{1,0:T(8,128)(2,1)S(1)}, bf16[112,512]{1,0:T(8,128)(2,1)S(1)}, u32[]{:S(2)}, u32[]{:S(2)}) %collective-permute-start.36) | collective-permute-done | bytes 114720 | tf_op jit(solution)/shard_map/ppermute | solution.py:308
  142.6 9.6 %collective-permute-done.29.back = bf16[144,512]{1,0:T(8,128)(2,1)S(1)} collective-permute-done((bf16[144,512]{1,0:T(8,128)(2,1)S(1)}, bf16[144,512]{1,0:T(8,128)(2,1)S(1)}, u32[]{:S(2)}, u32[]{:S(2)}) %collective-permute-start.29) | collective-permute-done | bytes 147488 | tf_op jit(solution)/shard_map/ppermute | solution.py:308
  153.9 2.0 %collective-permute-start.38 = (bf16[112,512]{1,0:T(8,128)(2,1)S(1)}, bf16[112,512]{1,0:T(8,128)(2,1)S(1)}, u32[]{:S(2)}, u32[]{:S(2)}) collective-permute-start(bf16[112,512]{1,0:T(8,128)(2,1)S(1)} %add_convert_fusion.13.half), channel_id=1, source_target_pairs={{0,1},{1,0},{2,3},{3,2},{4,5},{5,4},{6,7},{7,6},{8,9},{9,8},{10,11... | collective-permute-start | bytes 344072 | tf_op jit(solution)/shard_map/ppermute | solution.py:308
  157.1 2.0 %collective-permute-done.34.back = bf16[176,512]{1,0:T(8,128)(2,1)S(1)} collective-permute-done((bf16[176,512]{1,0:T(8,128)(2,1)S(1)}, bf16[176,512]{1,0:T(8,128)(2,1)S(1)}, u32[]{:S(2)}, u32[]{:S(2)}) %collective-permute-start.34) | collective-permute-done | bytes 180256 | tf_op jit(solution)/shard_map/ppermute | solution.py:308
  (174 shorter events, 38.1 us)
Async XLA Ops:
  7.2 49.0 %all-gather.3.cloned.1.call-start = ((), (), s32[]{:S(2)}) async-start(), calls=%async_computation | async-start | bytes 2654208 | tf_op jit(solution)/shard_map/all_gather | solution.py:769
  10.1 11.1 %collective-permute-start.1 = (bf16[288,512]{1,0:T(8,128)(2,1)}, bf16[288,512]{1,0:T(8,128)(2,1)S(1)}, u32[]{:S(2)}, u32[]{:S(2)}) collective-permute-start(bf16[288,512]{1,0:T(8,128)(2,1)} %get-tuple-element.118), channel_id=1, source_target_pairs={{0,8},{4,12},{8,0},{12,4},{16,24},{20,28},{24,16},{28,20},{1,9},{5... | collective-permute-start | bytes 884744 | tf_op jit(solution)/shard_map/ppermute | solution.py:308
  13.0 15.0 %collective-permute-start.3 = (bf16[288,512]{1,0:T(8,128)(2,1)}, bf16[288,512]{1,0:T(8,128)(2,1)S(1)}, u32[]{:S(2)}, u32[]{:S(2)}) collective-permute-start(bf16[288,512]{1,0:T(8,128)(2,1)} %get-tuple-element.118), channel_id=1, source_target_pairs={{0,16},{4,20},{8,24},{12,28},{16,0},{20,4},{24,8},{28,12},{1,17},{... | collective-permute-start | bytes 884744 | tf_op jit(solution)/shard_map/ppermute | solution.py:308
  14.6 13.5 %collective-permute-start.5 = (bf16[288,512]{1,0:T(8,128)(2,1)}, bf16[288,512]{1,0:T(8,128)(2,1)S(1)}, u32[]{:S(2)}, u32[]{:S(2)}) collective-permute-start(bf16[288,512]{1,0:T(8,128)(2,1)} %get-tuple-element.118), channel_id=1, source_target_pairs={{0,24},{4,28},{8,16},{12,20},{16,8},{20,12},{24,0},{28,4},{1,25},{... | collective-permute-start | bytes 884744 | tf_op jit(solution)/shard_map/ppermute | solution.py:308
  14.6 15.2 %collective-permute-start = (bf16[288,512]{1,0:T(8,128)(2,1)}, bf16[288,512]{1,0:T(8,128)(2,1)S(1)}, u32[]{:S(2)}, u32[]{:S(2)}) collective-permute-start(bf16[288,512]{1,0:T(8,128)(2,1)} %get-tuple-element.118), channel_id=1, source_target_pairs={{0,4},{4,0},{8,12},{12,8},{16,20},{20,16},{24,28},{28,24},{1,5},{5... | collective-permute-start | bytes 884744 | tf_op jit(solution)/shard_map/ppermute | solution.py:308
  16.3 20.8 %collective-permute-start.7 = (bf16[3,112,512]{2,1,0:T(8,128)(2,1)}, bf16[3,112,512]{2,1,0:T(8,128)(2,1)S(1)}, u32[]{:S(2)}, u32[]{:S(2)}) collective-permute-start(bf16[3,112,512]{2,1,0:T(8,128)(2,1)} %slice_bitcast_fusion.1), channel_id=1, source_target_pairs={{0,3},{1,0},{2,1},{3,2},{4,7},{5,4},{6,5},{7,6},{8,11},{9,8},{10,9... | collective-permute-start | bytes 1032200 | tf_op jit(solution)/shard_map/ppermute | solution.py:40
  21.2 8.6 %collective-permute-start.2 = (bf16[288,512]{1,0:T(8,128)(2,1)S(1)}, bf16[288,512]{1,0:T(8,128)(2,1)S(1)}, u32[]{:S(2)}, u32[]{:S(2)}) collective-permute-start(bf16[288,512]{1,0:T(8,128)(2,1)S(1)} %collective-permute-done.1), channel_id=1, source_target_pairs={{0,4},{4,0},{8,12},{12,8},{16,20},{20,16},{24,28},{28,24},{1,5},{5... | collective-permute-start | bytes 884744 | tf_op jit(solution)/shard_map/ppermute | solution.py:308
  30.0 22.2 %collective-permute-start.9 = (bf16[256,512]{1,0:T(8,128)(2,1)}, bf16[256,512]{1,0:T(8,128)(2,1)S(1)}, u32[]{:S(2)}, u32[]{:S(2)}) collective-permute-start(bf16[256,512]{1,0:T(8,128)(2,1)} %get-tuple-element.131), channel_id=1, source_target_pairs={{0,4},{4,0},{8,12},{12,8},{16,20},{20,16},{24,28},{28,24},{1,5},{5... | collective-permute-start | bytes 786440 | tf_op jit(solution)/shard_map/ppermute | solution.py:308
  30.2 21.4 %collective-permute-start.10 = (bf16[256,512]{1,0:T(8,128)(2,1)}, bf16[256,512]{1,0:T(8,128)(2,1)S(1)}, u32[]{:S(2)}, u32[]{:S(2)}) collective-permute-start(bf16[256,512]{1,0:T(8,128)(2,1)} %get-tuple-element.131), channel_id=1, source_target_pairs={{0,8},{4,12},{8,0},{12,4},{16,24},{20,28},{24,16},{28,20},{1,9},{5... | collective-permute-start | bytes 786440 | tf_op jit(solution)/shard_map/ppermute | solution.py:308
  31.1 20.5 %collective-permute-start.12 = (bf16[256,512]{1,0:T(8,128)(2,1)}, bf16[256,512]{1,0:T(8,128)(2,1)S(1)}, u32[]{:S(2)}, u32[]{:S(2)}) collective-permute-start(bf16[256,512]{1,0:T(8,128)(2,1)} %get-tuple-element.131), channel_id=1, source_target_pairs={{0,16},{4,20},{8,24},{12,28},{16,0},{20,4},{24,8},{28,12},{1,17},{... | collective-permute-start | bytes 786440 | tf_op jit(solution)/shard_map/ppermute | solution.py:308
  32.3 19.8 %collective-permute-start.14 = (bf16[256,512]{1,0:T(8,128)(2,1)}, bf16[256,512]{1,0:T(8,128)(2,1)S(1)}, u32[]{:S(2)}, u32[]{:S(2)}) collective-permute-start(bf16[256,512]{1,0:T(8,128)(2,1)} %get-tuple-element.131), channel_id=1, source_target_pairs={{0,24},{4,28},{8,16},{12,20},{16,8},{20,12},{24,0},{28,4},{1,25},{... | collective-permute-start | bytes 786440 | tf_op jit(solution)/shard_map/ppermute | solution.py:308
  37.1 18.3 %collective-permute-start.8 = (bf16[3,112,512]{2,1,0:T(8,128)(2,1)S(1)}, bf16[3,112,512]{2,1,0:T(8,128)(2,1)S(1)}, u32[]{:S(2)}, u32[]{:S(2)}) collective-permute-start(bf16[3,112,512]{2,1,0:T(8,128)(2,1)S(1)} %slice_bitcast_fusion), channel_id=1, source_target_pairs={{0,3},{1,0},{2,1},{3,2},{4,7},{5,4},{6,5},{7,6},{8,11},{9,8},{10,9... | collective-permute-start | bytes 1032200 | tf_op jit(solution)/shard_map/ppermute | solution.py:40
  76.7 6.2 %collective-permute-start.16 = (bf16[4,288,512]{2,1,0:T(8,128)(2,1)S(1)}, bf16[4,288,512]{2,1,0:T(8,128)(2,1)S(1)}, u32[]{:S(2)}, u32[]{:S(2)}) collective-permute-start(bf16[4,288,512]{2,1,0:T(8,128)(2,1)S(1)} %get-tuple-element.133), channel_id=1, source_target_pairs={{0,4},{4,0},{8,12},{12,8},{16,20},{20,16},{24,28},{28,24},{1,5},{5... | collective-permute-start | bytes 3538952 | tf_op jit(solution)/shard_map/ppermute | solution.py:308
  82.4 7.3 %collective-permute-start.20 = (bf16[4,352,512]{2,1,0:T(8,128)(2,1)S(1)}, bf16[4,352,512]{2,1,0:T(8,128)(2,1)S(1)}, u32[]{:S(2)}, u32[]{:S(2)}) collective-permute-start(bf16[4,352,512]{2,1,0:T(8,128)(2,1)S(1)} %get-tuple-element.148), channel_id=1, source_target_pairs={{0,4},{4,0},{8,12},{12,8},{16,20},{20,16},{24,28},{28,24},{1,5},{5... | collective-permute-start | bytes 4325384 | tf_op jit(solution)/shard_map/ppermute | solution.py:308
  83.1 9.9 %collective-permute-start.17 = (bf16[288,512]{1,0:T(8,128)(2,1)S(1)}, bf16[288,512]{1,0:T(8,128)(2,1)S(1)}, u32[]{:S(2)}, u32[]{:S(2)}) collective-permute-start(bf16[288,512]{1,0:T(8,128)(2,1)S(1)} %get-tuple-element.140), channel_id=1, source_target_pairs={{0,8},{4,12},{8,0},{12,4},{16,24},{20,28},{24,16},{28,20},{1,9},{5... | collective-permute-start | bytes 884744 | tf_op jit(solution)/shard_map/ppermute | solution.py:308
  84.1 13.8 %collective-permute-start.18 = (bf16[288,512]{1,0:T(8,128)(2,1)S(1)}, bf16[288,512]{1,0:T(8,128)(2,1)S(1)}, u32[]{:S(2)}, u32[]{:S(2)}) collective-permute-start(bf16[288,512]{1,0:T(8,128)(2,1)S(1)} %get-tuple-element.141), channel_id=1, source_target_pairs={{0,16},{4,20},{8,24},{12,28},{16,0},{20,4},{24,8},{28,12},{1,17},{... | collective-permute-start | bytes 884744 | tf_op jit(solution)/shard_map/ppermute | solution.py:308
  85.3 14.4 %collective-permute-start.19 = (bf16[288,512]{1,0:T(8,128)(2,1)S(1)}, bf16[288,512]{1,0:T(8,128)(2,1)S(1)}, u32[]{:S(2)}, u32[]{:S(2)}) collective-permute-start(bf16[288,512]{1,0:T(8,128)(2,1)S(1)} %get-tuple-element.142), channel_id=1, source_target_pairs={{0,24},{4,28},{8,16},{12,20},{16,8},{20,12},{24,0},{28,4},{1,25},{... | collective-permute-start | bytes 884744 | tf_op jit(solution)/shard_map/ppermute | solution.py:308
  86.7 16.9 %collective-permute-start.22 = (bf16[336,512]{1,0:T(8,128)(2,1)S(1)}, bf16[336,512]{1,0:T(8,128)(2,1)S(1)}, u32[]{:S(2)}, u32[]{:S(2)}) collective-permute-start(bf16[336,512]{1,0:T(8,128)(2,1)S(1)} %get-tuple-element.155), channel_id=1, source_target_pairs={{0,1},{1,2},{2,3},{3,0},{4,5},{5,6},{6,7},{7,4},{8,9},{9,10},{10,1... | collective-permute-start | bytes 1032200 | tf_op jit(solution)/shard_map/ppermute | solution.py:40
  99.9 8.7 %collective-permute-start.21 = (bf16[144,512]{1,0:T(8,128)(2,1)S(1)}, bf16[144,512]{1,0:T(8,128)(2,1)S(1)}, u32[]{:S(2)}, u32[]{:S(2)}) collective-permute-start(bf16[144,512]{1,0:T(8,128)(2,1)S(1)} %get-tuple-element.152), channel_id=1, source_target_pairs={{0,1},{1,0},{2,3},{3,2},{4,5},{5,4},{6,7},{7,6},{8,9},{9,8},{10,11... | collective-permute-start | bytes 442376 | tf_op jit(solution)/shard_map/ppermute | solution.py:308
  100.0 11.4 %collective-permute-start.23 = (bf16[352,512]{1,0:T(8,128)(2,1)S(1)}, bf16[352,512]{1,0:T(8,128)(2,1)S(1)}, u32[]{:S(2)}, u32[]{:S(2)}) collective-permute-start(bf16[352,512]{1,0:T(8,128)(2,1)S(1)} %get-tuple-element.164), channel_id=1, source_target_pairs={{0,8},{4,12},{8,0},{12,4},{16,24},{20,28},{24,16},{28,20},{1,9},{5... | collective-permute-start | bytes 1081352 | tf_op jit(solution)/shard_map/ppermute | solution.py:308
  100.6 16.9 %collective-permute-start.24 = (bf16[352,512]{1,0:T(8,128)(2,1)S(1)}, bf16[352,512]{1,0:T(8,128)(2,1)S(1)}, u32[]{:S(2)}, u32[]{:S(2)}) collective-permute-start(bf16[352,512]{1,0:T(8,128)(2,1)S(1)} %get-tuple-element.165), channel_id=1, source_target_pairs={{0,16},{4,20},{8,24},{12,28},{16,0},{20,4},{24,8},{28,12},{1,17},{... | collective-permute-start | bytes 1081352 | tf_op jit(solution)/shard_map/ppermute | solution.py:308
  102.4 15.1 %collective-permute-start.25 = (bf16[352,512]{1,0:T(8,128)(2,1)S(1)}, bf16[352,512]{1,0:T(8,128)(2,1)S(1)}, u32[]{:S(2)}, u32[]{:S(2)}) collective-permute-start(bf16[352,512]{1,0:T(8,128)(2,1)S(1)} %get-tuple-element.166), channel_id=1, source_target_pairs={{0,24},{4,28},{8,16},{12,20},{16,8},{20,12},{24,0},{28,4},{1,25},{... | collective-permute-start | bytes 1081352 | tf_op jit(solution)/shard_map/ppermute | solution.py:308
  108.7 9.1 %collective-permute-start.26 = (bf16[4,224,512]{2,1,0:T(8,128)(2,1)S(1)}, bf16[4,224,512]{2,1,0:T(8,128)(2,1)S(1)}, u32[]{:S(2)}, u32[]{:S(2)}) collective-permute-start(bf16[4,224,512]{2,1,0:T(8,128)(2,1)S(1)} %get-tuple-element.168), channel_id=1, source_target_pairs={{0,4},{4,0},{8,12},{12,8},{16,20},{20,16},{24,28},{28,24},{1,5},{5... | collective-permute-start | bytes 2752520 | tf_op jit(solution)/shard_map/ppermute | solution.py:308
  108.8 10.3 %collective-permute-start.27 = (bf16[144,512]{1,0:T(8,128)(2,1)S(1)}, bf16[144,512]{1,0:T(8,128)(2,1)S(1)}, u32[]{:S(2)}, u32[]{:S(2)}) collective-permute-start(bf16[144,512]{1,0:T(8,128)(2,1)S(1)} %add_convert_fusion.12), channel_id=1, source_target_pairs={{0,2},{1,3},{2,0},{3,1},{4,6},{5,7},{6,4},{7,5},{8,10},{9,11},{10,... | collective-permute-start | bytes 442376 | tf_op jit(solution)/shard_map/ppermute | solution.py:308
  119.7 8.5 %collective-permute-start.30 = (bf16[224,512]{1,0:T(8,128)(2,1)S(1)}, bf16[224,512]{1,0:T(8,128)(2,1)S(1)}, u32[]{:S(2)}, u32[]{:S(2)}) collective-permute-start(bf16[224,512]{1,0:T(8,128)(2,1)S(1)} %get-tuple-element.178), channel_id=1, source_target_pairs={{0,8},{4,12},{8,0},{12,4},{16,24},{20,28},{24,16},{28,20},{1,9},{5... | collective-permute-start | bytes 688136 | tf_op jit(solution)/shard_map/ppermute | solution.py:308
  121.3 11.1 %collective-permute-start.31 = (bf16[224,512]{1,0:T(8,128)(2,1)S(1)}, bf16[224,512]{1,0:T(8,128)(2,1)S(1)}, u32[]{:S(2)}, u32[]{:S(2)}) collective-permute-start(bf16[224,512]{1,0:T(8,128)(2,1)S(1)} %get-tuple-element.179), channel_id=1, source_target_pairs={{0,16},{4,20},{8,24},{12,28},{16,0},{20,4},{24,8},{28,12},{1,17},{... | collective-permute-start | bytes 688136 | tf_op jit(solution)/shard_map/ppermute | solution.py:308
  121.6 10.7 %collective-permute-start.32 = (bf16[224,512]{1,0:T(8,128)(2,1)S(1)}, bf16[224,512]{1,0:T(8,128)(2,1)S(1)}, u32[]{:S(2)}, u32[]{:S(2)}) collective-permute-start(bf16[224,512]{1,0:T(8,128)(2,1)S(1)} %get-tuple-element.180), channel_id=1, source_target_pairs={{0,24},{4,28},{8,16},{12,20},{16,8},{20,12},{24,0},{28,4},{1,25},{... | collective-permute-start | bytes 688136 | tf_op jit(solution)/shard_map/ppermute | solution.py:308
  125.2 9.4 %collective-permute-start.33 = (bf16[176,512]{1,0:T(8,128)(2,1)S(1)}, bf16[176,512]{1,0:T(8,128)(2,1)S(1)}, u32[]{:S(2)}, u32[]{:S(2)}) collective-permute-start(bf16[176,512]{1,0:T(8,128)(2,1)S(1)} %add_convert_fusion.10), channel_id=1, source_target_pairs={{0,2},{1,3},{2,0},{3,1},{4,6},{5,7},{6,4},{7,5},{8,10},{9,11},{10,... | collective-permute-start | bytes 540680 | tf_op jit(solution)/shard_map/ppermute | solution.py:308
  135.0 17.2 %collective-permute-start.29 = (bf16[144,512]{1,0:T(8,128)(2,1)S(1)}, bf16[144,512]{1,0:T(8,128)(2,1)S(1)}, u32[]{:S(2)}, u32[]{:S(2)}) collective-permute-start(bf16[144,512]{1,0:T(8,128)(2,1)S(1)} %add_convert_fusion.11.half), channel_id=1, source_target_pairs={{0,1},{1,0},{2,3},{3,2},{4,5},{5,4},{6,7},{7,6},{8,9},{9,8},{10,11... | collective-permute-start | bytes 442376 | tf_op jit(solution)/shard_map/ppermute | solution.py:308
  137.1 16.5 %collective-permute-start.35 = (bf16[336,512]{1,0:T(8,128)(2,1)S(1)}, bf16[336,512]{1,0:T(8,128)(2,1)S(1)}, u32[]{:S(2)}, u32[]{:S(2)}) collective-permute-start(bf16[336,512]{1,0:T(8,128)(2,1)S(1)} %get-tuple-element.192), channel_id=1, source_target_pairs={{0,1},{1,2},{2,3},{3,0},{4,5},{5,6},{6,7},{7,4},{8,9},{9,10},{10,1... | collective-permute-start | bytes 1032200 | tf_op jit(solution)/shard_map/ppermute | solution.py:40
  140.9 12.9 %collective-permute-start.37 = (bf16[112,512]{1,0:T(8,128)(2,1)S(1)}, bf16[112,512]{1,0:T(8,128)(2,1)S(1)}, u32[]{:S(2)}, u32[]{:S(2)}) collective-permute-start(bf16[112,512]{1,0:T(8,128)(2,1)S(1)} %add_convert_fusion.14), channel_id=1, source_target_pairs={{0,2},{1,3},{2,0},{3,1},{4,6},{5,7},{6,4},{7,5},{8,10},{9,11},{10,... | collective-permute-start | bytes 344072 | tf_op jit(solution)/shard_map/ppermute | solution.py:308
  153.9 6.7 %collective-permute-start.38 = (bf16[112,512]{1,0:T(8,128)(2,1)S(1)}, bf16[112,512]{1,0:T(8,128)(2,1)S(1)}, u32[]{:S(2)}, u32[]{:S(2)}) collective-permute-start(bf16[112,512]{1,0:T(8,128)(2,1)S(1)} %add_convert_fusion.13.half), channel_id=1, source_target_pairs={{0,1},{1,0},{2,3},{3,2},{4,5},{5,4},{6,7},{7,6},{8,9},{9,8},{10,11... | collective-permute-start | bytes 344072 | tf_op jit(solution)/shard_map/ppermute | solution.py:308
  (43 other events, 214.2 us)
Sparse Core Ops, SparseCore 0:
  20.5 32.9 all-gather.2

commit v6 on v5

--- a/solution.py
+++ b/solution.py
@@ -468,34 +468,43 @@
 
 def mlp_forward_body(
     mixed,
+    out_slab,
     cotangent,
     cot_halo,
-    slab,
-    out_slab,
+    slab_far,
     kept,
     sent,
-    cot,
+    cot_rows,
     actives,
     back_sum,
     vectors,
     same,
     other,
+    slab,
+    sems,
 ):
+    own = WIN - SHIFT
+    copies = [
+        pltpu.make_async_copy(slab_far, slab, sems.at[0]),
+        pltpu.make_async_copy(cotangent.at[SHIFT:], cot_rows.at[:own], sems.at[1]),
+        pltpu.make_async_copy(cot_halo, cot_rows.at[own:], sems.at[2]),
+    ]
+    for copy in copies:
+        copy.start()
     me = shard_place()
     shards, height = slab.shape[:2]
     depth = (height - SMALL) // 4
     span = shards * D // FF
     chunks = FF // D
+    parts = [slice(r * WIDTH, (r + 1) * WIDTH) for r in range(WIN)]
+    normeds = [norm_stats(mixed[part, :])[0] for part in parts]
+    for copy in copies:
+        copy.wait()
     small = smalls_of(slab, 4 * depth)
     vectors[...] = small
     gain, offset, bias_o = (small[r : r + 1] for r in range(3))
-    own = WIN - SHIFT
-    parts = [slice(r * WIDTH, (r + 1) * WIDTH) for r in range(WIN)]
-    lows = []
-    for r, part in enumerate(parts):
-        cot[part, :] = cotangent[SHIFT + r] if r < own else cot_halo[r - own]
-        normed, _ = norm_stats(mixed[part, :])
-        lows.append((normed * gain + offset).astype(BF))
+    cot = cot_rows[...].reshape(TOKENS, D)
+    lows = [(normed * gain + offset).astype(BF) for normed in normeds]
     normed_low = jnp.concatenate(lows, 0)
 
     def w_in(c):
@@ -511,7 +520,7 @@
         products = []
         if ahead < chunks:
             products.append(lambda: hiddens.update({ahead: dot(normed_low, w_in(ahead))}))
-            products.append(lambda: slopes.update({ahead: dot_nt(cot[...], w_out(ahead))}))
+            products.append(lambda: slopes.update({ahead: dot_nt(cot, w_out(ahead))}))
         if behind >= 0:
             active = actives[:, behind * D : (behind + 1) * D]
             grad = grads.pop(behind)
@@ -823,19 +832,21 @@
         [
             like((own * WIDTH, D), F32),
             like((SHIFT * WIDTH, D), BF),
-            like((TOKENS, D), BF),
+            like((WIN, WIDTH, D), BF),
             like((TOKENS, FF), BF),
             like((TOKENS, D), F32),
             like((SMALL, D), F32),
             share_a,
             share_a,
         ],
-        (mixed, cot_here, cot_halo, mlp_all, jnp.stack(out_pieces)),
+        (mixed, jnp.stack(out_pieces), cot_here, cot_halo, mlp_all),
+        scratch=[pltpu.VMEM(mlp_all.shape, BF), pltpu.SemaphoreType.DMA((3,))],
+        apart=3,
     )
     grad_mixed, grad_win, same_b, other_b = kernel_call(
         mlp_backward_body,
         [like((TOKENS, D), F32), like((PADDED, D), BF), share_b, share_b],
-        (mixed, cot, actives, back_sum, vectors, attn_all, restored),
+        (mixed, cot.reshape(TOKENS, D), actives, back_sum, vectors, attn_all, restored),
         scratch=[pltpu.VMEM((WINDOWS, WIN, SLOT, D), F32)],
     )
 
@@ -886,11 +897,11 @@
     sums, (far_a,) = tie(add_cores(attn_same, attn_came), [far_a])
     attn_parts = to_chips(sums)
     half_a = seq_rest(add_pair(half_a, far_a))
-    (half_a,), (near_b, tok_sent) = tie([half_a], [near_b, tok_sent])
+    (half_a,), (near_b,) = tie([half_a], [near_b])
     tok_halo = shifted_2(tok_sent, "seq", 1)
     half_b = add_pair(keep_b, near_b)
     far_b = exchange(half_b, "seq", 2)
-    attn_parts, (far_b,) = tie(attn_parts, [far_b])
+    (*attn_parts, tok_halo), (far_b,) = tie([*attn_parts, tok_halo], [far_b])
     half_b = seq_rest(add_pair(half_b, far_b))
     (half_b,), attn_parts = tie([half_b], attn_parts)
     keep, send = add_chips(attn_same, attn_came, attn_parts)

time: 169 us -> 172 us (1.018)
  waiting for transfers between devices: 49 us -> 51.6 us
    ppermute x35, starting transfers between devices: 29.6 us -> 26.5 us  [exchange(): return lax.ppermute(value, axis, [(i, i ^ mask) for i in range(peers)])]
    ppermute x35, waiting for transfers between devices: 49 us -> 51.5 us  [exchange(): return lax.ppermute(value, axis, [(i, i ^ mask) for i in range(peers)])]
    ppermute x4, starting transfers between devices: 7.79 us -> 9.76 us  [shifted_2(): lax.ppermute(value, axis, [(i, (i + by) % peers) for i in range(peers)])]
  transfers between devices with their start and end apart: 40 -> 40, of which waited for: 19 -> 20; matrix products, arithmetic and copies ran while one was open for 6% -> 6% of each run, Pallas kernels for 17% -> 17%
where the time goes in v6:
time: 172 us; the launch traced here: 171 us
  waiting for transfers between devices  51.6 us (30%)
  Pallas kernels  48.2 us (28%)
  starting transfers between devices  36.2 us (21%)
  local copies, waits for them, and re-layouts  16.5 us (10%)
  between operations  14.8 us (9%)
  other arithmetic  3.73 us (2%)
    ppermute x35, waiting for transfers between devices, exchange(): return lax.ppermute(value, axis, [(i, i ^ mask) for i in range(peers)])  51.5 us
    pallas_call x14, Pallas kernels, kernel_call(): pl.pallas_call(body, out_shape=tuple(outs), in_specs=in_specs, out_specs=...  48.2 us
    ppermute x35, starting transfers between devices, exchange(): return lax.ppermute(value, axis, [(i, i ^ mask) for i in range(peers)])  26.5 us
    unnamed x84, local copies, waits for them, and re-layouts  13.1 us
    ppermute x4, starting transfers between devices, shifted_2(): lax.ppermute(value, axis, [(i, (i + by) % peers) for i in range(peers)])  9.76 us
  transfers between devices with their start and end apart: 40, of which 20 were waited for; matrix products, arithmetic and copies ran while one was open for 6% of the time, Pallas kernels for 17%

profile of v6, /device:TPU:0, one launch (start us, length us, event | category | flops | bytes accessed | tf_op | source)
XLA Modules:
  0.0 171.1 jit_solution(5443539108289503150)
XLA Ops:
  7.2 2.9 %shard_map.271 = (bf16[288,512]{1,0:T(8,128)(2,1)}, bf16[288,512]{1,0:T(8,128)(2,1)}, bf16[256,512]{1,0:T(8,128)(2,1)}) custom-call(bf16[1,64]{1,0:T(2,128)(2,1)} %bitcast.89, bf16[1,64]{1,0:T(2,128)(2,1)} %bitcast.90, bf16[64,1536]{1,0:T(8,128)(2,1)} %wqkv.1, bf16[2,64]{1,0:T(2,128)(2,1)} %bqv.1, bf16[2,169]{1,0:T(2,128)(2,1)} %bitcast.88, ...), custom_call_target="tpu_custom_call" | custom-call | flops 1024 | bytes 1024 | tf_op jit(solution)/shard_map/pallas_call | solution.py:150
  10.1 2.9 %collective-permute-start.1 = (bf16[288,512]{1,0:T(8,128)(2,1)}, bf16[288,512]{1,0:T(8,128)(2,1)S(1)}, u32[]{:S(2)}, u32[]{:S(2)}) collective-permute-start(bf16[288,512]{1,0:T(8,128)(2,1)} %get-tuple-element.118), channel_id=1, source_target_pairs={{0,8},{4,12},{8,0},{12,4},{16,24},{20,28},{24,16},{28,20},{1,9},{5... | collective-permute-start | bytes 884744 | tf_op jit(solution)/shard_map/ppermute | solution.py:308
  13.0 1.5 collective-permute-start.3
  14.6 1.7 %slice_bitcast_fusion.1 = bf16[3,112,512]{2,1,0:T(8,128)(2,1)} fusion(bf16[1,7,112,512]{3,2,1,0:T(8,128)(2,1)} %param.16), kind=kLoop, calls=%fused_computation.17 | loop fusion | bytes 688128 | tf_op jit(solution)/shard_map/slice | solution.py:780
  16.3 4.1 %collective-permute-start.7 = (bf16[3,112,512]{2,1,0:T(8,128)(2,1)}, bf16[3,112,512]{2,1,0:T(8,128)(2,1)S(1)}, u32[]{:S(2)}, u32[]{:S(2)}) collective-permute-start(bf16[3,112,512]{2,1,0:T(8,128)(2,1)} %slice_bitcast_fusion.1), channel_id=1, source_target_pairs={{0,3},{1,0},{2,1},{3,2},{4,7},{5,4},{6,5},{7,6},{8,11},{9,8},{10,9... | collective-permute-start | bytes 1032200 | tf_op jit(solution)/shard_map/ppermute | solution.py:40
  21.2 6.9 %collective-permute-done.3 = bf16[288,512]{1,0:T(8,128)(2,1)S(1)} collective-permute-done((bf16[288,512]{1,0:T(8,128)(2,1)}, bf16[288,512]{1,0:T(8,128)(2,1)S(1)}, u32[]{:S(2)}, u32[]{:S(2)}) %collective-permute-start.3) | collective-permute-done | bytes 294944 | tf_op jit(solution)/shard_map/ppermute | solution.py:308
  37.1 3.7 %collective-permute-start.15 = (bf16[3,112,512]{2,1,0:T(8,128)(2,1)S(1)}, bf16[3,112,512]{2,1,0:T(8,128)(2,1)S(1)}, u32[]{:S(2)}, u32[]{:S(2)}) collective-permute-start(bf16[3,112,512]{2,1,0:T(8,128)(2,1)S(1)} %slice_bitcast_fusion), channel_id=1, source_target_pairs={{0,3},{1,0},{2,1},{3,2},{4,7},{5,4},{6,5},{7,6},{8,11},{9,8},{10,9... | collective-permute-start | bytes 1032200 | tf_op jit(solution)/shard_map/ppermute | solution.py:40
  40.8 2.4 %shard_map.272 = (bf16[896,512]{1,0:T(8,128)(2,1)S(1)}, bf16[896,512]{1,0:T(8,128)(2,1)S(1)}, bf16[896,512]{1,0:T(8,128)(2,1)S(1)}, bf16[896,512]{1,0:T(8,128)(2,1)S(1)}) custom-call(bf16[7,112,512]{2,1,0:T(8,128)(2,1)S(1)} %bitcast.79, bf16[3,112,512]{2,1,0:T(8,128)(2,1)S(1)} %collective-permute-done.7.halo, ...), custom_call_target="tpu_custom_call" | custom-call | flops 1024 | bytes 1024 | tf_op jit(solution)/shard_map/pallas_call | solution.py:150
  43.4 6.9 %shard_map.273 = (bf16[8,4,112,256]{3,2,1,0:T(8,128)(2,1)S(1)}, bf16[784,512]{1,0:T(8,128)(2,1)S(1)}, f32[784,512]{1,0:T(8,128)S(1)}) custom-call(bf16[8,288,512]{2,1,0:T(8,128)(2,1)S(1)} %bitcast_dynamic-update-slice_fusion.slab.attn_slab, f32[16,56,128]{2,1,0:T(8,128)S(1)} %broadcast_in_dim.35.reg_rows, f32[16,1,256]{2,1,0:T(1,128)S(1)} %tile.9.reg_lanes, ...), custom_call_target="tpu_custom_call" | custom-call | flops 1024 | bytes 1024 | tf_op jit(solution)/shard_map/pallas_call | solution.py:150
  57.4 1.6 copy-done.13
  59.0 1.7 copy-done.14
  62.8 14.5 %shard_map.274 = (f32[448,512]{1,0:T(8,128)S(1)}, bf16[336,512]{1,0:T(8,128)(2,1)S(1)}, bf16[7,112,512]{2,1,0:T(8,128)(2,1)S(1)}, bf16[784,2048]{1,0:T(8,128)(2,...) custom-call(f32[784,512]{1,0:T(8,128)S(1)} %copy-done.11, ...), custom_call_target="tpu_custom_call" | custom-call | flops 1024 | bytes 1024 | tf_op jit(solution)/shard_map/pallas_call | solution.py:150
  77.5 5.7 %shard_map.275 = (f32[784,512]{1,0:T(8,128)S(1)}, bf16[896,512]{1,0:T(8,128)(2,1)S(1)}, bf16[4,352,512]{2,1,0:T(8,128)(2,1)S(1)}, bf16[4,352,512]{2,1,0:T(8,128)(2,1)S(1)}) custom-call(f32[784,512]{1,0:T(8,128)S(1)} %copy-done.11, bf16[784,512]{1,0:T(8,128)(2,1)S(1)} %bitcast.84, bf16[784,2048]{1,0:T(8,128)(2,1)S(1)} %get-tuple-element.135.actives, ...), custom_call_target="tpu_custom_call" | custom-call | flops 1024 | bytes 1024 | tf_op jit(solution)/shard_map/pallas_call | solution.py:150
  86.0 1.5 collective-permute-start.19
  87.7 3.0 %shard_map.277 = (bf16[448,1536]{1,0:T(8,128)(2,1)S(1)}, f32[4,56,256]{2,1,0:T(8,128)S(1)}) custom-call(bf16[896,512]{1,0:T(8,128)(2,1)S(1)} %copy-done.3, bf16[896,512]{1,0:T(8,128)(2,1)S(1)} %copy-done.5, bf16[896,512]{1,0:T(8,128)(2,1)S(1)} %copy-done.7, bf16[8,4,112,256]{3,2,1,0:T(8,128)(2,1)S(1)} %copy-done.9, ...), custom_call_target="tpu_custom_call" | custom-call | flops 1024 | bytes 1024 | tf_op jit(solution)/shard_map/pallas_call | solution.py:150
  91.0 3.0 %shard_map.278 = (bf16[448,1536]{1,0:T(8,128)(2,1)S(1)}, f32[4,56,256]{2,1,0:T(8,128)S(1)}) custom-call(bf16[896,512]{1,0:T(8,128)(2,1)S(1)} %copy-done.3, bf16[896,512]{1,0:T(8,128)(2,1)S(1)} %copy-done.5, bf16[896,512]{1,0:T(8,128)(2,1)S(1)} %copy-done.7, bf16[8,4,112,256]{3,2,1,0:T(8,128)(2,1)S(1)} %copy-done.9, ...), custom_call_target="tpu_custom_call" | custom-call | flops 1024 | bytes 1024 | tf_op jit(solution)/shard_map/pallas_call | solution.py:150
  94.0 4.8 %collective-permute-done.18.refs_1_ = bf16[288,512]{1,0:T(8,128)(2,1)S(1)} collective-permute-done((bf16[288,512]{1,0:T(8,128)(2,1)S(1)}, bf16[288,512]{1,0:T(8,128)(2,1)S(1)}, u32[]{:S(2)}, u32[]{:S(2)}) %collective-permute-start.18) | collective-permute-done | bytes 294944 | tf_op jit(solution)/shard_map/ppermute | solution.py:308
  98.8 1.8 %collective-permute-done.19.refs_2_ = bf16[288,512]{1,0:T(8,128)(2,1)S(1)} collective-permute-done((bf16[288,512]{1,0:T(8,128)(2,1)S(1)}, bf16[288,512]{1,0:T(8,128)(2,1)S(1)}, u32[]{:S(2)}, u32[]{:S(2)}) %collective-permute-start.19) | collective-permute-done | bytes 294944 | tf_op jit(solution)/shard_map/ppermute | solution.py:308
  101.5 1.7 collective-permute-start.24
  104.4 5.1 %shard_map.279 = (f32[448,512]{1,0:T(8,128)S(1)}, bf16[336,512]{1,0:T(8,128)(2,1)S(1)}, bf16[4,224,512]{2,1,0:T(8,128)(2,1)S(1)}, bf16[4,224,512]{2,1,0:T(8,128)(2,1)S(1)}) custom-call(f32[784,512]{1,0:T(8,128)S(1)} %get-tuple-element.153.grad_mixed, bf16[7,112,512]{2,1,0:T(8,128)(2,1)S(1)} %bitcast.81, ...), custom_call_target="tpu_custom_call" | custom-call | flops 1024 | bytes 1024 | tf_op jit(solution)/shard_map/pallas_call | solution.py:150
  109.6 2.5 %collective-permute-start.27 = (bf16[144,512]{1,0:T(8,128)(2,1)S(1)}, bf16[144,512]{1,0:T(8,128)(2,1)S(1)}, u32[]{:S(2)}, u32[]{:S(2)}) collective-permute-start(bf16[144,512]{1,0:T(8,128)(2,1)S(1)} %add_convert_fusion.12), channel_id=1, source_target_pairs={{0,2},{1,3},{2,0},{3,1},{4,6},{5,7},{6,4},{7,5},{8,10},{9,11},{10,... | collective-permute-start | bytes 442376 | tf_op jit(solution)/shard_map/ppermute | solution.py:308
  112.3 1.9 %collective-permute-start.33 = (bf16[336,512]{1,0:T(8,128)(2,1)S(1)}, bf16[336,512]{1,0:T(8,128)(2,1)S(1)}, u32[]{:S(2)}, u32[]{:S(2)}) collective-permute-start(bf16[336,512]{1,0:T(8,128)(2,1)S(1)} %get-tuple-element.180), channel_id=1, source_target_pairs={{0,1},{1,2},{2,3},{3,0},{4,5},{5,6},{6,7},{7,4},{8,9},{9,10},{10,1... | collective-permute-start | bytes 1032200 | tf_op jit(solution)/shard_map/ppermute | solution.py:40
  114.2 4.2 %collective-permute-done.24.refs_1_ = bf16[352,512]{1,0:T(8,128)(2,1)S(1)} collective-permute-done((bf16[352,512]{1,0:T(8,128)(2,1)S(1)}, bf16[352,512]{1,0:T(8,128)(2,1)S(1)}, u32[]{:S(2)}, u32[]{:S(2)}) %collective-permute-start.24) | collective-permute-done | bytes 360480 | tf_op jit(solution)/shard_map/ppermute | solution.py:308
  118.8 8.5 %collective-permute-done.27 = bf16[144,512]{1,0:T(8,128)(2,1)S(1)} collective-permute-done((bf16[144,512]{1,0:T(8,128)(2,1)S(1)}, bf16[144,512]{1,0:T(8,128)(2,1)S(1)}, u32[]{:S(2)}, u32[]{:S(2)}) %collective-permute-start.27) | collective-permute-done | bytes 147488 | tf_op jit(solution)/shard_map/ppermute | solution.py:308
  130.8 2.6 %collective-permute-done.28 = bf16[176,512]{1,0:T(8,128)(2,1)S(1)} collective-permute-done((bf16[176,512]{1,0:T(8,128)(2,1)S(1)}, bf16[176,512]{1,0:T(8,128)(2,1)S(1)}, u32[]{:S(2)}, u32[]{:S(2)}) %collective-permute-start.28) | collective-permute-done | bytes 180256 | tf_op jit(solution)/shard_map/ppermute | solution.py:308
  133.6 2.3 %collective-permute-done.30.refs_0_ = bf16[224,512]{1,0:T(8,128)(2,1)S(1)} collective-permute-done((bf16[224,512]{1,0:T(8,128)(2,1)S(1)}, bf16[224,512]{1,0:T(8,128)(2,1)S(1)}, u32[]{:S(2)}, u32[]{:S(2)}) %collective-permute-start.30) | collective-permute-done | bytes 229408 | tf_op jit(solution)/shard_map/ppermute | solution.py:308
  135.8 5.0 %collective-permute-done.31.refs_1_ = bf16[224,512]{1,0:T(8,128)(2,1)S(1)} collective-permute-done((bf16[224,512]{1,0:T(8,128)(2,1)S(1)}, bf16[224,512]{1,0:T(8,128)(2,1)S(1)}, u32[]{:S(2)}, u32[]{:S(2)}) %collective-permute-start.31) | collective-permute-done | bytes 229408 | tf_op jit(solution)/shard_map/ppermute | solution.py:308
  140.8 2.7 %collective-permute-done.34 = bf16[176,512]{1,0:T(8,128)(2,1)S(1)} collective-permute-done((bf16[176,512]{1,0:T(8,128)(2,1)S(1)}, bf16[176,512]{1,0:T(8,128)(2,1)S(1)}, u32[]{:S(2)}, u32[]{:S(2)}) %collective-permute-start.34) | collective-permute-done | bytes 180256 | tf_op jit(solution)/shard_map/ppermute | solution.py:308
  143.9 2.1 %collective-permute-start.29 = (bf16[144,512]{1,0:T(8,128)(2,1)S(1)}, bf16[144,512]{1,0:T(8,128)(2,1)S(1)}, u32[]{:S(2)}, u32[]{:S(2)}) collective-permute-start(bf16[144,512]{1,0:T(8,128)(2,1)S(1)} %add_convert_fusion.11.half), channel_id=1, source_target_pairs={{0,1},{1,0},{2,3},{3,2},{4,5},{5,4},{6,7},{7,6},{8,9},{9,8},{10,11... | collective-permute-start | bytes 442376 | tf_op jit(solution)/shard_map/ppermute | solution.py:308
  146.0 3.8 %collective-permute-done.36 = bf16[112,512]{1,0:T(8,128)(2,1)S(1)} collective-permute-done((bf16[112,512]{1,0:T(8,128)(2,1)S(1)}, bf16[112,512]{1,0:T(8,128)(2,1)S(1)}, u32[]{:S(2)}, u32[]{:S(2)}) %collective-permute-start.36) | collective-permute-done | bytes 114720 | tf_op jit(solution)/shard_map/ppermute | solution.py:308
  154.4 2.1 %collective-permute-done.37 = bf16[112,512]{1,0:T(8,128)(2,1)S(1)} collective-permute-done((bf16[112,512]{1,0:T(8,128)(2,1)S(1)}, bf16[112,512]{1,0:T(8,128)(2,1)S(1)}, u32[]{:S(2)}, u32[]{:S(2)}) %collective-permute-start.37) | collective-permute-done | bytes 114720 | tf_op jit(solution)/shard_map/ppermute | solution.py:308
  158.0 3.1 %collective-permute-done.35.back = bf16[176,512]{1,0:T(8,128)(2,1)S(1)} collective-permute-done((bf16[176,512]{1,0:T(8,128)(2,1)S(1)}, bf16[176,512]{1,0:T(8,128)(2,1)S(1)}, u32[]{:S(2)}, u32[]{:S(2)}) %collective-permute-start.35) | collective-permute-done | bytes 180256 | tf_op jit(solution)/shard_map/ppermute | solution.py:308
  (174 shorter events, 38.1 us)
Async XLA Ops:
  7.2 48.8 %all-gather.3.cloned.1.call-start = ((), (), s32[]{:S(2)}) async-start(), calls=%async_computation | async-start | bytes 2654208 | tf_op jit(solution)/shard_map/all_gather | solution.py:778
  10.1 11.1 %collective-permute-start.1 = (bf16[288,512]{1,0:T(8,128)(2,1)}, bf16[288,512]{1,0:T(8,128)(2,1)S(1)}, u32[]{:S(2)}, u32[]{:S(2)}) collective-permute-start(bf16[288,512]{1,0:T(8,128)(2,1)} %get-tuple-element.118), channel_id=1, source_target_pairs={{0,8},{4,12},{8,0},{12,4},{16,24},{20,28},{24,16},{28,20},{1,9},{5... | collective-permute-start | bytes 884744 | tf_op jit(solution)/shard_map/ppermute | solution.py:308
  13.0 15.0 %collective-permute-start.3 = (bf16[288,512]{1,0:T(8,128)(2,1)}, bf16[288,512]{1,0:T(8,128)(2,1)S(1)}, u32[]{:S(2)}, u32[]{:S(2)}) collective-permute-start(bf16[288,512]{1,0:T(8,128)(2,1)} %get-tuple-element.118), channel_id=1, source_target_pairs={{0,16},{4,20},{8,24},{12,28},{16,0},{20,4},{24,8},{28,12},{1,17},{... | collective-permute-start | bytes 884744 | tf_op jit(solution)/shard_map/ppermute | solution.py:308
  14.6 13.5 %collective-permute-start.5 = (bf16[288,512]{1,0:T(8,128)(2,1)}, bf16[288,512]{1,0:T(8,128)(2,1)S(1)}, u32[]{:S(2)}, u32[]{:S(2)}) collective-permute-start(bf16[288,512]{1,0:T(8,128)(2,1)} %get-tuple-element.118), channel_id=1, source_target_pairs={{0,24},{4,28},{8,16},{12,20},{16,8},{20,12},{24,0},{28,4},{1,25},{... | collective-permute-start | bytes 884744 | tf_op jit(solution)/shard_map/ppermute | solution.py:308
  14.6 15.2 %collective-permute-start = (bf16[288,512]{1,0:T(8,128)(2,1)}, bf16[288,512]{1,0:T(8,128)(2,1)S(1)}, u32[]{:S(2)}, u32[]{:S(2)}) collective-permute-start(bf16[288,512]{1,0:T(8,128)(2,1)} %get-tuple-element.118), channel_id=1, source_target_pairs={{0,4},{4,0},{8,12},{12,8},{16,20},{20,16},{24,28},{28,24},{1,5},{5... | collective-permute-start | bytes 884744 | tf_op jit(solution)/shard_map/ppermute | solution.py:308
  16.3 20.8 %collective-permute-start.7 = (bf16[3,112,512]{2,1,0:T(8,128)(2,1)}, bf16[3,112,512]{2,1,0:T(8,128)(2,1)S(1)}, u32[]{:S(2)}, u32[]{:S(2)}) collective-permute-start(bf16[3,112,512]{2,1,0:T(8,128)(2,1)} %slice_bitcast_fusion.1), channel_id=1, source_target_pairs={{0,3},{1,0},{2,1},{3,2},{4,7},{5,4},{6,5},{7,6},{8,11},{9,8},{10,9... | collective-permute-start | bytes 1032200 | tf_op jit(solution)/shard_map/ppermute | solution.py:40
  21.2 8.6 %collective-permute-start.2 = (bf16[288,512]{1,0:T(8,128)(2,1)S(1)}, bf16[288,512]{1,0:T(8,128)(2,1)S(1)}, u32[]{:S(2)}, u32[]{:S(2)}) collective-permute-start(bf16[288,512]{1,0:T(8,128)(2,1)S(1)} %collective-permute-done.1), channel_id=1, source_target_pairs={{0,4},{4,0},{8,12},{12,8},{16,20},{20,16},{24,28},{28,24},{1,5},{5... | collective-permute-start | bytes 884744 | tf_op jit(solution)/shard_map/ppermute | solution.py:308
  30.0 22.0 %collective-permute-start.8 = (bf16[256,512]{1,0:T(8,128)(2,1)}, bf16[256,512]{1,0:T(8,128)(2,1)S(1)}, u32[]{:S(2)}, u32[]{:S(2)}) collective-permute-start(bf16[256,512]{1,0:T(8,128)(2,1)} %get-tuple-element.130), channel_id=1, source_target_pairs={{0,4},{4,0},{8,12},{12,8},{16,20},{20,16},{24,28},{28,24},{1,5},{5... | collective-permute-start | bytes 786440 | tf_op jit(solution)/shard_map/ppermute | solution.py:308
  30.2 21.2 %collective-permute-start.9 = (bf16[256,512]{1,0:T(8,128)(2,1)}, bf16[256,512]{1,0:T(8,128)(2,1)S(1)}, u32[]{:S(2)}, u32[]{:S(2)}) collective-permute-start(bf16[256,512]{1,0:T(8,128)(2,1)} %get-tuple-element.130), channel_id=1, source_target_pairs={{0,8},{4,12},{8,0},{12,4},{16,24},{20,28},{24,16},{28,20},{1,9},{5... | collective-permute-start | bytes 786440 | tf_op jit(solution)/shard_map/ppermute | solution.py:308
  31.1 20.3 %collective-permute-start.11 = (bf16[256,512]{1,0:T(8,128)(2,1)}, bf16[256,512]{1,0:T(8,128)(2,1)S(1)}, u32[]{:S(2)}, u32[]{:S(2)}) collective-permute-start(bf16[256,512]{1,0:T(8,128)(2,1)} %get-tuple-element.130), channel_id=1, source_target_pairs={{0,16},{4,20},{8,24},{12,28},{16,0},{20,4},{24,8},{28,12},{1,17},{... | collective-permute-start | bytes 786440 | tf_op jit(solution)/shard_map/ppermute | solution.py:308
  32.3 19.7 %collective-permute-start.13 = (bf16[256,512]{1,0:T(8,128)(2,1)}, bf16[256,512]{1,0:T(8,128)(2,1)S(1)}, u32[]{:S(2)}, u32[]{:S(2)}) collective-permute-start(bf16[256,512]{1,0:T(8,128)(2,1)} %get-tuple-element.130), channel_id=1, source_target_pairs={{0,24},{4,28},{8,16},{12,20},{16,8},{20,12},{24,0},{28,4},{1,25},{... | collective-permute-start | bytes 786440 | tf_op jit(solution)/shard_map/ppermute | solution.py:308
  37.1 18.1 %collective-permute-start.15 = (bf16[3,112,512]{2,1,0:T(8,128)(2,1)S(1)}, bf16[3,112,512]{2,1,0:T(8,128)(2,1)S(1)}, u32[]{:S(2)}, u32[]{:S(2)}) collective-permute-start(bf16[3,112,512]{2,1,0:T(8,128)(2,1)S(1)} %slice_bitcast_fusion), channel_id=1, source_target_pairs={{0,3},{1,0},{2,1},{3,2},{4,7},{5,4},{6,5},{7,6},{8,11},{9,8},{10,9... | collective-permute-start | bytes 1032200 | tf_op jit(solution)/shard_map/ppermute | solution.py:40
  77.3 6.4 %collective-permute-start.16 = (bf16[4,288,512]{2,1,0:T(8,128)(2,1)S(1)}, bf16[4,288,512]{2,1,0:T(8,128)(2,1)S(1)}, u32[]{:S(2)}, u32[]{:S(2)}) collective-permute-start(bf16[4,288,512]{2,1,0:T(8,128)(2,1)S(1)} %get-tuple-element.133), channel_id=1, source_target_pairs={{0,4},{4,0},{8,12},{12,8},{16,20},{20,16},{24,28},{28,24},{1,5},{5... | collective-permute-start | bytes 3538952 | tf_op jit(solution)/shard_map/ppermute | solution.py:308
  83.3 7.4 %collective-permute-start.20 = (bf16[4,352,512]{2,1,0:T(8,128)(2,1)S(1)}, bf16[4,352,512]{2,1,0:T(8,128)(2,1)S(1)}, u32[]{:S(2)}, u32[]{:S(2)}) collective-permute-start(bf16[4,352,512]{2,1,0:T(8,128)(2,1)S(1)} %get-tuple-element.148), channel_id=1, source_target_pairs={{0,4},{4,0},{8,12},{12,8},{16,20},{20,16},{24,28},{28,24},{1,5},{5... | collective-permute-start | bytes 4325384 | tf_op jit(solution)/shard_map/ppermute | solution.py:308
  84.0 10.0 %collective-permute-start.17 = (bf16[288,512]{1,0:T(8,128)(2,1)S(1)}, bf16[288,512]{1,0:T(8,128)(2,1)S(1)}, u32[]{:S(2)}, u32[]{:S(2)}) collective-permute-start(bf16[288,512]{1,0:T(8,128)(2,1)S(1)} %get-tuple-element.140), channel_id=1, source_target_pairs={{0,8},{4,12},{8,0},{12,4},{16,24},{20,28},{24,16},{28,20},{1,9},{5... | collective-permute-start | bytes 884744 | tf_op jit(solution)/shard_map/ppermute | solution.py:308
  85.0 13.8 %collective-permute-start.18 = (bf16[288,512]{1,0:T(8,128)(2,1)S(1)}, bf16[288,512]{1,0:T(8,128)(2,1)S(1)}, u32[]{:S(2)}, u32[]{:S(2)}) collective-permute-start(bf16[288,512]{1,0:T(8,128)(2,1)S(1)} %get-tuple-element.141), channel_id=1, source_target_pairs={{0,16},{4,20},{8,24},{12,28},{16,0},{20,4},{24,8},{28,12},{1,17},{... | collective-permute-start | bytes 884744 | tf_op jit(solution)/shard_map/ppermute | solution.py:308
  86.0 14.6 %collective-permute-start.19 = (bf16[288,512]{1,0:T(8,128)(2,1)S(1)}, bf16[288,512]{1,0:T(8,128)(2,1)S(1)}, u32[]{:S(2)}, u32[]{:S(2)}) collective-permute-start(bf16[288,512]{1,0:T(8,128)(2,1)S(1)} %get-tuple-element.142), channel_id=1, source_target_pairs={{0,24},{4,28},{8,16},{12,20},{16,8},{20,12},{24,0},{28,4},{1,25},{... | collective-permute-start | bytes 884744 | tf_op jit(solution)/shard_map/ppermute | solution.py:308
  87.5 16.9 %collective-permute-start.22 = (bf16[336,512]{1,0:T(8,128)(2,1)S(1)}, bf16[336,512]{1,0:T(8,128)(2,1)S(1)}, u32[]{:S(2)}, u32[]{:S(2)}) collective-permute-start(bf16[336,512]{1,0:T(8,128)(2,1)S(1)} %get-tuple-element.155), channel_id=1, source_target_pairs={{0,1},{1,2},{2,3},{3,0},{4,5},{5,6},{6,7},{7,4},{8,9},{9,10},{10,1... | collective-permute-start | bytes 1032200 | tf_op jit(solution)/shard_map/ppermute | solution.py:40
  100.8 8.7 %collective-permute-start.21 = (bf16[144,512]{1,0:T(8,128)(2,1)S(1)}, bf16[144,512]{1,0:T(8,128)(2,1)S(1)}, u32[]{:S(2)}, u32[]{:S(2)}) collective-permute-start(bf16[144,512]{1,0:T(8,128)(2,1)S(1)} %get-tuple-element.152), channel_id=1, source_target_pairs={{0,1},{1,0},{2,3},{3,2},{4,5},{5,4},{6,7},{7,6},{8,9},{9,8},{10,11... | collective-permute-start | bytes 442376 | tf_op jit(solution)/shard_map/ppermute | solution.py:308
  100.8 11.4 %collective-permute-start.23 = (bf16[352,512]{1,0:T(8,128)(2,1)S(1)}, bf16[352,512]{1,0:T(8,128)(2,1)S(1)}, u32[]{:S(2)}, u32[]{:S(2)}) collective-permute-start(bf16[352,512]{1,0:T(8,128)(2,1)S(1)} %get-tuple-element.164), channel_id=1, source_target_pairs={{0,8},{4,12},{8,0},{12,4},{16,24},{20,28},{24,16},{28,20},{1,9},{5... | collective-permute-start | bytes 1081352 | tf_op jit(solution)/shard_map/ppermute | solution.py:308
  101.5 16.9 %collective-permute-start.24 = (bf16[352,512]{1,0:T(8,128)(2,1)S(1)}, bf16[352,512]{1,0:T(8,128)(2,1)S(1)}, u32[]{:S(2)}, u32[]{:S(2)}) collective-permute-start(bf16[352,512]{1,0:T(8,128)(2,1)S(1)} %get-tuple-element.165), channel_id=1, source_target_pairs={{0,16},{4,20},{8,24},{12,28},{16,0},{20,4},{24,8},{28,12},{1,17},{... | collective-permute-start | bytes 1081352 | tf_op jit(solution)/shard_map/ppermute | solution.py:308
  103.2 15.2 %collective-permute-start.25 = (bf16[352,512]{1,0:T(8,128)(2,1)S(1)}, bf16[352,512]{1,0:T(8,128)(2,1)S(1)}, u32[]{:S(2)}, u32[]{:S(2)}) collective-permute-start(bf16[352,512]{1,0:T(8,128)(2,1)S(1)} %get-tuple-element.166), channel_id=1, source_target_pairs={{0,24},{4,28},{8,16},{12,20},{16,8},{20,12},{24,0},{28,4},{1,25},{... | collective-permute-start | bytes 1081352 | tf_op jit(solution)/shard_map/ppermute | solution.py:308
  109.5 9.1 %collective-permute-start.26 = (bf16[4,224,512]{2,1,0:T(8,128)(2,1)S(1)}, bf16[4,224,512]{2,1,0:T(8,128)(2,1)S(1)}, u32[]{:S(2)}, u32[]{:S(2)}) collective-permute-start(bf16[4,224,512]{2,1,0:T(8,128)(2,1)S(1)} %get-tuple-element.168), channel_id=1, source_target_pairs={{0,4},{4,0},{8,12},{12,8},{16,20},{20,16},{24,28},{28,24},{1,5},{5... | collective-permute-start | bytes 2752520 | tf_op jit(solution)/shard_map/ppermute | solution.py:308
  109.6 17.7 %collective-permute-start.27 = (bf16[144,512]{1,0:T(8,128)(2,1)S(1)}, bf16[144,512]{1,0:T(8,128)(2,1)S(1)}, u32[]{:S(2)}, u32[]{:S(2)}) collective-permute-start(bf16[144,512]{1,0:T(8,128)(2,1)S(1)} %add_convert_fusion.12), channel_id=1, source_target_pairs={{0,2},{1,3},{2,0},{3,1},{4,6},{5,7},{6,4},{7,5},{8,10},{9,11},{10,... | collective-permute-start | bytes 442376 | tf_op jit(solution)/shard_map/ppermute | solution.py:308
  112.3 21.3 %collective-permute-start.33 = (bf16[336,512]{1,0:T(8,128)(2,1)S(1)}, bf16[336,512]{1,0:T(8,128)(2,1)S(1)}, u32[]{:S(2)}, u32[]{:S(2)}) collective-permute-start(bf16[336,512]{1,0:T(8,128)(2,1)S(1)} %get-tuple-element.180), channel_id=1, source_target_pairs={{0,1},{1,2},{2,3},{3,0},{4,5},{5,6},{6,7},{7,4},{8,9},{9,10},{10,1... | collective-permute-start | bytes 1032200 | tf_op jit(solution)/shard_map/ppermute | solution.py:40
  127.3 8.5 %collective-permute-start.30 = (bf16[224,512]{1,0:T(8,128)(2,1)S(1)}, bf16[224,512]{1,0:T(8,128)(2,1)S(1)}, u32[]{:S(2)}, u32[]{:S(2)}) collective-permute-start(bf16[224,512]{1,0:T(8,128)(2,1)S(1)} %get-tuple-element.177), channel_id=1, source_target_pairs={{0,8},{4,12},{8,0},{12,4},{16,24},{20,28},{24,16},{28,20},{1,9},{5... | collective-permute-start | bytes 688136 | tf_op jit(solution)/shard_map/ppermute | solution.py:308
  128.8 12.0 %collective-permute-start.31 = (bf16[224,512]{1,0:T(8,128)(2,1)S(1)}, bf16[224,512]{1,0:T(8,128)(2,1)S(1)}, u32[]{:S(2)}, u32[]{:S(2)}) collective-permute-start(bf16[224,512]{1,0:T(8,128)(2,1)S(1)} %get-tuple-element.178), channel_id=1, source_target_pairs={{0,16},{4,20},{8,24},{12,28},{16,0},{20,4},{24,8},{28,12},{1,17},{... | collective-permute-start | bytes 688136 | tf_op jit(solution)/shard_map/ppermute | solution.py:308
  129.6 11.2 %collective-permute-start.32 = (bf16[224,512]{1,0:T(8,128)(2,1)S(1)}, bf16[224,512]{1,0:T(8,128)(2,1)S(1)}, u32[]{:S(2)}, u32[]{:S(2)}) collective-permute-start(bf16[224,512]{1,0:T(8,128)(2,1)S(1)} %get-tuple-element.179), channel_id=1, source_target_pairs={{0,24},{4,28},{8,16},{12,20},{16,8},{20,12},{24,0},{28,4},{1,25},{... | collective-permute-start | bytes 688136 | tf_op jit(solution)/shard_map/ppermute | solution.py:308
  133.5 10.0 %collective-permute-start.34 = (bf16[176,512]{1,0:T(8,128)(2,1)S(1)}, bf16[176,512]{1,0:T(8,128)(2,1)S(1)}, u32[]{:S(2)}, u32[]{:S(2)}) collective-permute-start(bf16[176,512]{1,0:T(8,128)(2,1)S(1)} %add_convert_fusion.10), channel_id=1, source_target_pairs={{0,2},{1,3},{2,0},{3,1},{4,6},{5,7},{6,4},{7,5},{8,10},{9,11},{10,... | collective-permute-start | bytes 540680 | tf_op jit(solution)/shard_map/ppermute | solution.py:308
  143.9 8.2 %collective-permute-start.29 = (bf16[144,512]{1,0:T(8,128)(2,1)S(1)}, bf16[144,512]{1,0:T(8,128)(2,1)S(1)}, u32[]{:S(2)}, u32[]{:S(2)}) collective-permute-start(bf16[144,512]{1,0:T(8,128)(2,1)S(1)} %add_convert_fusion.11.half), channel_id=1, source_target_pairs={{0,1},{1,0},{2,3},{3,2},{4,5},{5,4},{6,7},{7,6},{8,9},{9,8},{10,11... | collective-permute-start | bytes 442376 | tf_op jit(solution)/shard_map/ppermute | solution.py:308
  149.8 6.7 %collective-permute-start.37 = (bf16[112,512]{1,0:T(8,128)(2,1)S(1)}, bf16[112,512]{1,0:T(8,128)(2,1)S(1)}, u32[]{:S(2)}, u32[]{:S(2)}) collective-permute-start(bf16[112,512]{1,0:T(8,128)(2,1)S(1)} %add_convert_fusion.14), channel_id=1, source_target_pairs={{0,2},{1,3},{2,0},{3,1},{4,6},{5,7},{6,4},{7,5},{8,10},{9,11},{10,... | collective-permute-start | bytes 344072 | tf_op jit(solution)/shard_map/ppermute | solution.py:308
  153.5 7.6 %collective-permute-start.35 = (bf16[176,512]{1,0:T(8,128)(2,1)S(1)}, bf16[176,512]{1,0:T(8,128)(2,1)S(1)}, u32[]{:S(2)}, u32[]{:S(2)}) collective-permute-start(bf16[176,512]{1,0:T(8,128)(2,1)S(1)} %add_convert_fusion.9.half), channel_id=1, source_target_pairs={{0,1},{1,0},{2,3},{3,2},{4,5},{5,4},{6,7},{7,6},{8,9},{9,8},{10,11... | collective-permute-start | bytes 540680 | tf_op jit(solution)/shard_map/ppermute | solution.py:308
  (43 other events, 215.1 us)
Sparse Core Ops, SparseCore 0:
  20.5 33.1 all-gather.2

commit v7 on v5

--- a/solution.py
+++ b/solution.py
@@ -358,6 +358,10 @@
     first, second = list(first), list(second)
     out = lax.optimization_barrier((*first, *second))
     return list(out[: len(first)]), list(out[len(first) :])
+
+
+def after(first, second):
+    return list(first), tie(first, second)[1]
 
 
 def block_of(slab, c, depth):
@@ -877,22 +881,22 @@
         scratch=[pltpu.VMEM((WINDOWS, WIN, SLOT, D), F32)],
     )
     half_a = add_pair(keep_a, near_a)
-    (half_a,), (attn_other, tok_sent) = tie([half_a], [attn_other, tok_sent])
+    (half_a,), (attn_other, tok_sent) = after([half_a], [attn_other, tok_sent])
     far_a = exchange(half_a, "seq", 2)
     attn_came = exchange(attn_other, "shard", 1)
     keep_b, send = add_chips(same_b, came_b, parts_b, 10_000_000_000)
-    (send,), (attn_came,) = tie([send], [attn_came])
+    (send,), (attn_came,) = after([send], [attn_came])
     near_b = exchange(send, "seq", 1)
-    sums, (far_a,) = tie(add_cores(attn_same, attn_came), [far_a])
+    sums, (far_a,) = after(add_cores(attn_same, attn_came), [far_a])
     attn_parts = to_chips(sums)
     half_a = seq_rest(add_pair(half_a, far_a))
-    (half_a,), (near_b, tok_sent) = tie([half_a], [near_b, tok_sent])
+    (half_a,), (near_b, tok_sent) = after([half_a], [near_b, tok_sent])
     tok_halo = shifted_2(tok_sent, "seq", 1)
     half_b = add_pair(keep_b, near_b)
     far_b = exchange(half_b, "seq", 2)
-    attn_parts, (far_b,) = tie(attn_parts, [far_b])
+    attn_parts, (far_b,) = after(attn_parts, [far_b])
     half_b = seq_rest(add_pair(half_b, far_b))
-    (half_b,), attn_parts = tie([half_b], attn_parts)
+    (half_b,), attn_parts = after([half_b], attn_parts)
     keep, send = add_chips(attn_same, attn_came, attn_parts)
     def unpack(body, params, half, back):
         return kernel_call(
@@ -921,7 +925,7 @@
     out_grads = unpack(unpack_out_body, (w_out, w_proj, *[column] * 4), half_b, back_b)
     grad_tokens = joined(tok_halo, tok_kept)
     output = joined(out_halo, out_kept)
-    early, (back,) = tie([*in_grads, *out_grads, grad_tokens, output], [back])
+    early, (back,) = after([*in_grads, *out_grads, grad_tokens, output], [back])
     in_grads, out_grads, (grad_tokens, output) = early[:2], early[2:8], early[8:]
     attn_grads = unpack(unpack_attn_body, attn_params, half, back)
     g_wout, g_wproj, g_gain, g_offset, g_bout, g_bproj = out_grads

time: 169 us -> 166 us (0.982); the launches traced: 169 us -> 163 us
  waiting for transfers between devices: 49 us -> 37.4 us
  starting transfers between devices: 37.5 us -> 43.4 us
    ppermute x35, waiting for transfers between devices: 49 us -> 34.3 us  [exchange(): return lax.ppermute(value, axis, [(i, i ^ mask) for i in range(peers)])]
    ppermute x35, starting transfers between devices: 29.6 us -> 35.6 us  [exchange(): return lax.ppermute(value, axis, [(i, i ^ mask) for i in range(peers)])]
    ppermute x4, waiting for transfers between devices: 0.01 us -> 3.05 us  [shifted_2(): lax.ppermute(value, axis, [(i, (i + by) % peers) for i in range(peers)])]
  transfers between devices with their start and end apart: 40 -> 40, of which waited for: 19 -> 16; matrix products, arithmetic and copies ran while one was open for 6% -> 6% of each run, Pallas kernels for 17% -> 18%
where the time goes in v7:
time: 166 us; the launch traced here: 163 us
  Pallas kernels  47.3 us (28%)
  starting transfers between devices  43.4 us (26%)
  waiting for transfers between devices  37.4 us (23%)
  local copies, waits for them, and re-layouts  16.5 us (10%)
  between operations  14.8 us (9%)
  other arithmetic  3.72 us (2%)
    pallas_call x14, Pallas kernels, kernel_call(): pl.pallas_call(body, out_shape=tuple(outs), in_specs=in_specs, out_specs=...  47.3 us
    ppermute x35, starting transfers between devices, exchange(): return lax.ppermute(value, axis, [(i, i ^ mask) for i in range(peers)])  35.6 us
    ppermute x35, waiting for transfers between devices, exchange(): return lax.ppermute(value, axis, [(i, i ^ mask) for i in range(peers)])  34.3 us
    unnamed x84, local copies, waits for them, and re-layouts  13.1 us
    ppermute x4, starting transfers between devices, shifted_2(): lax.ppermute(value, axis, [(i, (i + by) % peers) for i in range(peers)])  7.79 us
  transfers between devices with their start and end apart: 40, of which 16 were waited for; matrix products, arithmetic and copies ran while one was open for 6% of the time, Pallas kernels for 18%

profile of v7, /device:TPU:0, one launch (start us, length us, event | category | flops | bytes accessed | tf_op | source)
XLA Modules:
  0.0 163.2 jit_solution(7688522662533156666)
XLA Ops:
  7.2 2.9 %shard_map.271 = (bf16[288,512]{1,0:T(8,128)(2,1)}, bf16[288,512]{1,0:T(8,128)(2,1)}, bf16[256,512]{1,0:T(8,128)(2,1)}) custom-call(bf16[1,64]{1,0:T(2,128)(2,1)} %bitcast.87, bf16[1,64]{1,0:T(2,128)(2,1)} %bitcast.88, bf16[64,1536]{1,0:T(8,128)(2,1)} %wqkv.1, bf16[2,64]{1,0:T(2,128)(2,1)} %bqv.1, bf16[2,169]{1,0:T(2,128)(2,1)} %bitcast.86, ...), custom_call_target="tpu_custom_call" | custom-call | flops 1024 | bytes 1024 | tf_op jit(solution)/shard_map/pallas_call | solution.py:150
  10.1 2.9 %collective-permute-start.1 = (bf16[288,512]{1,0:T(8,128)(2,1)}, bf16[288,512]{1,0:T(8,128)(2,1)S(1)}, u32[]{:S(2)}, u32[]{:S(2)}) collective-permute-start(bf16[288,512]{1,0:T(8,128)(2,1)} %get-tuple-element.98), channel_id=1, source_target_pairs={{0,8},{4,12},{8,0},{12,4},{16,24},{20,28},{24,16},{28,20},{1,9},{5... | collective-permute-start | bytes 884744 | tf_op jit(solution)/shard_map/ppermute | solution.py:308
  13.0 1.5 collective-permute-start.3
  14.6 1.7 %slice_bitcast_fusion.1 = bf16[3,112,512]{2,1,0:T(8,128)(2,1)} fusion(bf16[1,7,112,512]{3,2,1,0:T(8,128)(2,1)} %param.16), kind=kLoop, calls=%fused_computation.17 | loop fusion | bytes 688128 | tf_op jit(solution)/shard_map/slice | solution.py:775
  16.3 4.1 %collective-permute-start.7 = (bf16[3,112,512]{2,1,0:T(8,128)(2,1)}, bf16[3,112,512]{2,1,0:T(8,128)(2,1)S(1)}, u32[]{:S(2)}, u32[]{:S(2)}) collective-permute-start(bf16[3,112,512]{2,1,0:T(8,128)(2,1)} %slice_bitcast_fusion.1), channel_id=1, source_target_pairs={{0,3},{1,0},{2,1},{3,2},{4,7},{5,4},{6,5},{7,6},{8,11},{9,8},{10,9... | collective-permute-start | bytes 1032200 | tf_op jit(solution)/shard_map/ppermute | solution.py:40
  21.2 6.9 %collective-permute-done.3 = bf16[288,512]{1,0:T(8,128)(2,1)S(1)} collective-permute-done((bf16[288,512]{1,0:T(8,128)(2,1)}, bf16[288,512]{1,0:T(8,128)(2,1)S(1)}, u32[]{:S(2)}, u32[]{:S(2)}) %collective-permute-start.3) | collective-permute-done | bytes 294944 | tf_op jit(solution)/shard_map/ppermute | solution.py:308
  32.3 1.5 collective-permute-start.14
  37.1 3.7 %collective-permute-start.8 = (bf16[3,112,512]{2,1,0:T(8,128)(2,1)S(1)}, bf16[3,112,512]{2,1,0:T(8,128)(2,1)S(1)}, u32[]{:S(2)}, u32[]{:S(2)}) collective-permute-start(bf16[3,112,512]{2,1,0:T(8,128)(2,1)S(1)} %slice_bitcast_fusion), channel_id=1, source_target_pairs={{0,3},{1,0},{2,1},{3,2},{4,7},{5,4},{6,5},{7,6},{8,11},{9,8},{10,9... | collective-permute-start | bytes 1032200 | tf_op jit(solution)/shard_map/ppermute | solution.py:40
  40.8 2.4 %shard_map.272 = (bf16[896,512]{1,0:T(8,128)(2,1)S(1)}, bf16[896,512]{1,0:T(8,128)(2,1)S(1)}, bf16[896,512]{1,0:T(8,128)(2,1)S(1)}, bf16[896,512]{1,0:T(8,128)(2,1)S(1)}) custom-call(bf16[7,112,512]{2,1,0:T(8,128)(2,1)S(1)} %bitcast.78, bf16[3,112,512]{2,1,0:T(8,128)(2,1)S(1)} %collective-permute-done.7.halo, ...), custom_call_target="tpu_custom_call" | custom-call | flops 1024 | bytes 1024 | tf_op jit(solution)/shard_map/pallas_call | solution.py:150
  43.4 7.1 %shard_map.273 = (bf16[8,4,112,256]{3,2,1,0:T(8,128)(2,1)S(1)}, bf16[784,512]{1,0:T(8,128)(2,1)S(1)}, f32[784,512]{1,0:T(8,128)S(1)}) custom-call(bf16[8,288,512]{2,1,0:T(8,128)(2,1)S(1)} %bitcast_dynamic-update-slice_fusion.slab.attn_slab, f32[16,56,128]{2,1,0:T(8,128)S(1)} %broadcast_in_dim.35.reg_rows, f32[16,1,256]{2,1,0:T(1,128)S(1)} %tile.9.reg_lanes, ...), custom_call_target="tpu_custom_call" | custom-call | flops 1024 | bytes 1024 | tf_op jit(solution)/shard_map/pallas_call | solution.py:150
  57.6 1.6 copy-done.13
  59.2 1.7 %copy-done.14 = bf16[2304,512]{1,0:T(8,128)(2,1)S(1)} copy-done((bf16[2304,512]{1,0:T(8,128)(2,1)S(1)}, bf16[2304,512]{1,0:T(8,128)(2,1)}, u32[]{:S(2)}) %copy-start.14) | copy-done | bytes 2359320
  63.0 13.7 %shard_map.274 = (f32[448,512]{1,0:T(8,128)S(1)}, bf16[336,512]{1,0:T(8,128)(2,1)S(1)}, bf16[784,512]{1,0:T(8,128)(2,1)S(1)}, bf16[784,2048]{1,0:T(8,128)(2,1)S(...) custom-call(f32[784,512]{1,0:T(8,128)S(1)} %copy-done.11, ...), custom_call_target="tpu_custom_call" | custom-call | flops 1024 | bytes 1024 | tf_op jit(solution)/shard_map/pallas_call | solution.py:150
  76.9 5.5 %shard_map.275 = (f32[784,512]{1,0:T(8,128)S(1)}, bf16[896,512]{1,0:T(8,128)(2,1)S(1)}, bf16[4,352,512]{2,1,0:T(8,128)(2,1)S(1)}, bf16[4,352,512]{2,1,0:T(8,128)(2,1)S(1)}) custom-call(f32[784,512]{1,0:T(8,128)S(1)} %copy-done.11, bf16[784,512]{1,0:T(8,128)(2,1)S(1)} %get-tuple-element.115.cot, bf16[784,2048]{1,0:T(8,128)(2,1)S(1)} %get-tuple-element.116.actives, ...), custom_call_target="tpu_custom_call" | custom-call | flops 1024 | bytes 1024 | tf_op jit(solution)/shard_map/pallas_call | solution.py:150
  86.7 3.0 %shard_map.277 = (bf16[448,1536]{1,0:T(8,128)(2,1)S(1)}, f32[4,56,256]{2,1,0:T(8,128)S(1)}) custom-call(bf16[896,512]{1,0:T(8,128)(2,1)S(1)} %copy-done.3, bf16[896,512]{1,0:T(8,128)(2,1)S(1)} %copy-done.5, bf16[896,512]{1,0:T(8,128)(2,1)S(1)} %copy-done.7, bf16[8,4,112,256]{3,2,1,0:T(8,128)(2,1)S(1)} %copy-done.9, ...), custom_call_target="tpu_custom_call" | custom-call | flops 1024 | bytes 1024 | tf_op jit(solution)/shard_map/pallas_call | solution.py:150
  90.1 3.0 %shard_map.278 = (bf16[448,1536]{1,0:T(8,128)(2,1)S(1)}, f32[4,56,256]{2,1,0:T(8,128)S(1)}) custom-call(bf16[896,512]{1,0:T(8,128)(2,1)S(1)} %copy-done.3, bf16[896,512]{1,0:T(8,128)(2,1)S(1)} %copy-done.5, bf16[896,512]{1,0:T(8,128)(2,1)S(1)} %copy-done.7, bf16[8,4,112,256]{3,2,1,0:T(8,128)(2,1)S(1)} %copy-done.9, ...), custom_call_target="tpu_custom_call" | custom-call | flops 1024 | bytes 1024 | tf_op jit(solution)/shard_map/pallas_call | solution.py:150
  93.1 4.9 %collective-permute-done.19.refs_1_ = bf16[288,512]{1,0:T(8,128)(2,1)S(1)} collective-permute-done((bf16[288,512]{1,0:T(8,128)(2,1)S(1)}, bf16[288,512]{1,0:T(8,128)(2,1)S(1)}, u32[]{:S(2)}, u32[]{:S(2)}) %collective-permute-start.19) | collective-permute-done | bytes 294944 | tf_op jit(solution)/shard_map/ppermute | solution.py:308
  97.9 1.8 %collective-permute-done.20.refs_2_ = bf16[288,512]{1,0:T(8,128)(2,1)S(1)} collective-permute-done((bf16[288,512]{1,0:T(8,128)(2,1)S(1)}, bf16[288,512]{1,0:T(8,128)(2,1)S(1)}, u32[]{:S(2)}, u32[]{:S(2)}) %collective-permute-start.20) | collective-permute-done | bytes 294944 | tf_op jit(solution)/shard_map/ppermute | solution.py:308
  100.6 1.7 %collective-permute-start.24 = (bf16[352,512]{1,0:T(8,128)(2,1)S(1)}, bf16[352,512]{1,0:T(8,128)(2,1)S(1)}, u32[]{:S(2)}, u32[]{:S(2)}) collective-permute-start(bf16[352,512]{1,0:T(8,128)(2,1)S(1)} %get-tuple-element.144), channel_id=1, source_target_pairs={{0,16},{4,20},{8,24},{12,28},{16,0},{20,4},{24,8},{28,12},{1,17},{... | collective-permute-start | bytes 1081352 | tf_op jit(solution)/shard_map/ppermute | solution.py:308
  103.5 5.1 %shard_map.279 = (f32[448,512]{1,0:T(8,128)S(1)}, bf16[336,512]{1,0:T(8,128)(2,1)S(1)}, bf16[4,224,512]{2,1,0:T(8,128)(2,1)S(1)}, bf16[4,224,512]{2,1,0:T(8,128)(2,1)S(1)}) custom-call(f32[784,512]{1,0:T(8,128)S(1)} %get-tuple-element.137.grad_mixed, bf16[7,112,512]{2,1,0:T(8,128)(2,1)S(1)} %bitcast.80, ...), custom_call_target="tpu_custom_call" | custom-call | flops 1024 | bytes 1024 | tf_op jit(solution)/shard_map/pallas_call | solution.py:150
  108.7 2.3 %collective-permute-start.27 = (bf16[144,512]{1,0:T(8,128)(2,1)S(1)}, bf16[144,512]{1,0:T(8,128)(2,1)S(1)}, u32[]{:S(2)}, u32[]{:S(2)}) collective-permute-start(bf16[144,512]{1,0:T(8,128)(2,1)S(1)} %add_convert_fusion.12), channel_id=1, source_target_pairs={{0,2},{1,3},{2,0},{3,1},{4,6},{5,7},{6,4},{7,5},{8,10},{9,11},{10,... | collective-permute-start | bytes 442376 | tf_op jit(solution)/shard_map/ppermute | solution.py:308
  111.4 6.1 %collective-permute-done.24.refs_1_ = bf16[352,512]{1,0:T(8,128)(2,1)S(1)} collective-permute-done((bf16[352,512]{1,0:T(8,128)(2,1)S(1)}, bf16[352,512]{1,0:T(8,128)(2,1)S(1)}, u32[]{:S(2)}, u32[]{:S(2)}) %collective-permute-start.24) | collective-permute-done | bytes 360480 | tf_op jit(solution)/shard_map/ppermute | solution.py:308
  117.7 1.7 %collective-permute-start.28 = (bf16[176,512]{1,0:T(8,128)(2,1)S(1)}, bf16[176,512]{1,0:T(8,128)(2,1)S(1)}, u32[]{:S(2)}, u32[]{:S(2)}) collective-permute-start(bf16[176,512]{1,0:T(8,128)(2,1)S(1)} %get-tuple-element.146), channel_id=1, source_target_pairs={{0,1},{1,0},{2,3},{3,2},{4,5},{5,4},{6,7},{7,6},{8,9},{9,8},{10,11... | collective-permute-start | bytes 540680 | tf_op jit(solution)/shard_map/ppermute | solution.py:308
  119.7 1.7 %collective-permute-start.30 = (bf16[224,512]{1,0:T(8,128)(2,1)S(1)}, bf16[224,512]{1,0:T(8,128)(2,1)S(1)}, u32[]{:S(2)}, u32[]{:S(2)}) collective-permute-start(bf16[224,512]{1,0:T(8,128)(2,1)S(1)} %get-tuple-element.185), channel_id=1, source_target_pairs={{0,8},{4,12},{8,0},{12,4},{16,24},{20,28},{24,16},{28,20},{1,9},{5... | collective-permute-start | bytes 688136 | tf_op jit(solution)/shard_map/ppermute | solution.py:308
  121.7 1.5 collective-permute-start.32
  123.3 4.6 %collective-permute-start.33 = (bf16[176,512]{1,0:T(8,128)(2,1)S(1)}, bf16[176,512]{1,0:T(8,128)(2,1)S(1)}, u32[]{:S(2)}, u32[]{:S(2)}) collective-permute-start(bf16[176,512]{1,0:T(8,128)(2,1)S(1)} %add_convert_fusion.10), channel_id=1, source_target_pairs={{0,2},{1,3},{2,0},{3,1},{4,6},{5,7},{6,4},{7,5},{8,10},{9,11},{10,... | collective-permute-start | bytes 540680 | tf_op jit(solution)/shard_map/ppermute | solution.py:308
  127.9 5.0 %collective-permute-done.33 = bf16[176,512]{1,0:T(8,128)(2,1)S(1)} collective-permute-done((bf16[176,512]{1,0:T(8,128)(2,1)S(1)}, bf16[176,512]{1,0:T(8,128)(2,1)S(1)}, u32[]{:S(2)}, u32[]{:S(2)}) %collective-permute-start.33) | collective-permute-done | bytes 180256 | tf_op jit(solution)/shard_map/ppermute | solution.py:308
  133.3 2.1 %collective-permute-start.36 = (bf16[144,512]{1,0:T(8,128)(2,1)S(1)}, bf16[144,512]{1,0:T(8,128)(2,1)S(1)}, u32[]{:S(2)}, u32[]{:S(2)}) collective-permute-start(bf16[144,512]{1,0:T(8,128)(2,1)S(1)} %add_convert_fusion.11.half), channel_id=1, source_target_pairs={{0,1},{1,0},{2,3},{3,2},{4,5},{5,4},{6,7},{7,6},{8,9},{9,8},{10,11... | collective-permute-start | bytes 442376 | tf_op jit(solution)/shard_map/ppermute | solution.py:308
  135.5 5.9 %collective-permute-done.34 = bf16[112,512]{1,0:T(8,128)(2,1)S(1)} collective-permute-done((bf16[112,512]{1,0:T(8,128)(2,1)S(1)}, bf16[112,512]{1,0:T(8,128)(2,1)S(1)}, u32[]{:S(2)}, u32[]{:S(2)}) %collective-permute-start.34) | collective-permute-done | bytes 114720 | tf_op jit(solution)/shard_map/ppermute | solution.py:308
  144.8 1.7 %collective-permute-start.37 = (bf16[176,512]{1,0:T(8,128)(2,1)S(1)}, bf16[176,512]{1,0:T(8,128)(2,1)S(1)}, u32[]{:S(2)}, u32[]{:S(2)}) collective-permute-start(bf16[176,512]{1,0:T(8,128)(2,1)S(1)} %add_convert_fusion.9.half), channel_id=1, source_target_pairs={{0,1},{1,0},{2,3},{3,2},{4,5},{5,4},{6,7},{7,6},{8,9},{9,8},{10,11... | collective-permute-start | bytes 540680 | tf_op jit(solution)/shard_map/ppermute | solution.py:308
  146.5 3.0 %collective-permute-done.29 = bf16[336,512]{1,0:T(8,128)(2,1)S(1)} collective-permute-done((bf16[336,512]{1,0:T(8,128)(2,1)S(1)}, bf16[336,512]{1,0:T(8,128)(2,1)S(1)}, u32[]{:S(2)}, u32[]{:S(2)}) %collective-permute-start.29) | collective-permute-done | bytes 344096 | tf_op jit(solution)/shard_map/ppermute | solution.py:40
  150.0 1.6 collective-permute-start.38
  (174 shorter events, 34.5 us)
Async XLA Ops:
  7.2 49.0 %all-gather.3.cloned.1.call-start = ((), (), s32[]{:S(2)}) async-start(), calls=%async_computation | async-start | bytes 2654208 | tf_op jit(solution)/shard_map/all_gather | solution.py:773
  10.1 11.1 %collective-permute-start.1 = (bf16[288,512]{1,0:T(8,128)(2,1)}, bf16[288,512]{1,0:T(8,128)(2,1)S(1)}, u32[]{:S(2)}, u32[]{:S(2)}) collective-permute-start(bf16[288,512]{1,0:T(8,128)(2,1)} %get-tuple-element.98), channel_id=1, source_target_pairs={{0,8},{4,12},{8,0},{12,4},{16,24},{20,28},{24,16},{28,20},{1,9},{5... | collective-permute-start | bytes 884744 | tf_op jit(solution)/shard_map/ppermute | solution.py:308
  13.0 15.0 %collective-permute-start.3 = (bf16[288,512]{1,0:T(8,128)(2,1)}, bf16[288,512]{1,0:T(8,128)(2,1)S(1)}, u32[]{:S(2)}, u32[]{:S(2)}) collective-permute-start(bf16[288,512]{1,0:T(8,128)(2,1)} %get-tuple-element.98), channel_id=1, source_target_pairs={{0,16},{4,20},{8,24},{12,28},{16,0},{20,4},{24,8},{28,12},{1,17},{... | collective-permute-start | bytes 884744 | tf_op jit(solution)/shard_map/ppermute | solution.py:308
  14.6 13.5 %collective-permute-start.5 = (bf16[288,512]{1,0:T(8,128)(2,1)}, bf16[288,512]{1,0:T(8,128)(2,1)S(1)}, u32[]{:S(2)}, u32[]{:S(2)}) collective-permute-start(bf16[288,512]{1,0:T(8,128)(2,1)} %get-tuple-element.98), channel_id=1, source_target_pairs={{0,24},{4,28},{8,16},{12,20},{16,8},{20,12},{24,0},{28,4},{1,25},{... | collective-permute-start | bytes 884744 | tf_op jit(solution)/shard_map/ppermute | solution.py:308
  14.6 15.2 %collective-permute-start = (bf16[288,512]{1,0:T(8,128)(2,1)}, bf16[288,512]{1,0:T(8,128)(2,1)S(1)}, u32[]{:S(2)}, u32[]{:S(2)}) collective-permute-start(bf16[288,512]{1,0:T(8,128)(2,1)} %get-tuple-element.98), channel_id=1, source_target_pairs={{0,4},{4,0},{8,12},{12,8},{16,20},{20,16},{24,28},{28,24},{1,5},{5... | collective-permute-start | bytes 884744 | tf_op jit(solution)/shard_map/ppermute | solution.py:308
  16.3 20.8 %collective-permute-start.7 = (bf16[3,112,512]{2,1,0:T(8,128)(2,1)}, bf16[3,112,512]{2,1,0:T(8,128)(2,1)S(1)}, u32[]{:S(2)}, u32[]{:S(2)}) collective-permute-start(bf16[3,112,512]{2,1,0:T(8,128)(2,1)} %slice_bitcast_fusion.1), channel_id=1, source_target_pairs={{0,3},{1,0},{2,1},{3,2},{4,7},{5,4},{6,5},{7,6},{8,11},{9,8},{10,9... | collective-permute-start | bytes 1032200 | tf_op jit(solution)/shard_map/ppermute | solution.py:40
  21.2 8.6 %collective-permute-start.2 = (bf16[288,512]{1,0:T(8,128)(2,1)S(1)}, bf16[288,512]{1,0:T(8,128)(2,1)S(1)}, u32[]{:S(2)}, u32[]{:S(2)}) collective-permute-start(bf16[288,512]{1,0:T(8,128)(2,1)S(1)} %collective-permute-done.1), channel_id=1, source_target_pairs={{0,4},{4,0},{8,12},{12,8},{16,20},{20,16},{24,28},{28,24},{1,5},{5... | collective-permute-start | bytes 884744 | tf_op jit(solution)/shard_map/ppermute | solution.py:308
  30.0 22.2 %collective-permute-start.9 = (bf16[256,512]{1,0:T(8,128)(2,1)}, bf16[256,512]{1,0:T(8,128)(2,1)S(1)}, u32[]{:S(2)}, u32[]{:S(2)}) collective-permute-start(bf16[256,512]{1,0:T(8,128)(2,1)} %get-tuple-element.111), channel_id=1, source_target_pairs={{0,4},{4,0},{8,12},{12,8},{16,20},{20,16},{24,28},{28,24},{1,5},{5... | collective-permute-start | bytes 786440 | tf_op jit(solution)/shard_map/ppermute | solution.py:308
  30.2 21.4 %collective-permute-start.10 = (bf16[256,512]{1,0:T(8,128)(2,1)}, bf16[256,512]{1,0:T(8,128)(2,1)S(1)}, u32[]{:S(2)}, u32[]{:S(2)}) collective-permute-start(bf16[256,512]{1,0:T(8,128)(2,1)} %get-tuple-element.111), channel_id=1, source_target_pairs={{0,8},{4,12},{8,0},{12,4},{16,24},{20,28},{24,16},{28,20},{1,9},{5... | collective-permute-start | bytes 786440 | tf_op jit(solution)/shard_map/ppermute | solution.py:308
  31.1 20.5 %collective-permute-start.12 = (bf16[256,512]{1,0:T(8,128)(2,1)}, bf16[256,512]{1,0:T(8,128)(2,1)S(1)}, u32[]{:S(2)}, u32[]{:S(2)}) collective-permute-start(bf16[256,512]{1,0:T(8,128)(2,1)} %get-tuple-element.111), channel_id=1, source_target_pairs={{0,16},{4,20},{8,24},{12,28},{16,0},{20,4},{24,8},{28,12},{1,17},{... | collective-permute-start | bytes 786440 | tf_op jit(solution)/shard_map/ppermute | solution.py:308
  32.3 19.8 %collective-permute-start.14 = (bf16[256,512]{1,0:T(8,128)(2,1)}, bf16[256,512]{1,0:T(8,128)(2,1)S(1)}, u32[]{:S(2)}, u32[]{:S(2)}) collective-permute-start(bf16[256,512]{1,0:T(8,128)(2,1)} %get-tuple-element.111), channel_id=1, source_target_pairs={{0,24},{4,28},{8,16},{12,20},{16,8},{20,12},{24,0},{28,4},{1,25},{... | collective-permute-start | bytes 786440 | tf_op jit(solution)/shard_map/ppermute | solution.py:308
  37.1 18.3 %collective-permute-start.8 = (bf16[3,112,512]{2,1,0:T(8,128)(2,1)S(1)}, bf16[3,112,512]{2,1,0:T(8,128)(2,1)S(1)}, u32[]{:S(2)}, u32[]{:S(2)}) collective-permute-start(bf16[3,112,512]{2,1,0:T(8,128)(2,1)S(1)} %slice_bitcast_fusion), channel_id=1, source_target_pairs={{0,3},{1,0},{2,1},{3,2},{4,7},{5,4},{6,5},{7,6},{8,11},{9,8},{10,9... | collective-permute-start | bytes 1032200 | tf_op jit(solution)/shard_map/ppermute | solution.py:40
  82.4 7.3 %collective-permute-start.21 = (bf16[4,352,512]{2,1,0:T(8,128)(2,1)S(1)}, bf16[4,352,512]{2,1,0:T(8,128)(2,1)S(1)}, u32[]{:S(2)}, u32[]{:S(2)}) collective-permute-start(bf16[4,352,512]{2,1,0:T(8,128)(2,1)S(1)} %get-tuple-element.128), channel_id=1, source_target_pairs={{0,4},{4,0},{8,12},{12,8},{16,20},{20,16},{24,28},{28,24},{1,5},{5... | collective-permute-start | bytes 4325384 | tf_op jit(solution)/shard_map/ppermute | solution.py:308
  83.1 9.9 %collective-permute-start.18 = (bf16[288,512]{1,0:T(8,128)(2,1)S(1)}, bf16[288,512]{1,0:T(8,128)(2,1)S(1)}, u32[]{:S(2)}, u32[]{:S(2)}) collective-permute-start(bf16[288,512]{1,0:T(8,128)(2,1)S(1)} %get-tuple-element.121), channel_id=1, source_target_pairs={{0,8},{4,12},{8,0},{12,4},{16,24},{20,28},{24,16},{28,20},{1,9},{5... | collective-permute-start | bytes 884744 | tf_op jit(solution)/shard_map/ppermute | solution.py:308
  84.1 13.8 %collective-permute-start.19 = (bf16[288,512]{1,0:T(8,128)(2,1)S(1)}, bf16[288,512]{1,0:T(8,128)(2,1)S(1)}, u32[]{:S(2)}, u32[]{:S(2)}) collective-permute-start(bf16[288,512]{1,0:T(8,128)(2,1)S(1)} %get-tuple-element.122), channel_id=1, source_target_pairs={{0,16},{4,20},{8,24},{12,28},{16,0},{20,4},{24,8},{28,12},{1,17},{... | collective-permute-start | bytes 884744 | tf_op jit(solution)/shard_map/ppermute | solution.py:308
  85.3 14.4 %collective-permute-start.20 = (bf16[288,512]{1,0:T(8,128)(2,1)S(1)}, bf16[288,512]{1,0:T(8,128)(2,1)S(1)}, u32[]{:S(2)}, u32[]{:S(2)}) collective-permute-start(bf16[288,512]{1,0:T(8,128)(2,1)S(1)} %get-tuple-element.123), channel_id=1, source_target_pairs={{0,24},{4,28},{8,16},{12,20},{16,8},{20,12},{24,0},{28,4},{1,25},{... | collective-permute-start | bytes 884744 | tf_op jit(solution)/shard_map/ppermute | solution.py:308
  86.7 16.9 %collective-permute-start.16 = (bf16[336,512]{1,0:T(8,128)(2,1)S(1)}, bf16[336,512]{1,0:T(8,128)(2,1)S(1)}, u32[]{:S(2)}, u32[]{:S(2)}) collective-permute-start(bf16[336,512]{1,0:T(8,128)(2,1)S(1)} %get-tuple-element.112), channel_id=1, source_target_pairs={{0,1},{1,2},{2,3},{3,0},{4,5},{5,6},{6,7},{7,4},{8,9},{9,10},{10,1... | collective-permute-start | bytes 1032200 | tf_op jit(solution)/shard_map/ppermute | solution.py:40
  99.9 8.7 %collective-permute-start.22 = (bf16[144,512]{1,0:T(8,128)(2,1)S(1)}, bf16[144,512]{1,0:T(8,128)(2,1)S(1)}, u32[]{:S(2)}, u32[]{:S(2)}) collective-permute-start(bf16[144,512]{1,0:T(8,128)(2,1)S(1)} %get-tuple-element.136), channel_id=1, source_target_pairs={{0,1},{1,0},{2,3},{3,2},{4,5},{5,4},{6,7},{7,6},{8,9},{9,8},{10,11... | collective-permute-start | bytes 442376 | tf_op jit(solution)/shard_map/ppermute | solution.py:308
  100.0 11.4 %collective-permute-start.23 = (bf16[352,512]{1,0:T(8,128)(2,1)S(1)}, bf16[352,512]{1,0:T(8,128)(2,1)S(1)}, u32[]{:S(2)}, u32[]{:S(2)}) collective-permute-start(bf16[352,512]{1,0:T(8,128)(2,1)S(1)} %get-tuple-element.143), channel_id=1, source_target_pairs={{0,8},{4,12},{8,0},{12,4},{16,24},{20,28},{24,16},{28,20},{1,9},{5... | collective-permute-start | bytes 1081352 | tf_op jit(solution)/shard_map/ppermute | solution.py:308
  100.6 16.9 %collective-permute-start.24 = (bf16[352,512]{1,0:T(8,128)(2,1)S(1)}, bf16[352,512]{1,0:T(8,128)(2,1)S(1)}, u32[]{:S(2)}, u32[]{:S(2)}) collective-permute-start(bf16[352,512]{1,0:T(8,128)(2,1)S(1)} %get-tuple-element.144), channel_id=1, source_target_pairs={{0,16},{4,20},{8,24},{12,28},{16,0},{20,4},{24,8},{28,12},{1,17},{... | collective-permute-start | bytes 1081352 | tf_op jit(solution)/shard_map/ppermute | solution.py:308
  102.4 15.1 %collective-permute-start.25 = (bf16[352,512]{1,0:T(8,128)(2,1)S(1)}, bf16[352,512]{1,0:T(8,128)(2,1)S(1)}, u32[]{:S(2)}, u32[]{:S(2)}) collective-permute-start(bf16[352,512]{1,0:T(8,128)(2,1)S(1)} %get-tuple-element.145), channel_id=1, source_target_pairs={{0,24},{4,28},{8,16},{12,20},{16,8},{20,12},{24,0},{28,4},{1,25},{... | collective-permute-start | bytes 1081352 | tf_op jit(solution)/shard_map/ppermute | solution.py:308
  108.7 14.5 %collective-permute-start.27 = (bf16[144,512]{1,0:T(8,128)(2,1)S(1)}, bf16[144,512]{1,0:T(8,128)(2,1)S(1)}, u32[]{:S(2)}, u32[]{:S(2)}) collective-permute-start(bf16[144,512]{1,0:T(8,128)(2,1)S(1)} %add_convert_fusion.12), channel_id=1, source_target_pairs={{0,2},{1,3},{2,0},{3,1},{4,6},{5,7},{6,4},{7,5},{8,10},{9,11},{10,... | collective-permute-start | bytes 442376 | tf_op jit(solution)/shard_map/ppermute | solution.py:308
  111.0 8.4 %collective-permute-start.26 = (bf16[4,224,512]{2,1,0:T(8,128)(2,1)S(1)}, bf16[4,224,512]{2,1,0:T(8,128)(2,1)S(1)}, u32[]{:S(2)}, u32[]{:S(2)}) collective-permute-start(bf16[4,224,512]{2,1,0:T(8,128)(2,1)S(1)} %get-tuple-element.149), channel_id=1, source_target_pairs={{0,4},{4,0},{8,12},{12,8},{16,20},{20,16},{24,28},{28,24},{1,5},{5... | collective-permute-start | bytes 2752520 | tf_op jit(solution)/shard_map/ppermute | solution.py:308
  119.7 13.3 %collective-permute-start.30 = (bf16[224,512]{1,0:T(8,128)(2,1)S(1)}, bf16[224,512]{1,0:T(8,128)(2,1)S(1)}, u32[]{:S(2)}, u32[]{:S(2)}) collective-permute-start(bf16[224,512]{1,0:T(8,128)(2,1)S(1)} %get-tuple-element.185), channel_id=1, source_target_pairs={{0,8},{4,12},{8,0},{12,4},{16,24},{20,28},{24,16},{28,20},{1,9},{5... | collective-permute-start | bytes 688136 | tf_op jit(solution)/shard_map/ppermute | solution.py:308
  121.3 11.6 %collective-permute-start.31 = (bf16[224,512]{1,0:T(8,128)(2,1)S(1)}, bf16[224,512]{1,0:T(8,128)(2,1)S(1)}, u32[]{:S(2)}, u32[]{:S(2)}) collective-permute-start(bf16[224,512]{1,0:T(8,128)(2,1)S(1)} %get-tuple-element.184), channel_id=1, source_target_pairs={{0,16},{4,20},{8,24},{12,28},{16,0},{20,4},{24,8},{28,12},{1,17},{... | collective-permute-start | bytes 688136 | tf_op jit(solution)/shard_map/ppermute | solution.py:308
  121.7 11.3 %collective-permute-start.32 = (bf16[224,512]{1,0:T(8,128)(2,1)S(1)}, bf16[224,512]{1,0:T(8,128)(2,1)S(1)}, u32[]{:S(2)}, u32[]{:S(2)}) collective-permute-start(bf16[224,512]{1,0:T(8,128)(2,1)S(1)} %get-tuple-element.183), channel_id=1, source_target_pairs={{0,24},{4,28},{8,16},{12,20},{16,8},{20,12},{24,0},{28,4},{1,25},{... | collective-permute-start | bytes 688136 | tf_op jit(solution)/shard_map/ppermute | solution.py:308
  123.3 9.6 %collective-permute-start.33 = (bf16[176,512]{1,0:T(8,128)(2,1)S(1)}, bf16[176,512]{1,0:T(8,128)(2,1)S(1)}, u32[]{:S(2)}, u32[]{:S(2)}) collective-permute-start(bf16[176,512]{1,0:T(8,128)(2,1)S(1)} %add_convert_fusion.10), channel_id=1, source_target_pairs={{0,2},{1,3},{2,0},{3,1},{4,6},{5,7},{6,4},{7,5},{8,10},{9,11},{10,... | collective-permute-start | bytes 540680 | tf_op jit(solution)/shard_map/ppermute | solution.py:308
  133.2 8.2 %collective-permute-start.34 = (bf16[112,512]{1,0:T(8,128)(2,1)S(1)}, bf16[112,512]{1,0:T(8,128)(2,1)S(1)}, u32[]{:S(2)}, u32[]{:S(2)}) collective-permute-start(bf16[112,512]{1,0:T(8,128)(2,1)S(1)} %get-tuple-element.162), channel_id=1, source_target_pairs={{0,1},{1,0},{2,3},{3,2},{4,5},{5,4},{6,7},{7,6},{8,9},{9,8},{10,11... | collective-permute-start | bytes 344072 | tf_op jit(solution)/shard_map/ppermute | solution.py:308
  133.3 10.2 %collective-permute-start.36 = (bf16[144,512]{1,0:T(8,128)(2,1)S(1)}, bf16[144,512]{1,0:T(8,128)(2,1)S(1)}, u32[]{:S(2)}, u32[]{:S(2)}) collective-permute-start(bf16[144,512]{1,0:T(8,128)(2,1)S(1)} %add_convert_fusion.11.half), channel_id=1, source_target_pairs={{0,1},{1,0},{2,3},{3,2},{4,5},{5,4},{6,7},{7,6},{8,9},{9,8},{10,11... | collective-permute-start | bytes 442376 | tf_op jit(solution)/shard_map/ppermute | solution.py:308
  135.4 14.2 %collective-permute-start.29 = (bf16[336,512]{1,0:T(8,128)(2,1)S(1)}, bf16[336,512]{1,0:T(8,128)(2,1)S(1)}, u32[]{:S(2)}, u32[]{:S(2)}) collective-permute-start(bf16[336,512]{1,0:T(8,128)(2,1)S(1)} %get-tuple-element.153), channel_id=1, source_target_pairs={{0,1},{1,2},{2,3},{3,0},{4,5},{5,6},{6,7},{7,4},{8,9},{9,10},{10,1... | collective-permute-start | bytes 1032200 | tf_op jit(solution)/shard_map/ppermute | solution.py:40
  141.4 8.6 %collective-permute-start.35 = (bf16[112,512]{1,0:T(8,128)(2,1)S(1)}, bf16[112,512]{1,0:T(8,128)(2,1)S(1)}, u32[]{:S(2)}, u32[]{:S(2)}) collective-permute-start(bf16[112,512]{1,0:T(8,128)(2,1)S(1)} %add_convert_fusion.14), channel_id=1, source_target_pairs={{0,2},{1,3},{2,0},{3,1},{4,6},{5,7},{6,4},{7,5},{8,10},{9,11},{10,... | collective-permute-start | bytes 344072 | tf_op jit(solution)/shard_map/ppermute | solution.py:308
  144.8 8.3 %collective-permute-start.37 = (bf16[176,512]{1,0:T(8,128)(2,1)S(1)}, bf16[176,512]{1,0:T(8,128)(2,1)S(1)}, u32[]{:S(2)}, u32[]{:S(2)}) collective-permute-start(bf16[176,512]{1,0:T(8,128)(2,1)S(1)} %add_convert_fusion.9.half), channel_id=1, source_target_pairs={{0,1},{1,0},{2,3},{3,2},{4,5},{5,4},{6,7},{7,6},{8,9},{9,8},{10,11... | collective-permute-start | bytes 540680 | tf_op jit(solution)/shard_map/ppermute | solution.py:308
  (43 other events, 213.1 us)
Sparse Core Ops, SparseCore 0:
  20.5 32.9 all-gather.2

commit v8 on v7

--- a/solution.py
+++ b/solution.py
@@ -472,13 +472,11 @@
 
 def mlp_forward_body(
     mixed,
-    cotangent,
-    cot_halo,
+    cot,
     slab,
     out_slab,
     kept,
     sent,
-    cot,
     actives,
     back_sum,
     vectors,
@@ -496,8 +494,7 @@
     own = WIN - SHIFT
     parts = [slice(r * WIDTH, (r + 1) * WIDTH) for r in range(WIN)]
     lows = []
-    for r, part in enumerate(parts):
-        cot[part, :] = cotangent[SHIFT + r] if r < own else cot_halo[r - own]
+    for part in parts:
         normed, _ = norm_stats(mixed[part, :])
         lows.append((normed * gain + offset).astype(BF))
     normed_low = jnp.concatenate(lows, 0)
@@ -822,19 +819,20 @@
     )
     share_a = like((chips, 4 * depth + SMALL, D), BF)
     share_b = like((chips, 5 * depth + SMALL, D), BF)
-    out_kept, out_sent, cot, actives, back_sum, vectors, same_a, other_a = kernel_call(
+    _, (cot_halo,) = after([mixed], [cot_halo])
+    cot = jnp.concatenate([cot_here[SHIFT:], cot_halo], 0).reshape(TOKENS, D)
+    out_kept, out_sent, actives, back_sum, vectors, same_a, other_a = kernel_call(
         mlp_forward_body,
         [
             like((own * WIDTH, D), F32),
             like((SHIFT * WIDTH, D), BF),
-            like((TOKENS, D), BF),
             like((TOKENS, FF), BF),
             like((TOKENS, D), F32),
             like((SMALL, D), F32),
             share_a,
             share_a,
         ],
-        (mixed, cot_here, cot_halo, mlp_all, jnp.stack(out_pieces)),
+        (mixed, cot, mlp_all, jnp.stack(out_pieces)),
     )
     grad_mixed, grad_win, same_b, other_b = kernel_call(
         mlp_backward_body,

time: 166 us -> 167 us (level); the launches traced: 163 us -> 167 us
  waiting for transfers between devices: 37.4 us -> 42.6 us
    ppermute x35, waiting for transfers between devices: 34.3 us -> 42.5 us  [exchange(): return lax.ppermute(value, axis, [(i, i ^ mask) for i in range(peers)])]
    ppermute x35, starting transfers between devices: 35.6 us -> 32 us  [exchange(): return lax.ppermute(value, axis, [(i, i ^ mask) for i in range(peers)])]
    ppermute x4, waiting for transfers between devices: 3.05 us -> 0.01 us  [shifted_2(): lax.ppermute(value, axis, [(i, (i + by) % peers) for i in range(peers)])]
    ppermute x4, starting transfers between devices: 7.79 us -> 9.73 us  [shifted_2(): lax.ppermute(value, axis, [(i, (i + by) % peers) for i in range(peers)])]
    unnamed x84 -> x82, local copies, waits for them, and re-layouts: 13.1 us -> 11.5 us
  transfers between devices with their start and end apart: 40 -> 40, of which waited for: 16 -> 12; matrix products, arithmetic and copies ran while one was open for 6% -> 7% of each run, Pallas kernels for 18% -> 17%
where the time goes in v8:
time: 167 us
  Pallas kernels  47.5 us (28%)
  waiting for transfers between devices  42.6 us (26%)
  starting transfers between devices  41.8 us (25%)
  local copies, waits for them, and re-layouts  15.6 us (9%)
  between operations  14.8 us (9%)
  other arithmetic  4.76 us (3%)
    pallas_call x14, Pallas kernels, kernel_call(): pl.pallas_call(body, out_shape=tuple(outs), in_specs=in_specs, out_specs=...  47.5 us
    ppermute x35, waiting for transfers between devices, exchange(): return lax.ppermute(value, axis, [(i, i ^ mask) for i in range(peers)])  42.5 us
    ppermute x35, starting transfers between devices, exchange(): return lax.ppermute(value, axis, [(i, i ^ mask) for i in range(peers)])  32 us
    unnamed x82, local copies, waits for them, and re-layouts  11.5 us
    ppermute x4, starting transfers between devices, shifted_2(): lax.ppermute(value, axis, [(i, (i + by) % peers) for i in range(peers)])  9.73 us
  transfers between devices with their start and end apart: 40, of which 12 were waited for; matrix products, arithmetic and copies ran while one was open for 7% of the time, Pallas kernels for 17%

profile of v8, /device:TPU:0, one launch (start us, length us, event | category | flops | bytes accessed | tf_op | source)
XLA Modules:
  0.0 167.0 jit_solution(5260237936551203192)
XLA Ops:
  7.3 2.9 %shard_map.271 = (bf16[288,512]{1,0:T(8,128)(2,1)}, bf16[288,512]{1,0:T(8,128)(2,1)}, bf16[256,512]{1,0:T(8,128)(2,1)}) custom-call(bf16[1,64]{1,0:T(2,128)(2,1)} %bitcast.90, bf16[1,64]{1,0:T(2,128)(2,1)} %bitcast.91, bf16[64,1536]{1,0:T(8,128)(2,1)} %wqkv.1, bf16[2,64]{1,0:T(2,128)(2,1)} %bqv.1, bf16[2,169]{1,0:T(2,128)(2,1)} %bitcast.89, ...), custom_call_target="tpu_custom_call" | custom-call | flops 1024 | bytes 1024 | tf_op jit(solution)/shard_map/pallas_call | solution.py:150
  10.2 2.9 %collective-permute-start.1 = (bf16[288,512]{1,0:T(8,128)(2,1)}, bf16[288,512]{1,0:T(8,128)(2,1)S(1)}, u32[]{:S(2)}, u32[]{:S(2)}) collective-permute-start(bf16[288,512]{1,0:T(8,128)(2,1)} %get-tuple-element.98), channel_id=1, source_target_pairs={{0,8},{4,12},{8,0},{12,4},{16,24},{20,28},{24,16},{28,20},{1,9},{5... | collective-permute-start | bytes 884744 | tf_op jit(solution)/shard_map/ppermute | solution.py:308
  13.1 1.5 collective-permute-start.3
  14.6 1.7 %slice_bitcast_fusion.2 = bf16[3,112,512]{2,1,0:T(8,128)(2,1)} fusion(bf16[1,7,112,512]{3,2,1,0:T(8,128)(2,1)} %param.16), kind=kLoop, calls=%fused_computation.19 | loop fusion | bytes 688128 | tf_op jit(solution)/shard_map/slice | solution.py:772
  16.4 4.1 %collective-permute-start.7 = (bf16[3,112,512]{2,1,0:T(8,128)(2,1)}, bf16[3,112,512]{2,1,0:T(8,128)(2,1)S(1)}, u32[]{:S(2)}, u32[]{:S(2)}) collective-permute-start(bf16[3,112,512]{2,1,0:T(8,128)(2,1)} %slice_bitcast_fusion.2), channel_id=1, source_target_pairs={{0,3},{1,0},{2,1},{3,2},{4,7},{5,4},{6,5},{7,6},{8,11},{9,8},{10,9... | collective-permute-start | bytes 1032200 | tf_op jit(solution)/shard_map/ppermute | solution.py:40
  21.7 6.4 %collective-permute-done.3 = bf16[288,512]{1,0:T(8,128)(2,1)S(1)} collective-permute-done((bf16[288,512]{1,0:T(8,128)(2,1)}, bf16[288,512]{1,0:T(8,128)(2,1)S(1)}, u32[]{:S(2)}, u32[]{:S(2)}) %collective-permute-start.3) | collective-permute-done | bytes 294944 | tf_op jit(solution)/shard_map/ppermute | solution.py:308
  28.9 3.7 %collective-permute-start.8 = (bf16[3,112,512]{2,1,0:T(8,128)(2,1)S(1)}, bf16[3,112,512]{2,1,0:T(8,128)(2,1)S(1)}, u32[]{:S(2)}, u32[]{:S(2)}) collective-permute-start(bf16[3,112,512]{2,1,0:T(8,128)(2,1)S(1)} %slice_bitcast_fusion.1), channel_id=1, source_target_pairs={{0,3},{1,0},{2,1},{3,2},{4,7},{5,4},{6,5},{7,6},{8,11},{9,8},{10,9... | collective-permute-start | bytes 1032200 | tf_op jit(solution)/shard_map/ppermute | solution.py:40
  33.6 1.6 collective-permute-start.12
  40.6 2.4 %shard_map.272 = (bf16[896,512]{1,0:T(8,128)(2,1)S(1)}, bf16[896,512]{1,0:T(8,128)(2,1)S(1)}, bf16[896,512]{1,0:T(8,128)(2,1)S(1)}, bf16[896,512]{1,0:T(8,128)(2,1)S(1)}) custom-call(bf16[7,112,512]{2,1,0:T(8,128)(2,1)S(1)} %bitcast.80, bf16[3,112,512]{2,1,0:T(8,128)(2,1)S(1)} %collective-permute-done.7.halo, ...), custom_call_target="tpu_custom_call" | custom-call | flops 1024 | bytes 1024 | tf_op jit(solution)/shard_map/pallas_call | solution.py:150
  43.3 7.1 %shard_map.273 = (bf16[8,4,112,256]{3,2,1,0:T(8,128)(2,1)S(1)}, bf16[784,512]{1,0:T(8,128)(2,1)S(1)}, f32[784,512]{1,0:T(8,128)S(1)}) custom-call(bf16[8,288,512]{2,1,0:T(8,128)(2,1)S(1)} %bitcast_dynamic-update-slice_fusion.slab.attn_slab, f32[16,56,128]{2,1,0:T(8,128)S(1)} %broadcast_in_dim.35.reg_rows, f32[16,1,256]{2,1,0:T(1,128)S(1)} %tile.9.reg_lanes, ...), custom_call_target="tpu_custom_call" | custom-call | flops 1024 | bytes 1024 | tf_op jit(solution)/shard_map/pallas_call | solution.py:150
  53.0 1.8 %collective-permute-done.14 = bf16[256,512]{1,0:T(8,128)(2,1)S(1)} collective-permute-done((bf16[256,512]{1,0:T(8,128)(2,1)S(1)}, bf16[256,512]{1,0:T(8,128)(2,1)S(1)}, u32[]{:S(2)}, u32[]{:S(2)}) %collective-permute-start.14) | collective-permute-done | bytes 262176 | tf_op jit(solution)/shard_map/ppermute | solution.py:308
  60.3 1.6 copy-done.15
  61.9 1.7 copy-done.16
  63.5 13.8 %shard_map.274 = (f32[448,512]{1,0:T(8,128)S(1)}, bf16[336,512]{1,0:T(8,128)(2,1)S(1)}, bf16[784,2048]{1,0:T(8,128)(2,1)S(1)}, f32[784,512]{1,0:T(8,128)S(1)}, f...) custom-call(f32[784,512]{1,0:T(8,128)S(1)} %copy-done.13, ...), custom_call_target="tpu_custom_call" | custom-call | flops 1024 | bytes 1024 | tf_op jit(solution)/shard_map/pallas_call | solution.py:150
  77.5 5.5 %shard_map.275 = (f32[784,512]{1,0:T(8,128)S(1)}, bf16[896,512]{1,0:T(8,128)(2,1)S(1)}, bf16[4,352,512]{2,1,0:T(8,128)(2,1)S(1)}, bf16[4,352,512]{2,1,0:T(8,128)(2,1)S(1)}) custom-call(f32[784,512]{1,0:T(8,128)S(1)} %copy-done.13, bf16[784,512]{1,0:T(8,128)(2,1)S(1)} %bitcast.84, bf16[784,2048]{1,0:T(8,128)(2,1)S(1)} %get-tuple-element.116.actives, ...), custom_call_target="tpu_custom_call" | custom-call | flops 1024 | bytes 1024 | tf_op jit(solution)/shard_map/pallas_call | solution.py:150
  84.9 2.4 %collective-permute-start.20 = (bf16[288,512]{1,0:T(8,128)(2,1)S(1)}, bf16[288,512]{1,0:T(8,128)(2,1)S(1)}, u32[]{:S(2)}, u32[]{:S(2)}) collective-permute-start(bf16[288,512]{1,0:T(8,128)(2,1)S(1)} %get-tuple-element.123), channel_id=1, source_target_pairs={{0,24},{4,28},{8,16},{12,20},{16,8},{20,12},{24,0},{28,4},{1,25},{... | collective-permute-start | bytes 884744 | tf_op jit(solution)/shard_map/ppermute | solution.py:308
  87.3 3.0 %shard_map.277 = (bf16[448,1536]{1,0:T(8,128)(2,1)S(1)}, f32[4,56,256]{2,1,0:T(8,128)S(1)}) custom-call(bf16[896,512]{1,0:T(8,128)(2,1)S(1)} %copy-done.3, bf16[896,512]{1,0:T(8,128)(2,1)S(1)} %copy-done.5, bf16[896,512]{1,0:T(8,128)(2,1)S(1)} %copy-done.7, bf16[8,4,112,256]{3,2,1,0:T(8,128)(2,1)S(1)} %copy-done.9, ...), custom_call_target="tpu_custom_call" | custom-call | flops 1024 | bytes 1024 | tf_op jit(solution)/shard_map/pallas_call | solution.py:150
  90.7 3.0 %shard_map.278 = (bf16[448,1536]{1,0:T(8,128)(2,1)S(1)}, f32[4,56,256]{2,1,0:T(8,128)S(1)}) custom-call(bf16[896,512]{1,0:T(8,128)(2,1)S(1)} %copy-done.3, bf16[896,512]{1,0:T(8,128)(2,1)S(1)} %copy-done.5, bf16[896,512]{1,0:T(8,128)(2,1)S(1)} %copy-done.7, bf16[8,4,112,256]{3,2,1,0:T(8,128)(2,1)S(1)} %copy-done.9, ...), custom_call_target="tpu_custom_call" | custom-call | flops 1024 | bytes 1024 | tf_op jit(solution)/shard_map/pallas_call | solution.py:150
  93.7 5.6 %collective-permute-done.19.refs_1_ = bf16[288,512]{1,0:T(8,128)(2,1)S(1)} collective-permute-done((bf16[288,512]{1,0:T(8,128)(2,1)S(1)}, bf16[288,512]{1,0:T(8,128)(2,1)S(1)}, u32[]{:S(2)}, u32[]{:S(2)}) %collective-permute-start.19) | collective-permute-done | bytes 294944 | tf_op jit(solution)/shard_map/ppermute | solution.py:308
  99.5 1.7 %collective-permute-start.23 = (bf16[352,512]{1,0:T(8,128)(2,1)S(1)}, bf16[352,512]{1,0:T(8,128)(2,1)S(1)}, u32[]{:S(2)}, u32[]{:S(2)}) collective-permute-start(bf16[352,512]{1,0:T(8,128)(2,1)S(1)} %get-tuple-element.143), channel_id=1, source_target_pairs={{0,8},{4,12},{8,0},{12,4},{16,24},{20,28},{24,16},{28,20},{1,9},{5... | collective-permute-start | bytes 1081352 | tf_op jit(solution)/shard_map/ppermute | solution.py:308
  103.1 5.1 %shard_map.279 = (f32[448,512]{1,0:T(8,128)S(1)}, bf16[336,512]{1,0:T(8,128)(2,1)S(1)}, bf16[4,224,512]{2,1,0:T(8,128)(2,1)S(1)}, bf16[4,224,512]{2,1,0:T(8,128)(2,1)S(1)}) custom-call(f32[784,512]{1,0:T(8,128)S(1)} %get-tuple-element.137.grad_mixed, bf16[7,112,512]{2,1,0:T(8,128)(2,1)S(1)} %bitcast.82, ...), custom_call_target="tpu_custom_call" | custom-call | flops 1024 | bytes 1024 | tf_op jit(solution)/shard_map/pallas_call | solution.py:150
  108.2 2.1 %collective-permute-start.27 = (bf16[144,512]{1,0:T(8,128)(2,1)S(1)}, bf16[144,512]{1,0:T(8,128)(2,1)S(1)}, u32[]{:S(2)}, u32[]{:S(2)}) collective-permute-start(bf16[144,512]{1,0:T(8,128)(2,1)S(1)} %add_convert_fusion.12), channel_id=1, source_target_pairs={{0,2},{1,3},{2,0},{3,1},{4,6},{5,7},{6,4},{7,5},{8,10},{9,11},{10,... | collective-permute-start | bytes 442376 | tf_op jit(solution)/shard_map/ppermute | solution.py:308
  111.2 6.6 %collective-permute-done.25.refs_2_ = bf16[352,512]{1,0:T(8,128)(2,1)S(1)} collective-permute-done((bf16[352,512]{1,0:T(8,128)(2,1)S(1)}, bf16[352,512]{1,0:T(8,128)(2,1)S(1)}, u32[]{:S(2)}, u32[]{:S(2)}) %collective-permute-start.25) | collective-permute-done | bytes 360480 | tf_op jit(solution)/shard_map/ppermute | solution.py:308
  118.0 1.7 %collective-permute-start.28 = (bf16[176,512]{1,0:T(8,128)(2,1)S(1)}, bf16[176,512]{1,0:T(8,128)(2,1)S(1)}, u32[]{:S(2)}, u32[]{:S(2)}) collective-permute-start(bf16[176,512]{1,0:T(8,128)(2,1)S(1)} %get-tuple-element.146), channel_id=1, source_target_pairs={{0,1},{1,0},{2,3},{3,2},{4,5},{5,4},{6,7},{7,6},{8,9},{9,8},{10,11... | collective-permute-start | bytes 540680 | tf_op jit(solution)/shard_map/ppermute | solution.py:308
  120.7 1.6 collective-permute-start.31
  124.7 5.7 %collective-permute-done.33 = bf16[176,512]{1,0:T(8,128)(2,1)S(1)} collective-permute-done((bf16[176,512]{1,0:T(8,128)(2,1)S(1)}, bf16[176,512]{1,0:T(8,128)(2,1)S(1)}, u32[]{:S(2)}, u32[]{:S(2)}) %collective-permute-start.33) | collective-permute-done | bytes 180256 | tf_op jit(solution)/shard_map/ppermute | solution.py:308
  130.7 4.3 %collective-permute-start.34 = (bf16[112,512]{1,0:T(8,128)(2,1)S(1)}, bf16[112,512]{1,0:T(8,128)(2,1)S(1)}, u32[]{:S(2)}, u32[]{:S(2)}) collective-permute-start(bf16[112,512]{1,0:T(8,128)(2,1)S(1)} %get-tuple-element.162), channel_id=1, source_target_pairs={{0,1},{1,0},{2,3},{3,2},{4,5},{5,4},{6,7},{7,6},{8,9},{9,8},{10,11... | collective-permute-start | bytes 344072 | tf_op jit(solution)/shard_map/ppermute | solution.py:308
  135.1 2.0 %collective-permute-start.29 = (bf16[336,512]{1,0:T(8,128)(2,1)S(1)}, bf16[336,512]{1,0:T(8,128)(2,1)S(1)}, u32[]{:S(2)}, u32[]{:S(2)}) collective-permute-start(bf16[336,512]{1,0:T(8,128)(2,1)S(1)} %get-tuple-element.153), channel_id=1, source_target_pairs={{0,1},{1,2},{2,3},{3,0},{4,5},{5,6},{6,7},{7,4},{8,9},{9,10},{10,1... | collective-permute-start | bytes 1032200 | tf_op jit(solution)/shard_map/ppermute | solution.py:40
  137.1 5.8 %collective-permute-done.34 = bf16[112,512]{1,0:T(8,128)(2,1)S(1)} collective-permute-done((bf16[112,512]{1,0:T(8,128)(2,1)S(1)}, bf16[112,512]{1,0:T(8,128)(2,1)S(1)}, u32[]{:S(2)}, u32[]{:S(2)}) %collective-permute-start.34) | collective-permute-done | bytes 114720 | tf_op jit(solution)/shard_map/ppermute | solution.py:308
  144.4 6.0 %collective-permute-done.36.back = bf16[144,512]{1,0:T(8,128)(2,1)S(1)} collective-permute-done((bf16[144,512]{1,0:T(8,128)(2,1)S(1)}, bf16[144,512]{1,0:T(8,128)(2,1)S(1)}, u32[]{:S(2)}, u32[]{:S(2)}) %collective-permute-start.36) | collective-permute-done | bytes 147488 | tf_op jit(solution)/shard_map/ppermute | solution.py:308
  151.9 2.1 %collective-permute-start.38 = (bf16[112,512]{1,0:T(8,128)(2,1)S(1)}, bf16[112,512]{1,0:T(8,128)(2,1)S(1)}, u32[]{:S(2)}, u32[]{:S(2)}) collective-permute-start(bf16[112,512]{1,0:T(8,128)(2,1)S(1)} %add_convert_fusion.13.half), channel_id=1, source_target_pairs={{0,1},{1,0},{2,3},{3,2},{4,5},{5,4},{6,7},{7,6},{8,9},{9,8},{10,11... | collective-permute-start | bytes 344072 | tf_op jit(solution)/shard_map/ppermute | solution.py:308
  155.3 2.0 %collective-permute-done.37.back = bf16[176,512]{1,0:T(8,128)(2,1)S(1)} collective-permute-done((bf16[176,512]{1,0:T(8,128)(2,1)S(1)}, bf16[176,512]{1,0:T(8,128)(2,1)S(1)}, u32[]{:S(2)}, u32[]{:S(2)}) %collective-permute-start.37) | collective-permute-done | bytes 180256 | tf_op jit(solution)/shard_map/ppermute | solution.py:308
  (174 shorter events, 33.0 us)
Async XLA Ops:
  7.2 50.5 %all-gather.3.cloned.1.call-start = ((), (), s32[]{:S(2)}) async-start(), calls=%async_computation | async-start | bytes 2654208 | tf_op jit(solution)/shard_map/all_gather | solution.py:770
  10.2 11.4 %collective-permute-start.1 = (bf16[288,512]{1,0:T(8,128)(2,1)}, bf16[288,512]{1,0:T(8,128)(2,1)S(1)}, u32[]{:S(2)}, u32[]{:S(2)}) collective-permute-start(bf16[288,512]{1,0:T(8,128)(2,1)} %get-tuple-element.98), channel_id=1, source_target_pairs={{0,8},{4,12},{8,0},{12,4},{16,24},{20,28},{24,16},{28,20},{1,9},{5... | collective-permute-start | bytes 884744 | tf_op jit(solution)/shard_map/ppermute | solution.py:308
  13.1 15.0 %collective-permute-start.3 = (bf16[288,512]{1,0:T(8,128)(2,1)}, bf16[288,512]{1,0:T(8,128)(2,1)S(1)}, u32[]{:S(2)}, u32[]{:S(2)}) collective-permute-start(bf16[288,512]{1,0:T(8,128)(2,1)} %get-tuple-element.98), channel_id=1, source_target_pairs={{0,16},{4,20},{8,24},{12,28},{16,0},{20,4},{24,8},{28,12},{1,17},{... | collective-permute-start | bytes 884744 | tf_op jit(solution)/shard_map/ppermute | solution.py:308
  14.6 13.5 %collective-permute-start.5 = (bf16[288,512]{1,0:T(8,128)(2,1)}, bf16[288,512]{1,0:T(8,128)(2,1)S(1)}, u32[]{:S(2)}, u32[]{:S(2)}) collective-permute-start(bf16[288,512]{1,0:T(8,128)(2,1)} %get-tuple-element.98), channel_id=1, source_target_pairs={{0,24},{4,28},{8,16},{12,20},{16,8},{20,12},{24,0},{28,4},{1,25},{... | collective-permute-start | bytes 884744 | tf_op jit(solution)/shard_map/ppermute | solution.py:308
  14.6 14.2 %collective-permute-start = (bf16[288,512]{1,0:T(8,128)(2,1)}, bf16[288,512]{1,0:T(8,128)(2,1)S(1)}, u32[]{:S(2)}, u32[]{:S(2)}) collective-permute-start(bf16[288,512]{1,0:T(8,128)(2,1)} %get-tuple-element.98), channel_id=1, source_target_pairs={{0,4},{4,0},{8,12},{12,8},{16,20},{20,16},{24,28},{28,24},{1,5},{5... | collective-permute-start | bytes 884744 | tf_op jit(solution)/shard_map/ppermute | solution.py:308
  16.4 23.2 %collective-permute-start.7 = (bf16[3,112,512]{2,1,0:T(8,128)(2,1)}, bf16[3,112,512]{2,1,0:T(8,128)(2,1)S(1)}, u32[]{:S(2)}, u32[]{:S(2)}) collective-permute-start(bf16[3,112,512]{2,1,0:T(8,128)(2,1)} %slice_bitcast_fusion.2), channel_id=1, source_target_pairs={{0,3},{1,0},{2,1},{3,2},{4,7},{5,4},{6,5},{7,6},{8,11},{9,8},{10,9... | collective-permute-start | bytes 1032200 | tf_op jit(solution)/shard_map/ppermute | solution.py:40
  21.5 11.0 %collective-permute-start.2 = (bf16[288,512]{1,0:T(8,128)(2,1)S(1)}, bf16[288,512]{1,0:T(8,128)(2,1)S(1)}, u32[]{:S(2)}, u32[]{:S(2)}) collective-permute-start(bf16[288,512]{1,0:T(8,128)(2,1)S(1)} %collective-permute-done.1), channel_id=1, source_target_pairs={{0,4},{4,0},{8,12},{12,8},{16,20},{20,16},{24,28},{28,24},{1,5},{5... | collective-permute-start | bytes 884744 | tf_op jit(solution)/shard_map/ppermute | solution.py:308
  28.9 22.5 %collective-permute-start.8 = (bf16[3,112,512]{2,1,0:T(8,128)(2,1)S(1)}, bf16[3,112,512]{2,1,0:T(8,128)(2,1)S(1)}, u32[]{:S(2)}, u32[]{:S(2)}) collective-permute-start(bf16[3,112,512]{2,1,0:T(8,128)(2,1)S(1)} %slice_bitcast_fusion.1), channel_id=1, source_target_pairs={{0,3},{1,0},{2,1},{3,2},{4,7},{5,4},{6,5},{7,6},{8,11},{9,8},{10,9... | collective-permute-start | bytes 1032200 | tf_op jit(solution)/shard_map/ppermute | solution.py:40
  32.6 22.3 %collective-permute-start.9 = (bf16[256,512]{1,0:T(8,128)(2,1)}, bf16[256,512]{1,0:T(8,128)(2,1)S(1)}, u32[]{:S(2)}, u32[]{:S(2)}) collective-permute-start(bf16[256,512]{1,0:T(8,128)(2,1)} %get-tuple-element.112), channel_id=1, source_target_pairs={{0,4},{4,0},{8,12},{12,8},{16,20},{20,16},{24,28},{28,24},{1,5},{5... | collective-permute-start | bytes 786440 | tf_op jit(solution)/shard_map/ppermute | solution.py:308
  32.6 19.8 %collective-permute-start.10 = (bf16[256,512]{1,0:T(8,128)(2,1)}, bf16[256,512]{1,0:T(8,128)(2,1)S(1)}, u32[]{:S(2)}, u32[]{:S(2)}) collective-permute-start(bf16[256,512]{1,0:T(8,128)(2,1)} %get-tuple-element.112), channel_id=1, source_target_pairs={{0,8},{4,12},{8,0},{12,4},{16,24},{20,28},{24,16},{28,20},{1,9},{5... | collective-permute-start | bytes 786440 | tf_op jit(solution)/shard_map/ppermute | solution.py:308
  33.6 18.9 %collective-permute-start.12 = (bf16[256,512]{1,0:T(8,128)(2,1)}, bf16[256,512]{1,0:T(8,128)(2,1)S(1)}, u32[]{:S(2)}, u32[]{:S(2)}) collective-permute-start(bf16[256,512]{1,0:T(8,128)(2,1)} %get-tuple-element.112), channel_id=1, source_target_pairs={{0,16},{4,20},{8,24},{12,28},{16,0},{20,4},{24,8},{28,12},{1,17},{... | collective-permute-start | bytes 786440 | tf_op jit(solution)/shard_map/ppermute | solution.py:308
  39.6 15.3 %collective-permute-start.14 = (bf16[256,512]{1,0:T(8,128)(2,1)S(1)}, bf16[256,512]{1,0:T(8,128)(2,1)S(1)}, u32[]{:S(2)}, u32[]{:S(2)}) collective-permute-start(bf16[256,512]{1,0:T(8,128)(2,1)S(1)} %copy-done.33), channel_id=1, source_target_pairs={{0,24},{4,28},{8,16},{12,20},{16,8},{20,12},{24,0},{28,4},{1,25},{... | collective-permute-start | bytes 786440 | tf_op jit(solution)/shard_map/ppermute | solution.py:308
  83.0 7.3 %collective-permute-start.21 = (bf16[4,352,512]{2,1,0:T(8,128)(2,1)S(1)}, bf16[4,352,512]{2,1,0:T(8,128)(2,1)S(1)}, u32[]{:S(2)}, u32[]{:S(2)}) collective-permute-start(bf16[4,352,512]{2,1,0:T(8,128)(2,1)S(1)} %get-tuple-element.128), channel_id=1, source_target_pairs={{0,4},{4,0},{8,12},{12,8},{16,20},{20,16},{24,28},{28,24},{1,5},{5... | collective-permute-start | bytes 4325384 | tf_op jit(solution)/shard_map/ppermute | solution.py:308
  83.7 9.9 %collective-permute-start.18 = (bf16[288,512]{1,0:T(8,128)(2,1)S(1)}, bf16[288,512]{1,0:T(8,128)(2,1)S(1)}, u32[]{:S(2)}, u32[]{:S(2)}) collective-permute-start(bf16[288,512]{1,0:T(8,128)(2,1)S(1)} %get-tuple-element.121), channel_id=1, source_target_pairs={{0,8},{4,12},{8,0},{12,4},{16,24},{20,28},{24,16},{28,20},{1,9},{5... | collective-permute-start | bytes 884744 | tf_op jit(solution)/shard_map/ppermute | solution.py:308
  84.1 15.1 %collective-permute-start.19 = (bf16[288,512]{1,0:T(8,128)(2,1)S(1)}, bf16[288,512]{1,0:T(8,128)(2,1)S(1)}, u32[]{:S(2)}, u32[]{:S(2)}) collective-permute-start(bf16[288,512]{1,0:T(8,128)(2,1)S(1)} %get-tuple-element.122), channel_id=1, source_target_pairs={{0,16},{4,20},{8,24},{12,28},{16,0},{20,4},{24,8},{28,12},{1,17},{... | collective-permute-start | bytes 884744 | tf_op jit(solution)/shard_map/ppermute | solution.py:308
  84.9 14.3 %collective-permute-start.20 = (bf16[288,512]{1,0:T(8,128)(2,1)S(1)}, bf16[288,512]{1,0:T(8,128)(2,1)S(1)}, u32[]{:S(2)}, u32[]{:S(2)}) collective-permute-start(bf16[288,512]{1,0:T(8,128)(2,1)S(1)} %get-tuple-element.123), channel_id=1, source_target_pairs={{0,24},{4,28},{8,16},{12,20},{16,8},{20,12},{24,0},{28,4},{1,25},{... | collective-permute-start | bytes 884744 | tf_op jit(solution)/shard_map/ppermute | solution.py:308
  87.3 15.8 %collective-permute-start.16 = (bf16[336,512]{1,0:T(8,128)(2,1)S(1)}, bf16[336,512]{1,0:T(8,128)(2,1)S(1)}, u32[]{:S(2)}, u32[]{:S(2)}) collective-permute-start(bf16[336,512]{1,0:T(8,128)(2,1)S(1)} %get-tuple-element.113), channel_id=1, source_target_pairs={{0,1},{1,2},{2,3},{3,0},{4,5},{5,6},{6,7},{7,4},{8,9},{9,10},{10,1... | collective-permute-start | bytes 1032200 | tf_op jit(solution)/shard_map/ppermute | solution.py:40
  99.4 8.7 %collective-permute-start.22 = (bf16[144,512]{1,0:T(8,128)(2,1)S(1)}, bf16[144,512]{1,0:T(8,128)(2,1)S(1)}, u32[]{:S(2)}, u32[]{:S(2)}) collective-permute-start(bf16[144,512]{1,0:T(8,128)(2,1)S(1)} %get-tuple-element.136), channel_id=1, source_target_pairs={{0,1},{1,0},{2,3},{3,2},{4,5},{5,4},{6,7},{7,6},{8,9},{9,8},{10,11... | collective-permute-start | bytes 442376 | tf_op jit(solution)/shard_map/ppermute | solution.py:308
  99.5 11.4 %collective-permute-start.23 = (bf16[352,512]{1,0:T(8,128)(2,1)S(1)}, bf16[352,512]{1,0:T(8,128)(2,1)S(1)}, u32[]{:S(2)}, u32[]{:S(2)}) collective-permute-start(bf16[352,512]{1,0:T(8,128)(2,1)S(1)} %get-tuple-element.143), channel_id=1, source_target_pairs={{0,8},{4,12},{8,0},{12,4},{16,24},{20,28},{24,16},{28,20},{1,9},{5... | collective-permute-start | bytes 1081352 | tf_op jit(solution)/shard_map/ppermute | solution.py:308
  101.2 9.9 %collective-permute-start.24 = (bf16[352,512]{1,0:T(8,128)(2,1)S(1)}, bf16[352,512]{1,0:T(8,128)(2,1)S(1)}, u32[]{:S(2)}, u32[]{:S(2)}) collective-permute-start(bf16[352,512]{1,0:T(8,128)(2,1)S(1)} %get-tuple-element.144), channel_id=1, source_target_pairs={{0,16},{4,20},{8,24},{12,28},{16,0},{20,4},{24,8},{28,12},{1,17},{... | collective-permute-start | bytes 1081352 | tf_op jit(solution)/shard_map/ppermute | solution.py:308
  101.7 16.1 %collective-permute-start.25 = (bf16[352,512]{1,0:T(8,128)(2,1)S(1)}, bf16[352,512]{1,0:T(8,128)(2,1)S(1)}, u32[]{:S(2)}, u32[]{:S(2)}) collective-permute-start(bf16[352,512]{1,0:T(8,128)(2,1)S(1)} %get-tuple-element.145), channel_id=1, source_target_pairs={{0,24},{4,28},{8,16},{12,20},{16,8},{20,12},{24,0},{28,4},{1,25},{... | collective-permute-start | bytes 1081352 | tf_op jit(solution)/shard_map/ppermute | solution.py:308
  108.2 15.3 %collective-permute-start.27 = (bf16[144,512]{1,0:T(8,128)(2,1)S(1)}, bf16[144,512]{1,0:T(8,128)(2,1)S(1)}, u32[]{:S(2)}, u32[]{:S(2)}) collective-permute-start(bf16[144,512]{1,0:T(8,128)(2,1)S(1)} %add_convert_fusion.12), channel_id=1, source_target_pairs={{0,2},{1,3},{2,0},{3,1},{4,6},{5,7},{6,4},{7,5},{8,10},{9,11},{10,... | collective-permute-start | bytes 442376 | tf_op jit(solution)/shard_map/ppermute | solution.py:308
  110.3 9.4 %collective-permute-start.26 = (bf16[4,224,512]{2,1,0:T(8,128)(2,1)S(1)}, bf16[4,224,512]{2,1,0:T(8,128)(2,1)S(1)}, u32[]{:S(2)}, u32[]{:S(2)}) collective-permute-start(bf16[4,224,512]{2,1,0:T(8,128)(2,1)S(1)} %get-tuple-element.149), channel_id=1, source_target_pairs={{0,4},{4,0},{8,12},{12,8},{16,20},{20,16},{24,28},{28,24},{1,5},{5... | collective-permute-start | bytes 2752520 | tf_op jit(solution)/shard_map/ppermute | solution.py:308
  119.9 10.5 %collective-permute-start.30 = (bf16[224,512]{1,0:T(8,128)(2,1)S(1)}, bf16[224,512]{1,0:T(8,128)(2,1)S(1)}, u32[]{:S(2)}, u32[]{:S(2)}) collective-permute-start(bf16[224,512]{1,0:T(8,128)(2,1)S(1)} %get-tuple-element.185), channel_id=1, source_target_pairs={{0,8},{4,12},{8,0},{12,4},{16,24},{20,28},{24,16},{28,20},{1,9},{5... | collective-permute-start | bytes 688136 | tf_op jit(solution)/shard_map/ppermute | solution.py:308
  120.7 9.7 %collective-permute-start.31 = (bf16[224,512]{1,0:T(8,128)(2,1)S(1)}, bf16[224,512]{1,0:T(8,128)(2,1)S(1)}, u32[]{:S(2)}, u32[]{:S(2)}) collective-permute-start(bf16[224,512]{1,0:T(8,128)(2,1)S(1)} %get-tuple-element.184), channel_id=1, source_target_pairs={{0,16},{4,20},{8,24},{12,28},{16,0},{20,4},{24,8},{28,12},{1,17},{... | collective-permute-start | bytes 688136 | tf_op jit(solution)/shard_map/ppermute | solution.py:308
  122.3 8.2 %collective-permute-start.32 = (bf16[224,512]{1,0:T(8,128)(2,1)S(1)}, bf16[224,512]{1,0:T(8,128)(2,1)S(1)}, u32[]{:S(2)}, u32[]{:S(2)}) collective-permute-start(bf16[224,512]{1,0:T(8,128)(2,1)S(1)} %get-tuple-element.183), channel_id=1, source_target_pairs={{0,24},{4,28},{8,16},{12,20},{16,8},{20,12},{24,0},{28,4},{1,25},{... | collective-permute-start | bytes 688136 | tf_op jit(solution)/shard_map/ppermute | solution.py:308
  124.0 6.5 %collective-permute-start.33 = (bf16[176,512]{1,0:T(8,128)(2,1)S(1)}, bf16[176,512]{1,0:T(8,128)(2,1)S(1)}, u32[]{:S(2)}, u32[]{:S(2)}) collective-permute-start(bf16[176,512]{1,0:T(8,128)(2,1)S(1)} %add_convert_fusion.10), channel_id=1, source_target_pairs={{0,2},{1,3},{2,0},{3,1},{4,6},{5,7},{6,4},{7,5},{8,10},{9,11},{10,... | collective-permute-start | bytes 540680 | tf_op jit(solution)/shard_map/ppermute | solution.py:308
  130.7 12.3 %collective-permute-start.34 = (bf16[112,512]{1,0:T(8,128)(2,1)S(1)}, bf16[112,512]{1,0:T(8,128)(2,1)S(1)}, u32[]{:S(2)}, u32[]{:S(2)}) collective-permute-start(bf16[112,512]{1,0:T(8,128)(2,1)S(1)} %get-tuple-element.162), channel_id=1, source_target_pairs={{0,1},{1,0},{2,3},{3,2},{4,5},{5,4},{6,7},{7,6},{8,9},{9,8},{10,11... | collective-permute-start | bytes 344072 | tf_op jit(solution)/shard_map/ppermute | solution.py:308
  135.0 15.3 %collective-permute-start.36 = (bf16[144,512]{1,0:T(8,128)(2,1)S(1)}, bf16[144,512]{1,0:T(8,128)(2,1)S(1)}, u32[]{:S(2)}, u32[]{:S(2)}) collective-permute-start(bf16[144,512]{1,0:T(8,128)(2,1)S(1)} %add_convert_fusion.11.half), channel_id=1, source_target_pairs={{0,1},{1,0},{2,3},{3,2},{4,5},{5,4},{6,7},{7,6},{8,9},{9,8},{10,11... | collective-permute-start | bytes 442376 | tf_op jit(solution)/shard_map/ppermute | solution.py:308
  135.1 16.7 %collective-permute-start.29 = (bf16[336,512]{1,0:T(8,128)(2,1)S(1)}, bf16[336,512]{1,0:T(8,128)(2,1)S(1)}, u32[]{:S(2)}, u32[]{:S(2)}) collective-permute-start(bf16[336,512]{1,0:T(8,128)(2,1)S(1)} %get-tuple-element.153), channel_id=1, source_target_pairs={{0,1},{1,2},{2,3},{3,0},{4,5},{5,6},{6,7},{7,4},{8,9},{9,10},{10,1... | collective-permute-start | bytes 1032200 | tf_op jit(solution)/shard_map/ppermute | solution.py:40
  143.0 8.9 %collective-permute-start.35 = (bf16[112,512]{1,0:T(8,128)(2,1)S(1)}, bf16[112,512]{1,0:T(8,128)(2,1)S(1)}, u32[]{:S(2)}, u32[]{:S(2)}) collective-permute-start(bf16[112,512]{1,0:T(8,128)(2,1)S(1)} %add_convert_fusion.14), channel_id=1, source_target_pairs={{0,2},{1,3},{2,0},{3,1},{4,6},{5,7},{6,4},{7,5},{8,10},{9,11},{10,... | collective-permute-start | bytes 344072 | tf_op jit(solution)/shard_map/ppermute | solution.py:308
  151.9 6.8 %collective-permute-start.38 = (bf16[112,512]{1,0:T(8,128)(2,1)S(1)}, bf16[112,512]{1,0:T(8,128)(2,1)S(1)}, u32[]{:S(2)}, u32[]{:S(2)}) collective-permute-start(bf16[112,512]{1,0:T(8,128)(2,1)S(1)} %add_convert_fusion.13.half), channel_id=1, source_target_pairs={{0,1},{1,0},{2,3},{3,2},{4,5},{5,4},{6,7},{7,6},{8,9},{9,8},{10,11... | collective-permute-start | bytes 344072 | tf_op jit(solution)/shard_map/ppermute | solution.py:308
  (42 other events, 248.5 us)
Sparse Core Ops, SparseCore 0:
  20.6 33.8 all-gather.2
